TPU v7x, 32 devices: a whole 2x2x4 slice. The times are simulated.
32 devices in a mesh: group: 4 (over y, x), replica: 8 (over z, core).
Axes of the slice: x: 2, y: 2, z: 4, core: 2. Of those that a mesh axis runs over, the one named last changes fastest.
Arguments:
- inputs: bfloat16 [16, 1024, 2560], P('replica', 'group'), may hold values from -6 to 6
- segment_ids: int32 [16, 1024], P('replica'), may hold values from 0 to 4, as said below
- adapter_ids: int32 [16], P('replica'), may hold values from 0 to 7
- gain_mix: float32 [2560], replicated, may hold values from 0.25 to 1.75
- gain_mlp: float32 [2560], replicated, may hold values from 0.25 to 1.75
- w_branch: bfloat16 [2560, 2560], P(None, 'group'), may hold values from -0.125 to 0.125
- w_input: bfloat16 [2560, 2560], P(None, 'group'), may hold values from -0.125 to 0.125
- conv_taps: float32 [4, 2560], replicated, may hold values from -2.5 to 2.5
- decay_heads: bfloat16 [10, 256, 256], replicated, may hold values from -0.375 to 0.375
- admit_heads: bfloat16 [10, 256, 256], replicated, may hold values from -0.375 to 0.375
- decay_param: float32 [2560], replicated, may hold values from -9.5 to -3.5, as said below
- w_mixer: bfloat16 [2560, 2560], P('group'), may hold values from -0.25 to 0.25
- w_gate: bfloat16 [2560, 7680], P(None, 'group'), may hold values from -0.125 to 0.125
- w_upper: bfloat16 [2560, 7680], P(None, 'group'), may hold values from -0.125 to 0.125
- w_down: bfloat16 [7680, 2560], P('group'), may hold values from -0.09375 to 0.09375
- down_branch: bfloat16 [8, 2560, 16], P(None, 'group'), may hold values from -0.125 to 0.125
- lift_branch: bfloat16 [8, 16, 2560], P(None, None, 'group'), may hold values from -0.75 to 0.75
- down_input: bfloat16 [8, 2560, 16], P(None, 'group'), may hold values from -0.125 to 0.125
- lift_input: bfloat16 [8, 16, 2560], P(None, None, 'group'), may hold values from -0.75 to 0.75
- down_decay: bfloat16 [8, 2560, 16], P(None, 'group'), may hold values from -0.125 to 0.125
- lift_decay: bfloat16 [8, 16, 2560], P(None, None, 'group'), may hold values from -0.75 to 0.75
- down_admit: bfloat16 [8, 2560, 16], P(None, 'group'), may hold values from -0.125 to 0.125
- lift_admit: bfloat16 [8, 16, 2560], P(None, None, 'group'), may hold values from -0.75 to 0.75
- down_mixer: bfloat16 [8, 2560, 16], P(None, 'group'), may hold values from -0.125 to 0.125
- lift_mixer: bfloat16 [8, 16, 2560], P(None, None, 'group'), may hold values from -0.75 to 0.75
- down_gate: bfloat16 [8, 2560, 16], P(None, 'group'), may hold values from -0.125 to 0.125
- lift_gate: bfloat16 [8, 16, 7680], P(None, None, 'group'), may hold values from -0.75 to 0.75
- down_upper: bfloat16 [8, 2560, 16], P(None, 'group'), may hold values from -0.125 to 0.125
- lift_upper: bfloat16 [8, 16, 7680], P(None, None, 'group'), may hold values from -0.75 to 0.75
- down_outward: bfloat16 [8, 7680, 16], P(None, 'group'), may hold values from -0.0625 to 0.0625
- lift_outward: bfloat16 [8, 16, 2560], P(None, None, 'group'), may hold values from -0.75 to 0.75
- out_grad: bfloat16 [16, 1024, 2560], P('replica', 'group'), may hold values from -6 to 6
Outputs:
- block_out: bfloat16 [16, 1024, 2560], P('replica', 'group')
- grad_inputs: float32 [16, 1024, 2560], P('replica', 'group')
- grad_down_branch: float32 [8, 2560, 16], P(None, 'group')
- grad_lift_branch: float32 [8, 16, 2560], P(None, None, 'group')
- grad_down_input: float32 [8, 2560, 16], P(None, 'group')
- grad_lift_input: float32 [8, 16, 2560], P(None, None, 'group')
- grad_down_decay: float32 [8, 2560, 16], P(None, 'group')
- grad_lift_decay: float32 [8, 16, 2560], P(None, None, 'group')
- grad_down_admit: float32 [8, 2560, 16], P(None, 'group')
- grad_lift_admit: float32 [8, 16, 2560], P(None, None, 'group')
- grad_down_mixer: float32 [8, 2560, 16], P(None, 'group')
- grad_lift_mixer: float32 [8, 16, 2560], P(None, None, 'group')
- grad_down_gate: float32 [8, 2560, 16], P(None, 'group')
- grad_lift_gate: float32 [8, 16, 7680], P(None, None, 'group')
- grad_down_upper: float32 [8, 2560, 16], P(None, 'group')
- grad_lift_upper: float32 [8, 16, 7680], P(None, None, 'group')
- grad_down_outward: float32 [8, 7680, 16], P(None, 'group')
- grad_lift_outward: float32 [8, 16, 2560], P(None, None, 'group')
Inputs may be any that keep to these rules, and one draw needn't show every extreme that they name: `segment_ids`: within each sequence the ids start at 0 and rise by 0 or 1 from one token to the next; a rise marks a new document. In each aligned run of 2 sequences one sequence holds a document that starts before position 64 and runs to the sequence's end. Rates softplus(decay_param) are positive; some channels keep most of their state over a whole sequence.
All inputs are finite; a program needn't handle non-finite values.
Results may differ from a plain program's by a relative error of at most 0.017.
Values may be sent and summed in bfloat16 or wider, within the bound.
A program may use at most 576 MiB of HBM per device.

v0:
```python
import jax
import jax.numpy as jnp
from jax import lax
from jax.sharding import PartitionSpec as P

HIGH = lax.Precision.HIGHEST
EPS = 1e-06


def passed_along(block, axis, distance):
    devices = range(lax.axis_size(axis))
    route = [(i - distance, i) for i in devices if i - distance in devices]
    return lax.ppermute(block, axis, route)


def entering(value, axis, join, neutral):
    count, mine = (lax.axis_size(axis), lax.axis_index(axis))
    pieces = jax.tree.map(lambda part: lax.all_gather(part, axis), value)
    subtotal = jax.tree.map(
        lambda part, zero: jnp.full_like(part, 0) + jnp.asarray(zero, part.dtype), value, neutral
    )

    def lap(position, subtotal):
        longer = join(subtotal, jax.tree.map(lambda part: part[position], pieces))
        return jax.tree.map(lambda new, old: jnp.where(position < mine, new, old), longer, subtotal)

    return lax.fori_loop(0, count - 1, lap, subtotal)


def prefix(shard, axis, join, neutral):
    count = lax.axis_size(axis)
    place = lax.axis_index(axis)
    ahead = count - 1 - place
    gathered = jax.tree.map(
        lambda a, kind: lax.all_gather(a.astype(kind), axis), shard, (jnp.bfloat16, jnp.bfloat16)
    )
    state = jax.tree.map(lambda a, e: jnp.zeros_like(a) + jnp.asarray(e, a.dtype), shard, neutral)

    def one(lap, state):
        source = count - 1 - lap
        return join(
            state,
            jax.tree.map(
                lambda a, own: lax.dynamic_index_in_dim(a, source, 0, False).astype(own.dtype),
                gathered,
                shard,
            ),
        )

    return lax.fori_loop(0, ahead, one, state)


def norm_rows(values, gain):
    return values * lax.rsqrt(jnp.mean(values * values, axis=-1, keepdims=True) + EPS) * gain


def gelu_tanh(values):
    return jax.nn.gelu(values, approximate=True)


def pick_sets(table, onehot):
    return jnp.einsum("sk,kab->sab", onehot, table.astype(jnp.float32), precision=HIGH)


def spread_sets(grads, onehot):
    return jnp.einsum("sk,sab->kab", onehot, grads, precision=HIGH)


def dense(values, weight):
    return jnp.einsum("sti,ij->stj", values, weight, preferred_element_type=jnp.float32)


def dense_back(grads, weight):
    return jnp.einsum("stj,ij->sti", grads, weight, preferred_element_type=jnp.float32)


def low_rank(values, first, second):
    inner = jnp.einsum(
        "sti,sir->str", values, first.astype(jnp.bfloat16), preferred_element_type=jnp.float32
    )
    return (inner, jnp.einsum("str,sro->sto", inner, second, precision=HIGH))


def low_rank_back(values, inner, grads, first, second):
    through = jnp.einsum("sto,sro->str", grads, second, precision=HIGH)
    grad_values = jnp.einsum("str,sir->sti", through, first, precision=HIGH)
    grad_first = jnp.einsum("sti,str->sir", values.astype(jnp.float32), through, precision=HIGH)
    grad_second = jnp.einsum("str,sto->sro", inner, grads, precision=HIGH)
    return (grad_values, grad_first, grad_second)


def rank_product(values, first, second):
    inner = jnp.einsum("sti,sir->str", values, first, precision=HIGH)
    return jnp.einsum("str,sro->sto", inner, second, precision=HIGH)


def head_mix(values, table):
    shaped = values.reshape(values.shape[:2] + (table.shape[0], table.shape[1]))
    return jnp.einsum("sthi,hij->sthj", shaped, table, precision=HIGH).reshape(values.shape)


def affine_join(earlier, later):
    return (earlier[0] * later[0], later[0] * earlier[1] + later[1])


def gate_piece(
    rounded,
    convolved,
    first_decay,
    second_decay,
    first_admit,
    second_admit,
    restart,
    decay_table,
    admit_table,
    softrate,
):
    decay_gate = jax.nn.sigmoid(
        head_mix(rounded, decay_table) + rank_product(rounded, first_decay, second_decay)
    )
    admit_gate = jax.nn.sigmoid(
        head_mix(rounded, admit_table) + rank_product(rounded, first_admit, second_admit)
    )
    log_decay = -8.0 * decay_gate * softrate
    safe_log = jnp.where(restart, -1.0, log_decay)
    decays = jnp.where(restart, 0.0, jnp.exp(safe_log))
    scale_in = jnp.where(restart, 1.0, jnp.sqrt(-jnp.expm1(2.0 * safe_log)))
    return (decays, convolved * admit_gate * scale_in)


def body(
    inputs,
    segment_ids,
    adapter_ids,
    gain_mix,
    gain_mlp,
    w_branch,
    w_input,
    conv_taps,
    decay_heads,
    admit_heads,
    decay_param,
    w_mixer,
    w_gate,
    w_upper,
    w_down,
    down_branch,
    lift_branch,
    down_input,
    lift_input,
    down_decay,
    lift_decay,
    down_admit,
    lift_admit,
    down_mixer,
    lift_mixer,
    down_gate,
    lift_gate,
    down_upper,
    lift_upper,
    down_outward,
    lift_outward,
    out_grad,
):
    seqs_here, stretch, width = inputs.shape
    taps = conv_taps.shape[0]
    sets = down_branch.shape[0]
    begin = lax.axis_index("group") * stretch
    onehot = (adapter_ids[:, None] == jnp.arange(sets, dtype=jnp.int32)[None, :]).astype(
        jnp.float32
    )
    (
        w_branch,
        w_input,
        w_mixer,
        down_branch,
        lift_branch,
        down_input,
        lift_input,
        down_decay,
        lift_decay,
        down_admit,
        lift_admit,
        down_mixer,
        lift_mixer,
        down_gate,
        down_upper,
        lift_outward,
    ) = (
        lax.all_gather(w_branch, "group", axis=1, tiled=True),
        lax.all_gather(w_input, "group", axis=1, tiled=True),
        lax.all_gather(w_mixer, "group", axis=0, tiled=True),
        lax.all_gather(down_branch, "group", axis=1, tiled=True),
        lax.all_gather(lift_branch, "group", axis=2, tiled=True),
        lax.all_gather(down_input, "group", axis=1, tiled=True),
        lax.all_gather(lift_input, "group", axis=2, tiled=True),
        lax.all_gather(down_decay, "group", axis=1, tiled=True),
        lax.all_gather(lift_decay, "group", axis=2, tiled=True),
        lax.all_gather(down_admit, "group", axis=1, tiled=True),
        lax.all_gather(lift_admit, "group", axis=2, tiled=True),
        lax.all_gather(down_mixer, "group", axis=1, tiled=True),
        lax.all_gather(lift_mixer, "group", axis=2, tiled=True),
        lax.all_gather(down_gate, "group", axis=1, tiled=True),
        lax.all_gather(down_upper, "group", axis=1, tiled=True),
        lax.all_gather(lift_outward, "group", axis=2, tiled=True),
    )
    chosen = [
        pick_sets(table, onehot)
        for table in (
            down_branch,
            lift_branch,
            down_input,
            lift_input,
            down_decay,
            lift_decay,
            down_admit,
            lift_admit,
            down_mixer,
            lift_mixer,
            down_gate,
            down_upper,
            lift_outward,
        )
    ]
    padded_ids = jnp.pad(segment_ids, ((0, 0), (taps - 1, taps - 1)), constant_values=-1)
    window = lax.dynamic_slice_in_dim(padded_ids, begin, stretch + 2 * (taps - 1), 1)
    current = window[:, taps - 1 : taps - 1 + stretch + taps - 1]
    agree = [
        (
            (current == window[:, taps - 1 - j : taps - 1 - j + stretch + taps - 1])
            & (current >= 0)
        ).astype(jnp.float32)
        for j in range(taps)
    ]
    restart = (agree[1][:, :stretch] < 0.5)[..., None]
    x_float = inputs.astype(jnp.float32)
    normed_f, norm_one_back = jax.vjp(lambda rows: norm_rows(rows, gain_mix), x_float)
    normed = normed_f.astype(jnp.bfloat16)
    inner_branch, extra_branch = low_rank(normed, chosen[0], chosen[1])
    branch_pre = dense(normed, w_branch) + extra_branch
    branch, branch_back = jax.vjp(gelu_tanh, branch_pre)
    inner_input, extra_input = low_rank(normed, chosen[2], chosen[3])
    fed = (dense(normed, w_input) + extra_input).astype(jnp.bfloat16)
    halo = passed_along(fed[:, stretch - (taps - 1) :], "group", 1)
    extended = jnp.concatenate([halo, fed], axis=1).astype(jnp.float32)
    convolved = sum(
        (
            conv_taps[j]
            * agree[j][:, :stretch, None]
            * extended[:, taps - 1 - j : taps - 1 - j + stretch]
            for j in range(taps)
        )
    )
    rounded = lax.optimization_barrier(convolved.astype(jnp.bfloat16)).astype(jnp.float32)
    softrate = jax.nn.softplus(decay_param)
    decay_table = decay_heads.astype(jnp.float32)
    admit_table = admit_heads.astype(jnp.float32)

    def gates(rounded_in, conv_in, first_decay, second_decay, first_admit, second_admit):
        return gate_piece(
            rounded_in,
            conv_in,
            first_decay,
            second_decay,
            first_admit,
            second_admit,
            restart,
            decay_table,
            admit_table,
            softrate,
        )

    (decays, drive), gate_back = jax.vjp(
        gates, rounded, convolved, chosen[4], chosen[5], chosen[6], chosen[7]
    )
    cumulative, local_state = lax.associative_scan(affine_join, (decays, drive), axis=1)
    ones_rows = jnp.ones((seqs_here, width), jnp.float32)
    zero_rows = jnp.zeros((seqs_here, width), jnp.float32)
    spanned, carried = entering(
        (cumulative[:, -1], local_state[:, -1]), "group", affine_join, (ones_rows, zero_rows)
    )
    state = local_state + cumulative * carried[:, None]
    merged = (state * branch).astype(jnp.bfloat16)
    inner_mixer, extra_mixer = low_rank(merged, chosen[8], chosen[9])
    mixed = dense(merged, w_mixer) + extra_mixer
    resid = x_float + mixed
    normed_two_f, norm_two_back = jax.vjp(lambda rows: norm_rows(rows, gain_mlp), resid)
    normed_two = normed_two_f.astype(jnp.bfloat16)
    cotangent = out_grad.astype(jnp.float32)
    full_gate, full_upper, full_down, all_lift_gate, all_lift_upper, all_down_outward = (
        lax.all_gather(w_gate, "group", axis=1, tiled=True),
        lax.all_gather(w_upper, "group", axis=1, tiled=True),
        lax.all_gather(w_down, "group", axis=0, tiled=True),
        lax.all_gather(lift_gate, "group", axis=2, tiled=True),
        lax.all_gather(lift_upper, "group", axis=2, tiled=True),
        lax.all_gather(down_outward, "group", axis=1, tiled=True),
    )
    pick_lift_gate = pick_sets(all_lift_gate, onehot)
    pick_lift_upper = pick_sets(all_lift_upper, onehot)
    pick_down_outward = pick_sets(all_down_outward, onehot)
    inner_gate, extra_gate = low_rank(normed_two, chosen[10], pick_lift_gate)
    inner_upper, extra_upper = low_rank(normed_two, chosen[11], pick_lift_upper)
    gate_pre = dense(normed_two, full_gate) + extra_gate
    upper_pre = dense(normed_two, full_upper) + extra_upper
    hidden_f, hidden_back = jax.vjp(
        lambda gate_in, upper_in: gelu_tanh(gate_in) * upper_in, gate_pre, upper_pre
    )
    hidden = hidden_f.astype(jnp.bfloat16)
    inner_out, extra_out = low_rank(hidden, pick_down_outward, chosen[12])
    outward = dense(hidden, full_down) + extra_out
    block_out = resid + outward
    grad_hidden, grad_pick_down_outward, grad_pick_lift_outward = low_rank_back(
        hidden, inner_out, cotangent, pick_down_outward, chosen[12]
    )
    grad_hidden = grad_hidden + dense_back(out_grad, full_down)
    grad_gate_f, grad_upper_f = hidden_back(grad_hidden)
    grad_gate = grad_gate_f.astype(jnp.bfloat16)
    grad_upper = grad_upper_f.astype(jnp.bfloat16)
    gate_values, grad_pick_down_gate, grad_pick_lift_gate = low_rank_back(
        normed_two, inner_gate, grad_gate.astype(jnp.float32), chosen[10], pick_lift_gate
    )
    upper_values, grad_pick_down_upper, grad_pick_lift_upper = low_rank_back(
        normed_two, inner_upper, grad_upper.astype(jnp.float32), chosen[11], pick_lift_upper
    )
    grad_normed_two = (
        dense_back(grad_gate, full_gate)
        + dense_back(grad_upper, full_upper)
        + gate_values
        + upper_values
    )
    owned_lift_gate, owned_lift_upper, owned_down_outward = (
        lax.psum_scatter(
            spread_sets(grad_pick_lift_gate, onehot).astype(jnp.bfloat16),
            "group",
            scatter_dimension=2,
            tiled=True,
        ).astype(jnp.float32),
        lax.psum_scatter(
            spread_sets(grad_pick_lift_upper, onehot).astype(jnp.bfloat16),
            "group",
            scatter_dimension=2,
            tiled=True,
        ).astype(jnp.float32),
        lax.psum_scatter(
            spread_sets(grad_pick_down_outward, onehot).astype(jnp.bfloat16),
            "group",
            scatter_dimension=1,
            tiled=True,
        ).astype(jnp.float32),
    )
    grad_resid = cotangent + norm_two_back(grad_normed_two)[0]
    grad_mixed = grad_resid.astype(jnp.bfloat16)
    mixer_values, grad_pick_down_mixer, grad_pick_lift_mixer = low_rank_back(
        merged, inner_mixer, grad_mixed.astype(jnp.float32), chosen[8], chosen[9]
    )
    grad_merged = dense_back(grad_mixed, w_mixer) + mixer_values
    grad_state = grad_merged * branch
    grad_branch_pre = branch_back(grad_merged * state)[0].astype(jnp.bfloat16)
    prev_state = jnp.concatenate([carried[:, None], state[:, :-1]], axis=1)
    alphas = jnp.concatenate([decays[:, 1:], jnp.ones_like(decays[:, :1])], axis=1)
    spans, local_grad = lax.associative_scan(
        affine_join, (alphas, grad_state), axis=1, reverse=True
    )
    spanned_back, incoming = prefix(
        (decays[:, 0] * spans[:, 0], decays[:, 0] * local_grad[:, 0]),
        "group",
        affine_join,
        (ones_rows, zero_rows),
    )
    grad_drive = local_grad + spans * incoming[:, None]
    grad_decays = grad_drive * prev_state
    (
        grad_rounded,
        grad_conv_direct,
        grad_pick_down_decay,
        grad_pick_lift_decay,
        grad_pick_down_admit,
        grad_pick_lift_admit,
    ) = gate_back((grad_decays, grad_drive))
    grad_convolved = grad_rounded + grad_conv_direct
    below = passed_along(grad_convolved[:, : taps - 1].astype(jnp.bfloat16), "group", -1).astype(
        jnp.float32
    )
    grad_extended = jnp.concatenate([grad_convolved, below], axis=1)
    grad_fed = sum(
        (
            conv_taps[j] * agree[j][:, j : j + stretch, None] * grad_extended[:, j : j + stretch]
            for j in range(taps)
        )
    ).astype(jnp.bfloat16)
    branch_values, grad_pick_down_branch, grad_pick_lift_branch = low_rank_back(
        normed, inner_branch, grad_branch_pre.astype(jnp.float32), chosen[0], chosen[1]
    )
    input_values, grad_pick_down_input, grad_pick_lift_input = low_rank_back(
        normed, inner_input, grad_fed.astype(jnp.float32), chosen[2], chosen[3]
    )
    grad_normed = (
        dense_back(grad_branch_pre, w_branch)
        + dense_back(grad_fed, w_input)
        + branch_values
        + input_values
    )
    grad_inputs = grad_resid + norm_one_back(grad_normed)[0]
    picks = (
        grad_pick_down_branch,
        grad_pick_lift_branch,
        grad_pick_down_input,
        grad_pick_lift_input,
        grad_pick_down_decay,
        grad_pick_lift_decay,
        grad_pick_down_admit,
        grad_pick_lift_admit,
        grad_pick_down_mixer,
        grad_pick_lift_mixer,
        grad_pick_down_gate,
        grad_pick_down_upper,
        grad_pick_lift_outward,
    )
    partial_value = [spread_sets(grads, onehot) for grads in picks]
    owned = (
        lax.psum_scatter(
            partial_value[0].astype(jnp.bfloat16), "group", scatter_dimension=1, tiled=True
        ).astype(jnp.float32),
        lax.psum_scatter(
            partial_value[1].astype(jnp.bfloat16), "group", scatter_dimension=2, tiled=True
        ).astype(jnp.float32),
        lax.psum_scatter(
            partial_value[2].astype(jnp.bfloat16), "group", scatter_dimension=1, tiled=True
        ).astype(jnp.float32),
        lax.psum_scatter(
            partial_value[3].astype(jnp.bfloat16), "group", scatter_dimension=2, tiled=True
        ).astype(jnp.float32),
        lax.psum_scatter(
            partial_value[4].astype(jnp.bfloat16), "group", scatter_dimension=1, tiled=True
        ).astype(jnp.float32),
        lax.psum_scatter(
            partial_value[5].astype(jnp.bfloat16), "group", scatter_dimension=2, tiled=True
        ).astype(jnp.float32),
        lax.psum_scatter(
            partial_value[6].astype(jnp.bfloat16), "group", scatter_dimension=1, tiled=True
        ).astype(jnp.float32),
        lax.psum_scatter(
            partial_value[7].astype(jnp.bfloat16), "group", scatter_dimension=2, tiled=True
        ).astype(jnp.float32),
        lax.psum_scatter(
            partial_value[8].astype(jnp.bfloat16), "group", scatter_dimension=1, tiled=True
        ).astype(jnp.float32),
        lax.psum_scatter(
            partial_value[9].astype(jnp.bfloat16), "group", scatter_dimension=2, tiled=True
        ).astype(jnp.float32),
        lax.psum_scatter(
            partial_value[10].astype(jnp.bfloat16), "group", scatter_dimension=1, tiled=True
        ).astype(jnp.float32),
        lax.psum_scatter(
            partial_value[11].astype(jnp.bfloat16), "group", scatter_dimension=1, tiled=True
        ).astype(jnp.float32),
        lax.psum_scatter(
            partial_value[12].astype(jnp.bfloat16), "group", scatter_dimension=2, tiled=True
        ).astype(jnp.float32),
    )
    totals = (
        lax.psum(owned[0].astype(jnp.bfloat16), "replica").astype(jnp.float32),
        lax.psum(owned[1].astype(jnp.bfloat16), "replica").astype(jnp.float32),
        lax.psum(owned[2].astype(jnp.bfloat16), "replica").astype(jnp.float32),
        lax.psum(owned[3].astype(jnp.bfloat16), "replica").astype(jnp.float32),
        lax.psum(owned[4].astype(jnp.bfloat16), "replica").astype(jnp.float32),
        lax.psum(owned[5].astype(jnp.bfloat16), "replica").astype(jnp.float32),
        lax.psum(owned[6].astype(jnp.bfloat16), "replica").astype(jnp.float32),
        lax.psum(owned[7].astype(jnp.bfloat16), "replica").astype(jnp.float32),
        lax.psum(owned[8].astype(jnp.bfloat16), "replica").astype(jnp.float32),
        lax.psum(owned[9].astype(jnp.bfloat16), "replica").astype(jnp.float32),
        lax.psum(owned[10].astype(jnp.bfloat16), "replica").astype(jnp.float32),
        lax.psum(owned[11].astype(jnp.bfloat16), "replica").astype(jnp.float32),
        lax.psum(owned[12].astype(jnp.bfloat16), "replica").astype(jnp.float32),
        lax.psum(owned_lift_gate.astype(jnp.bfloat16), "replica").astype(jnp.float32),
        lax.psum(owned_lift_upper.astype(jnp.bfloat16), "replica").astype(jnp.float32),
        lax.psum(owned_down_outward.astype(jnp.bfloat16), "replica").astype(jnp.float32),
    )
    finals = list(totals[:13])
    rest = list(totals[13:])
    return (
        block_out.astype(jnp.bfloat16),
        grad_inputs,
        finals[0],
        finals[1],
        finals[2],
        finals[3],
        finals[4],
        finals[5],
        finals[6],
        finals[7],
        finals[8],
        finals[9],
        finals[10],
        rest[0],
        finals[11],
        rest[1],
        rest[2],
        finals[12],
    )


def solution(mesh):
    in_specs = (
        P("replica", "group", None),
        P("replica", None),
        P("replica"),
        P(),
        P(),
        P(None, "group"),
        P(None, "group"),
        P(),
        P(),
        P(),
        P(),
        P("group", None),
        P(None, "group"),
        P(None, "group"),
        P("group", None),
        P(None, "group", None),
        P(None, None, "group"),
        P(None, "group", None),
        P(None, None, "group"),
        P(None, "group", None),
        P(None, None, "group"),
        P(None, "group", None),
        P(None, None, "group"),
        P(None, "group", None),
        P(None, None, "group"),
        P(None, "group", None),
        P(None, None, "group"),
        P(None, "group", None),
        P(None, None, "group"),
        P(None, "group", None),
        P(None, None, "group"),
        P("replica", "group", None),
    )
    out_specs = (
        P("replica", "group", None),
        P("replica", "group", None),
        P(None, "group", None),
        P(None, None, "group"),
        P(None, "group", None),
        P(None, None, "group"),
        P(None, "group", None),
        P(None, None, "group"),
        P(None, "group", None),
        P(None, None, "group"),
        P(None, "group", None),
        P(None, None, "group"),
        P(None, "group", None),
        P(None, None, "group"),
        P(None, "group", None),
        P(None, None, "group"),
        P(None, "group", None),
        P(None, None, "group"),
    )
    return jax.shard_map(body, mesh=mesh, in_specs=in_specs, out_specs=out_specs, check_vma=False)
```

profile of v0, /device:TPU:0, one launch (start us, length us, event | category | flops | bytes accessed | tf_op | source)
XLA Modules:
  0.0 3218.5 jit_solution(14384183175252423251)
XLA Ops:
  37.3 17.2 all_gather.82
  117.7 17.2 all_gather.90
  151.1 18.5 all_gather.93
  170.8 19.3 all_gather.94
  209.0 17.0 all_gather.96
  227.2 17.0 all_gather.103
  273.3 19.3 all-gather.14.cloned.1.call-done
  313.0 106.5 %all-gather.16.cloned.1.call-done = bf16[2560,2560]{1,0:T(8,128)(2,1)} async-done(((bf16[2560,640]{1,0:T(8,128)(2,1)}), bf16[2560,2560]{1,0:T(8,128)(2,1)}) %all-gather.16.cloned.1.call-update) | async-done | bytes 13107216 | tf_op jit(solution)/shard_map/all_gather | solution.py:190
  859.9 21.2 slice.682
  881.1 20.9 slice.689
  901.9 21.3 slice.680
  991.1 31.8 fusion.23
  1022.9 222.3 %all-gather.20.cloned.1.call-done = bf16[2560,7680]{1,0:T(8,128)(2,1)} async-done(((bf16[2560,1920]{1,0:T(8,128)(2,1)}), bf16[2560,7680]{1,0:T(8,128)(2,1)}) %all-gather.20.cloned.1.call-update) | async-done | bytes 39321616 | tf_op jit(solution)/shard_map/all_gather | solution.py:291
  1245.2 38.2 %fusion.20 = f32[2,256,7680]{2,1,0:T(8,128)} fusion(f32[2,256,7680]{2,1,0:T(8,128)} %fusion.112, bf16[2,256,2560]{2,1,0:T(8,128)(2,1)} %copy-done.5, bf16[2560,7680]{1,0:T(8,128)(2,1)} %all-gather.20.cloned.1.call-done), kind=kOutput, calls=%fused_computation.29 | convolution fusion | flops 20136591360 | bytes 73400320 | tf_op jit(solution)/shard_map/sti,ij->stj/dot_general | solution.py:70
  1283.4 309.7 %all-gather.28.cloned.1.call-done = bf16[7680,2560]{1,0:T(8,128)(2,1)} async-done(((bf16[1920,2560]{1,0:T(8,128)(2,1)}), bf16[7680,2560]{1,0:T(8,128)(2,1)}) %all-gather.28.cloned.1.call-update) | async-done | bytes 39321616 | tf_op jit(solution)/shard_map/all_gather | solution.py:293
  1593.1 44.3 %multiply_convert_fusion = (bf16[2,256,7680]{2,1,0:T(8,128)(2,1)}, bf16[2,256,7680]{2,1,0:T(8,128)(2,1)}, bf16[2,256,7680]{2,1,0:T(8,128)(2,1)}) fusion(f32[2,256,7680]{2,1,0:T(8,128)} %fusion.20, f32[2,256,7680]{2,1,0:T(8,128)} %fusion.23, f32[2,256,7680]{2,1,0:T(8,128)} %fusion.104, bf16[2,256,2560]{2,1,0:T(8,128)(2,1)} %param.67, ...), kind=kOutput, calls=%fused_computation.26 | convolution fusion | flops 20238827520 | bytes 112721920 | tf_op jit(solution)/shard_map/stj,ij->sti/dot_general | solution.py:74
  1656.8 27.9 fusion.5
  1684.7 27.9 fusion.9
  1774.1 20.8 slice.684
  1794.9 20.8 slice.686
  2038.3 21.1 slice.742
  2149.8 40.6 %rev.9 = f32[2,256,2560]{2,1,0:T(8,128)} reverse(f32[2,256,2560]{2,1,0:T(8,128)} %add.661), dimensions={1} | reverse | bytes 10485760 | tf_op jit(solution)/shard_map/rev | solution.py:361
  2190.3 40.5 %rev.8 = f32[2,256,2560]{2,1,0:T(8,128)} reverse(f32[2,256,2560]{2,1,0:T(8,128)} %add.653), dimensions={1} | reverse | bytes 10485760 | tf_op jit(solution)/shard_map/rev | solution.py:361
  2256.9 18.9 fusion.60
  2678.6 23.1 copy.336
  2701.7 37.9 %reshape.202 = bf16[7680,128]{1,0:T(8,128)(2,1)} reshape(bf16[7680,16,8]{2,1,0:T(8,128)(2,1)} %bitcast.326) | data formatting | bytes 3932160
  2748.3 23.1 copy.340
  2771.4 37.9 %reshape.206 = bf16[7680,128]{1,0:T(8,128)(2,1)} reshape(bf16[7680,16,8]{2,1,0:T(8,128)(2,1)} %bitcast.327) | data formatting | bytes 3932160
  2818.0 23.1 copy.342
  2841.1 37.9 %reshape.208 = bf16[7680,128]{1,0:T(8,128)(2,1)} reshape(bf16[7680,16,8]{2,1,0:T(8,128)(2,1)} %bitcast.328) | data formatting | bytes 3932160
  2879.5 26.4 fusion.3
  3126.8 66.8 %all-reduce.70.cloned.1.call-done = (bf16[8,640,16]{1,0,2:T(8,128)(2,1)}, bf16[8,16,640]{2,0,1:T(8,128)(2,1)}, bf16[8,640,16]{1,0,2:T(8,128)(2,1)}, bf16[8,16,64...) async-done(((bf16[8,640,16]{1,0,2:T(8,128)(2,1)}, ...) | async-done | bytes 3604496 | tf_op jit(solution)/shard_map/psum | solution.py:462
  (979 shorter events, 1764.9 us)
Async XLA Ops:
  7.2 436.6 %copy-start = (bf16[10,256,256]{2,1,0:T(8,128)(2,1)S(1)}, bf16[10,256,256]{2,1,0:T(8,128)(2,1)}, u32[]{:S(2)}) copy-start(bf16[10,256,256]{2,1,0:T(8,128)(2,1)} %param.45) | copy-start | bytes 3932164
  7.2 241.4 %all-gather.30.cloned.1.call-start = ((), (), s32[]{:S(2)}) async-start(), calls=%async_computation.24 | async-start | bytes 2457600 | tf_op jit(solution)/shard_map/all_gather | solution.py:296
  9.3 257.6 %all-gather.26.cloned.1.call-start = ((), (), s32[]{:S(2)}) async-start(), calls=%async_computation.22 | async-start | bytes 2457600 | tf_op jit(solution)/shard_map/all_gather | solution.py:295
  11.2 258.8 %all-gather.22.cloned.1.call-start = ((), (), s32[]{:S(2)}) async-start(), calls=%async_computation.20 | async-start | bytes 2457600 | tf_op jit(solution)/shard_map/all_gather | solution.py:294
  13.2 279.4 %all-gather.14.cloned.1.call-start = ((), (), s32[]{:S(2)}) async-start(), calls=%async_computation.16 | async-start | bytes 16384000 | tf_op jit(solution)/shard_map/all_gather | solution.py:191
  13.8 405.8 %all-gather.16.cloned.1.call-start = ((), (), s32[]{:S(2)}) async-start(), calls=%async_computation.17 | async-start | bytes 16384000 | tf_op jit(solution)/shard_map/all_gather | solution.py:190
  14.4 926.9 %all-gather.18.cloned.1.call-start = ((), (), s32[]{:S(2)}) async-start(), calls=%async_computation.18 | async-start | bytes 16384000 | tf_op jit(solution)/shard_map/all_gather | solution.py:192
  14.9 976.2 %all-gather.24.cloned.1.call-start = ((), (), s32[]{:S(2)}) async-start(), calls=%async_computation.21 | async-start | bytes 49152000 | tf_op jit(solution)/shard_map/all_gather | solution.py:292
  15.7 1229.5 %all-gather.20.cloned.1.call-start = ((), (), s32[]{:S(2)}) async-start(), calls=%async_computation.19 | async-start | bytes 49152000 | tf_op jit(solution)/shard_map/all_gather | solution.py:291
  16.5 1576.6 %all-gather.28.cloned.1.call-start = ((), (), s32[]{:S(2)}) async-start(), calls=%async_computation.23 | async-start | bytes 49152000 | tf_op jit(solution)/shard_map/all_gather | solution.py:293
  17.3 2920.4 %reduce-scatter.67.cloned.1.call-start = ((), (), s32[]{:S(2)}) async-start(), calls=%async_computation.34 | async-start | bytes 819200
  17.5 465.5 %copy-start.184 = (pred[2,256]{1,0:T(4,128)(4,1)}, pred[2,256]{1,0:T(4,128)(4,1)S(1)}, u32[]{:S(2)}) copy-start(pred[2,256]{1,0:T(4,128)(4,1)S(1)} %broadcast_compare_fusion.1) | copy-start | bytes 1540
  18.8 414.1 %copy-start.168 = (f32[2,256]{1,0:T(2,128)}, f32[2,256]{1,0:T(2,128)S(1)}, u32[]{:S(2)}) copy-start(f32[2,256]{1,0:T(2,128)S(1)} %slice_convert_fusion.1) | copy-start | bytes 6148
  21.3 398.2 %copy-start.177 = (f32[2,256]{1,0:T(2,128)}, f32[2,256]{1,0:T(2,128)S(1)}, u32[]{:S(2)}) copy-start(f32[2,256]{1,0:T(2,128)S(1)} %fusion.238) | copy-start | bytes 6148
  309.8 122.2 %collective-permute-start = (bf16[2,3,2560]{2,1,0:T(4,128)(2,1)S(1)}, bf16[2,3,2560]{2,1,0:T(4,128)(2,1)S(1)}, u32[]{:S(2)}, u32[]{:S(2)}) collective-permute-start(bf16[2,3,2560]{2,1,0:T(4,128)(2,1)S(1)} %slice.768), channel_id=1, source_target_pairs={{0,8},{8,16},{16,24},{1,9},{9,17},{17,25},{2,10},{10,18},{18,26},{... | collective-permute-start | bytes 92168 | tf_op jit(solution)/shard_map/ppermute | solution.py:13
  2136.2 809.8 %reduce-scatter.65.cloned.1.call-start = ((), (), s32[]{:S(2)}) async-start(), calls=%async_computation.33 | async-start | bytes 819200
  2256.8 697.4 %reduce-scatter.57.cloned.1.call-start = ((), (), s32[]{:S(2)}) async-start(), calls=%async_computation.29 | async-start | bytes 819200
  2307.2 655.2 %reduce-scatter.59.cloned.1.call-start = ((), (), s32[]{:S(2)}) async-start(), calls=%async_computation.30 | async-start | bytes 819200
  2335.8 634.7 %reduce-scatter.61.cloned.1.call-start = ((), (), s32[]{:S(2)}) async-start(), calls=%async_computation.31 | async-start | bytes 819200
  2367.4 611.3 %reduce-scatter.63.cloned.1.call-start = ((), (), s32[]{:S(2)}) async-start(), calls=%async_computation.32 | async-start | bytes 819200
  2395.8 591.1 %reduce-scatter.69.cloned.1.call-start = ((), (), s32[]{:S(2)}) async-start(), calls=%async_computation.35 | async-start | bytes 819200
  2421.8 573.4 %reduce-scatter.73.cloned.1.call-start = ((), (), s32[]{:S(2)}) async-start(), calls=%async_computation.37 | async-start | bytes 819200
  2448.2 555.3 %reduce-scatter.51.cloned.1.call-start = ((), (), s32[]{:S(2)}) async-start(), calls=%async_computation.26 | async-start | bytes 819200
  2493.6 518.1 %reduce-scatter.49.cloned.1.call-start = ((), (), s32[]{:S(2)}) async-start(), calls=%async_computation.25 | async-start | bytes 819200
  2558.3 461.7 %reduce-scatter.79.cloned.1.call-start = ((), (), s32[]{:S(2)}) async-start(), calls=%async_computation.40 | async-start | bytes 819200
  2570.1 32.7 %collective-permute-start.1 = (bf16[2,3,2560]{2,1,0:T(4,128)(2,1)S(1)}, bf16[2,3,2560]{2,1,0:T(4,128)(2,1)S(1)}, u32[]{:S(2)}, u32[]{:S(2)}) collective-permute-start(bf16[2,3,2560]{2,1,0:T(4,128)(2,1)S(1)} %slice.1037), channel_id=1, source_target_pairs={{8,0},{16,8},{24,16},{9,1},{17,9},{25,17},{10,2},{18,10},{26,18},{... | collective-permute-start | bytes 92168 | tf_op jit(solution)/shard_map/ppermute | solution.py:13
  2602.4 425.7 %reduce-scatter.55.cloned.1.call-start = ((), (), s32[]{:S(2)}) async-start(), calls=%async_computation.28 | async-start | bytes 819200
  2639.9 396.4 %reduce-scatter.53.cloned.1.call-start = ((), (), s32[]{:S(2)}) async-start(), calls=%async_computation.27 | async-start | bytes 819200
  2670.1 374.4 %reduce-scatter.71.cloned.1.call-start = ((), (), s32[]{:S(2)}) async-start(), calls=%async_computation.36 | async-start | bytes 2457600
  2739.7 323.9 %reduce-scatter.75.cloned.1.call-start = ((), (), s32[]{:S(2)}) async-start(), calls=%async_computation.38 | async-start | bytes 2457600
  2809.3 273.2 %reduce-scatter.77.cloned.1.call-start = ((), (), s32[]{:S(2)}) async-start(), calls=%async_computation.39 | async-start | bytes 2457600
  2879.0 314.6 %all-reduce.70.cloned.1.call-start = ((), (), s32[]{:S(2)}) async-start(), calls=%async_computation.41 | async-start | bytes 7208960 | tf_op jit(solution)/shard_map/psum | solution.py:462
  (197 other events, 6249.1 us)
Sparse Core Ops, SparseCore 0:
  10.5 43.9 all-gather.29
  56.8 39.1 all-gather.25
  98.4 43.4 all-gather.21
  143.6 148.8 all-gather.13
  294.3 125.2 all-gather.15
  421.2 126.9 all-gather.17
  550.1 347.2 all-gather.23
  899.2 345.9 all-gather.19
  1247.1 345.9 all-gather.27
  2136.3 25.3 reduce-scatter.66
  2256.9 25.3 reduce-scatter.64
  2307.4 25.4 reduce-scatter.56
  2336.0 25.4 reduce-scatter.58
  2367.5 25.5 reduce-scatter.60
  2396.1 25.4 reduce-scatter.62
  2424.3 25.4 reduce-scatter.68
  2452.8 25.4 reduce-scatter.72
  2493.8 25.5 reduce-scatter.50
  2558.4 25.7 reduce-scatter.48
  2602.5 26.4 reduce-scatter.78
  2640.0 26.4 reduce-scatter.54
  2670.2 26.4 reduce-scatter.52
  2739.8 35.1 reduce-scatter.70
  2809.4 35.1 reduce-scatter.74
  2879.1 35.1 reduce-scatter.76
  3101.6 91.9 all-reduce.69
where the time goes:
time: 3260 us; the launch traced here: 3220 us
  local copies, waits for them, and re-layouts  1410 us (43%)
  waiting for transfers between devices  729 us (22%)
  matrix products  609 us (19%)
  blocking collectives  241 us (7%)
  other arithmetic  202 us (6%)
    unnamed x498, local copies, waits for them, and re-layouts  665 us
    all_gather x1, waiting for transfers between devices, body(): lax.all_gather(w_down, 'group', axis=0, tiled=True)  310 us
    slice x57, local copies, waits for them, and re-layouts, body(): lax.associative_scan(affine_join, (alphas, grad_state), axis=1, reverse=T...  278 us
    all_gather x1, waiting for transfers between devices, body(): lax.all_gather(w_gate, 'group', axis=1, tiled=True)  222 us
    slice x52, local copies, waits for them, and re-layouts, body(): lax.associative_scan(affine_join, (decays, drive), axis=1)  153 us
    dot_general x6, matrix products, dense_back(): jnp.einsum('stj,ij->sti', grads, weight, preferred_element_type=jnp.float32)  141 us
    dot_general x6, matrix products, dense(): jnp.einsum('sti,ij->stj', values, weight, preferred_element_type=jnp.floa...  131 us
    all_gather x1, waiting for transfers between devices, body(): lax.all_gather(w_branch, 'group', axis=1, tiled=True)  107 us
  transfers between devices with their start and end apart: 28, of which 5 were waited for; matrix products, arithmetic and copies ran while one was open for 51% of the time, Pallas kernels for 0%

commit v1 on v0

v1 whole, which is shorter than its diff:
```python
import functools

import jax
import jax.numpy as jnp
from jax import lax
from jax.experimental import pallas as pl
from jax.experimental.pallas import tpu as pltpu
from jax.sharding import PartitionSpec as P

EPS = 1e-06
F32 = jnp.float32
BF16 = jnp.bfloat16
GELU_C = 0.7978845608028654
GELU_A = 0.044715
NT = (((1,), (1,)), ((), ()))
NN = (((1,), (0,)), ((), ()))
TN = (((0,), (0,)), ((), ()))


def dot(a, b, dims=NN):
    return lax.dot_general(a, b, dims, preferred_element_type=F32)


def gelu(v):
    return 0.5 * v * (1.0 + jnp.tanh(GELU_C * (v + GELU_A * v * v * v)))


def gelu_both(v):
    th = jnp.tanh(GELU_C * (v + GELU_A * v * v * v))
    value = 0.5 * v * (1.0 + th)
    slope = 0.5 * (1.0 + th) + 0.5 * v * (1.0 - th * th) * GELU_C * (1.0 + 3.0 * GELU_A * v * v)
    return value, slope


def norm_rows(values, gain):
    rate = lax.rsqrt(jnp.mean(values * values, axis=-1, keepdims=True) + EPS)
    return values * rate * gain, rate


def norm_back(values, gain, rate, grads):
    scaled = grads * gain
    along = jnp.mean(scaled * values, axis=-1, keepdims=True)
    return rate * scaled - values * (rate * rate * rate * along)


def rows_shifted(values, by, fill):
    rows, width = values.shape
    if by % 8 == 0:
        return jnp.concatenate([jnp.full((by, width), fill, values.dtype), values[: rows - by]], 0)
    place = lax.broadcasted_iota(jnp.int32, values.shape, 0)
    return jnp.where(place >= by, pltpu.roll(values, by, 0), fill)


def rows_advanced(values, by, fill):
    rows, width = values.shape
    if by % 8 == 0:
        return jnp.concatenate([values[by:], jnp.full((by, width), fill, values.dtype)], 0)
    place = lax.broadcasted_iota(jnp.int32, values.shape, 0)
    return jnp.where(place < rows - by, pltpu.roll(values, rows - by, 0), fill)


def scan_rows(a, b, moved):
    by = 1
    while by < a.shape[0]:
        b = a * moved(b, by, 0.0) + b
        a = a * moved(a, by, 1.0)
        by *= 2
    return a, b


def gate_values(conv, inner, lift, table_d, table_a, softrate, restart):
    rounded = conv.astype(BF16)
    half = lift.shape[0] // 2
    pre_d = dot(rounded, table_d) + dot(inner[:, :half], lift[:half])
    pre_a = dot(rounded, table_a) + dot(inner[:, half:], lift[half:])
    decay_gate = 1.0 / (1.0 + jnp.exp(-pre_d))
    admit_gate = 1.0 / (1.0 + jnp.exp(-pre_a))
    safe = jnp.where(restart, -1.0, -8.0 * decay_gate * softrate)
    grown = jnp.exp(safe)
    scale = jnp.sqrt(jnp.tanh(-safe) * (1.0 + grown * grown))
    return decay_gate, admit_gate, grown, scale


def forward_gates_kernel(seqs, conv_ref, inner_ref, lift_ref, table_d_ref, table_a_ref, soft_ref, restart_ref,
                         cum_ref, local_ref):
    stretch = conv_ref.shape[0] // seqs
    for s in range(seqs):
        rows = pl.ds(s * stretch, stretch)
        conv = conv_ref[rows, :]
        restart = restart_ref[rows, :] > 0.5
        _, admit, grown, scale = gate_values(
            conv, inner_ref[rows, :], lift_ref[...], table_d_ref[0], table_a_ref[0], soft_ref[...], restart)
        decays = jnp.where(restart, 0.0, grown)
        drive = conv * admit * jnp.where(restart, 1.0, scale)
        cum, local = scan_rows(decays, drive, rows_shifted)
        cum_ref[rows, :] = cum
        local_ref[rows, :] = local


def forward_gates(seqs, conv, inner, lift, table_d, table_a, softrate, restart):
    rows, width = conv.shape
    heads, size = table_d.shape[:2]
    tile = pl.BlockSpec((rows, size), lambda h: (0, h))
    table = pl.BlockSpec((1, size, size), lambda h: (h, 0, 0))
    out = jax.ShapeDtypeStruct((rows, width), F32)
    return pl.pallas_call(
        functools.partial(forward_gates_kernel, seqs),
        out_shape=(out, out),
        grid=(heads,),
        in_specs=[
            tile,
            pl.BlockSpec(inner.shape, lambda h: (0, 0)),
            pl.BlockSpec((lift.shape[0], size), lambda h: (0, h)),
            table,
            table,
            pl.BlockSpec((1, size), lambda h: (0, h)),
            pl.BlockSpec(restart.shape, lambda h: (0, 0)),
        ],
        out_specs=(tile, tile),
        compiler_params=pltpu.CompilerParams(vmem_limit_bytes=40 * 2**20),
        cost_estimate=pl.CostEstimate(
            flops=4 * rows * width * size + 60 * rows * width,
            bytes_accessed=12 * rows * width,
            transcendentals=6 * rows * width),
    )(conv, inner, lift, table_d, table_a, softrate, restart)


def backward_scan_kernel(seqs, conv_ref, inner_ref, lift_ref, table_d_ref, soft_ref, restart_ref, cum_ref, local_ref,
                         carried_ref, pre_ref, grad_ref, span_ref, total_ref, first_ref, branch_grad_ref):
    stretch = conv_ref.shape[0] // seqs
    half = lift_ref.shape[0] // 2
    for s in range(seqs):
        rows = pl.ds(s * stretch, stretch)
        restart = restart_ref[rows, :] > 0.5
        rounded = conv_ref[rows, :].astype(BF16)
        pre_d = dot(rounded, table_d_ref[0]) + dot(inner_ref[rows, :half], lift_ref[:half, :])
        grown = jnp.exp(-8.0 * soft_ref[...] / (1.0 + jnp.exp(-pre_d)))
        decays = jnp.where(restart, 0.0, grown)
        state = local_ref[rows, :] + cum_ref[rows, :] * carried_ref[s : s + 1, :]
        value, slope = gelu_both(pre_ref[rows, :])
        grads = grad_ref[rows, :]
        branch_grad_ref[rows, :] = (grads * state * slope).astype(BF16)
        span, total = scan_rows(rows_advanced(decays, 1, 1.0), grads * value, rows_advanced)
        span_ref[rows, :] = span
        total_ref[rows, :] = total
        first_ref[s : s + 1, :] = decays[:1] * span[:1]
        first_ref[seqs + s : seqs + s + 1, :] = decays[:1] * total[:1]


def backward_scan(seqs, conv, inner, lift, table_d, softrate, restart, cum, local, carried, pre, grads):
    rows, width = conv.shape
    heads, size = table_d.shape[:2]
    tile = pl.BlockSpec((rows, size), lambda h: (0, h))
    table = pl.BlockSpec((1, size, size), lambda h: (h, 0, 0))
    out = jax.ShapeDtypeStruct((rows, width), F32)
    return pl.pallas_call(
        functools.partial(backward_scan_kernel, seqs),
        out_shape=(out, out, jax.ShapeDtypeStruct((2 * seqs, width), F32), jax.ShapeDtypeStruct((rows, width), BF16)),
        grid=(heads,),
        in_specs=[
            tile,
            pl.BlockSpec(inner.shape, lambda h: (0, 0)),
            pl.BlockSpec((lift.shape[0], size), lambda h: (0, h)),
            table,
            pl.BlockSpec((1, size), lambda h: (0, h)),
            pl.BlockSpec(restart.shape, lambda h: (0, 0)),
            tile,
            tile,
            pl.BlockSpec((seqs, size), lambda h: (0, h)),
            tile,
            tile,
        ],
        out_specs=(tile, tile, pl.BlockSpec((2 * seqs, size), lambda h: (0, h)), tile),
        compiler_params=pltpu.CompilerParams(vmem_limit_bytes=48 * 2**20),
        cost_estimate=pl.CostEstimate(
            flops=2 * rows * width * size + 80 * rows * width,
            bytes_accessed=30 * rows * width,
            transcendentals=4 * rows * width),
    )(conv, inner, lift, table_d, softrate, restart, cum, local, carried, pre, grads)


def backward_gates_kernel(seqs, conv_ref, inner_ref, lift_ref, table_d_ref, table_a_ref, soft_ref, restart_ref,
                          cum_ref, local_ref, carried_ref, span_ref, total_ref, incoming_ref,
                          conv_grad_ref, through_ref, lift_grad_ref):
    stretch = conv_ref.shape[0] // seqs
    half = lift_ref.shape[0] // 2

    @pl.when(pl.program_id(0) == 0)
    def _():
        through_ref[...] = jnp.zeros_like(through_ref)

    for s in range(seqs):
        rows = pl.ds(s * stretch, stretch)
        conv = conv_ref[rows, :]
        inner = inner_ref[rows, :]
        restart = restart_ref[rows, :] > 0.5
        softrate = soft_ref[...]
        decay_gate, admit, grown, scale = gate_values(
            conv, inner, lift_ref[...], table_d_ref[0], table_a_ref[0], softrate, restart)
        carried = carried_ref[s : s + 1, :]
        state = local_ref[rows, :] + cum_ref[rows, :] * carried
        place = lax.broadcasted_iota(jnp.int32, state.shape, 0)
        before = jnp.where(place >= 1, pltpu.roll(state, 1, 0), carried)
        grads = total_ref[rows, :] + span_ref[rows, :] * incoming_ref[s : s + 1, :]
        driven = grads * jnp.where(restart, 1.0, scale)
        grad_log = jnp.where(
            restart, 0.0, grads * (before * grown - conv * admit * grown * grown / scale))
        grad_d = (-8.0 * softrate) * grad_log * decay_gate * (1.0 - decay_gate)
        grad_a = driven * conv * admit * (1.0 - admit)
        low_d, low_a = grad_d.astype(BF16), grad_a.astype(BF16)
        conv_grad_ref[rows, :] = driven * admit + dot(low_d, table_d_ref[0], NT) + dot(low_a, table_a_ref[0], NT)
        through_ref[rows, :half] += dot(low_d, lift_ref[:half, :], NT)
        through_ref[rows, half:] += dot(low_a, lift_ref[half:, :], NT)
        first = dot(inner[:, :half], low_d, TN)
        second = dot(inner[:, half:], low_a, TN)
        if s == 0:
            lift_grad_ref[:half, :] = first
            lift_grad_ref[half:, :] = second
        else:
            lift_grad_ref[:half, :] += first
            lift_grad_ref[half:, :] += second


def backward_gates(seqs, conv, inner, lift, table_d, table_a, softrate, restart, cum, local, carried, span, total,
                   incoming):
    rows, width = conv.shape
    heads, size = table_d.shape[:2]
    tile = pl.BlockSpec((rows, size), lambda h: (0, h))
    table = pl.BlockSpec((1, size, size), lambda h: (h, 0, 0))
    edge = pl.BlockSpec((seqs, size), lambda h: (0, h))
    ranks = pl.BlockSpec((lift.shape[0], size), lambda h: (0, h))
    return pl.pallas_call(
        functools.partial(backward_gates_kernel, seqs),
        out_shape=(
            jax.ShapeDtypeStruct((rows, width), F32),
            jax.ShapeDtypeStruct(inner.shape, F32),
            jax.ShapeDtypeStruct(lift.shape, F32),
        ),
        grid=(heads,),
        in_specs=[
            tile,
            pl.BlockSpec(inner.shape, lambda h: (0, 0)),
            ranks,
            table,
            table,
            pl.BlockSpec((1, size), lambda h: (0, h)),
            pl.BlockSpec(restart.shape, lambda h: (0, 0)),
            tile,
            tile,
            edge,
            tile,
            tile,
            edge,
        ],
        out_specs=(tile, pl.BlockSpec(inner.shape, lambda h: (0, 0)), ranks),
        compiler_params=pltpu.CompilerParams(vmem_limit_bytes=48 * 2**20),
        cost_estimate=pl.CostEstimate(
            flops=8 * rows * width * size + 80 * rows * width,
            bytes_accessed=24 * rows * width,
            transcendentals=6 * rows * width),
    )(conv, inner, lift, table_d, table_a, softrate, restart, cum, local, carried, span, total, incoming)


def spread_kernel(tables, ids_ref, got_ref, *out_refs):
    replicas, seqs, ranks = got_ref.shape[0], ids_ref.shape[0] // got_ref.shape[0], out_refs[0].shape[1]
    for table in range(tables):
        out_refs[table][...] = jnp.zeros_like(out_refs[table])
    for replica in range(replicas):
        for s in range(seqs):
            place = ids_ref[replica * seqs + s]
            for table in range(tables):
                rows = pl.ds((table * seqs + s) * ranks, ranks)
                out_refs[table][place] += got_ref[replica, rows, :].astype(F32)


def spread(ids, got, tables, sets, seqs):
    replicas, rows, width = got.shape
    ranks = rows // (tables * seqs)
    return pl.pallas_call(
        functools.partial(spread_kernel, tables),
        out_shape=[jax.ShapeDtypeStruct((sets, ranks, width), F32)] * tables,
        in_specs=[pl.BlockSpec(memory_space=pltpu.SMEM), pl.BlockSpec(memory_space=pltpu.VMEM)],
        out_specs=[pl.BlockSpec(memory_space=pltpu.VMEM)] * tables,
        compiler_params=pltpu.CompilerParams(vmem_limit_bytes=56 * 2**20),
        cost_estimate=pl.CostEstimate(
            flops=replicas * rows * width,
            bytes_accessed=2 * replicas * rows * width + 4 * tables * sets * ranks * width, transcendentals=0),
    )(ids, got)


def passed_along(block, axis, distance):
    devices = range(lax.axis_size(axis))
    route = [(i - distance, i) for i in devices if i - distance in devices]
    return lax.ppermute(block, axis, route)


def gathered_halves(weight, split, join):
    count = weight.shape[split] // 2
    parity = lax.axis_index("replica") % 2
    part = lax.dynamic_slice_in_dim(weight, parity * count, count, split)
    mine = lax.all_gather(part, "group", axis=join, tiled=True)
    swap = [(i, i ^ 1) for i in range(lax.axis_size("replica"))]
    return mine, lax.ppermute(mine, "replica", swap)


def by_parity(mine, other, axis):
    parity = lax.axis_index("replica") % 2
    return lax.cond(
        parity == 0,
        lambda: jnp.concatenate([mine, other], axis),
        lambda: jnp.concatenate([other, mine], axis),
    )


def body(
    inputs, segment_ids, adapter_ids, gain_mix, gain_mlp, w_branch, w_input, conv_taps, decay_heads, admit_heads,
    decay_param, w_mixer, w_gate, w_upper, w_down, down_branch, lift_branch, down_input, lift_input, down_decay,
    lift_decay, down_admit, lift_admit, down_mixer, lift_mixer, down_gate, lift_gate, down_upper, lift_upper,
    down_outward, lift_outward, out_grad,
):
    seqs, stretch, width = inputs.shape
    rows = seqs * stretch
    taps = conv_taps.shape[0]
    sets, _, ranks = down_branch.shape
    group, place = lax.axis_size("group"), lax.axis_index("group")
    mask_cols = seqs * ranks

    def chosen(table, down):
        table = jnp.swapaxes(table, 1, 2) if down else table
        return jnp.concatenate(
            [lax.dynamic_index_in_dim(table, adapter_ids[s], 0, False) for s in range(seqs)], 0)

    full_names = [down_branch, down_input, down_decay, down_admit, down_mixer, down_gate, down_upper,
                  lift_branch, lift_input, lift_decay, lift_admit, lift_mixer, lift_outward]
    stack = jnp.concatenate([chosen(t, i < 7) for i, t in enumerate(full_names)], 0)
    stack = lax.all_gather(stack, "group", axis=1, tiled=True)
    pick = [stack[i * mask_cols : (i + 1) * mask_cols] for i in range(13)]
    (p_down_branch, p_down_input, p_down_decay, p_down_admit, p_down_mixer, p_down_gate, p_down_upper,
     p_lift_branch, p_lift_input, p_lift_decay, p_lift_admit, p_lift_mixer, p_lift_outward) = pick
    own_lift_gate, own_lift_upper, own_down_outward = (
        chosen(lift_gate, False), chosen(lift_upper, False), chosen(down_outward, True))
    all_ids = lax.all_gather(adapter_ids, "replica", axis=0, tiled=True)

    branch_mine, branch_other = gathered_halves(w_branch, 0, 1)
    input_mine, input_other = gathered_halves(w_input, 0, 1)
    mixer_mine, mixer_other = gathered_halves(w_mixer, 1, 0)
    half = width // 2

    row_seq = lax.broadcasted_iota(jnp.int32, (rows, mask_cols), 0) // stretch
    col_seq = lax.broadcasted_iota(jnp.int32, (rows, mask_cols), 1) // ranks
    own = (row_seq == col_seq).astype(F32)
    own_two = jnp.concatenate([own, own], 1)

    begin = place * stretch
    padded_ids = jnp.pad(segment_ids, ((0, 0), (taps - 1, taps - 1)), constant_values=-1)
    window = lax.dynamic_slice_in_dim(padded_ids, begin, stretch + 2 * (taps - 1), 1)
    current = window[:, taps - 1 : taps - 1 + stretch + taps - 1]
    agree = [
        ((current == window[:, taps - 1 - j : taps - 1 - j + stretch + taps - 1]) & (current >= 0)).astype(F32)
        for j in range(taps)
    ]
    restart = (1.0 - agree[1][:, :stretch]).reshape(rows, 1)

    x_float = inputs.reshape(rows, width).astype(F32)
    normed_f, rate_one = norm_rows(x_float, gain_mix)
    normed = normed_f.astype(BF16)
    parity = lax.axis_index("replica") % 2
    normed_mine = lax.dynamic_slice_in_dim(normed, parity * half, half, 1)
    normed_other = lax.dynamic_slice_in_dim(normed, (1 - parity) * half, half, 1)
    inner_one = (dot(normed, stack[: 2 * mask_cols], NT) * own_two).astype(BF16)
    inner_branch, inner_input = inner_one[:, :mask_cols], inner_one[:, mask_cols:]
    branch_pre = dot(normed_mine, branch_mine) + dot(normed_other, branch_other) + dot(inner_branch, p_lift_branch)
    fed = (dot(normed_mine, input_mine) + dot(normed_other, input_other) + dot(inner_input, p_lift_input)).astype(BF16)
    fed = fed.reshape(seqs, stretch, width)
    halo = passed_along(fed[:, stretch - (taps - 1) :], "group", 1)
    extended = jnp.concatenate([halo, fed], axis=1).astype(F32)
    convolved = sum(
        conv_taps[j] * agree[j][:, :stretch, None] * extended[:, taps - 1 - j : taps - 1 - j + stretch]
        for j in range(taps)
    ).reshape(rows, width)
    rounded = convolved.astype(BF16)
    softrate = jax.nn.softplus(decay_param).reshape(1, width)
    inner_gates = (dot(rounded, stack[2 * mask_cols : 4 * mask_cols], NT) * own_two).astype(BF16)
    lift_gates = stack[9 * mask_cols : 11 * mask_cols]
    cum, local = forward_gates(seqs, convolved, inner_gates, lift_gates, decay_heads, admit_heads, softrate, restart)
    ends = jnp.concatenate(
        [cum.reshape(seqs, stretch, width)[:, -1], local.reshape(seqs, stretch, width)[:, -1]], 0)
    all_ends = lax.all_gather(ends, "group")
    carried = jnp.zeros((seqs, width), F32)
    for g in range(group - 1):
        longer = all_ends[g, :seqs] * carried + all_ends[g, seqs:]
        carried = jnp.where(g < place, longer, carried)
    carried_rows = jnp.repeat(carried, stretch, axis=0)
    state = local + cum * carried_rows
    merged = (state * gelu(branch_pre)).astype(BF16)
    inner_mixer = (dot(merged, p_down_mixer, NT) * own).astype(BF16)
    mixed = by_parity(dot(merged, mixer_mine), dot(merged, mixer_other), 1) + dot(inner_mixer, p_lift_mixer)
    resid = x_float + mixed
    normed_two_f, rate_two = norm_rows(resid, gain_mlp)
    normed_two = normed_two_f.astype(BF16).reshape(seqs, stretch, width)

    outs, backs, down_parts, lift_parts = [], [], [], []
    grad_own_lift_gate, grad_own_lift_upper, grad_own_down_outward = [], [], []
    grad_down_gate, grad_down_upper, grad_lift_outward = [], [], []
    for s in range(seqs):
        at = slice(s * ranks, (s + 1) * ranks)
        cotangent = lax.all_gather(out_grad[s], "group", axis=0, tiled=True)
        tokens = lax.all_gather(normed_two[s], "group", axis=0, tiled=True)
        inner_gate = dot(tokens, p_down_gate[at], NT).astype(BF16)
        inner_upper = dot(tokens, p_down_upper[at], NT).astype(BF16)
        through_out = dot(cotangent, p_lift_outward[at], NT).astype(BF16)
        gate_pre = dot(tokens, w_gate) + dot(inner_gate, own_lift_gate[at])
        upper_pre = dot(tokens, w_upper) + dot(inner_upper, own_lift_upper[at])
        grad_hidden = dot(cotangent, w_down, NT) + dot(through_out, own_down_outward[at])
        value, slope = gelu_both(gate_pre)
        hidden = (value * upper_pre).astype(BF16)
        grad_gate = (grad_hidden * upper_pre * slope).astype(BF16)
        grad_upper = (grad_hidden * value).astype(BF16)
        inner_out = dot(hidden, own_down_outward[at], NT).astype(BF16)
        outward = dot(hidden, w_down) + dot(inner_out, p_lift_outward[at])
        through_gate = dot(grad_gate, own_lift_gate[at], NT).astype(BF16)
        through_upper = dot(grad_upper, own_lift_upper[at], NT).astype(BF16)
        back = (dot(grad_gate, w_gate, NT) + dot(grad_upper, w_upper, NT)
                + dot(through_gate, p_down_gate[at]) + dot(through_upper, p_down_upper[at]))
        backs.append(lax.psum_scatter(back.astype(BF16), "group", scatter_dimension=0, tiled=True))
        outs.append(lax.psum_scatter(outward.astype(BF16), "group", scatter_dimension=0, tiled=True))
        grad_own_lift_gate.append(dot(inner_gate, grad_gate, TN))
        grad_own_lift_upper.append(dot(inner_upper, grad_upper, TN))
        grad_own_down_outward.append(dot(through_out, hidden, TN))
        grad_down_gate.append(dot(through_gate, tokens, TN))
        grad_down_upper.append(dot(through_upper, tokens, TN))
        grad_lift_outward.append(dot(inner_out, cotangent, TN))
    outward = jnp.concatenate(outs, 0).astype(F32)
    grad_normed_two = jnp.concatenate(backs, 0).astype(F32)
    block_out = (resid + outward).astype(BF16).reshape(seqs, stretch, width)
    grad_resid = out_grad.reshape(rows, width).astype(F32) + norm_back(resid, gain_mlp, rate_two, grad_normed_two)

    grad_mixed = grad_resid.astype(BF16)
    grad_mixed_mine = lax.dynamic_slice_in_dim(grad_mixed, parity * half, half, 1)
    grad_mixed_other = lax.dynamic_slice_in_dim(grad_mixed, (1 - parity) * half, half, 1)
    through_mixer = (dot(grad_mixed, p_lift_mixer, NT) * own).astype(BF16)
    grad_merged = (dot(grad_mixed_mine, mixer_mine, NT) + dot(grad_mixed_other, mixer_other, NT)
                   + dot(through_mixer, p_down_mixer))
    span, total, firsts, grad_branch_pre = backward_scan(
        seqs, convolved, inner_gates, lift_gates, decay_heads, softrate, restart, cum, local, carried, branch_pre,
        grad_merged)
    all_firsts = lax.all_gather(firsts, "group")
    incoming = jnp.zeros((seqs, width), F32)
    for lap in range(group - 1):
        g = group - 1 - lap
        longer = all_firsts[g, :seqs] * incoming + all_firsts[g, seqs:]
        incoming = jnp.where(g > place, longer, incoming)
    grad_direct, through_gates, grad_lift_gates = backward_gates(
        seqs, convolved, inner_gates, lift_gates, decay_heads, admit_heads, softrate, restart, cum, local, carried,
        span, total, incoming)
    through_gates = (through_gates * own_two).astype(BF16)
    grad_convolved = grad_direct + dot(through_gates, stack[2 * mask_cols : 4 * mask_cols])
    grad_convolved = grad_convolved.reshape(seqs, stretch, width)
    below = passed_along(grad_convolved[:, : taps - 1].astype(BF16), "group", -1).astype(F32)
    grad_extended = jnp.concatenate([grad_convolved, below], axis=1)
    grad_fed = sum(
        conv_taps[j] * agree[j][:, j : j + stretch, None] * grad_extended[:, j : j + stretch] for j in range(taps)
    ).astype(BF16).reshape(rows, width)
    through_branch = (dot(grad_branch_pre, p_lift_branch, NT) * own).astype(BF16)
    through_input = (dot(grad_fed, p_lift_input, NT) * own).astype(BF16)
    through_one = jnp.concatenate([through_branch, through_input], 1)
    grad_normed = (
        by_parity(
            dot(grad_branch_pre, branch_mine, NT) + dot(grad_fed, input_mine, NT),
            dot(grad_branch_pre, branch_other, NT) + dot(grad_fed, input_other, NT), 1)
        + dot(through_one, stack[: 2 * mask_cols]))
    grad_inputs = grad_resid + norm_back(x_float, gain_mix, rate_one, grad_normed)

    partial = jnp.concatenate(
        [dot(through_one, normed, TN), dot(through_gates, rounded, TN), dot(through_mixer, merged, TN)]
        + grad_down_gate + grad_down_upper
        + [dot(inner_branch, grad_branch_pre, TN), dot(inner_input, grad_fed, TN), grad_lift_gates,
           dot(inner_mixer, grad_mixed, TN)]
        + grad_lift_outward, 0).astype(BF16)
    owned = lax.psum_scatter(partial, "group", scatter_dimension=1, tiled=True)
    wide = jnp.concatenate(grad_own_lift_gate + grad_own_lift_upper + grad_own_down_outward, 0).astype(BF16)
    totals = spread(all_ids, lax.all_gather(owned, "replica"), 13, sets, seqs)
    wides = spread(all_ids, lax.all_gather(wide, "replica"), 3, sets, seqs)
    turned = lambda table: jnp.swapaxes(table, 1, 2)
    return (
        block_out, grad_inputs.reshape(seqs, stretch, width),
        turned(totals[0]), totals[7], turned(totals[1]), totals[8], turned(totals[2]), totals[9],
        turned(totals[3]), totals[10], turned(totals[4]), totals[11], turned(totals[5]), wides[0],
        turned(totals[6]), wides[1], turned(wides[2]), totals[12],
    )


def solution(mesh):
    tokens = P("replica", "group", None)
    down, lift = P(None, "group", None), P(None, None, "group")
    cols, split = P(None, "group"), P("group", None)
    in_specs = (
        tokens, P("replica", None), P("replica"), P(), P(), cols, cols, P(), P(), P(), P(), split, cols, cols, split,
    ) + (down, lift) * 8 + (tokens,)
    out_specs = (tokens, tokens) + (down, lift) * 8
    return jax.shard_map(body, mesh=mesh, in_specs=in_specs, out_specs=out_specs, check_vma=False)
```

time: 3260 us -> 1140 us (0.35); the launches traced: 3220 us -> 1130 us
  local copies, waits for them, and re-layouts: 1410 us -> 62.9 us
  waiting for transfers between devices: 729 us -> 445 us
  blocking collectives: 241 us -> 28.7 us
  other arithmetic: 202 us -> 47.4 us
  matrix products: 609 us -> 455 us
  Pallas kernels: 0 us -> 66.4 us
    unnamed x498 -> x301, local copies, waits for them, and re-layouts: 665 us -> 47.4 us
    slice x111 -> x7, local copies, waits for them, and re-layouts: 435 us -> 8.03 us  [the longest x1 3.57 us: body(): cotangent = lax.all_gather(out_grad[s], 'group', axis=0, tiled=True)]
    all_gather x9 -> x10, waiting for transfers between devices: 658 us -> 296 us  [the longest x3 164 us: gathered_halves(): mine = lax.all_gather(part, 'group', axis=join, tiled=True)]
    all_gather x17 -> x2, blocking collectives: 241 us -> 18.3 us  [the longest x1 9.94 us: body(): all_ends = lax.all_gather(ends, 'group')]
    pad x56 -> x0, local copies, waits for them, and re-layouts: 168 us -> none  [the longest x28 85.2 us: body(): lax.associative_scan(affine_join, (decays, drive), axis=1)]
    dot_general x96 -> x78, matrix products: 609 us -> 455 us  [dot(): return lax.dot_general(a, b, dims, preferred_element_type=F32)]
    reduce_scatter x0 -> x4, waiting for transfers between devices: none -> 146 us  [the longest x2 90.8 us: body(): lax.psum_scatter(outward.astype(BF16), 'group', scatter_dimension=0, tile...]
    rev x2 -> x0, local copies, waits for them, and re-layouts: 81.1 us -> none  [body(): lax.associative_scan(affine_join, (alphas, grad_state), axis=1, reverse=T...]
  transfers between devices with their start and end apart: 28 -> 20, of which waited for: 5 -> 12; matrix products, arithmetic and copies ran while one was open for 51% -> 44% of each run, Pallas kernels for 0% -> 2%
where the time goes in v1:
time: 1140 us; the launch traced here: 1130 us
  matrix products  455 us (40%)
  waiting for transfers between devices  445 us (39%)
  Pallas kernels  66.4 us (6%)
  local copies, waits for them, and re-layouts  62.9 us (6%)
  other arithmetic  47.4 us (4%)
  blocking collectives  28.7 us (3%)
  between operations  20.7 us (2%)
    dot_general x78, matrix products, dot(): return lax.dot_general(a, b, dims, preferred_element_type=F32)  455 us
    all_gather x3, waiting for transfers between devices, gathered_halves(): mine = lax.all_gather(part, 'group', axis=join, tiled=True)  164 us
    reduce_scatter x2, waiting for transfers between devices, body(): lax.psum_scatter(outward.astype(BF16), 'group', scatter_dimension=0, tile...  90.8 us
    reduce_scatter x2, waiting for transfers between devices, body(): lax.psum_scatter(back.astype(BF16), 'group', scatter_dimension=0, tiled=T...  55.6 us
    unnamed x301, local copies, waits for them, and re-layouts  47.4 us
    all_gather x1, waiting for transfers between devices, body(): totals = spread(all_ids, lax.all_gather(owned, 'replica'), 13, sets, seqs)  35.6 us
    all_gather x1, waiting for transfers between devices, body(): stack = lax.all_gather(stack, 'group', axis=1, tiled=True)  32.9 us
    all_gather x2, waiting for transfers between devices, body(): tokens = lax.all_gather(normed_two[s], 'group', axis=0, tiled=True)  27.3 us
  transfers between devices with their start and end apart: 20, of which 12 were waited for; matrix products, arithmetic and copies ran while one was open for 44% of the time, Pallas kernels for 2%

profile of v1, /device:TPU:0, one launch (start us, length us, event | category | flops | bytes accessed | tf_op | source)
XLA Modules:
  0.0 1132.9 jit_solution(8860287988161378275)
XLA Ops:
  58.5 27.1 %all-gather.18.cloned.1.call-done = bf16[1280,2560]{1,0:T(8,128)(2,1)} async-done(((bf16[1280,640]{1,0:T(8,128)(2,1)}), bf16[1280,2560]{1,0:T(8,128)(2,1)}) %all-gather.18.cloned.1.call-update) | async-done | bytes 6553616 | tf_op jit(solution)/shard_map/all_gather | solution.py:301
  90.8 32.9 %all-gather.20.cloned.1.call-done = bf16[416,2560]{1,0:T(8,128)(2,1)} async-done(((bf16[416,640]{1,0:T(8,128)(2,1)}), bf16[416,2560]{1,0:T(8,128)(2,1)}) %all-gather.20.cloned.1.call-update) | async-done | bytes 2129936 | tf_op jit(solution)/shard_map/all_gather | solution.py:336
  126.3 72.2 %all-gather.22.cloned.1.call-done = bf16[1280,2560]{1,0:T(8,128)(2,1)} async-done(((bf16[1280,640]{1,0:T(8,128)(2,1)}), bf16[1280,2560]{1,0:T(8,128)(2,1)}) %all-gather.22.cloned.1.call-update) | async-done | bytes 6553616 | tf_op jit(solution)/shard_map/all_gather | solution.py:301
  207.9 64.6 %all-gather.24.cloned.1.call-done = bf16[2560,1280]{1,0:T(8,128)(2,1)} async-done(((bf16[640,1280]{1,0:T(8,128)(2,1)}), bf16[2560,1280]{1,0:T(8,128)(2,1)}) %all-gather.24.cloned.1.call-update) | async-done | bytes 6553616 | tf_op jit(solution)/shard_map/all_gather | solution.py:301
  306.0 16.8 %shard_map.439 = (f32[512,2560]{1,0:T(8,128)S(1)}, f32[512,2560]{1,0:T(8,128)S(1)}) custom-call(f32[512,2560]{1,0:T(8,128)} %bitcast.409, bf16[512,64]{1,0:T(8,128)(2,1)S(1)} %fusion.105.inner_ref, bf16[64,2560]{1,0:T(8,128)(2,1)S(1)} %slice.310.lift_ref, bf16[10,256,256]{2,1,0:T(8,128)(2,1)S(1)} %copy-done.4, bf16[10,256,256]{2,1,0:T(8,128)(2,1)S(1)} %copy-done.6, ...), custom_call_target="tpu_custom_call" | custom-call | flops 1420820480 | bytes 15728640 | tf_op jit(solution)/shard_map/pallas_call | solution.py:106
  333.0 15.1 %fusion.30 = (bf16[512,2560]{1,0:T(8,128)(2,1)}, f32[512,2560]{1,0:T(8,128)}) fusion(f32[512,2560]{1,0:T(8,128)S(1)} %get-tuple-element.73.local_ref, f32[512,2560]{1,0:T(8,128)S(1)} %get-tuple-element.74.cum_ref, f32[2,2560]{1,0:T(2,128)S(1)} %fusion.182.carried_ref, f32[512,2560]{1,0:T(8,128)} %fusion.126, f32[512,2560]{1,0:T(8,128)} %fusion.96, ...), kind=kOutput, calls=%fused_computation.53 | convolution fusion | flops 3373793280 | bytes 36720644 | tf_op jit(solution)/shard_map/dot_general | solution.py:21
  379.5 21.1 %all-gather.34.cloned.1.call-done = bf16[1,1024,2560]{2,1,0:T(8,128)(2,1)} async-done(((bf16[1,256,2560]{2,1,0:T(8,128)(2,1)}), bf16[1,1024,2560]{2,1,0:T(8,128)(2,1)}) %all-gather.34.cloned.1.call-update) | async-done | bytes 5242896 | tf_op jit(solution)/shard_map/all_gather | solution.py:407
  405.3 15.6 %fusion.42 = f32[1024,1920]{1,0:T(8,128)} fusion(bf16[1920,2560]{1,0:T(8,128)(2,1)} %param.50, bf16[1,1024,2560]{2,1,0:T(8,128)(2,1)S(1)} %copy-done.29), kind=kOutput, calls=%fused_computation.70 | convolution fusion | flops 10066329600 | bytes 22937600 | tf_op jit(solution)/shard_map/dot_general | solution.py:21
  421.0 15.6 %fusion.36 = f32[1024,1920]{1,0:T(8,128)} fusion(bf16[1920,2560]{1,0:T(8,128)(2,1)} %param.50, bf16[1,1024,2560]{2,1,0:T(8,128)(2,1)S(1)} %bitcast.424), kind=kOutput, calls=%fused_computation.64 | convolution fusion | flops 10066329600 | bytes 22937600 | tf_op jit(solution)/shard_map/dot_general | solution.py:21
  436.6 27.3 %all-gather.26.cloned.1.call-done = bf16[1024,2560]{1,0:T(8,128)(2,1)} async-done(((bf16[256,2560]{1,0:T(8,128)(2,1)}), bf16[1024,2560]{1,0:T(8,128)(2,1)}) %all-gather.26.cloned.1.call-update) | async-done | bytes 5242896 | tf_op jit(solution)/shard_map/all_gather | solution.py:408
  468.0 14.3 %fusion.226 = f32[1024,1920]{1,0:T(8,128)S(1)} fusion(bf16[1024,2560]{1,0:T(8,128)(2,1)S(1)} %copy-done.14, bf16[2560,1920]{1,0:T(8,128)(2,1)} %param.49), kind=kOutput, calls=%fused_computation.373 | convolution fusion | flops 10066329600 | bytes 22937600 | tf_op jit(solution)/shard_map/dot_general | solution.py:21
  489.0 11.0 fusion.225
  504.4 13.6 %multiply_convert_fusion.1 = (bf16[1024,1920]{1,0:T(8,128)(2,1)S(1)}, bf16[1024,1920]{1,0:T(8,128)(2,1)S(1)}, bf16[1024,1920]{1,0:T(8,128)(2,1)}) fusion(f32[1024,1920]{1,0:T(8,128)} %convolution_add_fusion.6, f32[1024,1920]{1,0:T(8,128)} %convolution_add_fusion.5, f32[1024,1920]{1,0:T(8,128)} %fusion.42, bf16[16,1024]{1,0:T(8,128)(2,1)S(1)} %fusion.108, ...), kind=kOutput, calls=%fused_computation.27 | convolution fusion | flops 114032640 | bytes 35483652 | tf_op jit(solution)/shard_map/dot_general | solution.py:21
  526.7 16.0 %fusion.231 = f32[1024,2560]{1,0:T(8,128)} fusion(bf16[1024,1920]{1,0:T(8,128)(2,1)S(1)} %get-tuple-element.105, bf16[2560,1920]{1,0:T(8,128)(2,1)} %param.48), kind=kOutput, calls=%fused_computation.378 | convolution fusion | flops 10066329600 | bytes 24248320 | tf_op jit(solution)/shard_map/dot_general | solution.py:21
  542.7 16.0 %fusion.232 = f32[1024,2560]{1,0:T(8,128)} fusion(bf16[1024,1920]{1,0:T(8,128)(2,1)S(1)} %get-tuple-element.104, bf16[2560,1920]{1,0:T(8,128)(2,1)} %param.49), kind=kOutput, calls=%fused_computation.379 | convolution fusion | flops 10066329600 | bytes 24248320 | tf_op jit(solution)/shard_map/dot_general | solution.py:21
  558.7 13.4 %add_convert_fusion.1 = bf16[1024,2560]{1,0:T(8,128)(2,1)} fusion(f32[1024,2560]{1,0:T(8,128)} %fusion.146, f32[1024,2560]{1,0:T(8,128)} %fusion.231, f32[1024,2560]{1,0:T(8,128)} %fusion.232, bf16[1024,16]{0,1:T(8,128)(2,1)S(1)} %convolution_convert_fusion.18, bf16[416,2560]{1,0:T(8,128)(2,1)} %all-gather.20.cloned.1.call-done), kind=kOutput, calls=%fused_computation.9 | convolution fusion | flops 94371840 | bytes 36814848 | tf_op jit(solution)/shard_map/dot_general | solution.py:21
  576.2 14.8 %fusion.229 = f32[1024,1920]{1,0:T(8,128)S(1)} fusion(bf16[1024,2560]{1,0:T(8,128)(2,1)S(1)} %copy-done.15, bf16[2560,1920]{1,0:T(8,128)(2,1)} %param.49), kind=kOutput, calls=%fused_computation.376 | convolution fusion | flops 10066329600 | bytes 22937600 | tf_op jit(solution)/shard_map/dot_general | solution.py:21
  591.1 14.2 %fusion.228 = f32[1024,1920]{1,0:T(8,128)S(1)} fusion(bf16[1024,2560]{1,0:T(8,128)(2,1)S(1)} %copy-done.15, bf16[2560,1920]{1,0:T(8,128)(2,1)} %param.48), kind=kOutput, calls=%fused_computation.375 | convolution fusion | flops 10066329600 | bytes 22937600 | tf_op jit(solution)/shard_map/dot_general | solution.py:21
  616.6 13.6 %multiply_convert_fusion = (bf16[1024,1920]{1,0:T(8,128)(2,1)S(1)}, bf16[1024,1920]{1,0:T(8,128)(2,1)S(1)}, bf16[1024,1920]{1,0:T(8,128)(2,1)}) fusion(f32[1024,1920]{1,0:T(8,128)} %convolution_add_fusion.4, f32[1024,1920]{1,0:T(8,128)} %convolution_add_fusion.3, f32[1024,1920]{1,0:T(8,128)} %fusion.36, bf16[16,1024]{1,0:T(8,128)(2,1)S(1)} %copy-done.68, ...), kind=kOutput, calls=%fused_computation.26 | convolution fusion | flops 114032640 | bytes 35483652 | tf_op jit(solution)/shard_map/dot_general | solution.py:21
  638.9 16.1 %fusion.233 = f32[1024,2560]{1,0:T(8,128)} fusion(bf16[1024,1920]{1,0:T(8,128)(2,1)S(1)} %get-tuple-element.108, bf16[2560,1920]{1,0:T(8,128)(2,1)} %param.48), kind=kOutput, calls=%fused_computation.380 | convolution fusion | flops 10066329600 | bytes 24248320 | tf_op jit(solution)/shard_map/dot_general | solution.py:21
  655.0 16.0 %fusion.234 = f32[1024,2560]{1,0:T(8,128)} fusion(bf16[1024,1920]{1,0:T(8,128)(2,1)S(1)} %get-tuple-element.107, bf16[2560,1920]{1,0:T(8,128)(2,1)} %param.49), kind=kOutput, calls=%fused_computation.381 | convolution fusion | flops 10066329600 | bytes 24248320 | tf_op jit(solution)/shard_map/dot_general | solution.py:21
  671.1 13.6 %add_convert_fusion = bf16[1024,2560]{1,0:T(8,128)(2,1)} fusion(f32[1024,2560]{1,0:T(8,128)} %fusion.139, f32[1024,2560]{1,0:T(8,128)} %fusion.233, f32[1024,2560]{1,0:T(8,128)} %fusion.234, bf16[1024,16]{0,1:T(8,128)(2,1)S(1)} %convolution_convert_fusion.16, bf16[416,2560]{1,0:T(8,128)(2,1)} %all-gather.20.cloned.1.call-done), kind=kOutput, calls=%fused_computation.8 | convolution fusion | flops 94371840 | bytes 36814848 | tf_op jit(solution)/shard_map/dot_general | solution.py:21
  690.6 55.6 %reduce-scatter.14.cloned.1.call-done = bf16[256,2560]{1,0:T(8,128)(2,1)} async-done(((bf16[1024,2560]{1,0:T(8,128)(2,1)}), bf16[256,2560]{1,0:T(8,128)(2,1)}) %reduce-scatter.14.cloned.1.call-update) | async-done | bytes 1310736 | tf_op jit(solution)/shard_map/reduce_scatter | solution.py:425
  777.0 20.9 %shard_map.440 = (f32[512,2560]{1,0:T(8,128)}, f32[512,2560]{1,0:T(8,128)}, f32[4,2560]{1,0:T(4,128)S(1)}, bf16[512,2560]{1,0:T(8,128)(2,1)S(1)}) custom-call(f32[512,2560]{1,0:T(8,128)} %bitcast.410, bf16[512,64]{1,0:T(8,128)(2,1)S(1)} %copy-done.9, bf16[64,2560]{1,0:T(8,128)(2,1)S(1)} %slice.310.lift_ref, bf16[10,256,256]{2,1,0:T(8,128)(2,1)S(1)} %copy-done.5, ...), custom_call_target="tpu_custom_call" | custom-call | flops 775946240 | bytes 39321600 | tf_op jit(solution)/shard_map/pallas_call | solution.py:156
  806.4 20.2 %shard_map.441 = (f32[512,2560]{1,0:T(8,128)}, f32[512,64]{1,0:T(8,128)S(1)}, f32[64,2560]{1,0:T(8,128)S(1)}) custom-call(f32[512,2560]{1,0:T(8,128)} %bitcast.411, bf16[512,64]{1,0:T(8,128)(2,1)S(1)} %copy-done.9, bf16[64,2560]{1,0:T(8,128)(2,1)S(1)} %slice.310.lift_ref, bf16[10,256,256]{2,1,0:T(8,128)(2,1)S(1)} %copy-done.5, ...), custom_call_target="tpu_custom_call" | custom-call | flops 2789212160 | bytes 31457280 | tf_op jit(solution)/shard_map/pallas_call | solution.py:232
  876.1 15.0 %fusion.227 = f32[1024,2560]{1,0:T(8,128)S(1)} fusion(bf16[1024,1920]{1,0:T(8,128)(2,1)} %get-tuple-element.106, bf16[1920,2560]{1,0:T(8,128)(2,1)} %param.50), kind=kOutput, calls=%fused_computation.374 | convolution fusion | flops 10066329600 | bytes 24248320 | tf_op jit(solution)/shard_map/dot_general | solution.py:21
  895.9 14.8 %fusion.230 = f32[1024,2560]{1,0:T(8,128)S(1)} fusion(bf16[1024,1920]{1,0:T(8,128)(2,1)} %get-tuple-element.109, bf16[1920,2560]{1,0:T(8,128)(2,1)} %param.50), kind=kOutput, calls=%fused_computation.377 | convolution fusion | flops 10066329600 | bytes 24248320 | tf_op jit(solution)/shard_map/dot_general | solution.py:21
  929.6 14.9 %all-gather.30.cloned.1.call-done.got_ref = bf16[8,96,1920]{2,1,0:T(8,128)(2,1)} async-done(((bf16[1,96,1920]{2,1,0:T(8,128)(2,1)}), bf16[8,96,1920]{2,1,0:T(8,128)(2,1)}) %all-gather.30.cloned.1.call-update) | async-done | bytes 2949136 | tf_op jit(solution)/shard_map/all_gather | solution.py:483
  981.4 26.5 %reduce-scatter.8.cloned.1.call-done = bf16[256,2560]{1,0:T(8,128)(2,1)} async-done(((bf16[1024,2560]{1,0:T(8,128)(2,1)}), bf16[256,2560]{1,0:T(8,128)(2,1)}) %reduce-scatter.8.cloned.1.call-update) | async-done | bytes 1310736 | tf_op jit(solution)/shard_map/reduce_scatter | solution.py:426
  1007.9 64.3 %reduce-scatter.10.cloned.1.call-done = bf16[256,2560]{1,0:T(8,128)(2,1)} async-done(((bf16[1024,2560]{1,0:T(8,128)(2,1)}), bf16[256,2560]{1,0:T(8,128)(2,1)}) %reduce-scatter.10.cloned.1.call-update) | async-done | bytes 1310736 | tf_op jit(solution)/shard_map/reduce_scatter | solution.py:426
  1072.2 13.7 %fusion.50 = (f32[512,2560]{1,0:T(8,128)}, bf16[512,2560]{1,0:T(8,128)(2,1)}) fusion(bf16[2,256,2560]{2,1,0:T(8,128)(2,1)} %param.36, f32[512]{0:T(512)S(1)} %fusion.208, f32[512]{0:T(512)} %bitcast.441, f32[2560]{0:T(1024)} %param.39, f32[512,2560]{1,0:T(8,128)} %get-tuple-element.140, f32[512,2560]{1,0:T(8,128)} %get-tuple-element.132, ...), kind=kLoop, calls=%fused_computation.84 | loop fusion | flops 30146560 | bytes 34107392 | tf_op jit(solution)/shard_map/add | solution.py:472
  1085.9 35.6 %all-gather.36.cloned.1.call-done = bf16[3328,640]{1,0:T(8,128)(2,1)} async-done(((bf16[416,640]{1,0:T(8,128)(2,1)}), bf16[3328,640]{1,0:T(8,128)(2,1)}) %all-gather.36.cloned.1.call-update) | async-done | bytes 4259856 | tf_op jit(solution)/shard_map/all_gather | solution.py:482
  (467 shorter events, 356.0 us)
Async XLA Ops:
  7.2 78.4 %all-gather.18.cloned.1.call-start = ((), (), s32[]{:S(2)}) async-start(), calls=%async_computation.5 | async-start | bytes 8192000 | tf_op jit(solution)/shard_map/all_gather | solution.py:301
  10.5 113.2 %all-gather.20.cloned.1.call-start = ((), (), s32[]{:S(2)}) async-start(), calls=%async_computation.6 | async-start | bytes 2662400 | tf_op jit(solution)/shard_map/all_gather | solution.py:336
  50.6 147.9 %all-gather.22.cloned.1.call-start = ((), (), s32[]{:S(2)}) async-start(), calls=%async_computation.7 | async-start | bytes 8192000 | tf_op jit(solution)/shard_map/all_gather | solution.py:301
  53.4 219.2 %all-gather.24.cloned.1.call-start = ((), (), s32[]{:S(2)}) async-start(), calls=%async_computation.8 | async-start | bytes 8192000 | tf_op jit(solution)/shard_map/all_gather | solution.py:301
  54.8 320.7 %all-gather.32.cloned.1.call-start = ((), (), s32[]{:S(2)}) async-start(), calls=%async_computation.16 | async-start | bytes 6553600 | tf_op jit(solution)/shard_map/all_gather | solution.py:407
  58.5 342.1 %all-gather.34.cloned.1.call-start = ((), (), s32[]{:S(2)}) async-start(), calls=%async_computation.17 | async-start | bytes 6553600 | tf_op jit(solution)/shard_map/all_gather | solution.py:407
  85.7 193.2 %collective-permute-start = (bf16[1280,2560]{1,0:T(8,128)(2,1)}, bf16[1280,2560]{1,0:T(8,128)(2,1)}, u32[]{:S(2)}, u32[]{:S(2)}) collective-permute-start(bf16[1280,2560]{1,0:T(8,128)(2,1)} %all-gather.18.cloned.1.call-done), channel_id=1, source_target_pairs={{0,1},{1,0},{2,3},{3,2},{4,5},{5,4},{6,7},{7,6},{8,9},{9,8},{10,11... | collective-permute-start | bytes 19660808 | tf_op jit(solution)/shard_map/ppermute | solution.py:303
  85.7 378.2 %all-gather.26.cloned.1.call-start = ((), (), s32[]{:S(2)}) async-start(), calls=%async_computation.9 | async-start | bytes 6553600 | tf_op jit(solution)/shard_map/all_gather | solution.py:408
  87.4 278.2 %copy-start.103 = (pred[32]{0:T(512)(128)(4,1)}, pred[32]{0:T(512)(128)(4,1)S(1)}, u32[]{:S(2)}) copy-start(pred[32]{0:T(512)(128)(4,1)S(1)} %compare_and_fusion) | copy-start | bytes 100
  87.4 278.1 %copy-start.105 = (pred[512]{0:T(512)(128)(4,1)}, pred[512]{0:T(512)(128)(4,1)S(1)}, u32[]{:S(2)}) copy-start(pred[512]{0:T(512)(128)(4,1)S(1)} %fusion.211) | copy-start | bytes 1540
  87.4 278.1 %copy-start.107 = (s32[32]{0:T(128)}, s32[32]{0:T(128)S(1)}, u32[]{:S(2)}) copy-start(s32[32]{0:T(128)S(1)} %get-tuple-element.135) | copy-start | bytes 388
  87.4 278.1 %copy-start.109 = (s32[32]{0:T(128)}, s32[32]{0:T(128)S(1)}, u32[]{:S(2)}) copy-start(s32[32]{0:T(128)S(1)} %get-tuple-element.136) | copy-start | bytes 388
  87.5 278.1 %copy-start.97 = (s32[512]{0:T(512)}, s32[512]{0:T(512)S(1)}, u32[]{:S(2)}) copy-start(s32[512]{0:T(512)S(1)} %get-tuple-element.133) | copy-start | bytes 6148
  87.5 278.1 %copy-start.99 = (s32[512]{0:T(512)}, s32[512]{0:T(512)S(1)}, u32[]{:S(2)}) copy-start(s32[512]{0:T(512)S(1)} %get-tuple-element.134) | copy-start | bytes 6148
  87.6 209.6 %copy-start.74 = (f32[2560]{0:T(1024)}, f32[2560]{0:T(1024)S(1)}, u32[]{:S(2)}) copy-start(f32[2560]{0:T(1024)S(1)} %get-tuple-element.98) | copy-start | bytes 30724
  87.6 209.6 %copy-start.76 = (f32[2560]{0:T(1024)}, f32[2560]{0:T(1024)S(1)}, u32[]{:S(2)}) copy-start(f32[2560]{0:T(1024)S(1)} %get-tuple-element.99) | copy-start | bytes 30724
  87.6 209.6 %copy-start.78 = (f32[2560]{0:T(1024)}, f32[2560]{0:T(1024)S(1)}, u32[]{:S(2)}) copy-start(f32[2560]{0:T(1024)S(1)} %get-tuple-element.100) | copy-start | bytes 30724
  87.6 209.6 %copy-start.80 = (f32[2560]{0:T(1024)}, f32[2560]{0:T(1024)S(1)}, u32[]{:S(2)}) copy-start(f32[2560]{0:T(1024)S(1)} %get-tuple-element.101) | copy-start | bytes 30724
  87.7 209.6 %copy-start.91 = (f32[2,256]{1,0:T(2,128)}, f32[2,256]{1,0:T(2,128)S(1)}, u32[]{:S(2)}) copy-start(f32[2,256]{1,0:T(2,128)S(1)} %slice_convert_fusion.1) | copy-start | bytes 6148
  88.6 213.6 %copy-start.40 = (pred[512,32]{1,0:T(32,128)(4,1)}, pred[512,32]{1,0:T(32,128)(4,1)S(1)}, u32[]{:S(2)}) copy-start(pred[512,32]{1,0:T(32,128)(4,1)S(1)} %select_compare_fusion) | copy-start | bytes 49156
  198.5 134.5 %collective-permute-start.2 = (bf16[1280,2560]{1,0:T(8,128)(2,1)}, bf16[1280,2560]{1,0:T(8,128)(2,1)}, u32[]{:S(2)}, u32[]{:S(2)}) collective-permute-start(bf16[1280,2560]{1,0:T(8,128)(2,1)} %all-gather.22.cloned.1.call-done), channel_id=1, source_target_pairs={{0,1},{1,0},{2,3},{3,2},{4,5},{5,4},{6,7},{7,6},{8,9},{9,8},{10,11... | collective-permute-start | bytes 19660808 | tf_op jit(solution)/shard_map/ppermute | solution.py:303
  272.6 83.2 %collective-permute-start.3 = (bf16[2560,1280]{1,0:T(8,128)(2,1)}, bf16[2560,1280]{1,0:T(8,128)(2,1)}, u32[]{:S(2)}, u32[]{:S(2)}) collective-permute-start(bf16[2560,1280]{1,0:T(8,128)(2,1)} %all-gather.24.cloned.1.call-done), channel_id=1, source_target_pairs={{0,1},{1,0},{2,3},{3,2},{4,5},{5,4},{6,7},{7,6},{8,9},{9,8},{10,11... | collective-permute-start | bytes 19660808 | tf_op jit(solution)/shard_map/ppermute | solution.py:303
  287.7 8.7 collective-permute-start.1
  375.4 196.7 %all-gather.28.cloned.1.call-start = ((), (), s32[]{:S(2)}) async-start(), calls=%async_computation.11 | async-start | bytes 6553600 | tf_op jit(solution)/shard_map/all_gather | solution.py:408
  436.6 254.0 %reduce-scatter.12.cloned.1.call-start = ((), (), s32[]{:S(2)}) async-start(), calls=%async_computation.13 | async-start | bytes 6553600 | tf_op jit(solution)/shard_map/reduce_scatter | solution.py:425
  572.0 174.1 %reduce-scatter.14.cloned.1.call-start = ((), (), s32[]{:S(2)}) async-start(), calls=%async_computation.14 | async-start | bytes 6553600 | tf_op jit(solution)/shard_map/reduce_scatter | solution.py:425
  684.7 230.8 %reduce-scatter.16.cloned.1.call-start = ((), (), s32[]{:S(2)}) async-start(), calls=%async_computation.19 | async-start | bytes 3276800
  830.2 5.9 collective-permute-start.4
  865.8 78.8 %all-gather.30.cloned.1.call-start = ((), (), s32[]{:S(2)}) async-start(), calls=%async_computation.15 | async-start | bytes 3317760 | tf_op jit(solution)/shard_map/all_gather | solution.py:483
  876.1 131.8 %reduce-scatter.8.cloned.1.call-start = ((), (), s32[]{:S(2)}) async-start(), calls=%async_computation.10 | async-start | bytes 6553600 | tf_op jit(solution)/shard_map/reduce_scatter | solution.py:426
  895.9 176.3 %reduce-scatter.10.cloned.1.call-start = ((), (), s32[]{:S(2)}) async-start(), calls=%async_computation.12 | async-start | bytes 6553600 | tf_op jit(solution)/shard_map/reduce_scatter | solution.py:426
  915.5 206.0 %all-gather.36.cloned.1.call-start = ((), (), s32[]{:S(2)}) async-start(), calls=%async_computation.18 | async-start | bytes 4792320 | tf_op jit(solution)/shard_map/all_gather | solution.py:482
  (121 other events, 1770.8 us)
Sparse Core Ops, SparseCore 0:
  10.6 75.0 all-gather.17
  88.1 35.5 all-gather.19
  126.1 72.3 all-gather.21
  200.2 72.3 all-gather.23
  274.2 63.1 all-gather.31
  339.1 61.4 all-gather.33
  402.4 61.4 all-gather.25
  465.7 61.4 all-gather.27
  572.2 61.4 reduce-scatter.11
  684.8 61.2 reduce-scatter.13
  865.9 39.6 reduce-scatter.15
  907.7 36.8 all-gather.29
  947.5 60.3 reduce-scatter.7
  1010.7 61.4 reduce-scatter.9
  1073.7 47.7 all-gather.35

commit v2 on v1

--- a/solution.py
+++ b/solution.py
@@ -261,6 +261,362 @@
     )(conv, inner, lift, table_d, table_a, softrate, restart, cum, local, carried, span, total, incoming)
 
 
+def resident(array):
+    return pl.BlockSpec(array.shape, lambda i: (0, 0), pipeline_mode=pl.Buffered(1))
+
+
+def tile_of(count, tile):
+    return tile if count % 128 == 0 and count > tile else count
+
+
+def grad_hidden_kernel(cot_ref, wd_ref, lift_out_ref, do_ref, out_ref, through_ref):
+    @pl.when(pl.program_id(0) == 0)
+    def _():
+        through_ref[...] = dot(cot_ref[...], lift_out_ref[...], NT).astype(BF16)
+
+    out_ref[...] = (dot(cot_ref[...], wd_ref[...], NT) + dot(through_ref[...], do_ref[...])).astype(BF16)
+
+
+def grad_hidden_call(cot, wd, lift_out, do):
+    rows, width = cot.shape
+    units, ranks = wd.shape[0], do.shape[0]
+    tile = tile_of(units, 512)
+    return pl.pallas_call(
+        grad_hidden_kernel,
+        grid=(pl.cdiv(units, tile),),
+        out_shape=[jax.ShapeDtypeStruct((rows, units), BF16), jax.ShapeDtypeStruct((rows, ranks), BF16)],
+        in_specs=[resident(cot), pl.BlockSpec((tile, width), lambda i: (i, 0)), resident(lift_out),
+                  pl.BlockSpec((ranks, tile), lambda i: (0, i))],
+        out_specs=[pl.BlockSpec((rows, tile), lambda i: (0, i)), pl.BlockSpec((rows, ranks), lambda i: (0, 0))],
+        compiler_params=pltpu.CompilerParams(vmem_limit_bytes=60 * 2**20),
+        cost_estimate=pl.CostEstimate(
+            flops=2 * rows * width * units, bytes_accessed=2 * width * units + 2 * rows * (units + width),
+            transcendentals=0),
+    )(cot, wd, lift_out, do)
+
+
+def hidden_kernel(tok_ref, gh_ref, wg_ref, wu_ref, down_ref, lg_ref, lu_ref, hidden_ref, gg_ref, gu_ref, inner_ref):
+    ranks = lg_ref.shape[0]
+
+    @pl.when(pl.program_id(0) == 0)
+    def _():
+        inner_ref[...] = dot(tok_ref[...], down_ref[...], NT).astype(BF16)
+
+    tokens, inner = tok_ref[...], inner_ref[...]
+    gate = dot(tokens, wg_ref[...]) + dot(inner[:, :ranks], lg_ref[...])
+    upper = dot(tokens, wu_ref[...]) + dot(inner[:, ranks:], lu_ref[...])
+    grad_hidden = gh_ref[...].astype(F32)
+    value, slope = gelu_both(gate)
+    hidden_ref[...] = (value * upper).astype(BF16)
+    gg_ref[...] = (grad_hidden * upper * slope).astype(BF16)
+    gu_ref[...] = (grad_hidden * value).astype(BF16)
+
+
+def hidden_call(tok, gh, wg, wu, down, lg, lu):
+    rows, width = tok.shape
+    units, ranks = wg.shape[1], lg.shape[0]
+    tile = tile_of(units, 512)
+    cols = pl.BlockSpec((width, tile), lambda i: (0, i))
+    rank = pl.BlockSpec((ranks, tile), lambda i: (0, i))
+    out = pl.BlockSpec((rows, tile), lambda i: (0, i))
+    wide = jax.ShapeDtypeStruct((rows, units), BF16)
+    return pl.pallas_call(
+        hidden_kernel,
+        grid=(pl.cdiv(units, tile),),
+        out_shape=[wide, wide, wide, jax.ShapeDtypeStruct((rows, 2 * ranks), BF16)],
+        in_specs=[resident(tok), out, cols, cols, resident(down), rank, rank],
+        out_specs=[out, out, out, pl.BlockSpec((rows, 2 * ranks), lambda i: (0, 0))],
+        compiler_params=pltpu.CompilerParams(vmem_limit_bytes=60 * 2**20),
+        cost_estimate=pl.CostEstimate(
+            flops=4 * rows * width * units, bytes_accessed=4 * width * units + 10 * rows * units,
+            transcendentals=rows * units),
+    )(tok, gh, wg, wu, down, lg, lu)
+
+
+def back_kernel(gg_ref, gu_ref, wg_ref, wu_ref, lg_ref, lu_ref, down_ref, back_ref, through_ref):
+    ranks = lg_ref.shape[0]
+
+    @pl.when(pl.program_id(0) == 0)
+    def _():
+        through_ref[:, :ranks] = dot(gg_ref[...], lg_ref[...], NT).astype(BF16)
+        through_ref[:, ranks:] = dot(gu_ref[...], lu_ref[...], NT).astype(BF16)
+
+    back_ref[...] = (dot(gg_ref[...], wg_ref[...], NT) + dot(gu_ref[...], wu_ref[...], NT)
+                     + dot(through_ref[...], down_ref[...])).astype(BF16)
+
+
+def back_call(gg, gu, wg, wu, lg, lu, down):
+    rows, units = gg.shape
+    width, ranks = wg.shape[0], lg.shape[0]
+    tile = tile_of(width, 512)
+    weight = pl.BlockSpec((tile, units), lambda i: (i, 0))
+    return pl.pallas_call(
+        back_kernel,
+        grid=(pl.cdiv(width, tile),),
+        out_shape=[jax.ShapeDtypeStruct((rows, width), BF16), jax.ShapeDtypeStruct((rows, 2 * ranks), BF16)],
+        in_specs=[resident(gg), resident(gu), weight, weight, resident(lg), resident(lu),
+                  pl.BlockSpec((2 * ranks, tile), lambda i: (0, i))],
+        out_specs=[pl.BlockSpec((rows, tile), lambda i: (0, i)),
+                   pl.BlockSpec((rows, 2 * ranks), lambda i: (0, 0))],
+        compiler_params=pltpu.CompilerParams(vmem_limit_bytes=60 * 2**20),
+        cost_estimate=pl.CostEstimate(
+            flops=4 * rows * width * units, bytes_accessed=4 * width * units + 4 * rows * units + 2 * rows * width,
+            transcendentals=0),
+    )(gg, gu, wg, wu, lg, lu, down)
+
+
+def outward_kernel(seqs, *refs):
+    hiddens, (wd_ref, do_ref, lift_out_ref, _, out_ref, inner_ref) = refs[:seqs], refs[seqs:]
+    ranks = do_ref.shape[0] // seqs
+
+    @pl.when(pl.program_id(0) == 0)
+    def _():
+        for s, hidden_ref in enumerate(hiddens):
+            inner_ref[s] = dot(hidden_ref[...], do_ref[s * ranks : (s + 1) * ranks, :], NT).astype(BF16)
+
+    for s, hidden_ref in enumerate(hiddens):
+        out_ref[s] = (dot(hidden_ref[...], wd_ref[...])
+                      + dot(inner_ref[s], lift_out_ref[s * ranks : (s + 1) * ranks, :])).astype(BF16)
+
+
+def outward_call(hiddens, wd, do, lift_out, earlier):
+    rows, units = hiddens[0].shape
+    seqs = len(hiddens)
+    width, ranks = wd.shape[1], do.shape[0] // seqs
+    tile = tile_of(width, 512)
+    return pl.pallas_call(
+        functools.partial(outward_kernel, seqs),
+        grid=(pl.cdiv(width, tile),),
+        out_shape=[jax.ShapeDtypeStruct((seqs, rows, width), BF16), jax.ShapeDtypeStruct((seqs, rows, ranks), BF16)],
+        in_specs=[resident(hidden) for hidden in hiddens]
+        + [pl.BlockSpec((units, tile), lambda i: (0, i)), resident(do),
+           pl.BlockSpec((seqs * ranks, tile), lambda i: (0, i)), pl.BlockSpec(memory_space=pl.ANY)],
+        out_specs=[pl.BlockSpec((seqs, rows, tile), lambda i: (0, 0, i)),
+                   pl.BlockSpec((seqs, rows, ranks), lambda i: (0, 0, 0))],
+        compiler_params=pltpu.CompilerParams(vmem_limit_bytes=60 * 2**20),
+        cost_estimate=pl.CostEstimate(
+            flops=2 * seqs * rows * width * units,
+            bytes_accessed=2 * width * units + 2 * seqs * rows * (units + width), transcendentals=0),
+    )(*hiddens, wd, do, lift_out, earlier)
+
+
+def pick_kernel(counts, ids_ref, *refs):
+    tables, (stack_ref, wide_ref) = refs[: sum(counts)], refs[sum(counts) :]
+    for i, table in enumerate(tables):
+        if i < counts[0]:
+            stack_ref[i, 0] = table[0]
+        else:
+            wide_ref[i - counts[0], 0] = table[0]
+
+
+def pick(ids, narrow, wide):
+    seqs, ranks = ids.shape[0], narrow[0].shape[1]
+    counts = (len(narrow), len(wide))
+    widths = (narrow[0].shape[2], wide[0].shape[2])
+    tables = [pl.BlockSpec((1, ranks, table.shape[2]), lambda s, ids: (ids[s], 0, 0)) for table in narrow + wide]
+    picked = pl.pallas_call(
+        functools.partial(pick_kernel, counts),
+        out_shape=[jax.ShapeDtypeStruct((count, seqs, ranks, width), BF16) for count, width in zip(counts, widths)],
+        grid_spec=pltpu.PrefetchScalarGridSpec(
+            num_scalar_prefetch=1,
+            grid=(seqs,),
+            in_specs=tables,
+            out_specs=[pl.BlockSpec((count, 1, ranks, width), lambda s, ids: (0, s, 0, 0))
+                       for count, width in zip(counts, widths)],
+        ),
+    )(ids, *narrow, *wide)
+    return [part.reshape(-1, part.shape[-1]) for part in picked]
+
+
+def gather_kernel(units, *refs):
+    weights, wholes, staged, (send, recv, local) = refs[:4], refs[4:8], refs[8:12], refs[12:]
+    group, replica = lax.axis_index("group"), lax.axis_index("replica")
+    beside, above, across = group + 1 - 2 * (group % 2), (group + 2) % 4, 3 - group
+    core, level = replica % 2, (replica // 2) % 2
+    at_beside, at_above = (beside, replica), (above, replica)
+    at_core, at_level = (group, replica + 1 - 2 * core), (group, replica + 2 - 4 * level)
+    partners = (at_beside, at_above, at_core, at_level)
+    mine, other = 2 * core + level, 2 * core + 1 - level
+
+    barrier = pltpu.get_barrier_semaphore()
+    for partner in partners:
+        pl.semaphore_signal(barrier, inc=1, device_id=partner, device_id_type=pl.DeviceIdType.MESH)
+    pl.semaphore_wait(barrier, 4)
+
+    kept = [pltpu.make_async_copy(weight, stage, local.at[m])
+            for m, (weight, stage) in enumerate(zip(weights, staged))]
+    for one in kept:
+        one.start()
+
+    def keep(m):
+        whole = wholes[m]
+        rows, cols = weights[m].shape
+        if m == 2:
+            into = whole.at[pl.ds(pl.multiple_of(group * rows, rows), rows), :]
+        else:
+            into = whole.at[:, pl.ds(pl.multiple_of(group * cols, cols), cols)]
+        kept[m].wait()
+        kept[m] = pltpu.make_async_copy(staged[m], into, local.at[m])
+        kept[m].start()
+
+    def own(m, part, quarter):
+        weight = weights[m]
+        size = wholes[m].shape[0] // 4
+        step = size // units
+        if m < 2:
+            return weight.at[pl.ds(pl.multiple_of(quarter * size + part * step, step), step), :]
+        return weight.at[pl.ds(part * step, step), pl.ds(pl.multiple_of(quarter * size, size), size)]
+
+    def piece(m, part, shard, quarter):
+        whole = wholes[m]
+        size = whole.shape[0] // 4
+        step = size // units
+        down, along = (quarter, shard) if m < 2 else (shard, quarter)
+        return whole.at[pl.ds(pl.multiple_of(down * size + part * step, step), step),
+                        pl.ds(pl.multiple_of(along * size, size), size)]
+
+    def copy(src, dst, k, slot, partner):
+        made = pltpu.make_async_remote_copy(
+            src_ref=src, dst_ref=dst, send_sem=send.at[k, slot], recv_sem=recv.at[k, slot], device_id=partner,
+            device_id_type=pl.DeviceIdType.MESH)
+        made.start()
+        return made
+
+    def forward(m, part, shard, quarter, k, slot, partner):
+        where = piece(m, part, shard, quarter)
+        return copy(where, where, k, slot, partner)
+
+    ranks, cols = weights[3].shape
+    last = 3 * units
+
+    def stack_piece(first, count, shard):
+        return wholes[3].at[pl.ds(first, count), pl.ds(pl.multiple_of(shard * cols, cols), cols)]
+
+    stack_beside = copy(weights[3], stack_piece(0, ranks, group), last, 0, at_beside)
+    stack_above = copy(weights[3], stack_piece(0, ranks, group), last, 1, at_above)
+
+    steps = [(m, part) for m in range(3) for part in range(units)]
+    made = {}
+
+    def begin(k):
+        m, part = steps[k]
+        made[k, 0] = copy(own(m, part, mine), piece(m, part, group, mine), k, 0, at_above)
+        made[k, 2] = copy(own(m, part, mine), piece(m, part, group, mine), k, 2, at_beside)
+        made[k, 1] = copy(own(m, part, other), piece(m, part, group, other), k, 1, at_above)
+
+    begin(0)
+    begin(1)
+    for m in range(4):
+        keep(m)
+    stack_beside.wait_recv()
+    stack_above.wait_recv()
+    half = ranks // 2
+    lower = stack_piece(0, half, above)
+    upper = stack_piece(half, half, beside)
+    stack_lower = copy(lower, lower, last, 2, at_beside)
+    stack_upper = copy(upper, upper, last, 3, at_above)
+    for t in range(len(steps) + 2):
+        if t < len(steps):
+            m, part = steps[t]
+            made[t, 0].wait_recv()
+            made[t, 4] = forward(m, part, above, mine, t, 4, at_beside)
+            made[t, 6] = forward(m, part, above, mine, t, 6, at_core)
+            made[t, 2].wait_recv()
+            made[t, 3] = forward(m, part, beside, mine, t, 3, at_level)
+            made[t, 8] = forward(m, part, beside, mine, t, 8, at_core)
+            if t + 2 < len(steps):
+                begin(t + 2)
+            made[t, 1].wait_recv()
+            made[t, 7] = forward(m, part, above, other, t, 7, at_core)
+        if 1 <= t <= len(steps):
+            m, part = steps[t - 1]
+            made[t - 1, 4].wait_recv()
+            made[t - 1, 5] = forward(m, part, across, mine, t - 1, 5, at_level)
+            made[t - 1, 10] = forward(m, part, across, mine, t - 1, 10, at_core)
+            made[t - 1, 3].wait_recv()
+            made[t - 1, 9] = forward(m, part, beside, other, t - 1, 9, at_core)
+        if 2 <= t:
+            m, part = steps[t - 2]
+            made[t - 2, 5].wait_recv()
+            made[t - 2, 11] = forward(m, part, across, other, t - 2, 11, at_core)
+    for k in range(len(steps)):
+        for slot in range(6, 12):
+            made[k, slot].wait_recv()
+    for k in range(len(steps)):
+        for slot in range(12):
+            made[k, slot].wait_send()
+    for one in (stack_lower, stack_upper):
+        one.wait_recv()
+    for one in (stack_beside, stack_above, stack_lower, stack_upper):
+        one.wait_send()
+    for one in kept:
+        one.wait()
+
+
+def gather_weights(w_branch, w_input, w_mixer, stack):
+    width = w_branch.shape[0]
+    if lax.axis_size("group") != 4 or lax.axis_size("replica") % 4 != 0:
+        return (lax.all_gather(w_branch, "group", axis=1, tiled=True),
+                lax.all_gather(w_input, "group", axis=1, tiled=True),
+                lax.all_gather(w_mixer, "group", axis=0, tiled=True),
+                lax.all_gather(stack, "group", axis=1, tiled=True))
+    units = 4
+    anywhere = pl.BlockSpec(memory_space=pl.ANY)
+    operands = (w_branch, w_input, w_mixer, stack)
+    return pl.pallas_call(
+        functools.partial(gather_kernel, units),
+        out_shape=[jax.ShapeDtypeStruct((width, width), BF16)] * 3
+        + [jax.ShapeDtypeStruct((stack.shape[0], width), BF16)],
+        in_specs=[anywhere] * 4,
+        out_specs=[anywhere] * 4,
+        scratch_shapes=[pltpu.VMEM(operand.shape, BF16) for operand in operands]
+        + [pltpu.SemaphoreType.DMA((3 * units + 1, 12)), pltpu.SemaphoreType.DMA((3 * units + 1, 12)),
+           pltpu.SemaphoreType.DMA((4,))],
+        compiler_params=pltpu.CompilerParams(
+            collective_id=0, has_side_effects=True, vmem_limit_bytes=32 * 2**20),
+        cost_estimate=pl.CostEstimate(flops=0, bytes_accessed=400 * 2**20, transcendentals=0),
+    )(*operands)
+
+
+def ordered_kernel(value_ref, *refs):
+    refs[-1][...] = value_ref[...]
+
+
+def ordered(value, *earlier):
+    flat = value.reshape(-1, value.shape[-1])
+    tile = pl.BlockSpec((flat.shape[0] // 2, flat.shape[1]), lambda i: (i, 0))
+    return pl.pallas_call(
+        ordered_kernel,
+        grid=(2,),
+        out_shape=jax.ShapeDtypeStruct(flat.shape, flat.dtype),
+        in_specs=[tile] + [pl.BlockSpec(memory_space=pl.ANY)] * len(earlier),
+        out_specs=tile,
+    )(flat, *earlier).reshape(value.shape)
+
+
+def finish_kernel(resid_ref, outward_ref, grad_resid_ref, inputs_ref, gain_ref, grads_ref, block_ref, out_ref):
+    block_ref[...] = (resid_ref[...] + outward_ref[...].astype(F32)).astype(BF16)
+    values = inputs_ref[...].astype(F32)
+    rate = lax.rsqrt(jnp.mean(values * values, axis=-1, keepdims=True) + EPS)
+    out_ref[...] = grad_resid_ref[...] + norm_back(values, gain_ref[...], rate, grads_ref[...])
+
+
+def finish(resid, outward, grad_resid, inputs, gain, grads):
+    rows, width = resid.shape
+    step = min(rows, 128)
+    tile = pl.BlockSpec((step, width), lambda i: (i, 0))
+    return pl.pallas_call(
+        finish_kernel,
+        grid=(rows // step,),
+        out_shape=[jax.ShapeDtypeStruct((rows, width), BF16), jax.ShapeDtypeStruct((rows, width), F32)],
+        in_specs=[tile, tile, tile, tile, pl.BlockSpec((1, width), lambda i: (0, 0)), tile],
+        out_specs=[tile, tile],
+        compiler_params=pltpu.CompilerParams(vmem_limit_bytes=40 * 2**20),
+        cost_estimate=pl.CostEstimate(
+            flops=20 * rows * width, bytes_accessed=22 * rows * width, transcendentals=rows),
+    )(resid, outward, grad_resid, inputs, gain, grads)
+
+
 def spread_kernel(tables, ids_ref, got_ref, *out_refs):
     replicas, seqs, ranks = got_ref.shape[0], ids_ref.shape[0] // got_ref.shape[0], out_refs[0].shape[1]
     for table in range(tables):
@@ -294,22 +650,12 @@
     return lax.ppermute(block, axis, route)
 
 
-def gathered_halves(weight, split, join):
-    count = weight.shape[split] // 2
-    parity = lax.axis_index("replica") % 2
-    part = lax.dynamic_slice_in_dim(weight, parity * count, count, split)
-    mine = lax.all_gather(part, "group", axis=join, tiled=True)
-    swap = [(i, i ^ 1) for i in range(lax.axis_size("replica"))]
-    return mine, lax.ppermute(mine, "replica", swap)
-
-
-def by_parity(mine, other, axis):
-    parity = lax.axis_index("replica") % 2
-    return lax.cond(
-        parity == 0,
-        lambda: jnp.concatenate([mine, other], axis),
-        lambda: jnp.concatenate([other, mine], axis),
-    )
+def over_replicas(value):
+    count = lax.axis_size("replica")
+    if count % 2:
+        return lax.all_gather(value, "replica")
+    got = lax.all_gather(value, "replica", axis_index_groups=[list(range(p, count, 2)) for p in range(2)])
+    return jnp.concatenate([got, lax.ppermute(got, "replica", [(i, i ^ 1) for i in range(count)])], 0)
 
 
 def body(
@@ -325,26 +671,21 @@
     group, place = lax.axis_size("group"), lax.axis_index("group")
     mask_cols = seqs * ranks
 
-    def chosen(table, down):
-        table = jnp.swapaxes(table, 1, 2) if down else table
-        return jnp.concatenate(
-            [lax.dynamic_index_in_dim(table, adapter_ids[s], 0, False) for s in range(seqs)], 0)
-
-    full_names = [down_branch, down_input, down_decay, down_admit, down_mixer, down_gate, down_upper,
-                  lift_branch, lift_input, lift_decay, lift_admit, lift_mixer, lift_outward]
-    stack = jnp.concatenate([chosen(t, i < 7) for i, t in enumerate(full_names)], 0)
-    stack = lax.all_gather(stack, "group", axis=1, tiled=True)
-    pick = [stack[i * mask_cols : (i + 1) * mask_cols] for i in range(13)]
+    turned = lambda table: jnp.swapaxes(table, 1, 2)
+    stack, own_tables = pick(
+        adapter_ids,
+        [turned(down_branch), turned(down_input), turned(down_decay), turned(down_admit), turned(down_mixer),
+         turned(down_gate), turned(down_upper), lift_branch, lift_input, lift_decay, lift_admit, lift_mixer,
+         lift_outward],
+        [lift_gate, lift_upper, turned(down_outward)])
+    full_branch, full_input, full_mixer, stack = gather_weights(w_branch, w_input, w_mixer, stack)
     (p_down_branch, p_down_input, p_down_decay, p_down_admit, p_down_mixer, p_down_gate, p_down_upper,
-     p_lift_branch, p_lift_input, p_lift_decay, p_lift_admit, p_lift_mixer, p_lift_outward) = pick
-    own_lift_gate, own_lift_upper, own_down_outward = (
-        chosen(lift_gate, False), chosen(lift_upper, False), chosen(down_outward, True))
-    all_ids = lax.all_gather(adapter_ids, "replica", axis=0, tiled=True)
-
-    branch_mine, branch_other = gathered_halves(w_branch, 0, 1)
-    input_mine, input_other = gathered_halves(w_input, 0, 1)
-    mixer_mine, mixer_other = gathered_halves(w_mixer, 1, 0)
-    half = width // 2
+     p_lift_branch, p_lift_input, p_lift_decay, p_lift_admit, p_lift_mixer, p_lift_outward) = [
+        stack[i * mask_cols : (i + 1) * mask_cols] for i in range(13)]
+    own_lift_gate, own_lift_upper, own_down_outward = [
+        own_tables[i * mask_cols : (i + 1) * mask_cols] for i in range(3)]
+    all_ids = over_replicas(adapter_ids).reshape(-1)
+    cotangents = lax.all_gather(ordered(out_grad, stack), "group", axis=1, tiled=True)
 
     row_seq = lax.broadcasted_iota(jnp.int32, (rows, mask_cols), 0) // stretch
     col_seq = lax.broadcasted_iota(jnp.int32, (rows, mask_cols), 1) // ranks
@@ -362,15 +703,12 @@
     restart = (1.0 - agree[1][:, :stretch]).reshape(rows, 1)
 
     x_float = inputs.reshape(rows, width).astype(F32)
-    normed_f, rate_one = norm_rows(x_float, gain_mix)
+    normed_f, _ = norm_rows(x_float, gain_mix)
     normed = normed_f.astype(BF16)
-    parity = lax.axis_index("replica") % 2
-    normed_mine = lax.dynamic_slice_in_dim(normed, parity * half, half, 1)
-    normed_other = lax.dynamic_slice_in_dim(normed, (1 - parity) * half, half, 1)
     inner_one = (dot(normed, stack[: 2 * mask_cols], NT) * own_two).astype(BF16)
     inner_branch, inner_input = inner_one[:, :mask_cols], inner_one[:, mask_cols:]
-    branch_pre = dot(normed_mine, branch_mine) + dot(normed_other, branch_other) + dot(inner_branch, p_lift_branch)
-    fed = (dot(normed_mine, input_mine) + dot(normed_other, input_other) + dot(inner_input, p_lift_input)).astype(BF16)
+    branch_pre = dot(normed, full_branch) + dot(inner_branch, p_lift_branch)
+    fed = (dot(normed, full_input) + dot(inner_input, p_lift_input)).astype(BF16)
     fed = fed.reshape(seqs, stretch, width)
     halo = passed_along(fed[:, stretch - (taps - 1) :], "group", 1)
     extended = jnp.concatenate([halo, fed], axis=1).astype(F32)
@@ -394,53 +732,44 @@
     state = local + cum * carried_rows
     merged = (state * gelu(branch_pre)).astype(BF16)
     inner_mixer = (dot(merged, p_down_mixer, NT) * own).astype(BF16)
-    mixed = by_parity(dot(merged, mixer_mine), dot(merged, mixer_other), 1) + dot(inner_mixer, p_lift_mixer)
+    mixed = dot(merged, full_mixer) + dot(inner_mixer, p_lift_mixer)
     resid = x_float + mixed
     normed_two_f, rate_two = norm_rows(resid, gain_mlp)
     normed_two = normed_two_f.astype(BF16).reshape(seqs, stretch, width)
 
-    outs, backs, down_parts, lift_parts = [], [], [], []
+    all_tokens, backs, hiddens, throughs = [], [], [], []
     grad_own_lift_gate, grad_own_lift_upper, grad_own_down_outward = [], [], []
     grad_down_gate, grad_down_upper, grad_lift_outward = [], [], []
+    spans = [slice(s * ranks, (s + 1) * ranks) for s in range(seqs)]
+    grad_hiddens = [
+        grad_hidden_call(cotangents[s], w_down, p_lift_outward[at], own_down_outward[at])
+        for s, at in enumerate(spans)]
+    all_tokens = [lax.all_gather(normed_two[s], "group", axis=0, tiled=True) for s in range(seqs)]
+    for s, at in enumerate(spans):
+        tokens = all_tokens[s]
+        grad_hidden, through_out = grad_hiddens[s]
+        two_downs = jnp.concatenate([p_down_gate[at], p_down_upper[at]], 0)
+        hidden, grad_gate, grad_upper, inner = hidden_call(
+            tokens, grad_hidden, w_gate, w_upper, two_downs, own_lift_gate[at], own_lift_upper[at])
+        back, through = back_call(
+            grad_gate, grad_upper, w_gate, w_upper, own_lift_gate[at], own_lift_upper[at], two_downs)
+        backs.append(lax.psum_scatter(back, "group", scatter_dimension=0, tiled=True))
+        hiddens.append(hidden)
+        grad_own_lift_gate.append(dot(inner[:, :ranks], grad_gate, TN))
+        grad_own_lift_upper.append(dot(inner[:, ranks:], grad_upper, TN))
+        grad_own_down_outward.append(dot(through_out, hidden, TN))
+        grad_down_gate.append(dot(through[:, :ranks], tokens, TN))
+        grad_down_upper.append(dot(through[:, ranks:], tokens, TN))
+    outward, inner_out = outward_call(hiddens, w_down, own_down_outward, p_lift_outward, back)
     for s in range(seqs):
-        at = slice(s * ranks, (s + 1) * ranks)
-        cotangent = lax.all_gather(out_grad[s], "group", axis=0, tiled=True)
-        tokens = lax.all_gather(normed_two[s], "group", axis=0, tiled=True)
-        inner_gate = dot(tokens, p_down_gate[at], NT).astype(BF16)
-        inner_upper = dot(tokens, p_down_upper[at], NT).astype(BF16)
-        through_out = dot(cotangent, p_lift_outward[at], NT).astype(BF16)
-        gate_pre = dot(tokens, w_gate) + dot(inner_gate, own_lift_gate[at])
-        upper_pre = dot(tokens, w_upper) + dot(inner_upper, own_lift_upper[at])
-        grad_hidden = dot(cotangent, w_down, NT) + dot(through_out, own_down_outward[at])
-        value, slope = gelu_both(gate_pre)
-        hidden = (value * upper_pre).astype(BF16)
-        grad_gate = (grad_hidden * upper_pre * slope).astype(BF16)
-        grad_upper = (grad_hidden * value).astype(BF16)
-        inner_out = dot(hidden, own_down_outward[at], NT).astype(BF16)
-        outward = dot(hidden, w_down) + dot(inner_out, p_lift_outward[at])
-        through_gate = dot(grad_gate, own_lift_gate[at], NT).astype(BF16)
-        through_upper = dot(grad_upper, own_lift_upper[at], NT).astype(BF16)
-        back = (dot(grad_gate, w_gate, NT) + dot(grad_upper, w_upper, NT)
-                + dot(through_gate, p_down_gate[at]) + dot(through_upper, p_down_upper[at]))
-        backs.append(lax.psum_scatter(back.astype(BF16), "group", scatter_dimension=0, tiled=True))
-        outs.append(lax.psum_scatter(outward.astype(BF16), "group", scatter_dimension=0, tiled=True))
-        grad_own_lift_gate.append(dot(inner_gate, grad_gate, TN))
-        grad_own_lift_upper.append(dot(inner_upper, grad_upper, TN))
-        grad_own_down_outward.append(dot(through_out, hidden, TN))
-        grad_down_gate.append(dot(through_gate, tokens, TN))
-        grad_down_upper.append(dot(through_upper, tokens, TN))
-        grad_lift_outward.append(dot(inner_out, cotangent, TN))
-    outward = jnp.concatenate(outs, 0).astype(F32)
+        grad_lift_outward.append(dot(inner_out[s], cotangents[s], TN))
+    outward = lax.psum_scatter(outward, "group", scatter_dimension=1, tiled=True).reshape(rows, width)
     grad_normed_two = jnp.concatenate(backs, 0).astype(F32)
-    block_out = (resid + outward).astype(BF16).reshape(seqs, stretch, width)
     grad_resid = out_grad.reshape(rows, width).astype(F32) + norm_back(resid, gain_mlp, rate_two, grad_normed_two)
 
     grad_mixed = grad_resid.astype(BF16)
-    grad_mixed_mine = lax.dynamic_slice_in_dim(grad_mixed, parity * half, half, 1)
-    grad_mixed_other = lax.dynamic_slice_in_dim(grad_mixed, (1 - parity) * half, half, 1)
     through_mixer = (dot(grad_mixed, p_lift_mixer, NT) * own).astype(BF16)
-    grad_merged = (dot(grad_mixed_mine, mixer_mine, NT) + dot(grad_mixed_other, mixer_other, NT)
-                   + dot(through_mixer, p_down_mixer))
+    grad_merged = dot(grad_mixed, full_mixer, NT) + dot(through_mixer, p_down_mixer)
     span, total, firsts, grad_branch_pre = backward_scan(
         seqs, convolved, inner_gates, lift_gates, decay_heads, softrate, restart, cum, local, carried, branch_pre,
         grad_merged)
@@ -464,29 +793,26 @@
     through_branch = (dot(grad_branch_pre, p_lift_branch, NT) * own).astype(BF16)
     through_input = (dot(grad_fed, p_lift_input, NT) * own).astype(BF16)
     through_one = jnp.concatenate([through_branch, through_input], 1)
-    grad_normed = (
-        by_parity(
-            dot(grad_branch_pre, branch_mine, NT) + dot(grad_fed, input_mine, NT),
-            dot(grad_branch_pre, branch_other, NT) + dot(grad_fed, input_other, NT), 1)
-        + dot(through_one, stack[: 2 * mask_cols]))
-    grad_inputs = grad_resid + norm_back(x_float, gain_mix, rate_one, grad_normed)
+    grad_normed = (dot(grad_branch_pre, full_branch, NT) + dot(grad_fed, full_input, NT)
+                   + dot(through_one, stack[: 2 * mask_cols]))
+    block_out, grad_inputs = finish(
+        resid, outward, grad_resid, inputs.reshape(rows, width), gain_mix.reshape(1, width), grad_normed)
 
     partial = jnp.concatenate(
-        [dot(through_one, normed, TN), dot(through_gates, rounded, TN), dot(through_mixer, merged, TN)]
-        + grad_down_gate + grad_down_upper
-        + [dot(inner_branch, grad_branch_pre, TN), dot(inner_input, grad_fed, TN), grad_lift_gates,
-           dot(inner_mixer, grad_mixed, TN)]
-        + grad_lift_outward, 0).astype(BF16)
+        [dot(through_one, normed, TN), dot(through_gates, rounded, TN), dot(through_mixer, merged, TN),
+         dot(inner_branch, grad_branch_pre, TN), dot(inner_input, grad_fed, TN), grad_lift_gates,
+         dot(inner_mixer, grad_mixed, TN)] + grad_down_gate + grad_down_upper + grad_lift_outward, 0).astype(BF16)
     owned = lax.psum_scatter(partial, "group", scatter_dimension=1, tiled=True)
     wide = jnp.concatenate(grad_own_lift_gate + grad_own_lift_upper + grad_own_down_outward, 0).astype(BF16)
-    totals = spread(all_ids, lax.all_gather(owned, "replica"), 13, sets, seqs)
-    wides = spread(all_ids, lax.all_gather(wide, "replica"), 3, sets, seqs)
-    turned = lambda table: jnp.swapaxes(table, 1, 2)
+    wides = spread(all_ids, over_replicas(wide), 3, sets, seqs)
+    totals = spread(all_ids, over_replicas(owned), 13, sets, seqs)
+    (t_down_branch, t_down_input, t_down_decay, t_down_admit, t_down_mixer, t_lift_branch, t_lift_input, t_lift_decay,
+     t_lift_admit, t_lift_mixer, t_down_gate, t_down_upper, t_lift_outward) = totals
     return (
-        block_out, grad_inputs.reshape(seqs, stretch, width),
-        turned(totals[0]), totals[7], turned(totals[1]), totals[8], turned(totals[2]), totals[9],
-        turned(totals[3]), totals[10], turned(totals[4]), totals[11], turned(totals[5]), wides[0],
-        turned(totals[6]), wides[1], turned(wides[2]), totals[12],
+        block_out.reshape(seqs, stretch, width), grad_inputs.reshape(seqs, stretch, width),
+        turned(t_down_branch), t_lift_branch, turned(t_down_input), t_lift_input, turned(t_down_decay), t_lift_decay,
+        turned(t_down_admit), t_lift_admit, turned(t_down_mixer), t_lift_mixer, turned(t_down_gate), wides[0],
+        turned(t_down_upper), wides[1], turned(wides[2]), t_lift_outward,
     )
 
 

time: 1140 us -> 923 us (0.81)
  Pallas kernels: 66.4 us -> 427 us
  matrix products: 455 us -> 135 us
  waiting for transfers between devices: 445 us -> 223 us
  local copies, waits for them, and re-layouts: 62.9 us -> 45.9 us
    pallas_call x0 -> x11, Pallas kernels: none -> 361 us  [the longest x1 144 us: gather_weights(): pl.pallas_call(functools.partial(gather_kernel, units), out_shape=[jax.Sh...]
    dot_general x78 -> x36, matrix products: 455 us -> 135 us  [dot(): return lax.dot_general(a, b, dims, preferred_element_type=F32)]
    all_gather x10 -> x5, waiting for transfers between devices: 296 us -> 85.3 us  [the longest x2 47.7 us: over_replicas(): lax.all_gather(value, 'replica', axis_index_groups=[list(range(p, count,...]
    reduce_scatter x4 -> x3, waiting for transfers between devices: 146 us -> 105 us  [the longest x1 79.8 us: body(): lax.psum_scatter(outward, 'group', scatter_dimension=1, tiled=True)]
    unnamed x16 -> x10, waiting for transfers between devices: 0.27 us -> 28.5 us
    unnamed x301 -> x204, local copies, waits for them, and re-layouts: 47.4 us -> 25.8 us
  transfers between devices with their start and end apart: 20 -> 14, of which waited for: 12 -> 9; matrix products, arithmetic and copies ran while one was open for 44% -> 15% of each run, Pallas kernels for 2% -> 25%
where the time goes in v2:
time: 923 us; the launch traced here: 914 us
  Pallas kernels  427 us (46%)
  waiting for transfers between devices  223 us (24%)
  matrix products  135 us (15%)
  local copies, waits for them, and re-layouts  45.9 us (5%)
  other arithmetic  36.9 us (4%)
  blocking collectives  25.7 us (3%)
  between operations  16.3 us (2%)
    pallas_call x1, Pallas kernels, gather_weights(): pl.pallas_call(functools.partial(gather_kernel, units), out_shape=[jax.Sh...  144 us
    dot_general x36, matrix products, dot(): return lax.dot_general(a, b, dims, preferred_element_type=F32)  135 us
    reduce_scatter x1, waiting for transfers between devices, body(): lax.psum_scatter(outward, 'group', scatter_dimension=1, tiled=True)  79.8 us
    pallas_call x2, Pallas kernels, back_call(): pl.pallas_call(back_kernel, grid=(pl.cdiv(width, tile),), out_shape=[jax....  65.9 us
    pallas_call x2, Pallas kernels, hidden_call(): pl.pallas_call(hidden_kernel, grid=(pl.cdiv(units, tile),), out_shape=[wi...  65.6 us
    all_gather x2, waiting for transfers between devices, over_replicas(): lax.all_gather(value, 'replica', axis_index_groups=[list(range(p, count,...  47.7 us
    pallas_call x2, Pallas kernels, grad_hidden_call(): pl.pallas_call(grad_hidden_kernel, grid=(pl.cdiv(units, tile),), out_shap...  37.5 us
    all_gather x2, waiting for transfers between devices, body(): lax.all_gather(normed_two[s], 'group', axis=0, tiled=True)  35.2 us
  transfers between devices with their start and end apart: 14, of which 9 were waited for; matrix products, arithmetic and copies ran while one was open for 15% of the time, Pallas kernels for 25%

profile of v2, /device:TPU:0, one launch (start us, length us, event | category | flops | bytes accessed | tf_op | source)
XLA Modules:
  0.0 914.5 jit_solution(2585667994716148763)
XLA Ops:
  17.1 144.0 %shard_map.440 = (bf16[2560,2560]{1,0:T(8,128)(2,1)}, bf16[2560,2560]{1,0:T(8,128)(2,1)}, bf16[2560,2560]{1,0:T(8,128)(2,1)}, bf16[416,2560]{1,0:T(8,128)(2,1)S(1)}) custom-call(bf16[2560,640]{1,0:T(8,128)(2,1)S(1)} %copy-done.8, bf16[2560,640]{1,0:T(8,128)(2,1)S(1)} %copy-done.9, bf16[640,2560]{1,0:T(8,128)(2,1)S(1)} %copy-done.10, ...), custom_call_target="tpu_custom_call" | custom-call | bytes 419430400 | tf_op jit(solution)/shard_map/pallas_call | solution.py:566
  169.4 10.4 %fusion.121 = f32[512,2560]{1,0:T(8,128)S(1)} fusion(bf16[512,2560]{1,0:T(8,128)(2,1)S(1)} %fusion.1, bf16[2560,2560]{1,0:T(8,128)(2,1)} %get-tuple-element.70), kind=kOutput, calls=%fused_computation.226 | convolution fusion | flops 6710886400 | bytes 20971520 | tf_op jit(solution)/shard_map/dot_general | solution.py:21
  187.7 12.2 %fusion.122 = f32[512,2560]{1,0:T(8,128)} fusion(bf16[512,2560]{1,0:T(8,128)(2,1)} %copy-done.26, bf16[2560,2560]{1,0:T(8,128)(2,1)} %get-tuple-element.74), kind=kOutput, calls=%fused_computation.227 | convolution fusion | flops 6710886400 | bytes 20971520 | tf_op jit(solution)/shard_map/dot_general | solution.py:21
  205.1 5.2 fusion.4
  214.2 16.8 %shard_map.441 = (f32[512,2560]{1,0:T(8,128)S(1)}, f32[512,2560]{1,0:T(8,128)S(1)}) custom-call(f32[512,2560]{1,0:T(8,128)} %bitcast.221, bf16[512,64]{1,0:T(8,128)(2,1)S(1)} %fusion.56.inner_ref, bf16[64,2560]{1,0:T(8,128)(2,1)S(1)} %slice.307.lift_ref, bf16[10,256,256]{2,1,0:T(8,128)(2,1)S(1)} %copy-done.6, bf16[10,256,256]{2,1,0:T(8,128)(2,1)S(1)} %copy-done.14, ...), custom_call_target="tpu_custom_call" | custom-call | flops 1420820480 | bytes 15728640 | tf_op jit(solution)/shard_map/pallas_call | solution.py:106
  231.2 9.9 %all-gather.4 = f32[4,4,2560]{2,1,0:T(4,128)S(1)} all-gather(f32[1,4,2560]{2,1,0:T(4,128)S(1)} %maximum_bitcast_fusion), channel_id=2, replica_groups=mesh['group'=4,'replica'=8] {'group'}, dimensions={0}, use_global_device_ids=true | all-gather | bytes 204800 | tf_op jit(solution)/shard_map/all_gather | solution.py:726
  241.2 5.9 fusion.18
  249.1 10.0 %fusion.123 = f32[512,2560]{1,0:T(8,128)S(1)} fusion(bf16[512,2560]{1,0:T(8,128)(2,1)S(1)} %get-tuple-element.151, bf16[2560,2560]{1,0:T(8,128)(2,1)} %get-tuple-element.75), kind=kOutput, calls=%fused_computation.228 | convolution fusion | flops 6710886400 | bytes 20971520 | tf_op jit(solution)/shard_map/dot_general | solution.py:21
  272.0 8.9 slice_bitcast_fusion
  280.9 19.2 %shard_map.443 = (bf16[1024,1920]{1,0:T(8,128)(2,1)}, bf16[1024,16]{1,0:T(8,128)(2,1)}) custom-call(bf16[1024,2560]{1,0:T(8,128)(2,1)} %get-tuple-element.125.cot_ref, bf16[1920,2560]{1,0:T(8,128)(2,1)} %refs_2_.3, bf16[16,2560]{1,0:T(8,128)(2,1)} %get-tuple-element.133.lift_out_ref, bf16[16,1920]{1,0:T(8,128)(2,1)} %get-tuple-element.139.do_ref), custom_call_target="tpu_custom_call" | custom-call | flops 10066329600 | bytes 19005440 | tf_op jit(solution)/shard_map/pallas_call | solution.py:284
  300.1 35.2 %all-gather.12.cloned.1.call-done.tok_ref = bf16[1024,2560]{1,0:T(8,128)(2,1)} async-done(((bf16[256,2560]{1,0:T(8,128)(2,1)}), bf16[1024,2560]{1,0:T(8,128)(2,1)}) %all-gather.12.cloned.1.call-update) | async-done | bytes 5242896 | tf_op jit(solution)/shard_map/all_gather | solution.py:747
  335.3 32.7 %shard_map.444 = (bf16[1024,1920]{1,0:T(8,128)(2,1)}, bf16[1024,1920]{1,0:T(8,128)(2,1)}, bf16[1024,1920]{1,0:T(8,128)(2,1)}, bf16[1024,32]{1,0:T(8,128)(2,1)}) custom-call(bf16[1024,2560]{1,0:T(8,128)(2,1)} %all-gather.12.cloned.1.call-done.tok_ref, bf16[1024,1920]{1,0:T(8,128)(2,1)} %get-tuple-element.77.gh_ref, bf16[2560,1920]{1,0:T(8,128)(2,1)} %wg_ref.7, ...), custom_call_target="tpu_custom_call" | custom-call | flops 20132659200 | bytes 39321600 | tf_op jit(solution)/shard_map/pallas_call | solution.py:323
  368.0 33.3 %shard_map.449 = (bf16[1024,2560]{1,0:T(8,128)(2,1)}, bf16[1024,32]{1,0:T(8,128)(2,1)}) custom-call(bf16[1024,1920]{1,0:T(8,128)(2,1)} %get-tuple-element.85.gg_ref, bf16[1024,1920]{1,0:T(8,128)(2,1)} %get-tuple-element.86.gu_ref, bf16[2560,1920]{1,0:T(8,128)(2,1)} %wg_ref.7, bf16[2560,1920]{1,0:T(8,128)(2,1)} %wu_ref.7, ...), custom_call_target="tpu_custom_call" | custom-call | flops 20132659200 | bytes 32768000 | tf_op jit(solution)/shard_map/pallas_call | solution.py:353
  402.5 18.4 %shard_map.445 = (bf16[1024,1920]{1,0:T(8,128)(2,1)}, bf16[1024,16]{1,0:T(8,128)(2,1)}) custom-call(bf16[1024,2560]{1,0:T(8,128)(2,1)} %get-tuple-element.124.cot_ref, bf16[1920,2560]{1,0:T(8,128)(2,1)} %refs_2_.3, bf16[16,2560]{1,0:T(8,128)(2,1)} %get-tuple-element.130.lift_out_ref, bf16[16,1920]{1,0:T(8,128)(2,1)} %get-tuple-element.136.do_ref), custom_call_target="tpu_custom_call" | custom-call | flops 10066329600 | bytes 19005440 | tf_op jit(solution)/shard_map/pallas_call | solution.py:284
  420.9 32.9 %shard_map.446 = (bf16[1024,1920]{1,0:T(8,128)(2,1)}, bf16[1024,1920]{1,0:T(8,128)(2,1)}, bf16[1024,1920]{1,0:T(8,128)(2,1)}, bf16[1024,32]{1,0:T(8,128)(2,1)}) custom-call(bf16[1024,2560]{1,0:T(8,128)(2,1)} %all-gather.16.cloned.1.call-done.tok_ref, bf16[1024,1920]{1,0:T(8,128)(2,1)} %get-tuple-element.79.gh_ref, bf16[2560,1920]{1,0:T(8,128)(2,1)} %wg_ref.7, ...), custom_call_target="tpu_custom_call" | custom-call | flops 20132659200 | bytes 39321600 | tf_op jit(solution)/shard_map/pallas_call | solution.py:323
  453.8 32.6 %shard_map.447 = (bf16[1024,2560]{1,0:T(8,128)(2,1)}, bf16[1024,32]{1,0:T(8,128)(2,1)}) custom-call(bf16[1024,1920]{1,0:T(8,128)(2,1)} %get-tuple-element.81.gg_ref, bf16[1024,1920]{1,0:T(8,128)(2,1)} %get-tuple-element.82.gu_ref, bf16[2560,1920]{1,0:T(8,128)(2,1)} %wg_ref.7, bf16[2560,1920]{1,0:T(8,128)(2,1)} %wu_ref.7, ...), custom_call_target="tpu_custom_call" | custom-call | flops 20132659200 | bytes 32768000 | tf_op jit(solution)/shard_map/pallas_call | solution.py:353
  489.8 33.3 %shard_map.448 = (bf16[2,1024,2560]{2,1,0:T(8,128)(2,1)}, bf16[2,1024,16]{2,1,0:T(8,128)(2,1)}) custom-call(bf16[1024,1920]{1,0:T(8,128)(2,1)} %get-tuple-element.78.refs_0_, bf16[1024,1920]{1,0:T(8,128)(2,1)} %get-tuple-element.80.refs_1_, bf16[1920,2560]{1,0:T(8,128)(2,1)} %refs_2_.3, bf16[32,1920]{1,0:T(8,128)(2,1)} %bitcast.256, ...), custom_call_target="tpu_custom_call" | custom-call | flops 20132659200 | bytes 28180480 | tf_op jit(solution)/shard_map/pallas_call | solution.py:387
  523.1 24.9 %reduce-scatter.11.cloned.1.call-done = bf16[256,2560]{1,0:T(8,128)(2,1)} async-done(((bf16[1024,2560]{1,0:T(8,128)(2,1)}), bf16[256,2560]{1,0:T(8,128)(2,1)}) %reduce-scatter.11.cloned.1.call-update) | async-done | bytes 1310736 | tf_op jit(solution)/shard_map/reduce_scatter | solution.py:756
  552.8 5.0 subtract_add_fusion.grad_resid_ref
  557.9 12.0 %fusion.112 = f32[512,2560]{1,0:T(8,128)S(1)} fusion(bf16[2560,2560]{1,0:T(8,128)(2,1)} %get-tuple-element.75, f32[512,2560]{1,0:T(8,128)S(1)} %subtract_add_fusion.grad_resid_ref), kind=kOutput, calls=%fused_computation.217 | convolution fusion | flops 6712197120 | bytes 23592960 | tf_op jit(solution)/shard_map/dot_general | solution.py:21
  576.0 20.9 %shard_map.450 = (f32[512,2560]{1,0:T(8,128)}, f32[512,2560]{1,0:T(8,128)}, f32[4,2560]{1,0:T(4,128)S(1)}, bf16[512,2560]{1,0:T(8,128)(2,1)S(1)}) custom-call(f32[512,2560]{1,0:T(8,128)} %bitcast.222, bf16[512,64]{1,0:T(8,128)(2,1)S(1)} %copy-done.17, bf16[64,2560]{1,0:T(8,128)(2,1)S(1)} %slice.307.lift_ref, bf16[10,256,256]{2,1,0:T(8,128)(2,1)S(1)} %copy-done.7, ...), custom_call_target="tpu_custom_call" | custom-call | flops 775946240 | bytes 39321600 | tf_op jit(solution)/shard_map/pallas_call | solution.py:156
  597.0 8.7 all-gather.5
  605.7 19.9 %shard_map.451 = (f32[512,2560]{1,0:T(8,128)}, f32[512,64]{1,0:T(8,128)S(1)}, f32[64,2560]{1,0:T(8,128)S(1)}) custom-call(f32[512,2560]{1,0:T(8,128)} %bitcast.223, bf16[512,64]{1,0:T(8,128)(2,1)S(1)} %copy-done.17, bf16[64,2560]{1,0:T(8,128)(2,1)S(1)} %slice.307.lift_ref, bf16[10,256,256]{2,1,0:T(8,128)(2,1)S(1)} %copy-done.7, ...), custom_call_target="tpu_custom_call" | custom-call | flops 2789212160 | bytes 31457280 | tf_op jit(solution)/shard_map/pallas_call | solution.py:232
  635.3 5.8 fusion.8
  677.8 27.1 %reduce-scatter.13.cloned.1.call-done = bf16[640,416]{1,0:T(8,128)(2,1)} async-done(((bf16[2560,416]{1,0:T(8,128)(2,1)}), bf16[640,416]{1,0:T(8,128)(2,1)}) %reduce-scatter.13.cloned.1.call-update) | async-done | bytes 532496
  707.8 34.8 %all-gather.18.cloned.1.call-done = bf16[4,96,1920]{2,1,0:T(8,128)(2,1)} async-done(((bf16[1,96,1920]{2,1,0:T(8,128)(2,1)}), bf16[4,96,1920]{2,1,0:T(8,128)(2,1)}) %all-gather.18.cloned.1.call-update) | async-done | bytes 1474576 | tf_op jit(solution)/shard_map/all_gather | solution.py:657
  744.1 7.2 all-reduce.1
  760.9 11.6 %fusion.124 = f32[512,2560]{1,0:T(8,128)} fusion(bf16[512,2560]{1,0:T(8,128)(2,1)S(1)} %copy-done.13, bf16[2560,2560]{1,0:T(8,128)(2,1)} %get-tuple-element.74), kind=kOutput, calls=%fused_computation.229 | convolution fusion | flops 6710886400 | bytes 20971520 | tf_op jit(solution)/shard_map/dot_general | solution.py:21
  776.6 13.0 %all-gather.20.cloned.1.call-done = bf16[1664,640]{1,0:T(8,128)(2,1)} async-done(((bf16[416,640]{1,0:T(8,128)(2,1)}), bf16[1664,640]{1,0:T(8,128)(2,1)}) %all-gather.20.cloned.1.call-update) | async-done | bytes 2129936 | tf_op jit(solution)/shard_map/all_gather | solution.py:657
  789.6 16.1 %add_add_fusion.grads_ref = f32[512,2560]{1,0:T(8,128)} fusion(f32[512,2560]{1,0:T(8,128)} %fusion.61, f32[512,2560]{1,0:T(8,128)} %fusion.124, bf16[512,2560]{1,0:T(8,128)(2,1)} %bitcast.241, bf16[2560,2560]{1,0:T(8,128)(2,1)} %get-tuple-element.70), kind=kOutput, calls=%fused_computation.35 | convolution fusion | flops 6713507840 | bytes 31457280 | tf_op jit(solution)/shard_map/dot_general | solution.py:21
  815.2 79.8 %reduce-scatter.7.cloned.1.call-done = bf16[2,256,2560]{2,1,0:T(8,128)(2,1)} async-done(((bf16[2,1024,2560]{2,1,0:T(8,128)(2,1)}), bf16[2,256,2560]{2,1,0:T(8,128)(2,1)}) %reduce-scatter.7.cloned.1.call-update) | async-done | bytes 2621456 | tf_op jit(solution)/shard_map/reduce_scatter | solution.py:766
  899.3 8.2 shard_map.452
  (316 shorter events, 142.3 us)
Async XLA Ops:
  7.2 264.8 %all-gather.14.cloned.1.call-start = ((), (), s32[]{:S(2)}) async-start(), calls=%async_computation.5 | async-start | bytes 13107200 | tf_op jit(solution)/shard_map/all_gather | solution.py:688
  165.6 169.8 %all-gather.12.cloned.1.call-start = ((), (), s32[]{:S(2)}) async-start(), calls=%async_computation.4 | async-start | bytes 6553600 | tf_op jit(solution)/shard_map/all_gather | solution.py:747
  166.2 13.6 %copy-start.72 = (pred[32]{0:T(512)(128)(4,1)}, pred[32]{0:T(512)(128)(4,1)S(1)}, u32[]{:S(2)}) copy-start(pred[32]{0:T(512)(128)(4,1)S(1)} %compare_and_fusion) | copy-start | bytes 100
  166.3 13.5 %copy-start.63 = (s32[512]{0:T(512)}, s32[512]{0:T(512)S(1)}, u32[]{:S(2)}) copy-start(s32[512]{0:T(512)S(1)} %get-tuple-element.156) | copy-start | bytes 6148
  166.3 80.8 %copy-start.61 = (s32[512]{0:T(512)}, s32[512]{0:T(512)S(1)}, u32[]{:S(2)}) copy-start(s32[512]{0:T(512)S(1)} %get-tuple-element.155) | copy-start | bytes 6148
  166.6 43.7 %copy-start.38 = (pred[512,32]{1,0:T(32,128)(4,1)}, pred[512,32]{1,0:T(32,128)(4,1)S(1)}, u32[]{:S(2)}) copy-start(pred[512,32]{1,0:T(32,128)(4,1)S(1)} %select_compare_fusion) | copy-start | bytes 49156
  167.3 12.5 %copy-start.26 = (bf16[512,2560]{1,0:T(8,128)(2,1)}, bf16[512,2560]{1,0:T(8,128)(2,1)S(1)}, u32[]{:S(2)}) copy-start(bf16[512,2560]{1,0:T(8,128)(2,1)S(1)} %fusion.1) | copy-start | bytes 7864324
  169.3 71.8 %copy-start.36 = (bf16[512,64]{1,0:T(8,128)(2,1)}, bf16[512,64]{1,0:T(8,128)(2,1)S(1)}, u32[]{:S(2)}) copy-start(bf16[512,64]{1,0:T(8,128)(2,1)S(1)} %fusion.55) | copy-start | bytes 196612
  183.2 19.3 %collective-permute-start = (bf16[2,3,2560]{2,1,0:T(4,128)(2,1)S(1)}, bf16[2,3,2560]{2,1,0:T(4,128)(2,1)S(1)}, u32[]{:S(2)}, u32[]{:S(2)}) collective-permute-start(bf16[2,3,2560]{2,1,0:T(4,128)(2,1)S(1)} %slice.370), channel_id=1, source_target_pairs={{0,8},{8,16},{16,24},{1,9},{9,17},{17,25},{2,10},{10,18},{18,26},{... | collective-permute-start | bytes 92168 | tf_op jit(solution)/shard_map/ppermute | solution.py:650
  187.7 12.2 %copy-start.60 = (f32[4,2560]{1,0:T(4,128)S(1)}, f32[4,2560]{1,0:T(4,128)}, u32[]{:S(2)}) copy-start(f32[4,2560]{1,0:T(4,128)} %param.39) | copy-start | bytes 122884
  212.5 18.5 %copy-start.16 = (bf16[512,64]{1,0:T(8,128)(2,1)}, bf16[512,64]{1,0:T(8,128)(2,1)S(1)}, u32[]{:S(2)}) copy-start(bf16[512,64]{1,0:T(8,128)(2,1)S(1)} %fusion.56.inner_ref) | copy-start | bytes 196612
  231.1 16.0 %copy-start.2 = (f32[512,2560]{1,0:T(8,128)}, f32[512,2560]{1,0:T(8,128)S(1)}, u32[]{:S(2)}) copy-start(f32[512,2560]{1,0:T(8,128)S(1)} %get-tuple-element.73.cum_ref) | copy-start | bytes 15728644
  231.1 16.0 %copy-start.3 = (f32[512,2560]{1,0:T(8,128)}, f32[512,2560]{1,0:T(8,128)S(1)}, u32[]{:S(2)}) copy-start(f32[512,2560]{1,0:T(8,128)S(1)} %get-tuple-element.72.local_ref) | copy-start | bytes 15728644
  264.5 156.4 %all-gather.16.cloned.1.call-start = ((), (), s32[]{:S(2)}) async-start(), calls=%async_computation.6 | async-start | bytes 6553600 | tf_op jit(solution)/shard_map/all_gather | solution.py:747
  265.2 257.9 %reduce-scatter.9.cloned.1.call-start = ((), (), s32[]{:S(2)}) async-start(), calls=%async_computation.8 | async-start | bytes 6553600 | tf_op jit(solution)/shard_map/reduce_scatter | solution.py:756
  401.3 146.7 %reduce-scatter.11.cloned.1.call-start = ((), (), s32[]{:S(2)}) async-start(), calls=%async_computation.9 | async-start | bytes 6553600 | tf_op jit(solution)/shard_map/reduce_scatter | solution.py:756
  486.4 218.5 %reduce-scatter.13.cloned.1.call-start = ((), (), s32[]{:S(2)}) async-start(), calls=%async_computation.12 | async-start | bytes 3276800
  557.9 12.1 %copy-start.22 = (f32[512,2560]{1,0:T(8,128)}, f32[512,2560]{1,0:T(8,128)S(1)}, u32[]{:S(2)}) copy-start(f32[512,2560]{1,0:T(8,128)S(1)} %subtract_add_fusion.grad_resid_ref) | copy-start | bytes 15728644
  557.9 12.1 %copy-start.62 = (s32[512]{0:T(512)S(1)}, s32[512]{0:T(512)}, u32[]{:S(2)}) copy-start(s32[512]{0:T(512)} %copy-done.61) | copy-start | bytes 6148
  576.0 29.7 %copy-start.15 = (bf16[10,256,256]{2,1,0:T(8,128)(2,1)S(1)}, bf16[10,256,256]{2,1,0:T(8,128)(2,1)}, u32[]{:S(2)}) copy-start(bf16[10,256,256]{2,1,0:T(8,128)(2,1)} %table_a_ref.3) | copy-start | bytes 3932164
  597.0 50.2 %copy-start.12 = (bf16[512,2560]{1,0:T(8,128)(2,1)}, bf16[512,2560]{1,0:T(8,128)(2,1)S(1)}, u32[]{:S(2)}) copy-start(bf16[512,2560]{1,0:T(8,128)(2,1)S(1)} %get-tuple-element.88) | copy-start | bytes 7864324
  605.7 20.0 %copy-start.39 = (pred[512,32]{1,0:T(32,128)(4,1)S(1)}, pred[512,32]{1,0:T(32,128)(4,1)}, u32[]{:S(2)}) copy-start(pred[512,32]{1,0:T(32,128)(4,1)} %copy-done.38) | copy-start | bytes 49156
  629.3 5.9 collective-permute-start.1
  665.1 77.5 %all-gather.18.cloned.1.call-start = ((), (), s32[]{:S(2)}) async-start(), calls=%async_computation.10 | async-start | bytes 1843200 | tf_op jit(solution)/shard_map/all_gather | solution.py:657
  677.8 111.8 %all-gather.20.cloned.1.call-start = ((), (), s32[]{:S(2)}) async-start(), calls=%async_computation.11 | async-start | bytes 2662400 | tf_op jit(solution)/shard_map/all_gather | solution.py:657
  707.1 188.0 %reduce-scatter.7.cloned.1.call-start = ((), (), s32[]{:S(2)}) async-start(), calls=%async_computation.7 | async-start | bytes 13107200 | tf_op jit(solution)/shard_map/reduce_scatter | solution.py:766
  707.1 35.5 %copy-start.85 = (u32[32]{0:T(128)S(1)}, u32[32]{0:T(128)}, u32[]{:S(2)}) copy-start(u32[32]{0:T(128)} %constant.88) | copy-start | bytes 388
  707.1 36.7 %copy-start.84 = (s32[2]{0:T(128)S(1)}, s32[2]{0:T(128)}, u32[]{:S(2)}) copy-start(s32[2]{0:T(128)} %ids_ref.1) | copy-start | bytes 28
  707.1 44.2 %copy-start.59 = (f32[2560]{0:T(1024)S(1)}, f32[2560]{0:T(1024)}, u32[]{:S(2)}) copy-start(f32[2560]{0:T(1024)} %param.35) | copy-start | bytes 30724
  742.6 10.6 %collective-permute-start.4 = (bf16[4,96,1920]{2,1,0:T(8,128)(2,1)}, bf16[4,96,1920]{2,1,0:T(8,128)(2,1)}, u32[]{:S(2)}, u32[]{:S(2)}) collective-permute-start(bf16[4,96,1920]{2,1,0:T(8,128)(2,1)} %all-gather.18.cloned.1.call-done), channel_id=1, source_target_pairs={{0,1},{1,0},{2,3},{3,2},{4,5},{5,4},{6,7},{7,6},{8,9},{9,8},{10,11... | collective-permute-start | bytes 4423688 | tf_op jit(solution)/shard_map/ppermute | solution.py:658
  751.3 1.2 collective-permute-start.2
  789.6 16.1 %collective-permute-start.3 = (bf16[4,416,640]{2,1,0:T(8,128)(2,1)}, bf16[4,416,640]{2,1,0:T(8,128)(2,1)}, u32[]{:S(2)}, u32[]{:S(2)}) collective-permute-start(bf16[4,416,640]{2,1,0:T(8,128)(2,1)} %bitcast.245), channel_id=1, source_target_pairs={{0,1},{1,0},{2,3},{3,2},{4,5},{5,4},{6,7},{7,6},{8,9},{9,8},{10,11... | collective-permute-start | bytes 6389768 | tf_op jit(solution)/shard_map/ppermute | solution.py:658
  (79 other events, 459.3 us)
Sparse Core Ops, SparseCore 0:
  165.7 106.2 all-gather.13
  273.9 61.4 all-gather.11
  337.7 61.4 all-gather.15
  402.1 61.4 reduce-scatter.8
  486.5 61.4 reduce-scatter.10
  665.2 39.6 reduce-scatter.12
  707.1 35.4 all-gather.17
  744.1 45.4 all-gather.19
  792.7 102.2 reduce-scatter.6

commit v3 on v2

--- a/solution.py
+++ b/solution.py
@@ -15,6 +15,7 @@
 NT = (((1,), (1,)), ((), ()))
 NN = (((1,), (0,)), ((), ()))
 TN = (((0,), (0,)), ((), ()))
+ANYWHERE = pl.BlockSpec(memory_space=pl.ANY)
 
 
 def dot(a, b, dims=NN):
@@ -277,15 +278,16 @@
     out_ref[...] = (dot(cot_ref[...], wd_ref[...], NT) + dot(through_ref[...], do_ref[...])).astype(BF16)
 
 
-def grad_hidden_call(cot, wd, lift_out, do):
-    rows, width = cot.shape
+def grad_hidden_call(cot, s, wd, lift_out, do):
+    rows, width = cot.shape[1:]
     units, ranks = wd.shape[0], do.shape[0]
     tile = tile_of(units, 512)
     return pl.pallas_call(
         grad_hidden_kernel,
         grid=(pl.cdiv(units, tile),),
         out_shape=[jax.ShapeDtypeStruct((rows, units), BF16), jax.ShapeDtypeStruct((rows, ranks), BF16)],
-        in_specs=[resident(cot), pl.BlockSpec((tile, width), lambda i: (i, 0)), resident(lift_out),
+        in_specs=[pl.BlockSpec((None, rows, width), lambda i: (s, 0, 0), pipeline_mode=pl.Buffered(1)),
+                  pl.BlockSpec((tile, width), lambda i: (i, 0)), resident(lift_out),
                   pl.BlockSpec((ranks, tile), lambda i: (0, i))],
         out_specs=[pl.BlockSpec((rows, tile), lambda i: (0, i)), pl.BlockSpec((rows, ranks), lambda i: (0, 0))],
         compiler_params=pltpu.CompilerParams(vmem_limit_bytes=60 * 2**20),
@@ -295,7 +297,8 @@
     )(cot, wd, lift_out, do)
 
 
-def hidden_kernel(tok_ref, gh_ref, wg_ref, wu_ref, down_ref, lg_ref, lu_ref, hidden_ref, gg_ref, gu_ref, inner_ref):
+def hidden_kernel(tok_ref, gh_ref, wg_ref, wu_ref, down_ref, lg_ref, lu_ref, *refs):
+    hidden_ref, gg_ref, gu_ref, inner_ref = refs[-4:]
     ranks = lg_ref.shape[0]
 
     @pl.when(pl.program_id(0) == 0)
@@ -312,7 +315,7 @@
     gu_ref[...] = (grad_hidden * value).astype(BF16)
 
 
-def hidden_call(tok, gh, wg, wu, down, lg, lu):
+def hidden_call(tok, gh, wg, wu, down, lg, lu, earlier):
     rows, width = tok.shape
     units, ranks = wg.shape[1], lg.shape[0]
     tile = tile_of(units, 512)
@@ -324,13 +327,13 @@
         hidden_kernel,
         grid=(pl.cdiv(units, tile),),
         out_shape=[wide, wide, wide, jax.ShapeDtypeStruct((rows, 2 * ranks), BF16)],
-        in_specs=[resident(tok), out, cols, cols, resident(down), rank, rank],
+        in_specs=[resident(tok), out, cols, cols, resident(down), rank, rank] + [ANYWHERE] * len(earlier),
         out_specs=[out, out, out, pl.BlockSpec((rows, 2 * ranks), lambda i: (0, 0))],
         compiler_params=pltpu.CompilerParams(vmem_limit_bytes=60 * 2**20),
         cost_estimate=pl.CostEstimate(
             flops=4 * rows * width * units, bytes_accessed=4 * width * units + 10 * rows * units,
             transcendentals=rows * units),
-    )(tok, gh, wg, wu, down, lg, lu)
+    )(tok, gh, wg, wu, down, lg, lu, *earlier)
 
 
 def back_kernel(gg_ref, gu_ref, wg_ref, wu_ref, lg_ref, lu_ref, down_ref, back_ref, through_ref):
@@ -573,7 +576,7 @@
         + [pltpu.SemaphoreType.DMA((3 * units + 1, 12)), pltpu.SemaphoreType.DMA((3 * units + 1, 12)),
            pltpu.SemaphoreType.DMA((4,))],
         compiler_params=pltpu.CompilerParams(
-            collective_id=0, has_side_effects=True, vmem_limit_bytes=32 * 2**20),
+            collective_id=0, has_side_effects=True, vmem_limit_bytes=60 * 2**20),
         cost_estimate=pl.CostEstimate(flops=0, bytes_accessed=400 * 2**20, transcendentals=0),
     )(*operands)
 
@@ -594,54 +597,157 @@
     )(flat, *earlier).reshape(value.shape)
 
 
-def finish_kernel(resid_ref, outward_ref, grad_resid_ref, inputs_ref, gain_ref, grads_ref, block_ref, out_ref):
+def row_tiles(rows, width, count):
+    step = min(rows, 128)
+    return (rows // step,), [pl.BlockSpec((step, width), lambda i: (i, 0))] * count
+
+
+def block_kernel(resid_ref, outward_ref, block_ref):
     block_ref[...] = (resid_ref[...] + outward_ref[...].astype(F32)).astype(BF16)
+
+
+def block_call(resid, outward):
+    rows, width = resid.shape
+    grid, tiles = row_tiles(rows, width, 3)
+    return pl.pallas_call(
+        block_kernel,
+        grid=grid,
+        out_shape=jax.ShapeDtypeStruct((rows, width), BF16),
+        in_specs=tiles[:2],
+        out_specs=tiles[2],
+        cost_estimate=pl.CostEstimate(flops=rows * width, bytes_accessed=8 * rows * width, transcendentals=0),
+    )(resid, outward)
+
+
+def resid_grad_kernel(resid_ref, cot_ref, gain_ref, grads_ref, *refs):
+    full_ref, low_ref = refs[-2:]
+    values = resid_ref[...]
+    rate = lax.rsqrt(jnp.mean(values * values, axis=-1, keepdims=True) + EPS)
+    grads = cot_ref[...].astype(F32) + norm_back(values, gain_ref[...], rate, grads_ref[...].astype(F32))
+    full_ref[...] = grads
+    low_ref[...] = grads.astype(BF16)
+
+
+def resid_grad(resid, cot, gain, grads, earlier):
+    rows, width = resid.shape
+    grid, tiles = row_tiles(rows, width, 5)
+    return pl.pallas_call(
+        resid_grad_kernel,
+        grid=grid,
+        out_shape=[jax.ShapeDtypeStruct((rows, width), F32), jax.ShapeDtypeStruct((rows, width), BF16)],
+        in_specs=[tiles[0], tiles[0], pl.BlockSpec((1, width), lambda i: (0, 0)), tiles[0]]
+        + [ANYWHERE] * len(earlier),
+        out_specs=tiles[:2],
+        compiler_params=pltpu.CompilerParams(vmem_limit_bytes=40 * 2**20),
+        cost_estimate=pl.CostEstimate(
+            flops=20 * rows * width, bytes_accessed=14 * rows * width, transcendentals=rows),
+    )(resid, cot, gain, grads, *earlier)
+
+
+def finish_kernel(grad_resid_ref, inputs_ref, gain_ref, grads_ref, out_ref):
     values = inputs_ref[...].astype(F32)
     rate = lax.rsqrt(jnp.mean(values * values, axis=-1, keepdims=True) + EPS)
     out_ref[...] = grad_resid_ref[...] + norm_back(values, gain_ref[...], rate, grads_ref[...])
 
 
-def finish(resid, outward, grad_resid, inputs, gain, grads):
-    rows, width = resid.shape
-    step = min(rows, 128)
-    tile = pl.BlockSpec((step, width), lambda i: (i, 0))
+def finish(grad_resid, inputs, gain, grads):
+    rows, width = inputs.shape
+    grid, tiles = row_tiles(rows, width, 3)
     return pl.pallas_call(
         finish_kernel,
-        grid=(rows // step,),
-        out_shape=[jax.ShapeDtypeStruct((rows, width), BF16), jax.ShapeDtypeStruct((rows, width), F32)],
-        in_specs=[tile, tile, tile, tile, pl.BlockSpec((1, width), lambda i: (0, 0)), tile],
-        out_specs=[tile, tile],
+        grid=grid,
+        out_shape=jax.ShapeDtypeStruct((rows, width), F32),
+        in_specs=[tiles[0], tiles[0], pl.BlockSpec((1, width), lambda i: (0, 0)), tiles[0]],
+        out_specs=tiles[0],
         compiler_params=pltpu.CompilerParams(vmem_limit_bytes=40 * 2**20),
         cost_estimate=pl.CostEstimate(
-            flops=20 * rows * width, bytes_accessed=22 * rows * width, transcendentals=rows),
-    )(resid, outward, grad_resid, inputs, gain, grads)
-
-
-def spread_kernel(tables, ids_ref, got_ref, *out_refs):
-    replicas, seqs, ranks = got_ref.shape[0], ids_ref.shape[0] // got_ref.shape[0], out_refs[0].shape[1]
+            flops=20 * rows * width, bytes_accessed=14 * rows * width, transcendentals=rows),
+    )(grad_resid, inputs, gain, grads)
+
+
+def spread_kernel(tables, pieces, ids_ref, from_ref, *refs):
+    gots, out_refs = refs[:pieces], refs[-tables:]
+    ranks = out_refs[0].shape[1]
+    replicas = from_ref.shape[0]
+    seqs = ids_ref.shape[0] // replicas
     for table in range(tables):
         out_refs[table][...] = jnp.zeros_like(out_refs[table])
-    for replica in range(replicas):
-        for s in range(seqs):
-            place = ids_ref[replica * seqs + s]
-            for table in range(tables):
-                rows = pl.ds((table * seqs + s) * ranks, ranks)
-                out_refs[table][place] += got_ref[replica, rows, :].astype(F32)
-
-
-def spread(ids, got, tables, sets, seqs):
-    replicas, rows, width = got.shape
+    replica = 0
+    for got_ref in gots:
+        for at in range(got_ref.shape[0]):
+            for s in range(seqs):
+                place = ids_ref[from_ref[replica] * seqs + s]
+                for table in range(tables):
+                    rows = pl.ds((table * seqs + s) * ranks, ranks)
+                    out_refs[table][place] += got_ref[at, rows, :].astype(F32)
+            replica += 1
+
+
+def spread(ids, source, gots, tables, sets, seqs, earlier=()):
+    rows, width = gots[0].shape[1:]
+    replicas = source.shape[0]
     ranks = rows // (tables * seqs)
-    return pl.pallas_call(
-        functools.partial(spread_kernel, tables),
+    scalars = pl.BlockSpec(memory_space=pltpu.SMEM)
+    return pl.pallas_call(
+        functools.partial(spread_kernel, tables, len(gots)),
         out_shape=[jax.ShapeDtypeStruct((sets, ranks, width), F32)] * tables,
-        in_specs=[pl.BlockSpec(memory_space=pltpu.SMEM), pl.BlockSpec(memory_space=pltpu.VMEM)],
+        in_specs=[scalars, scalars] + [pl.BlockSpec(memory_space=pltpu.VMEM)] * len(gots)
+        + [ANYWHERE] * len(earlier),
         out_specs=[pl.BlockSpec(memory_space=pltpu.VMEM)] * tables,
         compiler_params=pltpu.CompilerParams(vmem_limit_bytes=56 * 2**20),
         cost_estimate=pl.CostEstimate(
             flops=replicas * rows * width,
             bytes_accessed=2 * replicas * rows * width + 4 * tables * sets * ranks * width, transcendentals=0),
-    )(ids, got)
+    )(ids, source, *gots, *earlier)
+
+
+def products_kernel(plan, *refs):
+    out_ref, row = refs[-1], 0
+    for place, (kind, first, last) in plan:
+        if kind == "product":
+            result = dot(refs[place][:, first:last], refs[place + 1][...], TN)
+        else:
+            result = refs[place][...]
+        count = last - first
+        out_ref[row : row + count, :] = result.astype(BF16)
+        row += count
+
+
+def products(items, earlier=(), blocks=1):
+    operands, specs, plan, total = [], [], [], 0
+    width = items[0][3].shape[-1]
+    tile = width // blocks if blocks > 1 and width % (128 * blocks) == 0 else tile_of(width, 512)
+    for item in items:
+        if len(item) == 1:
+            plan.append((len(operands), ("rows", 0, item[0].shape[0])))
+            operands.append(item[0])
+            specs.append(pl.BlockSpec((item[0].shape[0], tile), lambda i: (0, i)))
+        else:
+            lhs, first, last, rhs = item
+            plan.append((len(operands), ("product", first, last)))
+            if isinstance(rhs, tuple):
+                rhs, s = rhs
+                block = pl.BlockSpec((None, rhs.shape[1], tile), lambda i, s=s: (s, 0, i))
+            else:
+                block = pl.BlockSpec((rhs.shape[0], tile), lambda i: (0, i))
+            operands += [lhs, rhs]
+            specs += [resident(lhs), block]
+        total += plan[-1][1][2] - plan[-1][1][1]
+    cells = sum(operand.size for operand in operands)
+    direct = blocks > 1 and tile * blocks == width
+    result = pl.pallas_call(
+        functools.partial(products_kernel, plan),
+        grid=(pl.cdiv(width, tile),),
+        out_shape=jax.ShapeDtypeStruct((blocks, total, tile) if direct else (total, width), BF16),
+        in_specs=specs + [ANYWHERE] * len(earlier),
+        out_specs=(pl.BlockSpec((None, total, tile), lambda i: (i, 0, 0)) if direct
+                   else pl.BlockSpec((total, tile), lambda i: (0, i))),
+        compiler_params=pltpu.CompilerParams(vmem_limit_bytes=60 * 2**20),
+        cost_estimate=pl.CostEstimate(flops=64 * cells, bytes_accessed=2 * cells, transcendentals=0),
+    )(*operands, *earlier)
+    if blocks > 1 and not direct:
+        result = jnp.swapaxes(result.reshape(total, blocks, width // blocks), 0, 1)
+    return result
 
 
 def passed_along(block, axis, distance):
@@ -650,12 +756,21 @@
     return lax.ppermute(block, axis, route)
 
 
-def over_replicas(value):
-    count = lax.axis_size("replica")
+def over_replicas(value, direct):
+    count, here = lax.axis_size("replica"), lax.axis_index("replica")
     if count % 2:
-        return lax.all_gather(value, "replica")
-    got = lax.all_gather(value, "replica", axis_index_groups=[list(range(p, count, 2)) for p in range(2)])
-    return jnp.concatenate([got, lax.ppermute(got, "replica", [(i, i ^ 1) for i in range(count)])], 0)
+        return [lax.all_gather(value, "replica")], jnp.arange(count, dtype=jnp.int32)
+    steps = jnp.arange(count // 2, dtype=jnp.int32)
+    if direct:
+        got = [value[None]] + [
+            lax.ppermute(value, "replica", [(i, (i + 2 * step) % count) for i in range(count)])[None]
+            for step in range(1, count // 2)]
+        source = (here + count - 2 * steps) % count
+    else:
+        got = [lax.all_gather(value, "replica", axis_index_groups=[list(range(p, count, 2)) for p in range(2)])]
+        source = here % 2 + 2 * steps
+    swapped = [lax.ppermute(part, "replica", [(i, i ^ 1) for i in range(count)]) for part in got]
+    return got + swapped, jnp.concatenate([source, source + 1 - 2 * (here % 2)], 0)
 
 
 def body(
@@ -684,7 +799,7 @@
         stack[i * mask_cols : (i + 1) * mask_cols] for i in range(13)]
     own_lift_gate, own_lift_upper, own_down_outward = [
         own_tables[i * mask_cols : (i + 1) * mask_cols] for i in range(3)]
-    all_ids = over_replicas(adapter_ids).reshape(-1)
+    all_ids = lax.all_gather(adapter_ids, "replica", axis=0, tiled=True)
     cotangents = lax.all_gather(ordered(out_grad, stack), "group", axis=1, tiled=True)
 
     row_seq = lax.broadcasted_iota(jnp.int32, (rows, mask_cols), 0) // stretch
@@ -734,40 +849,43 @@
     inner_mixer = (dot(merged, p_down_mixer, NT) * own).astype(BF16)
     mixed = dot(merged, full_mixer) + dot(inner_mixer, p_lift_mixer)
     resid = x_float + mixed
-    normed_two_f, rate_two = norm_rows(resid, gain_mlp)
+    normed_two_f, _ = norm_rows(resid, gain_mlp)
     normed_two = normed_two_f.astype(BF16).reshape(seqs, stretch, width)
 
-    all_tokens, backs, hiddens, throughs = [], [], [], []
-    grad_own_lift_gate, grad_own_lift_upper, grad_own_down_outward = [], [], []
-    grad_down_gate, grad_down_upper, grad_lift_outward = [], [], []
     spans = [slice(s * ranks, (s + 1) * ranks) for s in range(seqs)]
     grad_hiddens = [
-        grad_hidden_call(cotangents[s], w_down, p_lift_outward[at], own_down_outward[at])
+        grad_hidden_call(cotangents, s, w_down, p_lift_outward[at], own_down_outward[at])
         for s, at in enumerate(spans)]
     all_tokens = [lax.all_gather(normed_two[s], "group", axis=0, tiled=True) for s in range(seqs)]
+    backs, hiddens, throughs, inners, gates, uppers = [], [], [], [], [], []
     for s, at in enumerate(spans):
-        tokens = all_tokens[s]
-        grad_hidden, through_out = grad_hiddens[s]
         two_downs = jnp.concatenate([p_down_gate[at], p_down_upper[at]], 0)
+        earlier = (all_ids,) + tuple(grad_hidden for grad_hidden, _ in grad_hiddens) if s == 0 else ()
         hidden, grad_gate, grad_upper, inner = hidden_call(
-            tokens, grad_hidden, w_gate, w_upper, two_downs, own_lift_gate[at], own_lift_upper[at])
+            all_tokens[s], grad_hiddens[s][0], w_gate, w_upper, two_downs, own_lift_gate[at], own_lift_upper[at],
+            earlier)
         back, through = back_call(
             grad_gate, grad_upper, w_gate, w_upper, own_lift_gate[at], own_lift_upper[at], two_downs)
         backs.append(lax.psum_scatter(back, "group", scatter_dimension=0, tiled=True))
-        hiddens.append(hidden)
-        grad_own_lift_gate.append(dot(inner[:, :ranks], grad_gate, TN))
-        grad_own_lift_upper.append(dot(inner[:, ranks:], grad_upper, TN))
-        grad_own_down_outward.append(dot(through_out, hidden, TN))
-        grad_down_gate.append(dot(through[:, :ranks], tokens, TN))
-        grad_down_upper.append(dot(through[:, ranks:], tokens, TN))
+        for kept, value in zip((hiddens, throughs, inners, gates, uppers),
+                               (hidden, through, inner, grad_gate, grad_upper)):
+            kept.append(value)
     outward, inner_out = outward_call(hiddens, w_down, own_down_outward, p_lift_outward, back)
-    for s in range(seqs):
-        grad_lift_outward.append(dot(inner_out[s], cotangents[s], TN))
+    early = products(
+        [(throughs[s], 0, ranks, all_tokens[s]) for s in range(seqs)]
+        + [(throughs[s], ranks, 2 * ranks, all_tokens[s]) for s in range(seqs)]
+        + [(inner_out[s], 0, ranks, (cotangents, s)) for s in range(seqs)], (outward,))
+    wide = products(
+        [(inners[s], 0, ranks, gates[s]) for s in range(seqs)]
+        + [(inners[s], ranks, 2 * ranks, uppers[s]) for s in range(seqs)]
+        + [(grad_hiddens[s][1], 0, ranks, hiddens[s]) for s in range(seqs)], (outward,))
+    grad_normed_two = jnp.concatenate(backs, 0)
+    grad_resid, grad_mixed = resid_grad(
+        resid, out_grad.reshape(rows, width), gain_mlp.reshape(1, width), grad_normed_two, (early, wide))
     outward = lax.psum_scatter(outward, "group", scatter_dimension=1, tiled=True).reshape(rows, width)
-    grad_normed_two = jnp.concatenate(backs, 0).astype(F32)
-    grad_resid = out_grad.reshape(rows, width).astype(F32) + norm_back(resid, gain_mlp, rate_two, grad_normed_two)
-
-    grad_mixed = grad_resid.astype(BF16)
+    block_out = block_call(resid, outward)
+    all_wide, wide_source = over_replicas(wide, True)
+
     through_mixer = (dot(grad_mixed, p_lift_mixer, NT) * own).astype(BF16)
     grad_merged = dot(grad_mixed, full_mixer, NT) + dot(through_mixer, p_down_mixer)
     span, total, firsts, grad_branch_pre = backward_scan(
@@ -795,17 +913,17 @@
     through_one = jnp.concatenate([through_branch, through_input], 1)
     grad_normed = (dot(grad_branch_pre, full_branch, NT) + dot(grad_fed, full_input, NT)
                    + dot(through_one, stack[: 2 * mask_cols]))
-    block_out, grad_inputs = finish(
-        resid, outward, grad_resid, inputs.reshape(rows, width), gain_mix.reshape(1, width), grad_normed)
-
-    partial = jnp.concatenate(
-        [dot(through_one, normed, TN), dot(through_gates, rounded, TN), dot(through_mixer, merged, TN),
-         dot(inner_branch, grad_branch_pre, TN), dot(inner_input, grad_fed, TN), grad_lift_gates,
-         dot(inner_mixer, grad_mixed, TN)] + grad_down_gate + grad_down_upper + grad_lift_outward, 0).astype(BF16)
-    owned = lax.psum_scatter(partial, "group", scatter_dimension=1, tiled=True)
-    wide = jnp.concatenate(grad_own_lift_gate + grad_own_lift_upper + grad_own_down_outward, 0).astype(BF16)
-    wides = spread(all_ids, over_replicas(wide), 3, sets, seqs)
-    totals = spread(all_ids, over_replicas(owned), 13, sets, seqs)
+    grad_inputs = finish(grad_resid, inputs.reshape(rows, width), gain_mix.reshape(1, width), grad_normed)
+
+    both = 2 * mask_cols
+    partial = products(
+        [(through_one, 0, both, normed), (through_gates, 0, both, rounded), (through_mixer, 0, mask_cols, merged),
+         (inner_branch, 0, mask_cols, grad_branch_pre), (inner_input, 0, mask_cols, grad_fed), (grad_lift_gates,),
+         (inner_mixer, 0, mask_cols, grad_mixed), (early,)], (block_out, *all_wide), group)
+    owned = lax.psum_scatter(partial, "group", scatter_dimension=0, tiled=False)
+    wides = spread(all_ids, wide_source, all_wide, 3, sets, seqs, (partial,))
+    all_owned, owned_source = over_replicas(ordered(owned, grad_inputs, wides[0]), False)
+    totals = spread(all_ids, owned_source, all_owned, 13, sets, seqs)
     (t_down_branch, t_down_input, t_down_decay, t_down_admit, t_down_mixer, t_lift_branch, t_lift_input, t_lift_decay,
      t_lift_admit, t_lift_mixer, t_down_gate, t_down_upper, t_lift_outward) = totals
     return (

time: 923 us -> 774 us (0.84)
  waiting for transfers between devices: 223 us -> 86.3 us
  Pallas kernels: 427 us -> 472 us
  matrix products: 135 us -> 108 us
  local copies, waits for them, and re-layouts: 45.9 us -> 23.1 us
  other arithmetic: 36.9 us -> 21.7 us
    reduce_scatter x1, waiting for transfers between devices: 79.8 us -> 0.01 us  [body(): lax.psum_scatter(outward, 'group', scatter_dimension=1, tiled=True)]
    pallas_call x3 -> x8, Pallas kernels: 16.9 us -> 61.2 us  [the longest x3 37.8 us: products(): pl.pallas_call(functools.partial(products_kernel, plan), grid=(pl.cdiv(wi...]
    unnamed x10 -> x9, waiting for transfers between devices: 28.5 us -> 0.8 us
    dot_general x36 -> x18, matrix products: 135 us -> 108 us  [dot(): return lax.dot_general(a, b, dims, preferred_element_type=F32)]
    reduce_scatter x2, waiting for transfers between devices: 24.9 us -> 0.01 us  [body(): lax.psum_scatter(back, 'group', scatter_dimension=0, tiled=True)]
    all_gather x2, waiting for transfers between devices: 35.2 us -> 20.3 us  [body(): lax.all_gather(normed_two[s], 'group', axis=0, tiled=True)]
    unnamed x204 -> x166, local copies, waits for them, and re-layouts: 25.8 us -> 12.6 us
    all_gather x2 -> x1, waiting for transfers between devices: 47.7 us -> 51.8 us  [over_replicas(): lax.all_gather(value, 'replica', axis_index_groups=[list(range(p, count,...]
  transfers between devices with their start and end apart: 14 -> 18, of which waited for: 9 -> 5; matrix products, arithmetic and copies ran while one was open for 15% -> 18% of each run, Pallas kernels for 25% -> 40%
where the time goes in v3:
time: 774 us; the launch traced here: 766 us
  Pallas kernels  472 us (61%)
  matrix products  108 us (14%)
  waiting for transfers between devices  86.3 us (11%)
  blocking collectives  27.8 us (4%)
  local copies, waits for them, and re-layouts  23.1 us (3%)
  other arithmetic  21.7 us (3%)
  between operations  16.7 us (2%)
  starting transfers between devices  11.4 us (1%)
    pallas_call x1, Pallas kernels, gather_weights(): pl.pallas_call(functools.partial(gather_kernel, units), out_shape=[jax.Sh...  143 us
    dot_general x18, matrix products, dot(): return lax.dot_general(a, b, dims, preferred_element_type=F32)  108 us
    pallas_call x2, Pallas kernels, back_call(): pl.pallas_call(back_kernel, grid=(pl.cdiv(width, tile),), out_shape=[jax....  65.8 us
    pallas_call x2, Pallas kernels, hidden_call(): pl.pallas_call(hidden_kernel, grid=(pl.cdiv(units, tile),), out_shape=[wi...  65.4 us
    all_gather x1, waiting for transfers between devices, over_replicas(): lax.all_gather(value, 'replica', axis_index_groups=[list(range(p, count,...  51.8 us
    pallas_call x3, Pallas kernels, products(): pl.pallas_call(functools.partial(products_kernel, plan), grid=(pl.cdiv(wi...  37.8 us
    pallas_call x2, Pallas kernels, grad_hidden_call(): pl.pallas_call(grad_hidden_kernel, grid=(pl.cdiv(units, tile),), out_shap...  37.1 us
    pallas_call x1, Pallas kernels, outward_call(): pl.pallas_call(functools.partial(outward_kernel, seqs), grid=(pl.cdiv(wid...  32.6 us
  transfers between devices with their start and end apart: 18, of which 5 were waited for; matrix products, arithmetic and copies ran while one was open for 18% of the time, Pallas kernels for 40%

profile of v3, /device:TPU:0, one launch (start us, length us, event | category | flops | bytes accessed | tf_op | source)
XLA Modules:
  0.0 766.4 jit_solution(6319058170146334000)
XLA Ops:
  10.2 143.2 %shard_map.440 = (bf16[2560,2560]{1,0:T(8,128)(2,1)}, bf16[2560,2560]{1,0:T(8,128)(2,1)}, bf16[2560,2560]{1,0:T(8,128)(2,1)}, bf16[416,2560]{1,0:T(8,128)(2,1)}) custom-call(bf16[2560,640]{1,0:T(8,128)(2,1)} %refs_0_.1, bf16[2560,640]{1,0:T(8,128)(2,1)} %refs_1_.1, bf16[640,2560]{1,0:T(8,128)(2,1)} %refs_2_.2, bf16[416,640]{1,0:T(8,128)(2,1)} %bitcast.199), custom_call_target="tpu_custom_call" | custom-call | bytes 419430400 | tf_op jit(solution)/shard_map/pallas_call | solution.py:569
  160.4 10.4 %fusion.69 = f32[512,2560]{1,0:T(8,128)S(1)} fusion(bf16[512,2560]{1,0:T(8,128)(2,1)S(1)} %fusion.1.refs_1_, bf16[2560,2560]{1,0:T(8,128)(2,1)} %get-tuple-element.70), kind=kOutput, calls=%fused_computation.162 | convolution fusion | flops 6710886400 | bytes 20971520 | tf_op jit(solution)/shard_map/dot_general | solution.py:22
  178.8 12.3 %fusion.70 = f32[512,2560]{1,0:T(8,128)} fusion(bf16[512,2560]{1,0:T(8,128)(2,1)} %copy-done.30, bf16[2560,2560]{1,0:T(8,128)(2,1)} %get-tuple-element.74), kind=kOutput, calls=%fused_computation.163 | convolution fusion | flops 6710886400 | bytes 20971520 | tf_op jit(solution)/shard_map/dot_general | solution.py:22
  195.1 4.6 fusion.4
  203.8 16.9 %shard_map.441 = (f32[512,2560]{1,0:T(8,128)S(1)}, f32[512,2560]{1,0:T(8,128)S(1)}) custom-call(f32[512,2560]{1,0:T(8,128)} %bitcast.182, bf16[512,64]{1,0:T(8,128)(2,1)S(1)} %fusion.26.inner_ref, bf16[64,2560]{1,0:T(8,128)(2,1)S(1)} %slice.275.lift_ref, bf16[10,256,256]{2,1,0:T(8,128)(2,1)S(1)} %copy-done.5, bf16[10,256,256]{2,1,0:T(8,128)(2,1)S(1)} %copy-done.17, ...), custom_call_target="tpu_custom_call" | custom-call | flops 1420820480 | bytes 15728640 | tf_op jit(solution)/shard_map/pallas_call | solution.py:107
  220.9 9.8 %all-gather.3 = f32[4,4,2560]{2,1,0:T(4,128)S(1)} all-gather(f32[1,4,2560]{2,1,0:T(4,128)S(1)} %maximum_bitcast_fusion), channel_id=2, replica_groups=mesh['group'=4,'replica'=8] {'group'}, dimensions={0}, use_global_device_ids=true | all-gather | bytes 204800 | tf_op jit(solution)/shard_map/all_gather | solution.py:841
  230.8 6.0 fusion.18
  238.8 10.0 %fusion.71 = f32[512,2560]{1,0:T(8,128)S(1)} fusion(bf16[512,2560]{1,0:T(8,128)(2,1)S(1)} %get-tuple-element.153.refs_5_, bf16[2560,2560]{1,0:T(8,128)(2,1)} %get-tuple-element.75), kind=kOutput, calls=%fused_computation.164 | convolution fusion | flops 6710886400 | bytes 20971520 | tf_op jit(solution)/shard_map/dot_general | solution.py:22
  256.4 9.4 %all-reduce.1.refs_0_.ids_ref = s32[16]{0:T(128)} all-reduce(s32[16]{0:T(128)S(1)} %dynamic-update-slice), channel_id=1, replica_groups=mesh['group'=4,'replica'=8] {'replica'}, use_global_device_ids=true, to_apply=%add.1 | all-reduce | flops 16 | bytes 128
  269.0 18.7 %shard_map.444 = (bf16[1024,1920]{1,0:T(8,128)(2,1)}, bf16[1024,16]{1,0:T(8,128)(2,1)}) custom-call(bf16[2,1024,2560]{2,1,0:T(8,128)(2,1)} %all-gather.12.cloned.1.call-done.cot_ref.refs_9_.refs_11_, bf16[1920,2560]{1,0:T(8,128)(2,1)} %refs_2_.3, bf16[16,2560]{1,0:T(8,128)(2,1)} %get-tuple-element.128.lift_out_ref, bf16[16,1920]{1,0:T(8,128)(2,1)} %get-tuple-element.136.do_ref), custom_call_target="tpu_custom_call" | custom-call | flops 10066329600 | bytes 19005440 | tf_op jit(solution)/shard_map/pallas_call | solution.py:285
  287.7 18.3 %shard_map.443 = (bf16[1024,1920]{1,0:T(8,128)(2,1)}, bf16[1024,16]{1,0:T(8,128)(2,1)}) custom-call(bf16[2,1024,2560]{2,1,0:T(8,128)(2,1)} %all-gather.12.cloned.1.call-done.cot_ref.refs_9_.refs_11_, bf16[1920,2560]{1,0:T(8,128)(2,1)} %refs_2_.3, bf16[16,2560]{1,0:T(8,128)(2,1)} %get-tuple-element.131.lift_out_ref, bf16[16,1920]{1,0:T(8,128)(2,1)} %get-tuple-element.139.do_ref), custom_call_target="tpu_custom_call" | custom-call | flops 10066329600 | bytes 19005440 | tf_op jit(solution)/shard_map/pallas_call | solution.py:285
  306.1 20.3 %all-gather.10.cloned.1.call-done.tok_ref.refs_1_.refs_5_ = bf16[1024,2560]{1,0:T(8,128)(2,1)} async-done(((bf16[256,2560]{1,0:T(8,128)(2,1)}), bf16[1024,2560]{1,0:T(8,128)(2,1)}) %all-gather.10.cloned.1.call-update) | async-done | bytes 5242896 | tf_op jit(solution)/shard_map/all_gather | solution.py:859
  326.4 32.7 %shard_map.445 = (bf16[1024,1920]{1,0:T(8,128)(2,1)}, bf16[1024,1920]{1,0:T(8,128)(2,1)}, bf16[1024,1920]{1,0:T(8,128)(2,1)}, bf16[1024,32]{1,0:T(8,128)(2,1)}) custom-call(bf16[1024,2560]{1,0:T(8,128)(2,1)} %all-gather.10.cloned.1.call-done.tok_ref.refs_1_.refs_5_, bf16[1024,1920]{1,0:T(8,128)(2,1)} %get-tuple-element.77.gh_ref.refs_1_, ...), custom_call_target="tpu_custom_call" | custom-call | flops 20132659200 | bytes 39321600 | tf_op jit(solution)/shard_map/pallas_call | solution.py:326
  359.1 33.2 %shard_map.450 = (bf16[1024,2560]{1,0:T(8,128)(2,1)}, bf16[1024,32]{1,0:T(8,128)(2,1)}) custom-call(bf16[1024,1920]{1,0:T(8,128)(2,1)} %get-tuple-element.85.gg_ref.refs_1_, bf16[1024,1920]{1,0:T(8,128)(2,1)} %get-tuple-element.86.gu_ref.refs_5_, bf16[2560,1920]{1,0:T(8,128)(2,1)} %wg_ref.7, bf16[2560,1920]{1,0:T(8,128)(2,1)} %wu_ref.7, ...), custom_call_target="tpu_custom_call" | custom-call | flops 20132659200 | bytes 32768000 | tf_op jit(solution)/shard_map/pallas_call | solution.py:356
  393.3 32.7 %shard_map.446 = (bf16[1024,1920]{1,0:T(8,128)(2,1)}, bf16[1024,1920]{1,0:T(8,128)(2,1)}, bf16[1024,1920]{1,0:T(8,128)(2,1)}, bf16[1024,32]{1,0:T(8,128)(2,1)}) custom-call(bf16[1024,2560]{1,0:T(8,128)(2,1)} %all-gather.14.cloned.1.call-done.tok_ref.refs_3_.refs_7_, bf16[1024,1920]{1,0:T(8,128)(2,1)} %get-tuple-element.78.refs_2_.gh_ref, ...), custom_call_target="tpu_custom_call" | custom-call | flops 20132659200 | bytes 39321600 | tf_op jit(solution)/shard_map/pallas_call | solution.py:326
  426.0 32.5 %shard_map.447 = (bf16[1024,2560]{1,0:T(8,128)(2,1)}, bf16[1024,32]{1,0:T(8,128)(2,1)}) custom-call(bf16[1024,1920]{1,0:T(8,128)(2,1)} %get-tuple-element.81.gg_ref.refs_3_, bf16[1024,1920]{1,0:T(8,128)(2,1)} %get-tuple-element.82.gu_ref.refs_7_, bf16[2560,1920]{1,0:T(8,128)(2,1)} %wg_ref.7, bf16[2560,1920]{1,0:T(8,128)(2,1)} %wu_ref.7, ...), custom_call_target="tpu_custom_call" | custom-call | flops 20132659200 | bytes 32768000 | tf_op jit(solution)/shard_map/pallas_call | solution.py:356
  460.9 32.6 %shard_map.448 = (bf16[2,1024,2560]{2,1,0:T(8,128)(2,1)}, bf16[2,1024,16]{2,1,0:T(8,128)(2,1)}) custom-call(bf16[1024,1920]{1,0:T(8,128)(2,1)} %get-tuple-element.79.refs_0_.refs_9_, bf16[1024,1920]{1,0:T(8,128)(2,1)} %get-tuple-element.80.refs_1_.refs_11_, bf16[1920,2560]{1,0:T(8,128)(2,1)} %refs_2_.3, bf16[32,1920]{1,0:T(8,128)(2,1)} %bitcast.208, ...), custom_call_target="tpu_custom_call" | custom-call | flops 20132659200 | bytes 28180480 | tf_op jit(solution)/shard_map/pallas_call | solution.py:390
  495.6 13.0 %shard_map.452.refs_1_ = bf16[96,1920]{1,0:T(8,128)(2,1)} custom-call(bf16[1024,32]{1,0:T(8,128)(2,1)} %get-tuple-element.91.refs_0_.refs_4_, bf16[1024,1920]{1,0:T(8,128)(2,1)} %get-tuple-element.85.gg_ref.refs_1_, bf16[1024,32]{1,0:T(8,128)(2,1)} %get-tuple-element.92.refs_2_.refs_6_, bf16[1024,1920]{1,0:T(8,128)(2,1)} %get-tuple-element.81.gg_ref.refs_3_, ...), custom_call_target="tpu_custom_call" | custom-call | flops 765460480 | bytes 23920640 | tf_op jit(solution)/shard_map/pallas_call | solution.py:738
  515.0 15.5 %shard_map.451.refs_0_.refs_13_ = bf16[96,2560]{1,0:T(8,128)(2,1)} custom-call(bf16[1024,32]{1,0:T(8,128)(2,1)} %get-tuple-element.88.refs_0_.refs_4_, bf16[1024,2560]{1,0:T(8,128)(2,1)} %all-gather.10.cloned.1.call-done.tok_ref.refs_1_.refs_5_, bf16[1024,32]{1,0:T(8,128)(2,1)} %get-tuple-element.89.refs_2_.refs_6_, ...), custom_call_target="tpu_custom_call" | custom-call | flops 1352663040 | bytes 42270720 | tf_op jit(solution)/shard_map/pallas_call | solution.py:738
  531.1 6.1 collective-permute-done.3
  540.3 5.3 shard_map.453
  547.7 11.3 %fusion.72 = f32[512,2560]{1,0:T(8,128)S(1)} fusion(bf16[512,2560]{1,0:T(8,128)(2,1)S(1)} %get-tuple-element.96.refs_12_, bf16[2560,2560]{1,0:T(8,128)(2,1)} %get-tuple-element.75), kind=kOutput, calls=%fused_computation.165 | convolution fusion | flops 6710886400 | bytes 20971520 | tf_op jit(solution)/shard_map/dot_general | solution.py:22
  563.4 21.4 %shard_map.454 = (f32[512,2560]{1,0:T(8,128)}, f32[512,2560]{1,0:T(8,128)}, f32[4,2560]{1,0:T(4,128)S(1)}, bf16[512,2560]{1,0:T(8,128)(2,1)S(1)}) custom-call(f32[512,2560]{1,0:T(8,128)} %bitcast.183, bf16[512,64]{1,0:T(8,128)(2,1)S(1)} %copy-done.21, bf16[64,2560]{1,0:T(8,128)(2,1)S(1)} %copy-done.12, bf16[10,256,256]{2,1,0:T(8,128)(2,1)S(1)} %copy-done.6, ...), custom_call_target="tpu_custom_call" | custom-call | flops 775946240 | bytes 39321600 | tf_op jit(solution)/shard_map/pallas_call | solution.py:157
  584.8 8.6 %all-gather.4 = f32[4,4,2560]{2,1,0:T(4,128)S(1)} all-gather(f32[1,4,2560]{2,1,0:T(4,128)S(1)} %bitcast.181), channel_id=3, replica_groups=mesh['group'=4,'replica'=8] {'group'}, dimensions={0}, use_global_device_ids=true | all-gather | bytes 204800 | tf_op jit(solution)/shard_map/all_gather | solution.py:894
  593.4 20.2 %shard_map.455 = (f32[512,2560]{1,0:T(8,128)}, f32[512,64]{1,0:T(8,128)S(1)}, f32[64,2560]{1,0:T(8,128)S(1)}) custom-call(f32[512,2560]{1,0:T(8,128)} %bitcast.184, bf16[512,64]{1,0:T(8,128)(2,1)S(1)} %copy-done.21, bf16[64,2560]{1,0:T(8,128)(2,1)S(1)} %copy-done.12, bf16[10,256,256]{2,1,0:T(8,128)(2,1)S(1)} %copy-done.6, ...), custom_call_target="tpu_custom_call" | custom-call | flops 2789212160 | bytes 31457280 | tf_op jit(solution)/shard_map/pallas_call | solution.py:233
  624.3 5.7 fusion.8
  634.0 5.2 shard_map.449.refs_14_
  639.2 9.3 %shard_map.457.refs_8_ = bf16[4,416,640]{2,1,0:T(8,128)(2,1)} custom-call(bf16[512,64]{1,0:T(8,128)(2,1)} %pad_maximum_fusion.4.refs_0_, bf16[512,2560]{1,0:T(8,128)(2,1)} %copy-done.30, bf16[512,64]{1,0:T(8,128)(2,1)} %copy-done.36, bf16[512,2560]{1,0:T(8,128)(2,1)} %copy-done.31, bf16[512,32]{1,0:T(8,128)(2,1)} %copy-done.40, ...), custom_call_target="tpu_custom_call" | custom-call | flops 537919488 | bytes 16809984 | tf_op jit(solution)/shard_map/pallas_call | solution.py:738
  648.6 12.3 %fusion.73 = f32[512,2560]{1,0:T(8,128)} fusion(bf16[512,2560]{1,0:T(8,128)(2,1)} %copy-done.13, bf16[2560,2560]{1,0:T(8,128)(2,1)} %get-tuple-element.74), kind=kOutput, calls=%fused_computation.166 | convolution fusion | flops 6710886400 | bytes 20971520 | tf_op jit(solution)/shard_map/dot_general | solution.py:22
  665.1 16.7 %add_add_fusion.grads_ref = f32[512,2560]{1,0:T(8,128)} fusion(f32[512,2560]{1,0:T(8,128)} %fusion.29, f32[512,2560]{1,0:T(8,128)} %fusion.73, bf16[512,2560]{1,0:T(8,128)(2,1)} %bitcast.193, bf16[2560,2560]{1,0:T(8,128)(2,1)} %get-tuple-element.70), kind=kOutput, calls=%fused_computation.33 | convolution fusion | flops 6713507840 | bytes 31457280 | tf_op jit(solution)/shard_map/dot_general | solution.py:22
  696.7 51.8 %all-gather.16.cloned.1.call-done = bf16[1664,640]{1,0:T(8,128)(2,1)} async-done(((bf16[416,640]{1,0:T(8,128)(2,1)}), bf16[1664,640]{1,0:T(8,128)(2,1)}) %all-gather.16.cloned.1.call-update) | async-done | bytes 2129936 | tf_op jit(solution)/shard_map/all_gather | solution.py:770
  754.3 4.8 shard_map.460
  (269 shorter events, 98.6 us)
Async XLA Ops:
  7.2 261.8 %all-gather.12.cloned.1.call-start = ((), (), s32[]{:S(2)}) async-start(), calls=%async_computation.5 | async-start | bytes 13107200 | tf_op jit(solution)/shard_map/all_gather | solution.py:803
  156.6 169.8 %all-gather.10.cloned.1.call-start = ((), (), s32[]{:S(2)}) async-start(), calls=%async_computation.4 | async-start | bytes 6553600 | tf_op jit(solution)/shard_map/all_gather | solution.py:859
  157.3 79.5 %copy-start.67 = (pred[32]{0:T(512)(128)(4,1)}, pred[32]{0:T(512)(128)(4,1)S(1)}, u32[]{:S(2)}) copy-start(pred[32]{0:T(512)(128)(4,1)S(1)} %compare_and_fusion) | copy-start | bytes 100
  157.3 79.5 %copy-start.69 = (pred[512]{0:T(512)(128)(4,1)}, pred[512]{0:T(512)(128)(4,1)S(1)}, u32[]{:S(2)}) copy-start(pred[512]{0:T(512)(128)(4,1)S(1)} %fusion.58) | copy-start | bytes 1540
  157.3 79.4 %copy-start.62 = (s32[512]{0:T(512)}, s32[512]{0:T(512)S(1)}, u32[]{:S(2)}) copy-start(s32[512]{0:T(512)S(1)} %get-tuple-element.159) | copy-start | bytes 6148
  157.4 79.4 %copy-start.64 = (s32[512]{0:T(512)}, s32[512]{0:T(512)S(1)}, u32[]{:S(2)}) copy-start(s32[512]{0:T(512)S(1)} %get-tuple-element.160) | copy-start | bytes 6148
  157.6 42.4 %copy-start.42 = (pred[512,32]{1,0:T(32,128)(4,1)}, pred[512,32]{1,0:T(32,128)(4,1)S(1)}, u32[]{:S(2)}) copy-start(pred[512,32]{1,0:T(32,128)(4,1)S(1)} %select_compare_fusion) | copy-start | bytes 49156
  160.4 70.3 %copy-start.34 = (bf16[512,64]{1,0:T(8,128)(2,1)}, bf16[512,64]{1,0:T(8,128)(2,1)S(1)}, u32[]{:S(2)}) copy-start(bf16[512,64]{1,0:T(8,128)(2,1)S(1)} %fusion.25) | copy-start | bytes 196612
  174.9 17.6 %collective-permute-start = (bf16[2,3,2560]{2,1,0:T(4,128)(2,1)}, bf16[2,3,2560]{2,1,0:T(4,128)(2,1)S(1)}, u32[]{:S(2)}, u32[]{:S(2)}) collective-permute-start(bf16[2,3,2560]{2,1,0:T(4,128)(2,1)} %slice.328), channel_id=1, source_target_pairs={{0,8},{8,16},{16,24},{1,9},{9,17},{17,25},{2,10},{10,18},{18,26},{... | collective-permute-start | bytes 92168 | tf_op jit(solution)/shard_map/ppermute | solution.py:756
  177.5 17.6 %copy-start.56 = (f32[2,256]{1,0:T(2,128)}, f32[2,256]{1,0:T(2,128)S(1)}, u32[]{:S(2)}) copy-start(f32[2,256]{1,0:T(2,128)S(1)} %slice_convert_fusion.1) | copy-start | bytes 6148
  200.1 20.6 %copy-start.31 = (bf16[512,2560]{1,0:T(8,128)(2,1)}, bf16[512,2560]{1,0:T(8,128)(2,1)S(1)}, u32[]{:S(2)}) copy-start(bf16[512,2560]{1,0:T(8,128)(2,1)S(1)} %bitcast_convert_fusion.refs_3_) | copy-start | bytes 7864324
  203.4 17.3 %copy-start.20 = (bf16[512,64]{1,0:T(8,128)(2,1)}, bf16[512,64]{1,0:T(8,128)(2,1)S(1)}, u32[]{:S(2)}) copy-start(bf16[512,64]{1,0:T(8,128)(2,1)S(1)} %fusion.26.inner_ref) | copy-start | bytes 196612
  251.6 16.7 %copy-start.38 = (bf16[3,2,16,1920]{3,2,1,0:T(8,128)(2,1)S(1)}, bf16[3,2,16,1920]{3,2,1,0:T(8,128)(2,1)}, u32[]{:S(2)}) copy-start(bf16[3,2,16,1920]{3,2,1,0:T(8,128)(2,1)} %get-tuple-element.76) | copy-start | bytes 1105924
  254.1 139.2 %all-gather.14.cloned.1.call-start = ((), (), s32[]{:S(2)}) async-start(), calls=%async_computation.6 | async-start | bytes 6553600 | tf_op jit(solution)/shard_map/all_gather | solution.py:859
  254.8 282.9 %reduce-scatter.9.cloned.1.call-start = ((), (), s32[]{:S(2)}) async-start(), calls=%async_computation.8 | async-start | bytes 6553600 | tf_op jit(solution)/shard_map/reduce_scatter | solution.py:869
  392.4 145.4 %reduce-scatter.11.cloned.1.call-start = ((), (), s32[]{:S(2)}) async-start(), calls=%async_computation.9 | async-start | bytes 6553600 | tf_op jit(solution)/shard_map/reduce_scatter | solution.py:869
  458.6 175.4 %reduce-scatter.7.cloned.1.call-start = ((), (), s32[]{:S(2)}) async-start(), calls=%async_computation.7 | async-start | bytes 13107200 | tf_op jit(solution)/shard_map/reduce_scatter | solution.py:885
  493.5 201.4 %reduce-scatter.13.cloned.1.call-start = ((), (), s32[]{:S(2)}) async-start(), calls=%async_computation.11 | async-start | bytes 2662400
  495.6 18.6 %copy-start.41 = (bf16[2,1024,16]{2,1,0:T(8,128)(2,1)S(1)}, bf16[2,1024,16]{2,1,0:T(8,128)(2,1)}, u32[]{:S(2)}) copy-start(bf16[2,1024,16]{2,1,0:T(8,128)(2,1)} %get-tuple-element.90) | copy-start | bytes 196612
  508.6 21.9 %collective-permute-start.2 = (bf16[96,1920]{1,0:T(8,128)(2,1)}, bf16[96,1920]{1,0:T(8,128)(2,1)}, u32[]{:S(2)}, u32[]{:S(2)}) collective-permute-start(bf16[96,1920]{1,0:T(8,128)(2,1)} %shard_map.452.refs_1_), channel_id=1, source_target_pairs={{0,2},{1,3},{2,4},{3,5},{4,6},{5,7},{6,0},{7,1},{8,10},{9,11},{10,... | collective-permute-start | bytes 1105928 | tf_op jit(solution)/shard_map/ppermute | solution.py:766
  510.3 26.9 %collective-permute-start.3 = (bf16[96,1920]{1,0:T(8,128)(2,1)}, bf16[96,1920]{1,0:T(8,128)(2,1)}, u32[]{:S(2)}, u32[]{:S(2)}) collective-permute-start(bf16[96,1920]{1,0:T(8,128)(2,1)} %shard_map.452.refs_1_), channel_id=1, source_target_pairs={{0,4},{1,5},{2,6},{3,7},{4,0},{5,1},{6,2},{7,3},{8,12},{9,13},{10,... | collective-permute-start | bytes 1105928 | tf_op jit(solution)/shard_map/ppermute | solution.py:766
  512.7 24.5 %collective-permute-start.4 = (bf16[96,1920]{1,0:T(8,128)(2,1)}, bf16[96,1920]{1,0:T(8,128)(2,1)}, u32[]{:S(2)}, u32[]{:S(2)}) collective-permute-start(bf16[96,1920]{1,0:T(8,128)(2,1)} %shard_map.452.refs_1_), channel_id=1, source_target_pairs={{0,6},{1,7},{2,0},{3,1},{4,2},{5,3},{6,4},{7,5},{8,14},{9,15},{10,... | collective-permute-start | bytes 1105928 | tf_op jit(solution)/shard_map/ppermute | solution.py:766
  514.1 125.0 %collective-permute-start.5 = (bf16[1,96,1920]{2,1,0:T(8,128)(2,1)}, bf16[1,96,1920]{2,1,0:T(8,128)(2,1)}, u32[]{:S(2)}, u32[]{:S(2)}) collective-permute-start(bf16[1,96,1920]{2,1,0:T(8,128)(2,1)} %bitcast.175), channel_id=1, source_target_pairs={{0,1},{1,0},{2,3},{3,2},{4,5},{5,4},{6,7},{7,6},{8,9},{9,8},{10,11... | collective-permute-start | bytes 1105928 | tf_op jit(solution)/shard_map/ppermute | solution.py:772
  530.5 108.7 %collective-permute-start.6 = (bf16[1,96,1920]{2,1,0:T(8,128)(2,1)}, bf16[1,96,1920]{2,1,0:T(8,128)(2,1)}, u32[]{:S(2)}, u32[]{:S(2)}) collective-permute-start(bf16[1,96,1920]{2,1,0:T(8,128)(2,1)} %bitcast.46.refs_16_.refs_1_), channel_id=1, source_target_pairs={{0,1},{1,0},{2,3},{3,2},{4,5},{5,4},{6,7},{7,6},{8,9},{9,8},{10,11... | collective-permute-start | bytes 1105928 | tf_op jit(solution)/shard_map/ppermute | solution.py:772
  537.2 102.0 %collective-permute-start.7 = (bf16[1,96,1920]{2,1,0:T(8,128)(2,1)}, bf16[1,96,1920]{2,1,0:T(8,128)(2,1)}, u32[]{:S(2)}, u32[]{:S(2)}) collective-permute-start(bf16[1,96,1920]{2,1,0:T(8,128)(2,1)} %bitcast.47.refs_17_.refs_2_), channel_id=1, source_target_pairs={{0,1},{1,0},{2,3},{3,2},{4,5},{5,4},{6,7},{7,6},{8,9},{9,8},{10,11... | collective-permute-start | bytes 1105928 | tf_op jit(solution)/shard_map/ppermute | solution.py:772
  537.3 102.0 %collective-permute-start.8 = (bf16[1,96,1920]{2,1,0:T(8,128)(2,1)}, bf16[1,96,1920]{2,1,0:T(8,128)(2,1)}, u32[]{:S(2)}, u32[]{:S(2)}) collective-permute-start(bf16[1,96,1920]{2,1,0:T(8,128)(2,1)} %bitcast.48.refs_18_.refs_3_), channel_id=1, source_target_pairs={{0,1},{1,0},{2,3},{3,2},{4,5},{5,4},{6,7},{7,6},{8,9},{9,8},{10,11... | collective-permute-start | bytes 1105928 | tf_op jit(solution)/shard_map/ppermute | solution.py:772
  563.4 30.0 %copy-start.18 = (bf16[10,256,256]{2,1,0:T(8,128)(2,1)S(1)}, bf16[10,256,256]{2,1,0:T(8,128)(2,1)}, u32[]{:S(2)}) copy-start(bf16[10,256,256]{2,1,0:T(8,128)(2,1)} %table_a_ref.3) | copy-start | bytes 3932164
  584.8 34.3 %copy-start.13 = (bf16[512,2560]{1,0:T(8,128)(2,1)}, bf16[512,2560]{1,0:T(8,128)(2,1)S(1)}, u32[]{:S(2)}) copy-start(bf16[512,2560]{1,0:T(8,128)(2,1)S(1)} %get-tuple-element.97.refs_7_) | copy-start | bytes 7864324
  593.4 20.2 %copy-start.43 = (pred[512,32]{1,0:T(32,128)(4,1)S(1)}, pred[512,32]{1,0:T(32,128)(4,1)}, u32[]{:S(2)}) copy-start(pred[512,32]{1,0:T(32,128)(4,1)} %copy-done.42) | copy-start | bytes 49156
  617.5 6.7 collective-permute-start.1
  648.6 100.0 %all-gather.16.cloned.1.call-start = ((), (), s32[]{:S(2)}) async-start(), calls=%async_computation.10 | async-start | bytes 2662400 | tf_op jit(solution)/shard_map/all_gather | solution.py:770
  748.6 4.4 collective-permute-start.9
  (65 other events, 470.2 us)
Sparse Core Ops, SparseCore 0:
  156.7 106.3 all-gather.11
  264.9 61.4 all-gather.9
  328.8 61.4 all-gather.13
  393.1 61.4 reduce-scatter.8
  458.7 61.4 reduce-scatter.10
  523.2 104.2 reduce-scatter.6
  648.7 40.9 reduce-scatter.12
  696.9 51.6 all-gather.15

commit v4 on v3

--- a/solution.py
+++ b/solution.py
@@ -27,10 +27,10 @@
 
 
 def gelu_both(v):
-    th = jnp.tanh(GELU_C * (v + GELU_A * v * v * v))
-    value = 0.5 * v * (1.0 + th)
-    slope = 0.5 * (1.0 + th) + 0.5 * v * (1.0 - th * th) * GELU_C * (1.0 + 3.0 * GELU_A * v * v)
-    return value, slope
+    square = v * v
+    half = 0.5 + 0.5 * jnp.tanh(v * (GELU_C + GELU_C * GELU_A * square))
+    value = v * half
+    return value, half + (value - value * half) * (2.0 * GELU_C + 6.0 * GELU_C * GELU_A * square)
 
 
 def norm_rows(values, gain):
@@ -262,6 +262,200 @@
     )(conv, inner, lift, table_d, table_a, softrate, restart, cum, local, carried, span, total, incoming)
 
 
+def sequence_mask(rows, cols, seqs):
+    row = lax.broadcasted_iota(jnp.int32, (rows, cols), 0) // (rows // seqs)
+    col = lax.broadcasted_iota(jnp.int32, (rows, cols), 1) % (cols // 2) // (cols // 2 // seqs)
+    return (row == col).astype(F32)
+
+
+def mixer_back_kernel(
+    seqs, heads, mixed_ref, w_ref, thr_mixer_ref, down_mixer_ref, conv_ref, inner_ref, lift_ref, table_d_ref,
+    table_a_ref, soft_ref, restart_ref, cum_ref, local_ref, carried_ref, pre_ref, lift_branch_ref, lift_input_ref,
+    down_gates_ref, taps_ref, agree_ref,
+    branch_grad_ref, through_one_ref, through_gates_ref, lift_grad_ref, fed_grad_ref,
+    span_ref, total_ref, ends_ref, all_ends_ref, incoming_ref, halo_ref, below_ref, one_ref, gates_ref, send, recv,
+):
+    rows, size = conv_ref.shape
+    stretch = rows // seqs
+    half = lift_ref.shape[0] // 2
+    ranks = lift_branch_ref.shape[0]
+    step = pl.program_id(0)
+    group, replica = lax.axis_index("group"), lax.axis_index("replica")
+    partners = [(group + 1 - 2 * (group % 2), replica), ((group + 2) % 4, replica), (3 - group, replica)]
+
+    def copy(src, dst, slot, partner):
+        return pltpu.make_async_remote_copy(
+            src_ref=src, dst_ref=dst, send_sem=send.at[slot], recv_sem=recv.at[slot], device_id=partner,
+            device_id_type=pl.DeviceIdType.MESH)
+
+    exchange = [copy(ends_ref, all_ends_ref.at[group], slot, partner) for slot, partner in enumerate(partners)]
+    downward = copy(halo_ref, below_ref, 3, ((group + 3) % 4, replica))
+
+    @pl.when(step == 0)
+    def _():
+        barrier = pltpu.get_barrier_semaphore()
+        for partner in partners:
+            pl.semaphore_signal(barrier, inc=1, device_id=partner, device_id_type=pl.DeviceIdType.MESH)
+        pl.semaphore_wait(barrier, 3)
+        one_ref[...] = jnp.zeros_like(one_ref)
+        gates_ref[...] = jnp.zeros_like(gates_ref)
+        ends_ref[...] = jnp.zeros_like(ends_ref)
+
+    @pl.when(step < heads)
+    def _():
+        cols = pl.ds(pl.multiple_of(step * size, size), size)
+        merged = dot(mixed_ref[...], w_ref[...], NT) + dot(thr_mixer_ref[...], down_mixer_ref[...])
+        for s in range(seqs):
+            at = slice(s * stretch, (s + 1) * stretch)
+            restart = restart_ref[at, :] > 0.5
+            rounded = conv_ref[at, :].astype(BF16)
+            pre_d = dot(rounded, table_d_ref[0]) + dot(inner_ref[at, :half], lift_ref[:half, :])
+            grown = jnp.exp(-8.0 * soft_ref[...] / (1.0 + jnp.exp(-pre_d)))
+            decays = jnp.where(restart, 0.0, grown)
+            state = local_ref[at, :] + cum_ref[at, :] * carried_ref[s : s + 1, :]
+            value, slope = gelu_both(pre_ref[at, :])
+            grads = merged[at, :]
+            low = (grads * state * slope).astype(BF16)
+            branch_grad_ref[at, :] = low
+            one_ref[at, :ranks] += dot(low, lift_branch_ref[...], NT)
+            span, total = scan_rows(rows_advanced(decays, 1, 1.0), grads * value, rows_advanced)
+            span_ref[step, at, :] = span
+            total_ref[step, at, :] = total
+            ends_ref[s : s + 1, cols] = decays[:1] * span[:1]
+            ends_ref[seqs + s : seqs + s + 1, cols] = decays[:1] * total[:1]
+
+    @pl.when(step == heads - 1)
+    def _():
+        for one in exchange:
+            one.start()
+
+    @pl.when(step == heads)
+    def _():
+        for one in exchange:
+            one.wait_recv()
+        incoming = jnp.zeros(incoming_ref.shape, F32)
+        for g in (3, 2, 1):
+            longer = all_ends_ref[g, :seqs, :] * incoming + all_ends_ref[g, seqs : 2 * seqs, :]
+            incoming = jnp.where(group < g, longer, incoming)
+        incoming_ref[...] = incoming
+
+    @pl.when((step >= heads) & (step < 2 * heads))
+    def _():
+        head = step - heads
+        cols = pl.ds(pl.multiple_of(head * size, size), size)
+        softrate = soft_ref[...]
+        for s in range(seqs):
+            at = slice(s * stretch, (s + 1) * stretch)
+            conv, inner = conv_ref[at, :], inner_ref[at, :]
+            restart = restart_ref[at, :] > 0.5
+            decay_gate, admit, grown, scale = gate_values(
+                conv, inner, lift_ref[...], table_d_ref[0], table_a_ref[0], softrate, restart)
+            carried = carried_ref[s : s + 1, :]
+            state = local_ref[at, :] + cum_ref[at, :] * carried
+            place = lax.broadcasted_iota(jnp.int32, state.shape, 0)
+            before = jnp.where(place >= 1, pltpu.roll(state, 1, 0), carried)
+            grads = total_ref[head, at, :] + span_ref[head, at, :] * incoming_ref[s : s + 1, cols]
+            driven = grads * jnp.where(restart, 1.0, scale)
+            grad_log = jnp.where(
+                restart, 0.0, grads * (before * grown - conv * admit * grown * grown / scale))
+            grad_d = (-8.0 * softrate) * grad_log * decay_gate * (1.0 - decay_gate)
+            grad_a = driven * conv * admit * (1.0 - admit)
+            low_d, low_a = grad_d.astype(BF16), grad_a.astype(BF16)
+            total_ref[head, at, :] = (
+                driven * admit + dot(low_d, table_d_ref[0], NT) + dot(low_a, table_a_ref[0], NT))
+            gates_ref[at, :half] += dot(low_d, lift_ref[:half, :], NT)
+            gates_ref[at, half:] += dot(low_a, lift_ref[half:, :], NT)
+            first = dot(inner[:, :half], low_d, TN)
+            second = dot(inner[:, half:], low_a, TN)
+            if s == 0:
+                lift_grad_ref[:half, :] = first
+                lift_grad_ref[half:, :] = second
+            else:
+                lift_grad_ref[:half, :] += first
+                lift_grad_ref[half:, :] += second
+
+    @pl.when(step == 2 * heads)
+    def _():
+        through_gates_ref[...] = (gates_ref[...] * sequence_mask(rows, 2 * half, seqs)).astype(BF16)
+        tops = []
+        for s in range(seqs):
+            top = slice(s * stretch, s * stretch + 8)
+            direct = jnp.concatenate([total_ref[h, top, :] for h in range(heads)], 1)
+            tops.append(direct + dot(through_gates_ref[top, :], down_gates_ref[...]))
+        halo_ref[...] = jnp.concatenate(tops, 0).astype(BF16)
+        downward.start()
+        downward.wait_recv()
+
+    @pl.when(step >= 2 * heads)
+    def _():
+        head = step - 2 * heads
+        cols = pl.ds(pl.multiple_of(head * size, size), size)
+        grads = total_ref[head] + dot(through_gates_ref[...], down_gates_ref[:, cols])
+        for s in range(seqs):
+            at = slice(s * stretch, (s + 1) * stretch)
+            longer = jnp.concatenate([grads[at, :], below_ref[s * 8 : (s + 1) * 8, cols].astype(F32)], 0)
+            total = taps_ref[0:1, :] * agree_ref[at, 0:1] * grads[at, :]
+            for j in range(1, taps_ref.shape[0]):
+                moved = pltpu.roll(longer, stretch + 8 - j, 0)[:stretch]
+                total += taps_ref[j : j + 1, :] * agree_ref[at, j : j + 1] * moved
+            low = total.astype(BF16)
+            fed_grad_ref[at, :] = low
+            one_ref[at, ranks:] += dot(low, lift_input_ref[...], NT)
+
+    @pl.when(step == 3 * heads - 1)
+    def _():
+        through_one_ref[...] = (one_ref[...] * sequence_mask(rows, 2 * ranks, seqs)).astype(BF16)
+        for one in exchange:
+            one.wait_send()
+        downward.wait_send()
+
+
+def mixer_back(seqs, mixed, w_mixer, thr_mixer, down_mixer, conv, inner, lift, table_d, table_a, softrate, restart,
+               cum, local, carried, pre, lift_branch, lift_input, down_gates, taps, agree):
+    rows, width = conv.shape
+    heads, size = table_d.shape[:2]
+    first = lambda i: jnp.minimum(i, heads - 1)
+    second = lambda i: jnp.clip(i - heads, 0, heads - 1)
+    third = lambda i: jnp.maximum(i - 2 * heads, 0)
+    either = lambda i: jnp.minimum(i, 2 * heads - 1) % heads
+    full = lambda array: pl.BlockSpec(array.shape, lambda i: (0, 0), pipeline_mode=pl.Buffered(1))
+    cols = lambda array, at: pl.BlockSpec((array.shape[0], size), lambda i: (0, at(i)))
+    table = pl.BlockSpec((1, size, size), lambda i: (either(i), 0, 0))
+    middle = inner.shape[1]
+    tile = lambda at: pl.BlockSpec((rows, size), lambda i: (0, at(i)))
+    whole = lambda count: pl.BlockSpec((rows, count), lambda i: (0, 0))
+    return pl.pallas_call(
+        functools.partial(mixer_back_kernel, seqs, heads),
+        grid=(3 * heads,),
+        out_shape=[
+            jax.ShapeDtypeStruct((rows, width), BF16),
+            jax.ShapeDtypeStruct((rows, 2 * lift_branch.shape[0]), BF16),
+            jax.ShapeDtypeStruct((rows, middle), BF16),
+            jax.ShapeDtypeStruct(lift.shape, F32),
+            jax.ShapeDtypeStruct((rows, width), BF16),
+        ],
+        in_specs=[
+            full(mixed), pl.BlockSpec((size, width), lambda i: (first(i), 0)), full(thr_mixer), cols(down_mixer, first),
+            cols(conv, either), full(inner), cols(lift, either), table, table, cols(softrate, either), full(restart),
+            cols(cum, either), cols(local, either), cols(carried, either), cols(pre, first), cols(lift_branch, first),
+            cols(lift_input, third), full(down_gates), cols(taps, third), full(agree),
+        ],
+        out_specs=[tile(first), whole(2 * lift_branch.shape[0]), whole(middle),
+                   pl.BlockSpec((lift.shape[0], size), lambda i: (0, second(i))), tile(third)],
+        scratch_shapes=[
+            pltpu.VMEM((heads, rows, size), F32), pltpu.VMEM((heads, rows, size), F32), pltpu.VMEM((8, width), F32),
+            pltpu.VMEM((4, 8, width), F32), pltpu.VMEM((seqs, width), F32), pltpu.VMEM((8 * seqs, width), BF16),
+            pltpu.VMEM((8 * seqs, width), BF16), pltpu.VMEM((rows, 2 * lift_branch.shape[0]), F32),
+            pltpu.VMEM((rows, middle), F32), pltpu.SemaphoreType.DMA((4,)), pltpu.SemaphoreType.DMA((4,))],
+        compiler_params=pltpu.CompilerParams(
+            vmem_limit_bytes=60 * 2**20, collective_id=3, has_side_effects=True),
+        cost_estimate=pl.CostEstimate(
+            flops=2 * rows * width * width + 20 * rows * width * size + 200 * rows * width,
+            bytes_accessed=40 * rows * width + 2 * width * width, transcendentals=12 * rows * width),
+    )(mixed, w_mixer, thr_mixer, down_mixer, conv, inner, lift, table_d, table_a, softrate, restart, cum, local,
+      carried, pre, lift_branch, lift_input, down_gates, taps, agree)
+
+
 def resident(array):
     return pl.BlockSpec(array.shape, lambda i: (0, 0), pipeline_mode=pl.Buffered(1))
 
@@ -270,109 +464,225 @@
     return tile if count % 128 == 0 and count > tile else count
 
 
-def grad_hidden_kernel(cot_ref, wd_ref, lift_out_ref, do_ref, out_ref, through_ref):
-    @pl.when(pl.program_id(0) == 0)
-    def _():
-        through_ref[...] = dot(cot_ref[...], lift_out_ref[...], NT).astype(BF16)
-
-    out_ref[...] = (dot(cot_ref[...], wd_ref[...], NT) + dot(through_ref[...], do_ref[...])).astype(BF16)
-
-
-def grad_hidden_call(cot, s, wd, lift_out, do):
-    rows, width = cot.shape[1:]
-    units, ranks = wd.shape[0], do.shape[0]
+def grad_hidden_kernel(seqs, gather, steps, *refs):
+    if gather:
+        cot_ref, wd_ref, lift_out_ref, do_ref, block_ref, out_ref, through_ref, all_ref = refs[:8]
+        staged_ref, send, recv, local = refs[8:]
+    else:
+        cot_ref, wd_ref, lift_out_ref, do_ref, out_ref, through_ref = refs
+    ranks = do_ref.shape[0] // seqs
+    step = pl.program_id(0)
+
+    if gather:
+        group, replica = lax.axis_index("group"), lax.axis_index("replica")
+        beside, above = group + 1 - 2 * (group % 2), (group + 2) % 4
+        at_beside, at_above = (beside, replica), (above, replica)
+        rows = block_ref.shape[0]
+        half = rows // 2
+
+        def place(owner, part):
+            return all_ref.at[pl.ds(pl.multiple_of(owner * rows + part * half, half), half), :]
+
+        def own(part):
+            return block_ref.at[pl.ds(part * half, half), :]
+
+        def copy(src, dst, slot, partner):
+            return pltpu.make_async_remote_copy(
+                src_ref=src, dst_ref=dst, send_sem=send.at[slot], recv_sem=recv.at[slot], device_id=partner,
+                device_id_type=pl.DeviceIdType.MESH)
+
+        firsts = [copy(own(1), place(group, 1), 0, at_beside), copy(own(0), place(group, 0), 1, at_above),
+                  copy(own(0), place(group, 0), 2, at_beside), copy(own(1), place(group, 1), 3, at_above)]
+        seconds = [copy(place(beside, 1), place(beside, 1), 4, at_above),
+                   copy(place(above, 0), place(above, 0), 5, at_beside)]
+        stage = pltpu.make_async_copy(block_ref, staged_ref, local.at[0])
+        keep = pltpu.make_async_copy(
+            staged_ref, all_ref.at[pl.ds(pl.multiple_of(group * rows, rows), rows), :], local.at[1])
+
+        @pl.when(step == 0)
+        def _():
+            barrier = pltpu.get_barrier_semaphore()
+            for partner in (at_beside, at_above):
+                pl.semaphore_signal(barrier, inc=1, device_id=partner, device_id_type=pl.DeviceIdType.MESH)
+            pl.semaphore_wait(barrier, 2)
+            for one in firsts[:2]:
+                one.start()
+            stage.start()
+
+    @pl.when(step == 0)
+    def _():
+        for s in range(seqs):
+            through_ref[s] = dot(cot_ref[s], lift_out_ref[s * ranks : (s + 1) * ranks, :], NT).astype(BF16)
+
+    for s in range(seqs):
+        out_ref[s] = (dot(cot_ref[s], wd_ref[...], NT)
+                      + dot(through_ref[s], do_ref[s * ranks : (s + 1) * ranks, :])).astype(BF16)
+
+    if gather:
+        @pl.when(step == 0)
+        def _():
+            stage.wait()
+            keep.start()
+            for one in firsts[2:]:
+                one.start()
+
+        @pl.when(step == min(1, steps - 1))
+        def _():
+            for one, then in zip(firsts[:2], seconds):
+                one.wait_recv()
+                then.start()
+
+        @pl.when(step == steps - 1)
+        def _():
+            for one in firsts[2:] + seconds:
+                one.wait_recv()
+            for one in firsts + seconds:
+                one.wait_send()
+            keep.wait()
+
+
+def grad_hidden_call(cot, wd, lift_out, do, block):
+    seqs, rows, width = cot.shape
+    units, ranks = wd.shape[0], do.shape[0] // seqs
     tile = tile_of(units, 512)
-    return pl.pallas_call(
-        grad_hidden_kernel,
+    gather = lax.axis_size("group") == 4
+    got = pl.pallas_call(
+        functools.partial(grad_hidden_kernel, seqs, gather, pl.cdiv(units, tile)),
         grid=(pl.cdiv(units, tile),),
-        out_shape=[jax.ShapeDtypeStruct((rows, units), BF16), jax.ShapeDtypeStruct((rows, ranks), BF16)],
-        in_specs=[pl.BlockSpec((None, rows, width), lambda i: (s, 0, 0), pipeline_mode=pl.Buffered(1)),
+        out_shape=[jax.ShapeDtypeStruct((seqs, rows, units), BF16), jax.ShapeDtypeStruct((seqs, rows, ranks), BF16)]
+        + [jax.ShapeDtypeStruct((rows, width), BF16)] * gather,
+        in_specs=[pl.BlockSpec(cot.shape, lambda i: (0, 0, 0), pipeline_mode=pl.Buffered(1)),
                   pl.BlockSpec((tile, width), lambda i: (i, 0)), resident(lift_out),
-                  pl.BlockSpec((ranks, tile), lambda i: (0, i))],
-        out_specs=[pl.BlockSpec((rows, tile), lambda i: (0, i)), pl.BlockSpec((rows, ranks), lambda i: (0, 0))],
-        compiler_params=pltpu.CompilerParams(vmem_limit_bytes=60 * 2**20),
+                  pl.BlockSpec((seqs * ranks, tile), lambda i: (0, i))] + [ANYWHERE] * gather,
+        out_specs=[pl.BlockSpec((seqs, rows, tile), lambda i: (0, 0, i)),
+                   pl.BlockSpec((seqs, rows, ranks), lambda i: (0, 0, 0))] + [ANYWHERE] * gather,
+        scratch_shapes=[pltpu.VMEM(block.shape, BF16), pltpu.SemaphoreType.DMA((6,)), pltpu.SemaphoreType.DMA((6,)),
+                        pltpu.SemaphoreType.DMA((2,))] if gather else [],
+        compiler_params=pltpu.CompilerParams(
+            vmem_limit_bytes=60 * 2**20, **(dict(collective_id=1, has_side_effects=True) if gather else {})),
         cost_estimate=pl.CostEstimate(
-            flops=2 * rows * width * units, bytes_accessed=2 * width * units + 2 * rows * (units + width),
-            transcendentals=0),
-    )(cot, wd, lift_out, do)
-
-
-def hidden_kernel(tok_ref, gh_ref, wg_ref, wu_ref, down_ref, lg_ref, lu_ref, *refs):
-    hidden_ref, gg_ref, gu_ref, inner_ref = refs[-4:]
+            flops=2 * seqs * rows * width * units,
+            bytes_accessed=2 * width * units + 2 * seqs * rows * (units + width), transcendentals=0),
+    )(cot, wd, lift_out, do, *([block] if gather else []))
+    return got if gather else list(got) + [lax.all_gather(block, "group", axis=0, tiled=True)]
+
+
+def feed_kernel(steps, tile, units, tok_ref, gh_ref, wg_ref, wu_ref, wg_rows_ref, wu_rows_ref, down_ref, lg_ref,
+                lu_ref, through_out_ref, lg_full_ref, lu_full_ref, down_cols_ref, *refs):
+    hidden_ref, back_ref, wide_ref, through_ref, inner_ref, gg_ref, gu_ref = refs[-7:]
     ranks = lg_ref.shape[0]
-
-    @pl.when(pl.program_id(0) == 0)
+    step = pl.program_id(0)
+
+    @pl.when(step == 0)
     def _():
         inner_ref[...] = dot(tok_ref[...], down_ref[...], NT).astype(BF16)
 
-    tokens, inner = tok_ref[...], inner_ref[...]
-    gate = dot(tokens, wg_ref[...]) + dot(inner[:, :ranks], lg_ref[...])
-    upper = dot(tokens, wu_ref[...]) + dot(inner[:, ranks:], lu_ref[...])
-    grad_hidden = gh_ref[...].astype(F32)
-    value, slope = gelu_both(gate)
-    hidden_ref[...] = (value * upper).astype(BF16)
-    gg_ref[...] = (grad_hidden * upper * slope).astype(BF16)
-    gu_ref[...] = (grad_hidden * value).astype(BF16)
-
-
-def hidden_call(tok, gh, wg, wu, down, lg, lu, earlier):
+    @pl.when(step < steps)
+    def _():
+        tokens, inner = tok_ref[...], inner_ref[...]
+        gate = dot(tokens, wg_ref[...]) + dot(inner[:, :ranks], lg_ref[...])
+        upper = dot(tokens, wu_ref[...]) + dot(inner[:, ranks:], lu_ref[...])
+        grad_hidden = gh_ref[...].astype(F32)
+        value, slope = gelu_both(gate)
+        hidden = (value * upper).astype(BF16)
+        grad_gate = (grad_hidden * upper * slope).astype(BF16)
+        grad_upper = (grad_hidden * value).astype(BF16)
+        hidden_ref[...] = hidden
+        cols = pl.ds(pl.multiple_of(step * tile, tile), tile) if steps > 1 else slice(0, tile)
+        gg_ref[:, cols] = grad_gate
+        gu_ref[:, cols] = grad_upper
+        wide_ref[:ranks, :] = dot(inner[:, :ranks], grad_gate, TN).astype(BF16)
+        wide_ref[ranks : 2 * ranks, :] = dot(inner[:, ranks:], grad_upper, TN).astype(BF16)
+        wide_ref[2 * ranks :, :] = dot(through_out_ref[...], hidden, TN).astype(BF16)
+
+    @pl.when(step == steps)
+    def _():
+        through_ref[:, :ranks] = dot(gg_ref[:, :units], lg_full_ref[...], NT).astype(BF16)
+        through_ref[:, ranks:] = dot(gu_ref[:, :units], lu_full_ref[...], NT).astype(BF16)
+
+    @pl.when(step >= steps)
+    def _():
+        back_ref[...] = (dot(gg_ref[:, :units], wg_rows_ref[...], NT) + dot(gu_ref[:, :units], wu_rows_ref[...], NT)
+                         + dot(through_ref[...], down_cols_ref[...])).astype(BF16)
+
+
+def feed_call(s, tok, gh, wg, wu, down, lg, lu, through_out):
     rows, width = tok.shape
     units, ranks = wg.shape[1], lg.shape[0]
-    tile = tile_of(units, 512)
-    cols = pl.BlockSpec((width, tile), lambda i: (0, i))
-    rank = pl.BlockSpec((ranks, tile), lambda i: (0, i))
-    out = pl.BlockSpec((rows, tile), lambda i: (0, i))
-    wide = jax.ShapeDtypeStruct((rows, units), BF16)
+    tile, span = tile_of(units, 512), tile_of(width, 512)
+    steps, laps = pl.cdiv(units, tile), pl.cdiv(width, span)
+    first = lambda i: jnp.minimum(i, steps - 1)
+    second = lambda i: jnp.maximum(i - steps, 0)
+    cols = pl.BlockSpec((width, tile), lambda i: (0, first(i)))
+    across = pl.BlockSpec((span, units), lambda i: (second(i), 0))
+    rank = pl.BlockSpec((ranks, tile), lambda i: (0, first(i)))
+    out = pl.BlockSpec((rows, tile), lambda i: (0, first(i)))
     return pl.pallas_call(
-        hidden_kernel,
-        grid=(pl.cdiv(units, tile),),
-        out_shape=[wide, wide, wide, jax.ShapeDtypeStruct((rows, 2 * ranks), BF16)],
-        in_specs=[resident(tok), out, cols, cols, resident(down), rank, rank] + [ANYWHERE] * len(earlier),
-        out_specs=[out, out, out, pl.BlockSpec((rows, 2 * ranks), lambda i: (0, 0))],
-        compiler_params=pltpu.CompilerParams(vmem_limit_bytes=60 * 2**20),
+        functools.partial(feed_kernel, steps, tile, units),
+        grid=(steps + laps,),
+        out_shape=[jax.ShapeDtypeStruct((rows, units), BF16), jax.ShapeDtypeStruct((rows, width), BF16),
+                   jax.ShapeDtypeStruct((3 * ranks, units), BF16), jax.ShapeDtypeStruct((rows, 2 * ranks), BF16)],
+        in_specs=[resident(tok), pl.BlockSpec((None, rows, tile), lambda i: (s, 0, first(i))), cols, cols, across,
+                  across, resident(down), rank, rank, pl.BlockSpec((None, rows, ranks), lambda i: (s, 0, 0)),
+                  resident(lg), resident(lu), pl.BlockSpec((2 * ranks, span), lambda i: (0, second(i)))],
+        out_specs=[out, pl.BlockSpec((rows, span), lambda i: (0, second(i))),
+                   pl.BlockSpec((3 * ranks, tile), lambda i: (0, first(i))),
+                   pl.BlockSpec((rows, 2 * ranks), lambda i: (0, 0))],
+        scratch_shapes=[pltpu.VMEM((rows, 2 * ranks), BF16), pltpu.VMEM((rows, steps * tile), BF16),
+                        pltpu.VMEM((rows, steps * tile), BF16)],
+        compiler_params=pltpu.CompilerParams(vmem_limit_bytes=62 * 2**20),
         cost_estimate=pl.CostEstimate(
-            flops=4 * rows * width * units, bytes_accessed=4 * width * units + 10 * rows * units,
+            flops=8 * rows * width * units, bytes_accessed=8 * width * units + 6 * rows * units,
             transcendentals=rows * units),
-    )(tok, gh, wg, wu, down, lg, lu, *earlier)
-
-
-def back_kernel(gg_ref, gu_ref, wg_ref, wu_ref, lg_ref, lu_ref, down_ref, back_ref, through_ref):
-    ranks = lg_ref.shape[0]
-
-    @pl.when(pl.program_id(0) == 0)
-    def _():
-        through_ref[:, :ranks] = dot(gg_ref[...], lg_ref[...], NT).astype(BF16)
-        through_ref[:, ranks:] = dot(gu_ref[...], lu_ref[...], NT).astype(BF16)
-
-    back_ref[...] = (dot(gg_ref[...], wg_ref[...], NT) + dot(gu_ref[...], wu_ref[...], NT)
-                     + dot(through_ref[...], down_ref[...])).astype(BF16)
-
-
-def back_call(gg, gu, wg, wu, lg, lu, down):
-    rows, units = gg.shape
-    width, ranks = wg.shape[0], lg.shape[0]
-    tile = tile_of(width, 512)
-    weight = pl.BlockSpec((tile, units), lambda i: (i, 0))
-    return pl.pallas_call(
-        back_kernel,
-        grid=(pl.cdiv(width, tile),),
-        out_shape=[jax.ShapeDtypeStruct((rows, width), BF16), jax.ShapeDtypeStruct((rows, 2 * ranks), BF16)],
-        in_specs=[resident(gg), resident(gu), weight, weight, resident(lg), resident(lu),
-                  pl.BlockSpec((2 * ranks, tile), lambda i: (0, i))],
-        out_specs=[pl.BlockSpec((rows, tile), lambda i: (0, i)),
-                   pl.BlockSpec((rows, 2 * ranks), lambda i: (0, 0))],
-        compiler_params=pltpu.CompilerParams(vmem_limit_bytes=60 * 2**20),
-        cost_estimate=pl.CostEstimate(
-            flops=4 * rows * width * units, bytes_accessed=4 * width * units + 4 * rows * units + 2 * rows * width,
-            transcendentals=0),
-    )(gg, gu, wg, wu, lg, lu, down)
-
-
-def outward_kernel(seqs, *refs):
-    hiddens, (wd_ref, do_ref, lift_out_ref, _, out_ref, inner_ref) = refs[:seqs], refs[seqs:]
+    )(tok, gh, wg, wu, wg, wu, down, lg, lu, through_out, lg, lu, down)
+
+
+def outward_kernel(seqs, reduce, steps, *refs):
+    hiddens, tokens, throughs, cot_ref, refs = (
+        refs[:seqs], refs[seqs : 2 * seqs], refs[2 * seqs : 3 * seqs], refs[3 * seqs], refs[3 * seqs + 1 :])
+    if reduce:
+        wd_ref, do_ref, lift_out_ref, back_ref, out_ref, inner_ref, early_ref, sum_ref = refs[:8]
+        first_a, first_b, second_a, second_b, pass_a, pass_b, own_ref, send, recv, local = refs[8:]
+    else:
+        wd_ref, do_ref, lift_out_ref, out_ref, inner_ref, early_ref = refs
     ranks = do_ref.shape[0] // seqs
-
-    @pl.when(pl.program_id(0) == 0)
+    step = pl.program_id(0)
+
+    if reduce:
+        group, replica = lax.axis_index("group"), lax.axis_index("replica")
+        beside, above, across = group + 1 - 2 * (group % 2), (group + 2) % 4, 3 - group
+        at_beside, at_above = (beside, replica), (above, replica)
+        rows, width = own_ref.shape
+        half = width // 2
+
+        def part(owner, side):
+            return back_ref.at[pl.ds(pl.multiple_of(owner * rows, rows), rows), pl.ds(side * half, half)]
+
+        def copy(src, dst, slot, partner):
+            return pltpu.make_async_remote_copy(
+                src_ref=src, dst_ref=dst, send_sem=send.at[slot], recv_sem=recv.at[slot], device_id=partner,
+                device_id_type=pl.DeviceIdType.MESH)
+
+        firsts = [copy(part(across, 0), first_a.at[1], 0, at_beside), copy(part(across, 1), first_b.at[1], 1, at_above),
+                  copy(part(beside, 0), first_a.at[0], 2, at_beside), copy(part(above, 1), first_b.at[0], 3, at_above)]
+        seconds = [copy(pass_a, second_a, 4, at_above), copy(pass_b, second_b, 5, at_beside)]
+        loads = [pltpu.make_async_copy(part(above, 0), pass_a, local.at[0]),
+                 pltpu.make_async_copy(part(beside, 1), pass_b, local.at[1]),
+                 pltpu.make_async_copy(
+                     back_ref.at[pl.ds(pl.multiple_of(group * rows, rows), rows), :], own_ref, local.at[2])]
+
+        @pl.when(step == 0)
+        def _():
+            barrier = pltpu.get_barrier_semaphore()
+            for partner in (at_beside, at_above):
+                pl.semaphore_signal(barrier, inc=1, device_id=partner, device_id_type=pl.DeviceIdType.MESH)
+            pl.semaphore_wait(barrier, 2)
+            for one in firsts:
+                one.start()
+            for one in loads:
+                one.start()
+
+    @pl.when(step == 0)
     def _():
         for s, hidden_ref in enumerate(hiddens):
             inner_ref[s] = dot(hidden_ref[...], do_ref[s * ranks : (s + 1) * ranks, :], NT).astype(BF16)
@@ -380,27 +690,69 @@
     for s, hidden_ref in enumerate(hiddens):
         out_ref[s] = (dot(hidden_ref[...], wd_ref[...])
                       + dot(inner_ref[s], lift_out_ref[s * ranks : (s + 1) * ranks, :])).astype(BF16)
-
-
-def outward_call(hiddens, wd, do, lift_out, earlier):
+        both = dot(throughs[s][...], tokens[s][...], TN).astype(BF16)
+        for kind, rows_of in enumerate((both[:ranks], both[ranks:], dot(inner_ref[s], cot_ref[s], TN).astype(BF16))):
+            row = (kind * seqs + s) * ranks
+            early_ref[row : row + ranks, :] = rows_of
+
+    if reduce:
+        @pl.when(step == max(steps - 2, 0))
+        def _():
+            for one in loads:
+                one.wait()
+            for one in firsts:
+                one.wait_recv()
+            pass_a[...] = (pass_a[...].astype(F32) + first_a[1].astype(F32)).astype(BF16)
+            pass_b[...] = (pass_b[...].astype(F32) + first_b[1].astype(F32)).astype(BF16)
+            for one in seconds:
+                one.start()
+
+        @pl.when(step == steps - 1)
+        def _():
+            for one in seconds:
+                one.wait_recv()
+            sum_ref[:, :half] = (own_ref[:, :half].astype(F32) + first_a[0].astype(F32)
+                                 + second_a[...].astype(F32)).astype(BF16)
+            sum_ref[:, half:] = (own_ref[:, half:].astype(F32) + first_b[0].astype(F32)
+                                 + second_b[...].astype(F32)).astype(BF16)
+            for one in firsts + seconds:
+                one.wait_send()
+
+
+def outward_call(hiddens, tokens, throughs, cot, wd, do, lift_out, back):
     rows, units = hiddens[0].shape
     seqs = len(hiddens)
     width, ranks = wd.shape[1], do.shape[0] // seqs
     tile = tile_of(width, 512)
-    return pl.pallas_call(
-        functools.partial(outward_kernel, seqs),
-        grid=(pl.cdiv(width, tile),),
-        out_shape=[jax.ShapeDtypeStruct((seqs, rows, width), BF16), jax.ShapeDtypeStruct((seqs, rows, ranks), BF16)],
-        in_specs=[resident(hidden) for hidden in hiddens]
+    steps = pl.cdiv(width, tile)
+    group = lax.axis_size("group")
+    reduce = group == 4 and width % 256 == 0
+    own, half = rows // group, width // 2
+    scratch = [pltpu.VMEM((2, own, half), BF16)] * 2 + [pltpu.VMEM((own, half), BF16)] * 4 + [
+        pltpu.VMEM((own, width), BF16), pltpu.SemaphoreType.DMA((6,)), pltpu.SemaphoreType.DMA((6,)),
+        pltpu.SemaphoreType.DMA((3,))]
+    got = pl.pallas_call(
+        functools.partial(outward_kernel, seqs, reduce, steps),
+        grid=(steps,),
+        out_shape=[jax.ShapeDtypeStruct((seqs, rows, width), BF16), jax.ShapeDtypeStruct((seqs, rows, ranks), BF16),
+                   jax.ShapeDtypeStruct((3 * seqs * ranks, width), BF16)]
+        + [jax.ShapeDtypeStruct((own, width), BF16)] * reduce,
+        in_specs=[resident(hidden) for hidden in hiddens] + [pl.BlockSpec((rows, tile), lambda i: (0, i))] * seqs
+        + [resident(through) for through in throughs] + [pl.BlockSpec((seqs, rows, tile), lambda i: (0, 0, i))]
         + [pl.BlockSpec((units, tile), lambda i: (0, i)), resident(do),
-           pl.BlockSpec((seqs * ranks, tile), lambda i: (0, i)), pl.BlockSpec(memory_space=pl.ANY)],
+           pl.BlockSpec((seqs * ranks, tile), lambda i: (0, i))] + [ANYWHERE] * reduce,
         out_specs=[pl.BlockSpec((seqs, rows, tile), lambda i: (0, 0, i)),
-                   pl.BlockSpec((seqs, rows, ranks), lambda i: (0, 0, 0))],
-        compiler_params=pltpu.CompilerParams(vmem_limit_bytes=60 * 2**20),
+                   pl.BlockSpec((seqs, rows, ranks), lambda i: (0, 0, 0)),
+                   pl.BlockSpec((3 * seqs * ranks, tile), lambda i: (0, i))]
+        + [pl.BlockSpec((own, width), lambda i: (0, 0))] * reduce,
+        scratch_shapes=scratch if reduce else [],
+        compiler_params=pltpu.CompilerParams(
+            vmem_limit_bytes=60 * 2**20, **(dict(collective_id=2, has_side_effects=True) if reduce else {})),
         cost_estimate=pl.CostEstimate(
             flops=2 * seqs * rows * width * units,
             bytes_accessed=2 * width * units + 2 * seqs * rows * (units + width), transcendentals=0),
-    )(*hiddens, wd, do, lift_out, earlier)
+    )(*hiddens, *tokens, *throughs, cot, wd, do, lift_out, *([back] if reduce else []))
+    return got if reduce else list(got) + [lax.psum_scatter(back, "group", scatter_dimension=0, tiled=True)]
 
 
 def pick_kernel(counts, ids_ref, *refs):
@@ -581,20 +933,33 @@
     )(*operands)
 
 
-def ordered_kernel(value_ref, *refs):
-    refs[-1][...] = value_ref[...]
+def ordered_kernel(*refs):
+    del refs
 
 
 def ordered(value, *earlier):
-    flat = value.reshape(-1, value.shape[-1])
-    tile = pl.BlockSpec((flat.shape[0] // 2, flat.shape[1]), lambda i: (i, 0))
     return pl.pallas_call(
         ordered_kernel,
-        grid=(2,),
-        out_shape=jax.ShapeDtypeStruct(flat.shape, flat.dtype),
-        in_specs=[tile] + [pl.BlockSpec(memory_space=pl.ANY)] * len(earlier),
-        out_specs=tile,
-    )(flat, *earlier).reshape(value.shape)
+        out_shape=jax.ShapeDtypeStruct(value.shape, value.dtype),
+        in_specs=[ANYWHERE] * (1 + len(earlier)),
+        out_specs=ANYWHERE,
+        input_output_aliases={0: 0},
+    )(value, *earlier)
+
+
+def ordered_stack_kernel(count, *refs):
+    for i in range(count):
+        refs[-1][i] = refs[i][...]
+
+
+def ordered_stack(values, *earlier):
+    vmem = pl.BlockSpec(memory_space=pltpu.VMEM)
+    return pl.pallas_call(
+        functools.partial(ordered_stack_kernel, len(values)),
+        out_shape=jax.ShapeDtypeStruct((len(values),) + values[0].shape, values[0].dtype),
+        in_specs=[vmem] * len(values) + [ANYWHERE] * len(earlier),
+        out_specs=vmem,
+    )(*values, *earlier)
 
 
 def row_tiles(rows, width, count):
@@ -683,10 +1048,9 @@
             replica += 1
 
 
-def spread(ids, source, gots, tables, sets, seqs, earlier=()):
+def spread(ids, source, gots, tables, sets, seqs, ranks, earlier=()):
     rows, width = gots[0].shape[1:]
     replicas = source.shape[0]
-    ranks = rows // (tables * seqs)
     scalars = pl.BlockSpec(memory_space=pltpu.SMEM)
     return pl.pallas_call(
         functools.partial(spread_kernel, tables, len(gots)),
@@ -756,21 +1120,21 @@
     return lax.ppermute(block, axis, route)
 
 
-def over_replicas(value, direct):
+def over_replicas(value, direct, *earlier):
     count, here = lax.axis_size("replica"), lax.axis_index("replica")
     if count % 2:
         return [lax.all_gather(value, "replica")], jnp.arange(count, dtype=jnp.int32)
     steps = jnp.arange(count // 2, dtype=jnp.int32)
     if direct:
-        got = [value[None]] + [
-            lax.ppermute(value, "replica", [(i, (i + 2 * step) % count) for i in range(count)])[None]
-            for step in range(1, count // 2)]
+        got = ordered_stack([value] + [
+            lax.ppermute(value, "replica", [(i, (i + 2 * step) % count) for i in range(count)])
+            for step in range(1, count // 2)], *earlier)
         source = (here + count - 2 * steps) % count
     else:
-        got = [lax.all_gather(value, "replica", axis_index_groups=[list(range(p, count, 2)) for p in range(2)])]
+        got = lax.all_gather(value, "replica", axis_index_groups=[list(range(p, count, 2)) for p in range(2)])
         source = here % 2 + 2 * steps
-    swapped = [lax.ppermute(part, "replica", [(i, i ^ 1) for i in range(count)]) for part in got]
-    return got + swapped, jnp.concatenate([source, source + 1 - 2 * (here % 2)], 0)
+    swapped = lax.ppermute(got, "replica", [(i, i ^ 1) for i in range(count)])
+    return [got, swapped], jnp.concatenate([source, source + 1 - 2 * (here % 2)], 0)
 
 
 def body(
@@ -799,7 +1163,6 @@
         stack[i * mask_cols : (i + 1) * mask_cols] for i in range(13)]
     own_lift_gate, own_lift_upper, own_down_outward = [
         own_tables[i * mask_cols : (i + 1) * mask_cols] for i in range(3)]
-    all_ids = lax.all_gather(adapter_ids, "replica", axis=0, tiled=True)
     cotangents = lax.all_gather(ordered(out_grad, stack), "group", axis=1, tiled=True)
 
     row_seq = lax.broadcasted_iota(jnp.int32, (rows, mask_cols), 0) // stretch
@@ -853,77 +1216,83 @@
     normed_two = normed_two_f.astype(BF16).reshape(seqs, stretch, width)
 
     spans = [slice(s * ranks, (s + 1) * ranks) for s in range(seqs)]
-    grad_hiddens = [
-        grad_hidden_call(cotangents, s, w_down, p_lift_outward[at], own_down_outward[at])
-        for s, at in enumerate(spans)]
-    all_tokens = [lax.all_gather(normed_two[s], "group", axis=0, tiled=True) for s in range(seqs)]
-    backs, hiddens, throughs, inners, gates, uppers = [], [], [], [], [], []
+    grad_hiddens, through_out, first_tokens = grad_hidden_call(
+        cotangents, w_down, p_lift_outward, own_down_outward, normed_two[0])
+    all_tokens = [first_tokens] + [
+        lax.all_gather(ordered(normed_two[s], first_tokens), "group", axis=0, tiled=True) for s in range(1, seqs)]
+    backs, hiddens, throughs, wides = [], [], [], []
     for s, at in enumerate(spans):
         two_downs = jnp.concatenate([p_down_gate[at], p_down_upper[at]], 0)
-        earlier = (all_ids,) + tuple(grad_hidden for grad_hidden, _ in grad_hiddens) if s == 0 else ()
-        hidden, grad_gate, grad_upper, inner = hidden_call(
-            all_tokens[s], grad_hiddens[s][0], w_gate, w_upper, two_downs, own_lift_gate[at], own_lift_upper[at],
-            earlier)
-        back, through = back_call(
-            grad_gate, grad_upper, w_gate, w_upper, own_lift_gate[at], own_lift_upper[at], two_downs)
-        backs.append(lax.psum_scatter(back, "group", scatter_dimension=0, tiled=True))
-        for kept, value in zip((hiddens, throughs, inners, gates, uppers),
-                               (hidden, through, inner, grad_gate, grad_upper)):
-            kept.append(value)
-    outward, inner_out = outward_call(hiddens, w_down, own_down_outward, p_lift_outward, back)
-    early = products(
-        [(throughs[s], 0, ranks, all_tokens[s]) for s in range(seqs)]
-        + [(throughs[s], ranks, 2 * ranks, all_tokens[s]) for s in range(seqs)]
-        + [(inner_out[s], 0, ranks, (cotangents, s)) for s in range(seqs)], (outward,))
-    wide = products(
-        [(inners[s], 0, ranks, gates[s]) for s in range(seqs)]
-        + [(inners[s], ranks, 2 * ranks, uppers[s]) for s in range(seqs)]
-        + [(grad_hiddens[s][1], 0, ranks, hiddens[s]) for s in range(seqs)], (outward,))
+        hidden, back, wide, through = feed_call(
+            s, all_tokens[s], grad_hiddens, w_gate, w_upper, two_downs, own_lift_gate[at], own_lift_upper[at],
+            through_out)
+        if s < seqs - 1:
+            backs.append(lax.psum_scatter(back, "group", scatter_dimension=0, tiled=True))
+        hiddens.append(hidden)
+        throughs.append(through)
+        wides.append(wide)
+    outward, _, early, reduced = outward_call(
+        hiddens, all_tokens, throughs, cotangents, w_down, own_down_outward, p_lift_outward, back)
+    backs.append(reduced)
+    named = jnp.broadcast_to(jnp.pad(adapter_ids, (0, -seqs % 16)).astype(BF16)[:, None], (-(-seqs // 16) * 16,
+                                                                                   wides[0].shape[1]))
+    wide = jnp.concatenate(
+        [wides[s][i * ranks : (i + 1) * ranks] for i in range(3) for s in range(seqs)] + [named], 0)
     grad_normed_two = jnp.concatenate(backs, 0)
     grad_resid, grad_mixed = resid_grad(
-        resid, out_grad.reshape(rows, width), gain_mlp.reshape(1, width), grad_normed_two, (early, wide))
+        resid, out_grad.reshape(rows, width), gain_mlp.reshape(1, width), grad_normed_two, ())
     outward = lax.psum_scatter(outward, "group", scatter_dimension=1, tiled=True).reshape(rows, width)
     block_out = block_call(resid, outward)
-    all_wide, wide_source = over_replicas(wide, True)
 
     through_mixer = (dot(grad_mixed, p_lift_mixer, NT) * own).astype(BF16)
-    grad_merged = dot(grad_mixed, full_mixer, NT) + dot(through_mixer, p_down_mixer)
-    span, total, firsts, grad_branch_pre = backward_scan(
-        seqs, convolved, inner_gates, lift_gates, decay_heads, softrate, restart, cum, local, carried, branch_pre,
-        grad_merged)
-    all_firsts = lax.all_gather(firsts, "group")
-    incoming = jnp.zeros((seqs, width), F32)
-    for lap in range(group - 1):
-        g = group - 1 - lap
-        longer = all_firsts[g, :seqs] * incoming + all_firsts[g, seqs:]
-        incoming = jnp.where(g > place, longer, incoming)
-    grad_direct, through_gates, grad_lift_gates = backward_gates(
-        seqs, convolved, inner_gates, lift_gates, decay_heads, admit_heads, softrate, restart, cum, local, carried,
-        span, total, incoming)
-    through_gates = (through_gates * own_two).astype(BF16)
-    grad_convolved = grad_direct + dot(through_gates, stack[2 * mask_cols : 4 * mask_cols])
-    grad_convolved = grad_convolved.reshape(seqs, stretch, width)
-    below = passed_along(grad_convolved[:, : taps - 1].astype(BF16), "group", -1).astype(F32)
-    grad_extended = jnp.concatenate([grad_convolved, below], axis=1)
-    grad_fed = sum(
-        conv_taps[j] * agree[j][:, j : j + stretch, None] * grad_extended[:, j : j + stretch] for j in range(taps)
-    ).astype(BF16).reshape(rows, width)
-    through_branch = (dot(grad_branch_pre, p_lift_branch, NT) * own).astype(BF16)
-    through_input = (dot(grad_fed, p_lift_input, NT) * own).astype(BF16)
-    through_one = jnp.concatenate([through_branch, through_input], 1)
+    if group == 4 and 2 * seqs <= 8 and stretch % 8 == 0:
+        agree_cols = jnp.stack([agree[j][:, j : j + stretch].reshape(rows) for j in range(taps)], 1)
+        grad_branch_pre, through_one, through_gates, grad_lift_gates, grad_fed = mixer_back(
+            seqs, grad_mixed, full_mixer, through_mixer, p_down_mixer, convolved, inner_gates, lift_gates, decay_heads,
+            admit_heads, softrate, restart, cum, local, carried, branch_pre, p_lift_branch, p_lift_input,
+            stack[2 * mask_cols : 4 * mask_cols], conv_taps, agree_cols)
+    else:
+        grad_merged = dot(grad_mixed, full_mixer, NT) + dot(through_mixer, p_down_mixer)
+        span, total, firsts, grad_branch_pre = backward_scan(
+            seqs, convolved, inner_gates, lift_gates, decay_heads, softrate, restart, cum, local, carried, branch_pre,
+            grad_merged)
+        all_firsts = lax.all_gather(firsts, "group")
+        incoming = jnp.zeros((seqs, width), F32)
+        for lap in range(group - 1):
+            g = group - 1 - lap
+            longer = all_firsts[g, :seqs] * incoming + all_firsts[g, seqs:]
+            incoming = jnp.where(g > place, longer, incoming)
+        grad_direct, through_gates, grad_lift_gates = backward_gates(
+            seqs, convolved, inner_gates, lift_gates, decay_heads, admit_heads, softrate, restart, cum, local, carried,
+            span, total, incoming)
+        through_gates = (through_gates * own_two).astype(BF16)
+        grad_convolved = grad_direct + dot(through_gates, stack[2 * mask_cols : 4 * mask_cols])
+        grad_convolved = grad_convolved.reshape(seqs, stretch, width)
+        below = passed_along(grad_convolved[:, : taps - 1].astype(BF16), "group", -1).astype(F32)
+        grad_extended = jnp.concatenate([grad_convolved, below], axis=1)
+        grad_fed = sum(
+            conv_taps[j] * agree[j][:, j : j + stretch, None] * grad_extended[:, j : j + stretch] for j in range(taps)
+        ).astype(BF16).reshape(rows, width)
+        through_branch = (dot(grad_branch_pre, p_lift_branch, NT) * own).astype(BF16)
+        through_input = (dot(grad_fed, p_lift_input, NT) * own).astype(BF16)
+        through_one = jnp.concatenate([through_branch, through_input], 1)
     grad_normed = (dot(grad_branch_pre, full_branch, NT) + dot(grad_fed, full_input, NT)
                    + dot(through_one, stack[: 2 * mask_cols]))
     grad_inputs = finish(grad_resid, inputs.reshape(rows, width), gain_mix.reshape(1, width), grad_normed)
 
+    all_wide, wide_source = over_replicas(wide, True, through_gates)
     both = 2 * mask_cols
+    got_ids = jnp.concatenate([part[:, 3 * mask_cols : 3 * mask_cols + seqs, 0] for part in all_wide], 0)
+    in_order = wide_source[:, None] == jnp.arange(wide_source.shape[0], dtype=jnp.int32)[None, :]
+    all_ids = jnp.sum(jnp.where(in_order[:, :, None], got_ids.astype(jnp.int32)[:, None, :], 0), 0).reshape(-1)
     partial = products(
         [(through_one, 0, both, normed), (through_gates, 0, both, rounded), (through_mixer, 0, mask_cols, merged),
          (inner_branch, 0, mask_cols, grad_branch_pre), (inner_input, 0, mask_cols, grad_fed), (grad_lift_gates,),
-         (inner_mixer, 0, mask_cols, grad_mixed), (early,)], (block_out, *all_wide), group)
-    owned = lax.psum_scatter(partial, "group", scatter_dimension=0, tiled=False)
-    wides = spread(all_ids, wide_source, all_wide, 3, sets, seqs, (partial,))
-    all_owned, owned_source = over_replicas(ordered(owned, grad_inputs, wides[0]), False)
-    totals = spread(all_ids, owned_source, all_owned, 13, sets, seqs)
+         (inner_mixer, 0, mask_cols, grad_mixed), (early,)], all_wide, group)
+    owned = lax.psum_scatter(ordered(partial, outward), "group", scatter_dimension=0, tiled=False)
+    wides = spread(all_ids, wide_source, all_wide, 3, sets, seqs, ranks)
+    all_owned, owned_source = over_replicas(ordered(owned, grad_normed), False)
+    totals = spread(all_ids, owned_source, all_owned, 13, sets, seqs, ranks, (block_out, wides[0], grad_inputs))
     (t_down_branch, t_down_input, t_down_decay, t_down_admit, t_down_mixer, t_lift_branch, t_lift_input, t_lift_decay,
      t_lift_admit, t_lift_mixer, t_down_gate, t_down_upper, t_lift_outward) = totals
     return (

time: 774 us -> 735 us (0.950)
  Pallas kernels: 472 us -> 505 us
  matrix products: 108 us -> 79 us
  waiting for transfers between devices: 86.3 us -> 59.3 us
  blocking collectives: 27.8 us -> 9.92 us
  local copies, waits for them, and re-layouts: 23.1 us -> 34.5 us
    pallas_call x11 -> x10, Pallas kernels: 247 us -> 310 us  [the longest x2 126 us: feed_call(): pl.pallas_call(functools.partial(feed_kernel, steps, tile, units), grid=(...]
    dot_general x18 -> x13, matrix products: 108 us -> 79 us  [dot(): return lax.dot_general(a, b, dims, preferred_element_type=F32)]
    pallas_call x3 -> x1, Pallas kernels: 37.8 us -> 9.35 us  [products(): pl.pallas_call(functools.partial(products_kernel, plan), grid=(pl.cdiv(wi...]
    all_gather x2 -> x1, waiting for transfers between devices: 20.3 us -> 0.01 us  [body(): lax.all_gather(ordered(normed_two[s], first_tokens), 'group', axis=0, til...]
    unnamed x1 -> x0, blocking collectives: 9.44 us -> none
    unnamed x166 -> x143, local copies, waits for them, and re-layouts: 12.6 us -> 21.4 us
    all_gather x1 -> x0, blocking collectives: 8.57 us -> none  [body(): all_firsts = lax.all_gather(firsts, 'group')]
  transfers between devices with their start and end apart: 18 -> 12, of which waited for: 5 -> 4; matrix products, arithmetic and copies ran while one was open for 18% -> 15% of each run, Pallas kernels for 40% -> 42%
where the time goes in v4:
time: 735 us; the launch traced here: 728 us
  Pallas kernels  505 us (69%)
  matrix products  79 us (11%)
  waiting for transfers between devices  59.3 us (8%)
  local copies, waits for them, and re-layouts  34.5 us (5%)
  between operations  15.8 us (2%)
  other arithmetic  15.7 us (2%)
  blocking collectives  9.92 us (1%)
  starting transfers between devices  8.6 us (1%)
    pallas_call x1, Pallas kernels, gather_weights(): pl.pallas_call(functools.partial(gather_kernel, units), out_shape=[jax.Sh...  143 us
    pallas_call x2, Pallas kernels, feed_call(): pl.pallas_call(functools.partial(feed_kernel, steps, tile, units), grid=(...  126 us
    dot_general x13, matrix products, dot(): return lax.dot_general(a, b, dims, preferred_element_type=F32)  79 us
    pallas_call x1, Pallas kernels, mixer_back(): pl.pallas_call(functools.partial(mixer_back_kernel, seqs, heads), grid=(3...  77.2 us
    pallas_call x1, Pallas kernels, outward_call(): pl.pallas_call(functools.partial(outward_kernel, seqs, reduce, steps), gr...  52.4 us
    pallas_call x1, Pallas kernels, grad_hidden_call(): pl.pallas_call(functools.partial(grad_hidden_kernel, seqs, gather, pl.cdi...  51.3 us
    all_gather x1, waiting for transfers between devices, over_replicas(): lax.all_gather(value, 'replica', axis_index_groups=[list(range(p, count,...  48 us
    unnamed x143, local copies, waits for them, and re-layouts  21.4 us
  transfers between devices with their start and end apart: 12, of which 4 were waited for; matrix products, arithmetic and copies ran while one was open for 15% of the time, Pallas kernels for 42%

profile of v4, /device:TPU:0, one launch (start us, length us, event | category | flops | bytes accessed | tf_op | source)
XLA Modules:
  0.0 727.7 jit_solution(1972432428419605826)
XLA Ops:
  7.2 3.4 copy.115.refs_0_
  10.6 3.0 shard_map.439
  13.6 143.2 %shard_map.440 = (bf16[2560,2560]{1,0:T(8,128)(2,1)}, bf16[2560,2560]{1,0:T(8,128)(2,1)}, bf16[2560,2560]{1,0:T(8,128)(2,1)}, bf16[416,2560]{1,0:T(8,128)(2,1)}) custom-call(bf16[2560,640]{1,0:T(8,128)(2,1)} %refs_0_.2, bf16[2560,640]{1,0:T(8,128)(2,1)} %refs_1_.2, bf16[640,2560]{1,0:T(8,128)(2,1)} %refs_2_.1, bf16[416,640]{1,0:T(8,128)(2,1)} %bitcast.152), custom_call_target="tpu_custom_call" | custom-call | bytes 419430400 | tf_op jit(solution)/shard_map/pallas_call | solution.py:921
  162.2 11.3 %fusion.45 = f32[512,2560]{1,0:T(8,128)S(1)} fusion(bf16[512,2560]{1,0:T(8,128)(2,1)S(1)} %fusion.1.refs_1_, bf16[2560,2560]{1,0:T(8,128)(2,1)} %get-tuple-element.64), kind=kOutput, calls=%fused_computation.131 | convolution fusion | flops 6710886400 | bytes 20971520 | tf_op jit(solution)/shard_map/dot_general | solution.py:22
  185.2 12.4 %fusion.46 = f32[512,2560]{1,0:T(8,128)} fusion(bf16[512,2560]{1,0:T(8,128)(2,1)} %copy-done.18, bf16[2560,2560]{1,0:T(8,128)(2,1)} %get-tuple-element.68), kind=kOutput, calls=%fused_computation.132 | convolution fusion | flops 6710886400 | bytes 20971520 | tf_op jit(solution)/shard_map/dot_general | solution.py:22
  199.5 2.5 maximum_convert_fusion
  202.1 5.3 fusion.8
  207.6 3.3 fusion.15.inner_ref
  211.3 16.7 %shard_map.441 = (f32[512,2560]{1,0:T(8,128)S(1)}, f32[512,2560]{1,0:T(8,128)S(1)}) custom-call(f32[512,2560]{1,0:T(8,128)} %bitcast.142, bf16[512,64]{1,0:T(8,128)(2,1)S(1)} %fusion.15.inner_ref, bf16[64,2560]{1,0:T(8,128)(2,1)S(1)} %get-tuple-element.115.lift_ref, bf16[10,256,256]{2,1,0:T(8,128)(2,1)S(1)} %copy-done.12, ...), custom_call_target="tpu_custom_call" | custom-call | flops 1420820480 | bytes 15728640 | tf_op jit(solution)/shard_map/pallas_call | solution.py:107
  228.2 9.9 %all-gather.2 = f32[4,4,2560]{2,1,0:T(4,128)S(1)} all-gather(f32[1,4,2560]{2,1,0:T(4,128)S(1)} %maximum_bitcast_fusion), channel_id=2, replica_groups=mesh['group'=4,'replica'=8] {'group'}, dimensions={0}, use_global_device_ids=true | all-gather | bytes 204800 | tf_op jit(solution)/shard_map/all_gather | solution.py:1204
  238.2 5.9 fusion.7
  246.1 10.0 %fusion.47 = f32[512,2560]{1,0:T(8,128)S(1)} fusion(bf16[512,2560]{1,0:T(8,128)(2,1)S(1)} %get-tuple-element.143.refs_5_, bf16[2560,2560]{1,0:T(8,128)(2,1)} %get-tuple-element.69.w_ref), kind=kOutput, calls=%fused_computation.133 | convolution fusion | flops 6710886400 | bytes 20971520 | tf_op jit(solution)/shard_map/dot_general | solution.py:22
  263.3 51.3 %shard_map.443 = (bf16[2,1024,1920]{2,1,0:T(8,128)(2,1)}, bf16[2,1024,16]{2,1,0:T(8,128)(2,1)}, bf16[1024,2560]{1,0:T(8,128)(2,1)}) custom-call(bf16[2,1024,2560]{2,1,0:T(8,128)(2,1)} %all-gather.7.cloned.1.call-done.refs_0_.refs_6_, bf16[1920,2560]{1,0:T(8,128)(2,1)} %refs_7_.3, bf16[32,2560]{1,0:T(8,128)(2,1)} %get-tuple-element.117.refs_2_.refs_9_, ...), custom_call_target="tpu_custom_call" | custom-call | flops 20132659200 | bytes 28180480 | tf_op jit(solution)/shard_map/pallas_call | solution.py:549
  317.6 63.4 %shard_map.444 = (bf16[1024,1920]{1,0:T(8,128)(2,1)}, bf16[1024,2560]{1,0:T(8,128)(2,1)}, bf16[48,1920]{1,0:T(8,128)(2,1)}, bf16[1024,32]{1,0:T(8,128)(2,1)}) custom-call(bf16[1024,2560]{1,0:T(8,128)(2,1)} %get-tuple-element.71.tok_ref.refs_1_.refs_2_, bf16[2,1024,1920]{2,1,0:T(8,128)(2,1)} %get-tuple-element.72.gh_ref, bf16[2560,1920]{1,0:T(8,128)(2,1)} %wg_rows_ref.3, ...), custom_call_target="tpu_custom_call" | custom-call | flops 40265318400 | bytes 51118080 | tf_op jit(solution)/shard_map/pallas_call | solution.py:620
  381.9 62.5 %shard_map.446 = (bf16[1024,1920]{1,0:T(8,128)(2,1)}, bf16[1024,2560]{1,0:T(8,128)(2,1)}, bf16[48,1920]{1,0:T(8,128)(2,1)}, bf16[1024,32]{1,0:T(8,128)(2,1)}) custom-call(bf16[1024,2560]{1,0:T(8,128)(2,1)} %all-gather.9.cloned.1.call-done.tok_ref.refs_3_, bf16[2,1024,1920]{2,1,0:T(8,128)(2,1)} %get-tuple-element.72.gh_ref, bf16[2560,1920]{1,0:T(8,128)(2,1)} %wg_rows_ref.3, ...), custom_call_target="tpu_custom_call" | custom-call | flops 40265318400 | bytes 51118080 | tf_op jit(solution)/shard_map/pallas_call | solution.py:620
  444.5 52.4 %shard_map.447 = (bf16[2,1024,2560]{2,1,0:T(8,128)(2,1)}, bf16[2,1024,16]{2,1,0:T(8,128)(2,1)}, bf16[96,2560]{1,0:T(8,128)(2,1)}, bf16[256,2560]{1,0:T(8,128)(2,1)}) custom-call(bf16[1024,1920]{1,0:T(8,128)(2,1)} %get-tuple-element.74.refs_0_, bf16[1024,1920]{1,0:T(8,128)(2,1)} %get-tuple-element.75.refs_1_, ...), custom_call_target="tpu_custom_call" | custom-call | flops 20132659200 | bytes 28180480 | tf_op jit(solution)/shard_map/pallas_call | solution.py:734
  506.0 5.2 shard_map.449
  517.5 77.2 %shard_map.450 = (bf16[512,2560]{1,0:T(8,128)(2,1)}, bf16[512,64]{1,0:T(8,128)(2,1)}, bf16[512,64]{1,0:T(8,128)(2,1)}, f32[64,2560]{1,0:T(8,128)}, bf16[512,2560]{1,0:T(8,128)(2,1)}) custom-call(bf16[512,2560]{1,0:T(8,128)(2,1)} %copy-done.8, bf16[2560,2560]{1,0:T(8,128)(2,1)} %get-tuple-element.69.w_ref, bf16[512,32]{1,0:T(8,128)(2,1)} %fusion.13.thr_mixer_ref.refs_4_, ...), custom_call_target="tpu_custom_call" | custom-call | flops 13683916800 | bytes 65536000 | tf_op jit(solution)/shard_map/pallas_call | solution.py:427
  595.5 2.7 shard_map.452.refs_14_.refs_0_
  598.9 3.1 collective-permute-done.4.refs_15_.refs_1_
  603.2 9.4 %shard_map.453.refs_0_ = bf16[4,416,640]{2,1,0:T(8,128)(2,1)} custom-call(bf16[512,64]{1,0:T(8,128)(2,1)} %get-tuple-element.86.refs_0_, bf16[512,2560]{1,0:T(8,128)(2,1)} %copy-done.18, bf16[512,64]{1,0:T(8,128)(2,1)} %get-tuple-element.89.refs_4_.refs_2_, bf16[512,2560]{1,0:T(8,128)(2,1)} %copy-done.19, bf16[512,32]{1,0:T(8,128)(2,1)} %fusion.13.thr_mixer_ref.refs_4_, ...), custom_call_target="tpu_custom_call" | custom-call | flops 537919488 | bytes 16809984 | tf_op jit(solution)/shard_map/pallas_call | solution.py:1102
  612.7 11.3 %fusion.48 = f32[512,2560]{1,0:T(8,128)S(1)} fusion(bf16[512,2560]{1,0:T(8,128)(2,1)} %get-tuple-element.84.refs_7_, bf16[2560,2560]{1,0:T(8,128)(2,1)} %get-tuple-element.68), kind=kOutput, calls=%fused_computation.134 | convolution fusion | flops 6710886400 | bytes 20971520 | tf_op jit(solution)/shard_map/dot_general | solution.py:22
  624.0 10.3 %fusion.49 = f32[512,2560]{1,0:T(8,128)S(1)} fusion(bf16[512,2560]{1,0:T(8,128)(2,1)S(1)} %copy-done.22, bf16[2560,2560]{1,0:T(8,128)(2,1)} %get-tuple-element.64), kind=kOutput, calls=%fused_computation.135 | convolution fusion | flops 6710886400 | bytes 20971520 | tf_op jit(solution)/shard_map/dot_general | solution.py:22
  634.4 4.2 add_add_fusion.grads_ref.refs_1_
  638.5 7.6 %reduce-scatter.10.cloned.1.call-done = bf16[1,416,640]{2,1,0:T(8,128)(2,1)} async-done(((bf16[4,416,640]{2,1,0:T(8,128)(2,1)}), bf16[1,416,640]{2,1,0:T(8,128)(2,1)}) %reduce-scatter.10.cloned.1.call-update) | async-done | bytes 532496
  646.1 48.0 %all-gather.11.cloned.1.call-done = bf16[1664,640]{1,0:T(8,128)(2,1)} async-done(((bf16[416,640]{1,0:T(8,128)(2,1)}), bf16[1664,640]{1,0:T(8,128)(2,1)}) %all-gather.11.cloned.1.call-update) | async-done | bytes 2129936 | tf_op jit(solution)/shard_map/all_gather | solution.py:1134
  695.7 2.5 copy-done
  698.2 2.5 copy-done.7
  700.7 4.1 shard_map.451.refs_4_
  706.4 4.0 shard_map.456
  710.5 5.2 shard_map.448.refs_2_
  715.6 4.7 shard_map.457
  (228 shorter events, 53.7 us)
Async XLA Ops:
  7.2 256.2 %all-gather.7.cloned.1.call-start = ((), (), s32[]{:S(2)}) async-start(), calls=%async_computation.3 | async-start | bytes 13107200 | tf_op jit(solution)/shard_map/all_gather | solution.py:1166
  156.9 225.1 %all-gather.9.cloned.1.call-start = ((), (), s32[]{:S(2)}) async-start(), calls=%async_computation.4 | async-start | bytes 6553600 | tf_op jit(solution)/shard_map/all_gather | solution.py:1222
  160.1 13.4 %copy-start.18 = (bf16[512,2560]{1,0:T(8,128)(2,1)}, bf16[512,2560]{1,0:T(8,128)(2,1)S(1)}, u32[]{:S(2)}) copy-start(bf16[512,2560]{1,0:T(8,128)(2,1)S(1)} %fusion.1.refs_1_) | copy-start | bytes 7864324
  162.2 75.9 %copy-start.23 = (bf16[512,64]{1,0:T(8,128)(2,1)}, bf16[512,64]{1,0:T(8,128)(2,1)S(1)}, u32[]{:S(2)}) copy-start(bf16[512,64]{1,0:T(8,128)(2,1)S(1)} %fusion.14) | copy-start | bytes 196612
  176.9 22.6 %collective-permute-start = (bf16[2,3,2560]{2,1,0:T(4,128)(2,1)S(1)}, bf16[2,3,2560]{2,1,0:T(4,128)(2,1)S(1)}, u32[]{:S(2)}, u32[]{:S(2)}) collective-permute-start(bf16[2,3,2560]{2,1,0:T(4,128)(2,1)S(1)} %slice.275), channel_id=1, source_target_pairs={{0,8},{8,16},{16,24},{1,9},{9,17},{17,25},{2,10},{10,18},{18,26},{... | collective-permute-start | bytes 92168 | tf_op jit(solution)/shard_map/ppermute | solution.py:1120
  185.2 25.8 %copy-start.9 = (bf16[64,2560]{1,0:T(8,128)(2,1)}, bf16[64,2560]{1,0:T(8,128)(2,1)S(1)}, u32[]{:S(2)}) copy-start(bf16[64,2560]{1,0:T(8,128)(2,1)S(1)} %get-tuple-element.115.lift_ref) | copy-start | bytes 983044
  185.2 12.4 %copy-start.36 = (f32[4,2560]{1,0:T(4,128)S(1)}, f32[4,2560]{1,0:T(4,128)}, u32[]{:S(2)}) copy-start(f32[4,2560]{1,0:T(4,128)} %taps_ref.1) | copy-start | bytes 122884
  197.7 13.3 %copy-start.11 = (f32[1,2560]{1,0:T(1,128)}, f32[1,2560]{1,0:T(1,128)S(1)}, u32[]{:S(2)}) copy-start(f32[1,2560]{1,0:T(1,128)S(1)} %reshape.178.soft_ref) | copy-start | bytes 30724
  197.9 13.1 %copy-start.10 = (f32[1,512]{0,1:T(8,128)}, f32[1,512]{0,1:T(8,128)S(1)}, u32[]{:S(2)}) copy-start(f32[1,512]{0,1:T(8,128)S(1)} %copy.106) | copy-start | bytes 6148
  207.6 20.4 %copy-start.19 = (bf16[512,2560]{1,0:T(8,128)(2,1)}, bf16[512,2560]{1,0:T(8,128)(2,1)S(1)}, u32[]{:S(2)}) copy-start(bf16[512,2560]{1,0:T(8,128)(2,1)S(1)} %bitcast_convert_fusion.refs_3_) | copy-start | bytes 7864324
  211.0 17.1 %copy-start.14 = (bf16[512,64]{1,0:T(8,128)(2,1)}, bf16[512,64]{1,0:T(8,128)(2,1)S(1)}, u32[]{:S(2)}) copy-start(bf16[512,64]{1,0:T(8,128)(2,1)S(1)} %fusion.15.inner_ref) | copy-start | bytes 196612
  228.0 16.1 %copy-start.4 = (f32[512,2560]{1,0:T(8,128)}, f32[512,2560]{1,0:T(8,128)S(1)}, u32[]{:S(2)}) copy-start(f32[512,2560]{1,0:T(8,128)S(1)} %get-tuple-element.67.cum_ref) | copy-start | bytes 15728644
  228.0 16.1 %copy-start.5 = (f32[512,2560]{1,0:T(8,128)}, f32[512,2560]{1,0:T(8,128)S(1)}, u32[]{:S(2)}) copy-start(f32[512,2560]{1,0:T(8,128)S(1)} %get-tuple-element.66.local_ref) | copy-start | bytes 15728644
  244.1 12.1 %copy-start.20 = (bf16[512,2560]{1,0:T(8,128)(2,1)}, bf16[512,2560]{1,0:T(8,128)(2,1)S(1)}, u32[]{:S(2)}) copy-start(bf16[512,2560]{1,0:T(8,128)(2,1)S(1)} %get-tuple-element.143.refs_5_) | copy-start | bytes 7864324
  246.1 10.1 %copy-start.26 = (bf16[512,32]{1,0:T(8,128)(2,1)}, bf16[512,32]{1,0:T(8,128)(2,1)S(1)}, u32[]{:S(2)}) copy-start(bf16[512,32]{1,0:T(8,128)(2,1)S(1)} %fusion.12.refs_11_) | copy-start | bytes 98308
  314.7 189.3 %reduce-scatter.8.cloned.1.call-start = ((), (), s32[]{:S(2)}) async-start(), calls=%async_computation.6 | async-start | bytes 6553600 | tf_op jit(solution)/shard_map/reduce_scatter | solution.py:1230
  381.0 231.5 %reduce-scatter.6.cloned.1.call-start = ((), (), s32[]{:S(2)}) async-start(), calls=%async_computation.5 | async-start | bytes 13107200 | tf_op jit(solution)/shard_map/reduce_scatter | solution.py:1244
  497.0 149.1 %reduce-scatter.10.cloned.1.call-start = ((), (), s32[]{:S(2)}) async-start(), calls=%async_computation.8 | async-start | bytes 2662400
  498.7 12.5 %copy-start.25 = (bf16[112,1920]{1,0:T(8,128)(2,1)}, bf16[112,1920]{1,0:T(8,128)(2,1)S(1)}, u32[]{:S(2)}) copy-start(bf16[112,1920]{1,0:T(8,128)(2,1)S(1)} %broadcast_dynamic-update-slice_fusion.refs_0_) | copy-start | bytes 1290244
  498.7 96.0 %collective-permute-start.1 = (bf16[112,1920]{1,0:T(8,128)(2,1)S(1)}, bf16[112,1920]{1,0:T(8,128)(2,1)S(1)}, u32[]{:S(2)}, u32[]{:S(2)}) collective-permute-start(bf16[112,1920]{1,0:T(8,128)(2,1)S(1)} %broadcast_dynamic-update-slice_fusion.refs_0_), channel_id=1, source_target_pairs={{0,2},{1,3},{2,4},{3,5},{4,6},{5,7},{6,0},{7,1},{8,10},{9,11},{10,... | collective-permute-start | bytes 1290248 | tf_op jit(solution)/shard_map/ppermute | solution.py:1130
  500.2 94.5 %collective-permute-start.2 = (bf16[112,1920]{1,0:T(8,128)(2,1)S(1)}, bf16[112,1920]{1,0:T(8,128)(2,1)}, u32[]{:S(2)}, u32[]{:S(2)}) collective-permute-start(bf16[112,1920]{1,0:T(8,128)(2,1)S(1)} %broadcast_dynamic-update-slice_fusion.refs_0_), channel_id=1, source_target_pairs={{0,4},{1,5},{2,6},{3,7},{4,0},{5,1},{6,2},{7,3},{8,12},{9,13},{10,... | collective-permute-start | bytes 1290248 | tf_op jit(solution)/shard_map/ppermute | solution.py:1130
  502.6 92.2 %collective-permute-start.3 = (bf16[112,1920]{1,0:T(8,128)(2,1)S(1)}, bf16[112,1920]{1,0:T(8,128)(2,1)}, u32[]{:S(2)}, u32[]{:S(2)}) collective-permute-start(bf16[112,1920]{1,0:T(8,128)(2,1)S(1)} %broadcast_dynamic-update-slice_fusion.refs_0_), channel_id=1, source_target_pairs={{0,6},{1,7},{2,0},{3,1},{4,2},{5,3},{6,4},{7,5},{8,14},{9,15},{10,... | collective-permute-start | bytes 1290248 | tf_op jit(solution)/shard_map/ppermute | solution.py:1130
  505.9 9.1 %copy-start.40 = (s32[512]{0:T(512)S(1)}, s32[512]{0:T(512)}, u32[]{:S(2)}) copy-start(s32[512]{0:T(512)} %copy-done.38) | copy-start | bytes 6148
  517.5 80.7 %copy-start.24 = (bf16[512,64]{1,0:T(8,128)(2,1)S(1)}, bf16[512,64]{1,0:T(8,128)(2,1)}, u32[]{:S(2)}) copy-start(bf16[512,64]{1,0:T(8,128)(2,1)} %copy-done.23) | copy-start | bytes 196612
  598.2 3.8 collective-permute-start.4
  612.6 11.4 %copy-start.22 = (bf16[512,2560]{1,0:T(8,128)(2,1)S(1)}, bf16[512,2560]{1,0:T(8,128)(2,1)}, u32[]{:S(2)}) copy-start(bf16[512,2560]{1,0:T(8,128)(2,1)} %get-tuple-element.85.refs_9_) | copy-start | bytes 7864324
  612.6 81.5 %all-gather.11.cloned.1.call-start = ((), (), s32[]{:S(2)}) async-start(), calls=%async_computation.7 | async-start | bytes 2662400 | tf_op jit(solution)/shard_map/all_gather | solution.py:1134
  624.0 10.4 %copy-start.27 = (bf16[512,64]{1,0:T(8,128)(2,1)S(1)}, bf16[512,64]{1,0:T(8,128)(2,1)}, u32[]{:S(2)}) copy-start(bf16[512,64]{1,0:T(8,128)(2,1)} %get-tuple-element.86.refs_0_) | copy-start | bytes 196612
  638.5 55.6 %copy-start.35 = (f32[2560]{0:T(1024)S(1)}, f32[2560]{0:T(1024)}, u32[]{:S(2)}) copy-start(f32[2560]{0:T(1024)} %param.35) | copy-start | bytes 30724
  638.5 57.2 %copy-start.2 = (bf16[2,256,2560]{2,1,0:T(8,128)(2,1)S(1)}, bf16[2,256,2560]{2,1,0:T(8,128)(2,1)}, u32[]{:S(2)}) copy-start(bf16[2,256,2560]{2,1,0:T(8,128)(2,1)} %param.32) | copy-start | bytes 7864324
  694.1 21.5 %collective-permute-start.5 = (bf16[4,416,640]{2,1,0:T(8,128)(2,1)}, bf16[4,416,640]{2,1,0:T(8,128)(2,1)}, u32[]{:S(2)}, u32[]{:S(2)}) collective-permute-start(bf16[4,416,640]{2,1,0:T(8,128)(2,1)} %bitcast.150), channel_id=1, source_target_pairs={{0,1},{1,0},{2,3},{3,2},{4,5},{5,4},{6,7},{7,6},{8,9},{9,8},{10,11... | collective-permute-start | bytes 6389768 | tf_op jit(solution)/shard_map/ppermute | solution.py:1136
  694.2 10.5 %copy-start.61 = (s32[8]{0:T(128)}, s32[8]{0:T(128)S(1)}, u32[]{:S(2)}) copy-start(s32[8]{0:T(128)S(1)} %pad_add_fusion.1.from_ref) | copy-start | bytes 100
  (43 other events, 183.0 us)
Sparse Core Ops, SparseCore 0:
  157.0 106.3 all-gather.6
  314.8 61.4 all-gather.8
  381.1 61.3 reduce-scatter.7
  497.1 108.6 reduce-scatter.5
  612.7 33.3 reduce-scatter.9
  647.5 46.5 all-gather.10

commit v5 on v4

--- a/solution.py
+++ b/solution.py
@@ -16,6 +16,7 @@
 NN = (((1,), (0,)), ((), ()))
 TN = (((0,), (0,)), ((), ()))
 ANYWHERE = pl.BlockSpec(memory_space=pl.ANY)
+VMEM = 62 * 2**20
 
 
 def dot(a, b, dims=NN):
@@ -269,10 +270,10 @@
 
 
 def mixer_back_kernel(
-    seqs, heads, mixed_ref, w_ref, thr_mixer_ref, down_mixer_ref, conv_ref, inner_ref, lift_ref, table_d_ref,
+    seqs, heads, mixed_ref, w_ref, lift_mixer_ref, down_mixer_ref, conv_ref, inner_ref, lift_ref, table_d_ref,
     table_a_ref, soft_ref, restart_ref, cum_ref, local_ref, carried_ref, pre_ref, lift_branch_ref, lift_input_ref,
     down_gates_ref, taps_ref, agree_ref,
-    branch_grad_ref, through_one_ref, through_gates_ref, lift_grad_ref, fed_grad_ref,
+    branch_grad_ref, through_one_ref, through_gates_ref, lift_grad_ref, fed_grad_ref, thr_mixer_ref,
     span_ref, total_ref, ends_ref, all_ends_ref, incoming_ref, halo_ref, below_ref, one_ref, gates_ref, send, recv,
 ):
     rows, size = conv_ref.shape
@@ -300,6 +301,10 @@
         one_ref[...] = jnp.zeros_like(one_ref)
         gates_ref[...] = jnp.zeros_like(gates_ref)
         ends_ref[...] = jnp.zeros_like(ends_ref)
+        row = lax.broadcasted_iota(jnp.int32, thr_mixer_ref.shape, 0) // stretch
+        col = lax.broadcasted_iota(jnp.int32, thr_mixer_ref.shape, 1) // (thr_mixer_ref.shape[1] // seqs)
+        through = dot(mixed_ref[...], lift_mixer_ref[...], NT)
+        thr_mixer_ref[...] = jnp.where(row == col, through, 0.0).astype(BF16)
 
     @pl.when(step < heads)
     def _():
@@ -410,7 +415,7 @@
         downward.wait_send()
 
 
-def mixer_back(seqs, mixed, w_mixer, thr_mixer, down_mixer, conv, inner, lift, table_d, table_a, softrate, restart,
+def mixer_back(seqs, mixed, w_mixer, lift_mixer, down_mixer, conv, inner, lift, table_d, table_a, softrate, restart,
                cum, local, carried, pre, lift_branch, lift_input, down_gates, taps, agree):
     rows, width = conv.shape
     heads, size = table_d.shape[:2]
@@ -433,26 +438,28 @@
             jax.ShapeDtypeStruct((rows, middle), BF16),
             jax.ShapeDtypeStruct(lift.shape, F32),
             jax.ShapeDtypeStruct((rows, width), BF16),
+            jax.ShapeDtypeStruct((rows, lift_mixer.shape[0]), BF16),
         ],
         in_specs=[
-            full(mixed), pl.BlockSpec((size, width), lambda i: (first(i), 0)), full(thr_mixer), cols(down_mixer, first),
+            full(mixed), pl.BlockSpec((size, width), lambda i: (first(i), 0)), full(lift_mixer), cols(down_mixer, first),
             cols(conv, either), full(inner), cols(lift, either), table, table, cols(softrate, either), full(restart),
             cols(cum, either), cols(local, either), cols(carried, either), cols(pre, first), cols(lift_branch, first),
             cols(lift_input, third), full(down_gates), cols(taps, third), full(agree),
         ],
         out_specs=[tile(first), whole(2 * lift_branch.shape[0]), whole(middle),
-                   pl.BlockSpec((lift.shape[0], size), lambda i: (0, second(i))), tile(third)],
+                   pl.BlockSpec((lift.shape[0], size), lambda i: (0, second(i))), tile(third),
+                   whole(lift_mixer.shape[0])],
         scratch_shapes=[
             pltpu.VMEM((heads, rows, size), F32), pltpu.VMEM((heads, rows, size), F32), pltpu.VMEM((8, width), F32),
             pltpu.VMEM((4, 8, width), F32), pltpu.VMEM((seqs, width), F32), pltpu.VMEM((8 * seqs, width), BF16),
             pltpu.VMEM((8 * seqs, width), BF16), pltpu.VMEM((rows, 2 * lift_branch.shape[0]), F32),
             pltpu.VMEM((rows, middle), F32), pltpu.SemaphoreType.DMA((4,)), pltpu.SemaphoreType.DMA((4,))],
         compiler_params=pltpu.CompilerParams(
-            vmem_limit_bytes=60 * 2**20, collective_id=3, has_side_effects=True),
+            vmem_limit_bytes=VMEM, collective_id=3, has_side_effects=True),
         cost_estimate=pl.CostEstimate(
             flops=2 * rows * width * width + 20 * rows * width * size + 200 * rows * width,
             bytes_accessed=40 * rows * width + 2 * width * width, transcendentals=12 * rows * width),
-    )(mixed, w_mixer, thr_mixer, down_mixer, conv, inner, lift, table_d, table_a, softrate, restart, cum, local,
+    )(mixed, w_mixer, lift_mixer, down_mixer, conv, inner, lift, table_d, table_a, softrate, restart, cum, local,
       carried, pre, lift_branch, lift_input, down_gates, taps, agree)
 
 
@@ -559,7 +566,7 @@
         scratch_shapes=[pltpu.VMEM(block.shape, BF16), pltpu.SemaphoreType.DMA((6,)), pltpu.SemaphoreType.DMA((6,)),
                         pltpu.SemaphoreType.DMA((2,))] if gather else [],
         compiler_params=pltpu.CompilerParams(
-            vmem_limit_bytes=60 * 2**20, **(dict(collective_id=1, has_side_effects=True) if gather else {})),
+            vmem_limit_bytes=VMEM, **(dict(collective_id=1, has_side_effects=True) if gather else {})),
         cost_estimate=pl.CostEstimate(
             flops=2 * seqs * rows * width * units,
             bytes_accessed=2 * width * units + 2 * seqs * rows * (units + width), transcendentals=0),
@@ -630,7 +637,7 @@
                    pl.BlockSpec((rows, 2 * ranks), lambda i: (0, 0))],
         scratch_shapes=[pltpu.VMEM((rows, 2 * ranks), BF16), pltpu.VMEM((rows, steps * tile), BF16),
                         pltpu.VMEM((rows, steps * tile), BF16)],
-        compiler_params=pltpu.CompilerParams(vmem_limit_bytes=62 * 2**20),
+        compiler_params=pltpu.CompilerParams(vmem_limit_bytes=VMEM),
         cost_estimate=pl.CostEstimate(
             flops=8 * rows * width * units, bytes_accessed=8 * width * units + 6 * rows * units,
             transcendentals=rows * units),
@@ -747,7 +754,7 @@
         + [pl.BlockSpec((own, width), lambda i: (0, 0))] * reduce,
         scratch_shapes=scratch if reduce else [],
         compiler_params=pltpu.CompilerParams(
-            vmem_limit_bytes=60 * 2**20, **(dict(collective_id=2, has_side_effects=True) if reduce else {})),
+            vmem_limit_bytes=VMEM, **(dict(collective_id=2, has_side_effects=True) if reduce else {})),
         cost_estimate=pl.CostEstimate(
             flops=2 * seqs * rows * width * units,
             bytes_accessed=2 * width * units + 2 * seqs * rows * (units + width), transcendentals=0),
@@ -784,7 +791,8 @@
 
 
 def gather_kernel(units, *refs):
-    weights, wholes, staged, (send, recv, local) = refs[:4], refs[4:8], refs[8:12], refs[12:]
+    weights, passed, wholes, handed_out = refs[:4], refs[4], refs[5:9], refs[9]
+    staged, handed, (send, recv, local) = refs[10:14], refs[14], refs[15:]
     group, replica = lax.axis_index("group"), lax.axis_index("replica")
     beside, above, across = group + 1 - 2 * (group % 2), (group + 2) % 4, 3 - group
     core, level = replica % 2, (replica // 2) % 2
@@ -847,9 +855,6 @@
     def stack_piece(first, count, shard):
         return wholes[3].at[pl.ds(first, count), pl.ds(pl.multiple_of(shard * cols, cols), cols)]
 
-    stack_beside = copy(weights[3], stack_piece(0, ranks, group), last, 0, at_beside)
-    stack_above = copy(weights[3], stack_piece(0, ranks, group), last, 1, at_above)
-
     steps = [(m, part) for m in range(3) for part in range(units)]
     made = {}
 
@@ -863,13 +868,8 @@
     begin(1)
     for m in range(4):
         keep(m)
-    stack_beside.wait_recv()
-    stack_above.wait_recv()
-    half = ranks // 2
-    lower = stack_piece(0, half, above)
-    upper = stack_piece(half, half, beside)
-    stack_lower = copy(lower, lower, last, 2, at_beside)
-    stack_upper = copy(upper, upper, last, 3, at_above)
+    onward = pltpu.make_async_copy(passed, handed, local.at[4])
+    onward.start()
     for t in range(len(steps) + 2):
         if t < len(steps):
             m, part = steps[t]
@@ -881,6 +881,9 @@
             made[t, 8] = forward(m, part, beside, mine, t, 8, at_core)
             if t + 2 < len(steps):
                 begin(t + 2)
+            if t + 3 == len(steps):
+                stack_beside = copy(weights[3], stack_piece(0, ranks, group), last, 0, at_beside)
+                stack_above = copy(weights[3], stack_piece(0, ranks, group), last, 1, at_above)
             made[t, 1].wait_recv()
             made[t, 7] = forward(m, part, above, other, t, 7, at_core)
         if 1 <= t <= len(steps):
@@ -894,6 +897,17 @@
             m, part = steps[t - 2]
             made[t - 2, 5].wait_recv()
             made[t - 2, 11] = forward(m, part, across, other, t - 2, 11, at_core)
+        if t == len(steps):
+            stack_beside.wait_recv()
+            stack_above.wait_recv()
+            half = ranks // 2
+            lower = stack_piece(0, half, above)
+            upper = stack_piece(half, half, beside)
+            stack_lower = copy(lower, lower, last, 2, at_beside)
+            stack_upper = copy(upper, upper, last, 3, at_above)
+    onward.wait()
+    onward = pltpu.make_async_copy(handed, handed_out, local.at[4])
+    onward.start()
     for k in range(len(steps)):
         for slot in range(6, 12):
             made[k, slot].wait_recv()
@@ -904,31 +918,30 @@
         one.wait_recv()
     for one in (stack_beside, stack_above, stack_lower, stack_upper):
         one.wait_send()
-    for one in kept:
+    for one in kept + [onward]:
         one.wait()
 
 
-def gather_weights(w_branch, w_input, w_mixer, stack):
+def gather_weights(w_branch, w_input, w_mixer, stack, passed):
     width = w_branch.shape[0]
     if lax.axis_size("group") != 4 or lax.axis_size("replica") % 4 != 0:
         return (lax.all_gather(w_branch, "group", axis=1, tiled=True),
                 lax.all_gather(w_input, "group", axis=1, tiled=True),
                 lax.all_gather(w_mixer, "group", axis=0, tiled=True),
-                lax.all_gather(stack, "group", axis=1, tiled=True))
+                lax.all_gather(stack, "group", axis=1, tiled=True), passed)
     units = 4
-    anywhere = pl.BlockSpec(memory_space=pl.ANY)
-    operands = (w_branch, w_input, w_mixer, stack)
+    operands = (w_branch, w_input, w_mixer, stack, passed)
     return pl.pallas_call(
         functools.partial(gather_kernel, units),
         out_shape=[jax.ShapeDtypeStruct((width, width), BF16)] * 3
-        + [jax.ShapeDtypeStruct((stack.shape[0], width), BF16)],
-        in_specs=[anywhere] * 4,
-        out_specs=[anywhere] * 4,
+        + [jax.ShapeDtypeStruct((stack.shape[0], width), BF16), jax.ShapeDtypeStruct(passed.shape, passed.dtype)],
+        in_specs=[ANYWHERE] * 5,
+        out_specs=[ANYWHERE] * 5,
         scratch_shapes=[pltpu.VMEM(operand.shape, BF16) for operand in operands]
         + [pltpu.SemaphoreType.DMA((3 * units + 1, 12)), pltpu.SemaphoreType.DMA((3 * units + 1, 12)),
-           pltpu.SemaphoreType.DMA((4,))],
+           pltpu.SemaphoreType.DMA((5,))],
         compiler_params=pltpu.CompilerParams(
-            collective_id=0, has_side_effects=True, vmem_limit_bytes=60 * 2**20),
+            collective_id=0, has_side_effects=True, vmem_limit_bytes=VMEM),
         cost_estimate=pl.CostEstimate(flops=0, bytes_accessed=400 * 2**20, transcendentals=0),
     )(*operands)
 
@@ -967,67 +980,212 @@
     return (rows // step,), [pl.BlockSpec((step, width), lambda i: (i, 0))] * count
 
 
-def block_kernel(resid_ref, outward_ref, block_ref):
-    block_ref[...] = (resid_ref[...] + outward_ref[...].astype(F32)).astype(BF16)
-
-
-def block_call(resid, outward):
-    rows, width = resid.shape
-    grid, tiles = row_tiles(rows, width, 3)
-    return pl.pallas_call(
-        block_kernel,
-        grid=grid,
-        out_shape=jax.ShapeDtypeStruct((rows, width), BF16),
-        in_specs=tiles[:2],
-        out_specs=tiles[2],
-        cost_estimate=pl.CostEstimate(flops=rows * width, bytes_accessed=8 * rows * width, transcendentals=0),
-    )(resid, outward)
-
-
-def resid_grad_kernel(resid_ref, cot_ref, gain_ref, grads_ref, *refs):
-    full_ref, low_ref = refs[-2:]
+def resid_grad_kernel(per, resid_ref, cot_ref, gain_ref, *refs):
+    pieces, (full_ref, low_ref) = refs[:-2], refs[-2:]
+    grads = pieces[0][...]
+    for s, piece in enumerate(pieces[1:], 1):
+        grads = jnp.where(pl.program_id(0) >= s * per, piece[...], grads)
     values = resid_ref[...]
     rate = lax.rsqrt(jnp.mean(values * values, axis=-1, keepdims=True) + EPS)
-    grads = cot_ref[...].astype(F32) + norm_back(values, gain_ref[...], rate, grads_ref[...].astype(F32))
+    grads = cot_ref[...].astype(F32) + norm_back(values, gain_ref[...], rate, grads.astype(F32))
     full_ref[...] = grads
     low_ref[...] = grads.astype(BF16)
 
 
-def resid_grad(resid, cot, gain, grads, earlier):
+def resid_grad(resid, cot, gain, pieces):
     rows, width = resid.shape
-    grid, tiles = row_tiles(rows, width, 5)
+    step = min(pieces[0].shape[0], 128)
+    per = pieces[0].shape[0] // step
+    tile = pl.BlockSpec((step, width), lambda i: (i, 0))
     return pl.pallas_call(
-        resid_grad_kernel,
-        grid=grid,
+        functools.partial(resid_grad_kernel, per),
+        grid=(rows // step,),
         out_shape=[jax.ShapeDtypeStruct((rows, width), F32), jax.ShapeDtypeStruct((rows, width), BF16)],
-        in_specs=[tiles[0], tiles[0], pl.BlockSpec((1, width), lambda i: (0, 0)), tiles[0]]
-        + [ANYWHERE] * len(earlier),
-        out_specs=tiles[:2],
-        compiler_params=pltpu.CompilerParams(vmem_limit_bytes=40 * 2**20),
+        in_specs=[tile, tile, pl.BlockSpec((1, width), lambda i: (0, 0))] + [
+            pl.BlockSpec((step, width), lambda i, s=s: (jnp.clip(i - s * per, 0, per - 1), 0))
+            for s in range(len(pieces))],
+        out_specs=[tile, tile],
+        compiler_params=pltpu.CompilerParams(vmem_limit_bytes=VMEM),
         cost_estimate=pl.CostEstimate(
             flops=20 * rows * width, bytes_accessed=14 * rows * width, transcendentals=rows),
-    )(resid, cot, gain, grads, *earlier)
-
-
-def finish_kernel(grad_resid_ref, inputs_ref, gain_ref, grads_ref, out_ref):
+    )(resid, cot, gain, *pieces)
+
+
+def finish_kernel(grad_resid_ref, inputs_ref, gain_ref, grads_ref, resid_ref, outward_ref, out_ref, block_ref):
     values = inputs_ref[...].astype(F32)
     rate = lax.rsqrt(jnp.mean(values * values, axis=-1, keepdims=True) + EPS)
     out_ref[...] = grad_resid_ref[...] + norm_back(values, gain_ref[...], rate, grads_ref[...])
-
-
-def finish(grad_resid, inputs, gain, grads):
+    block_ref[...] = (resid_ref[...] + outward_ref[...].astype(F32)).astype(BF16)
+
+
+def finish(grad_resid, inputs, gain, grads, resid, outward):
     rows, width = inputs.shape
-    grid, tiles = row_tiles(rows, width, 3)
+    grid, tiles = row_tiles(rows, width, 5)
     return pl.pallas_call(
         finish_kernel,
         grid=grid,
-        out_shape=jax.ShapeDtypeStruct((rows, width), F32),
-        in_specs=[tiles[0], tiles[0], pl.BlockSpec((1, width), lambda i: (0, 0)), tiles[0]],
-        out_specs=tiles[0],
-        compiler_params=pltpu.CompilerParams(vmem_limit_bytes=40 * 2**20),
+        out_shape=[jax.ShapeDtypeStruct((rows, width), F32), jax.ShapeDtypeStruct((rows, width), BF16)],
+        in_specs=tiles[:2] + [pl.BlockSpec((1, width), lambda i: (0, 0))] + tiles[:3],
+        out_specs=tiles[:2],
+        compiler_params=pltpu.CompilerParams(vmem_limit_bytes=VMEM),
         cost_estimate=pl.CostEstimate(
-            flops=20 * rows * width, bytes_accessed=14 * rows * width, transcendentals=rows),
-    )(grad_resid, inputs, gain, grads)
+            flops=21 * rows * width, bytes_accessed=22 * rows * width, transcendentals=rows),
+    )(grad_resid, inputs, gain, grads, resid, outward)
+
+
+def tail_kernel(
+    steps, branch_grad_ref, fed_grad_ref, w_branch_ref, w_input_ref, through_ref, down_ref, partial_ref,
+    out_ref, got_ref, first_a, first_b, second_a, second_b, pass_a, pass_b, own_ref, send, recv, up_send, low_recv,
+    down_send, high_recv, core_send, core_recv, local,
+):
+    step = pl.program_id(0)
+    group, replica = lax.axis_index("group"), lax.axis_index("replica")
+    beside, above, across = group + 1 - 2 * (group % 2), (group + 2) % 4, 3 - group
+    at_beside, at_above = (beside, replica), (above, replica)
+    count = got_ref.shape[0]
+    levels = count // 2
+    core, level = replica % 2, replica // 2
+    at_core = (group, replica + 1 - 2 * core)
+    at_up, at_down = (group, (replica + 2) % count), (group, (replica + count - 2) % count)
+    rows = own_ref.shape[0]
+    half = rows // 2
+
+    def part(owner, side):
+        return partial_ref.at[owner, pl.ds(side * half, half), :]
+
+    def copy(src, dst, send_sem, recv_sem, partner):
+        return pltpu.make_async_remote_copy(
+            src_ref=src, dst_ref=dst, send_sem=send_sem, recv_sem=recv_sem, device_id=partner,
+            device_id_type=pl.DeviceIdType.MESH)
+
+    pairs = [(part(across, 0), first_a.at[1], at_beside), (part(across, 1), first_b.at[1], at_above),
+             (part(beside, 0), first_a.at[0], at_beside), (part(above, 1), first_b.at[0], at_above),
+             (pass_a, second_a, at_above), (pass_b, second_b, at_beside)]
+    moves = [copy(src, dst, send.at[slot], recv.at[slot], partner) for slot, (src, dst, partner) in enumerate(pairs)]
+    firsts, seconds = moves[:4], moves[4:]
+    loads = [pltpu.make_async_copy(part(above, 0), pass_a, local.at[0]),
+             pltpu.make_async_copy(part(beside, 1), pass_b, local.at[1]),
+             pltpu.make_async_copy(partial_ref.at[group], own_ref, local.at[2])]
+
+    @pl.when(step == 0)
+    def _():
+        barrier = pltpu.get_barrier_semaphore()
+
+        def greet(partner):
+            pl.semaphore_signal(barrier, inc=1, device_id=partner, device_id_type=pl.DeviceIdType.MESH)
+
+        for partner in (at_beside, at_above, at_core):
+            greet(partner)
+
+        @pl.when(level > 0)
+        def _():
+            greet(at_down)
+
+        @pl.when(level < levels - 1)
+        def _():
+            greet(at_up)
+
+        ends = (level + levels - 1) // levels + (2 * levels - 2 - level) // levels
+        pl.semaphore_wait(barrier, 3 + ends)
+        for one in firsts + loads:
+            one.start()
+
+    out_ref[...] = (dot(branch_grad_ref[...], w_branch_ref[...], NT) + dot(fed_grad_ref[...], w_input_ref[...], NT)
+                    + dot(through_ref[...], down_ref[...]))
+
+    @pl.when(step == max(steps - 2, 0))
+    def _():
+        for one in loads:
+            one.wait()
+        for one in firsts:
+            one.wait_recv()
+        pass_a[...] = (pass_a[...].astype(F32) + first_a[1].astype(F32)).astype(BF16)
+        pass_b[...] = (pass_b[...].astype(F32) + first_b[1].astype(F32)).astype(BF16)
+        for one in seconds:
+            one.start()
+
+    @pl.when(step == steps - 1)
+    def _():
+        for one in seconds:
+            one.wait_recv()
+        own_ref[:half] = (own_ref[:half].astype(F32) + first_a[0].astype(F32) + second_a[...].astype(F32)).astype(BF16)
+        own_ref[half:] = (own_ref[half:].astype(F32) + first_b[0].astype(F32) + second_b[...].astype(F32)).astype(BF16)
+        keep = pltpu.make_async_copy(own_ref, got_ref.at[replica], local.at[3])
+        keep.start()
+
+        def piece(source):
+            return got_ref.at[(source + count) % count]
+
+        to_up = [copy(own_ref, piece(replica), up_send.at[0], low_recv.at[0], at_up)]
+        to_down = [copy(own_ref, piece(replica), down_send.at[0], high_recv.at[0], at_down)]
+        to_core = [copy(own_ref, piece(replica), core_send.at[0], core_recv.at[0], at_core)]
+        has_up, has_down = level < levels - 1, level > 0
+
+        def when(condition, action):
+            pl.when(condition)(action)
+
+        when(has_up, to_up[0].start)
+        when(has_down, to_down[0].start)
+        to_core[0].start()
+        for d in range(1, levels):
+            low, high = piece(replica - 2 * d), piece(replica + 2 * d)
+            to_up.append(copy(low, low, up_send.at[d], low_recv.at[d], at_up))
+            to_down.append(copy(high, high, down_send.at[d], high_recv.at[d], at_down))
+            core_low = copy(low, low, core_send.at[2 * d - 1], core_recv.at[2 * d - 1], at_core)
+            core_high = copy(high, high, core_send.at[2 * d], core_recv.at[2 * d], at_core)
+            to_core += [core_low, core_high]
+            from_low, from_high = level >= d, level + d < levels
+
+            @pl.when(from_low)
+            def _(d=d, core_low=core_low):
+                to_up[d - 1].wait_recv()
+                when(has_up, to_up[d].start)
+                core_low.start()
+
+            @pl.when(from_high)
+            def _(d=d, core_high=core_high):
+                to_down[d - 1].wait_recv()
+                when(has_down, to_down[d].start)
+                core_high.start()
+
+        to_core[0].wait()
+        when(has_up, to_up[0].wait_send)
+        when(has_down, to_down[0].wait_send)
+        for d in range(1, levels):
+            when(level >= d, to_core[2 * d - 1].wait)
+            when(level + d < levels, to_core[2 * d].wait)
+            when((level >= d) & has_up, to_up[d].wait_send)
+            when((level + d < levels) & has_down, to_down[d].wait_send)
+        for one in firsts + seconds:
+            one.wait_send()
+        keep.wait()
+
+
+def tail_call(branch_grad, fed_grad, w_branch, w_input, through, down, partial):
+    rows, width = branch_grad.shape
+    ranks, cols = partial.shape[1:]
+    count = lax.axis_size("replica")
+    levels = count // 2
+    tile = tile_of(width, 512)
+    steps = pl.cdiv(width, tile)
+    weight = pl.BlockSpec((tile, width), lambda i: (i, 0))
+    half = ranks // 2
+    dma = pltpu.SemaphoreType.DMA
+    return pl.pallas_call(
+        functools.partial(tail_kernel, steps),
+        grid=(steps,),
+        out_shape=[jax.ShapeDtypeStruct((rows, width), F32), jax.ShapeDtypeStruct((count, ranks, cols), BF16)],
+        in_specs=[resident(branch_grad), resident(fed_grad), weight, weight, resident(through),
+                  pl.BlockSpec((down.shape[0], tile), lambda i: (0, i)), ANYWHERE],
+        out_specs=[pl.BlockSpec((rows, tile), lambda i: (0, i)), ANYWHERE],
+        scratch_shapes=[pltpu.VMEM((2, half, cols), BF16)] * 2 + [pltpu.VMEM((half, cols), BF16)] * 4
+        + [pltpu.VMEM((ranks, cols), BF16), dma((6,)), dma((6,)), dma((levels,)), dma((levels,)), dma((levels,)),
+           dma((levels,)), dma((count,)), dma((count,)), dma((4,))],
+        compiler_params=pltpu.CompilerParams(
+            vmem_limit_bytes=VMEM, collective_id=4, has_side_effects=True),
+        cost_estimate=pl.CostEstimate(
+            flops=4 * rows * width * width, bytes_accessed=4 * width * width + 8 * rows * width, transcendentals=0),
+    )(branch_grad, fed_grad, w_branch, w_input, through, down, partial)
 
 
 def spread_kernel(tables, pieces, ids_ref, from_ref, *refs):
@@ -1106,7 +1264,7 @@
         in_specs=specs + [ANYWHERE] * len(earlier),
         out_specs=(pl.BlockSpec((None, total, tile), lambda i: (i, 0, 0)) if direct
                    else pl.BlockSpec((total, tile), lambda i: (0, i))),
-        compiler_params=pltpu.CompilerParams(vmem_limit_bytes=60 * 2**20),
+        compiler_params=pltpu.CompilerParams(vmem_limit_bytes=VMEM),
         cost_estimate=pl.CostEstimate(flops=64 * cells, bytes_accessed=2 * cells, transcendentals=0),
     )(*operands, *earlier)
     if blocks > 1 and not direct:
@@ -1157,13 +1315,14 @@
          turned(down_gate), turned(down_upper), lift_branch, lift_input, lift_decay, lift_admit, lift_mixer,
          lift_outward],
         [lift_gate, lift_upper, turned(down_outward)])
-    full_branch, full_input, full_mixer, stack = gather_weights(w_branch, w_input, w_mixer, stack)
+    full_branch, full_input, full_mixer, stack, late_grad = gather_weights(
+        w_branch, w_input, w_mixer, stack, out_grad)
     (p_down_branch, p_down_input, p_down_decay, p_down_admit, p_down_mixer, p_down_gate, p_down_upper,
      p_lift_branch, p_lift_input, p_lift_decay, p_lift_admit, p_lift_mixer, p_lift_outward) = [
         stack[i * mask_cols : (i + 1) * mask_cols] for i in range(13)]
     own_lift_gate, own_lift_upper, own_down_outward = [
         own_tables[i * mask_cols : (i + 1) * mask_cols] for i in range(3)]
-    cotangents = lax.all_gather(ordered(out_grad, stack), "group", axis=1, tiled=True)
+    cotangents = lax.all_gather(late_grad, "group", axis=1, tiled=True)
 
     row_seq = lax.broadcasted_iota(jnp.int32, (rows, mask_cols), 0) // stretch
     col_seq = lax.broadcasted_iota(jnp.int32, (rows, mask_cols), 1) // ranks
@@ -1238,20 +1397,18 @@
                                                                                    wides[0].shape[1]))
     wide = jnp.concatenate(
         [wides[s][i * ranks : (i + 1) * ranks] for i in range(3) for s in range(seqs)] + [named], 0)
-    grad_normed_two = jnp.concatenate(backs, 0)
     grad_resid, grad_mixed = resid_grad(
-        resid, out_grad.reshape(rows, width), gain_mlp.reshape(1, width), grad_normed_two, ())
+        resid, out_grad.reshape(rows, width), gain_mlp.reshape(1, width), backs)
     outward = lax.psum_scatter(outward, "group", scatter_dimension=1, tiled=True).reshape(rows, width)
-    block_out = block_call(resid, outward)
-
-    through_mixer = (dot(grad_mixed, p_lift_mixer, NT) * own).astype(BF16)
+
     if group == 4 and 2 * seqs <= 8 and stretch % 8 == 0:
         agree_cols = jnp.stack([agree[j][:, j : j + stretch].reshape(rows) for j in range(taps)], 1)
-        grad_branch_pre, through_one, through_gates, grad_lift_gates, grad_fed = mixer_back(
-            seqs, grad_mixed, full_mixer, through_mixer, p_down_mixer, convolved, inner_gates, lift_gates, decay_heads,
+        grad_branch_pre, through_one, through_gates, grad_lift_gates, grad_fed, through_mixer = mixer_back(
+            seqs, grad_mixed, full_mixer, p_lift_mixer, p_down_mixer, convolved, inner_gates, lift_gates, decay_heads,
             admit_heads, softrate, restart, cum, local, carried, branch_pre, p_lift_branch, p_lift_input,
             stack[2 * mask_cols : 4 * mask_cols], conv_taps, agree_cols)
     else:
+        through_mixer = (dot(grad_mixed, p_lift_mixer, NT) * own).astype(BF16)
         grad_merged = dot(grad_mixed, full_mixer, NT) + dot(through_mixer, p_down_mixer)
         span, total, firsts, grad_branch_pre = backward_scan(
             seqs, convolved, inner_gates, lift_gates, decay_heads, softrate, restart, cum, local, carried, branch_pre,
@@ -1276,10 +1433,6 @@
         through_branch = (dot(grad_branch_pre, p_lift_branch, NT) * own).astype(BF16)
         through_input = (dot(grad_fed, p_lift_input, NT) * own).astype(BF16)
         through_one = jnp.concatenate([through_branch, through_input], 1)
-    grad_normed = (dot(grad_branch_pre, full_branch, NT) + dot(grad_fed, full_input, NT)
-                   + dot(through_one, stack[: 2 * mask_cols]))
-    grad_inputs = finish(grad_resid, inputs.reshape(rows, width), gain_mix.reshape(1, width), grad_normed)
-
     all_wide, wide_source = over_replicas(wide, True, through_gates)
     both = 2 * mask_cols
     got_ids = jnp.concatenate([part[:, 3 * mask_cols : 3 * mask_cols + seqs, 0] for part in all_wide], 0)
@@ -1288,11 +1441,20 @@
     partial = products(
         [(through_one, 0, both, normed), (through_gates, 0, both, rounded), (through_mixer, 0, mask_cols, merged),
          (inner_branch, 0, mask_cols, grad_branch_pre), (inner_input, 0, mask_cols, grad_fed), (grad_lift_gates,),
-         (inner_mixer, 0, mask_cols, grad_mixed), (early,)], all_wide, group)
-    owned = lax.psum_scatter(ordered(partial, outward), "group", scatter_dimension=0, tiled=False)
+         (inner_mixer, 0, mask_cols, grad_mixed), (early,)], (), group)
+    if group == 4 and lax.axis_size("replica") % 2 == 0 and partial.shape[1] % 32 == 0:
+        grad_normed, got = tail_call(
+            grad_branch_pre, grad_fed, full_branch, full_input, through_one, stack[:both], partial)
+        all_owned, owned_source = [got], jnp.arange(lax.axis_size("replica"), dtype=jnp.int32)
+    else:
+        grad_normed = (dot(grad_branch_pre, full_branch, NT) + dot(grad_fed, full_input, NT)
+                       + dot(through_one, stack[:both]))
+        owned = lax.psum_scatter(partial, "group", scatter_dimension=0, tiled=False)
+        all_owned, owned_source = over_replicas(owned, False)
+    grad_inputs, block_out = finish(
+        grad_resid, inputs.reshape(rows, width), gain_mix.reshape(1, width), grad_normed, resid, outward)
     wides = spread(all_ids, wide_source, all_wide, 3, sets, seqs, ranks)
-    all_owned, owned_source = over_replicas(ordered(owned, grad_normed), False)
-    totals = spread(all_ids, owned_source, all_owned, 13, sets, seqs, ranks, (block_out, wides[0], grad_inputs))
+    totals = spread(all_ids, owned_source, all_owned, 13, sets, seqs, ranks)
     (t_down_branch, t_down_input, t_down_decay, t_down_admit, t_down_mixer, t_lift_branch, t_lift_input, t_lift_decay,
      t_lift_admit, t_lift_mixer, t_down_gate, t_down_upper, t_lift_outward) = totals
     return (

time: 735 us -> 696 us (0.947)
  Pallas kernels: 505 us -> 567 us
  waiting for transfers between devices: 59.3 us -> 0.09 us
  matrix products: 79 us -> 50.7 us
  local copies, waits for them, and re-layouts: 34.5 us -> 20.9 us
    pallas_call x3, Pallas kernels: 14.4 us -> 86.9 us  [the longest x1 66.9 us: tail_call(): pl.pallas_call(functools.partial(tail_kernel, steps), grid=(steps,), out_...]
    all_gather x2 -> x1, waiting for transfers between devices: 48.5 us -> 0.01 us  [body(): cotangents = lax.all_gather(late_grad, 'group', axis=1, tiled=True)]
    dot_general x13 -> x9, matrix products: 79 us -> 50.7 us  [dot(): return lax.dot_general(a, b, dims, preferred_element_type=F32)]
    unnamed x143 -> x118, local copies, waits for them, and re-layouts: 21.4 us -> 6.39 us
    pallas_call x1, Pallas kernels: 143 us -> 133 us  [gather_weights(): pl.pallas_call(functools.partial(gather_kernel, units), out_shape=[jax.Sh...]
    unnamed x7 -> x4, waiting for transfers between devices: 7.67 us -> 0.07 us
  transfers between devices with their start and end apart: 12 -> 9, of which waited for: 4 -> 0; matrix products, arithmetic and copies ran while one was open for 15% -> 12% of each run, Pallas kernels for 42% -> 54%
where the time goes in v5:
time: 696 us; the launch traced here: 689 us
  Pallas kernels  567 us (81%)
  matrix products  50.7 us (7%)
  local copies, waits for them, and re-layouts  20.9 us (3%)
  other arithmetic  15.2 us (2%)
  between operations  15 us (2%)
  blocking collectives  10.1 us (1%)
  starting transfers between devices  9.36 us (1%)
    pallas_call x1, Pallas kernels, gather_weights(): pl.pallas_call(functools.partial(gather_kernel, units), out_shape=[jax.Sh...  133 us
    pallas_call x2, Pallas kernels, feed_call(): pl.pallas_call(functools.partial(feed_kernel, steps, tile, units), grid=(...  126 us
    pallas_call x1, Pallas kernels, mixer_back(): pl.pallas_call(functools.partial(mixer_back_kernel, seqs, heads), grid=(3...  78.3 us
    pallas_call x1, Pallas kernels, tail_call(): pl.pallas_call(functools.partial(tail_kernel, steps), grid=(steps,), out_...  66.9 us
    pallas_call x1, Pallas kernels, outward_call(): pl.pallas_call(functools.partial(outward_kernel, seqs, reduce, steps), gr...  52 us
    dot_general x9, matrix products, dot(): return lax.dot_general(a, b, dims, preferred_element_type=F32)  50.7 us
    pallas_call x1, Pallas kernels, grad_hidden_call(): pl.pallas_call(functools.partial(grad_hidden_kernel, seqs, gather, pl.cdi...  50.5 us
    pallas_call x1, Pallas kernels, forward_gates(): pl.pallas_call(functools.partial(forward_gates_kernel, seqs), out_shape=(...  16.7 us
  transfers between devices with their start and end apart: 9, of which 0 were waited for; matrix products, arithmetic and copies ran while one was open for 12% of the time, Pallas kernels for 54%

profile of v5, /device:TPU:0, one launch (start us, length us, event | category | flops | bytes accessed | tf_op | source)
XLA Modules:
  0.0 688.7 jit_solution(7311549164691304466)
XLA Ops:
  7.2 3.0 shard_map.439
  10.2 133.1 %shard_map.440 = (bf16[2560,2560]{1,0:T(8,128)(2,1)}, bf16[2560,2560]{1,0:T(8,128)(2,1)}, bf16[2560,2560]{1,0:T(8,128)(2,1)}, bf16[416,2560]{1,0:T(8,128)(2,1)}, bf16[2,256,2560]{2,1,0:T(8,128)(2,1)}) custom-call(bf16[2560,640]{1,0:T(8,128)(2,1)} %refs_0_.1, bf16[2560,640]{1,0:T(8,128)(2,1)} %refs_1_.2, bf16[640,2560]{1,0:T(8,128)(2,1)} %refs_2_.1, ...), custom_call_target="tpu_custom_call" | custom-call | bytes 419430400 | tf_op jit(solution)/shard_map/pallas_call | solution.py:934
  143.6 2.5 multiply_reduce_fusion.1
  147.1 2.0 fusion.13
  149.2 11.3 %fusion.41 = f32[512,2560]{1,0:T(8,128)S(1)} fusion(bf16[512,2560]{1,0:T(8,128)(2,1)S(1)} %fusion.1.refs_1_, bf16[2560,2560]{1,0:T(8,128)(2,1)} %get-tuple-element.70.w_input_ref), kind=kOutput, calls=%fused_computation.121 | convolution fusion | flops 6710886400 | bytes 20971520 | tf_op jit(solution)/shard_map/dot_general | solution.py:23
  163.8 3.4 collective-permute-start
  169.3 2.1 fusion.38
  171.4 2.1 fusion.37
  173.5 12.4 %fusion.42 = f32[512,2560]{1,0:T(8,128)} fusion(bf16[512,2560]{1,0:T(8,128)(2,1)} %copy-done.12, bf16[2560,2560]{1,0:T(8,128)(2,1)} %get-tuple-element.74.w_branch_ref), kind=kOutput, calls=%fused_computation.122 | convolution fusion | flops 6710886400 | bytes 20971520 | tf_op jit(solution)/shard_map/dot_general | solution.py:23
  187.8 2.5 maximum_convert_fusion
  190.3 5.3 fusion.8
  196.0 3.3 fusion.14.inner_ref
  199.7 16.7 %shard_map.441 = (f32[512,2560]{1,0:T(8,128)S(1)}, f32[512,2560]{1,0:T(8,128)S(1)}) custom-call(f32[512,2560]{1,0:T(8,128)} %bitcast.131, bf16[512,64]{1,0:T(8,128)(2,1)S(1)} %fusion.14.inner_ref, bf16[64,2560]{1,0:T(8,128)(2,1)S(1)} %get-tuple-element.127.lift_ref, bf16[10,256,256]{2,1,0:T(8,128)(2,1)S(1)} %copy-done.5, ...), custom_call_target="tpu_custom_call" | custom-call | flops 1420820480 | bytes 15728640 | tf_op jit(solution)/shard_map/pallas_call | solution.py:108
  216.5 10.1 %all-gather.1 = f32[4,4,2560]{2,1,0:T(4,128)S(1)} all-gather(f32[1,4,2560]{2,1,0:T(4,128)S(1)} %maximum_bitcast_fusion), channel_id=2, replica_groups=mesh['group'=4,'replica'=8] {'group'}, dimensions={0}, use_global_device_ids=true | all-gather | bytes 204800 | tf_op jit(solution)/shard_map/all_gather | solution.py:1363
  226.7 5.9 fusion.7
  232.7 1.9 fusion.12.refs_11_
  234.6 10.0 %fusion.43 = f32[512,2560]{1,0:T(8,128)S(1)} fusion(bf16[512,2560]{1,0:T(8,128)(2,1)S(1)} %get-tuple-element.157.refs_5_, bf16[2560,2560]{1,0:T(8,128)(2,1)} %get-tuple-element.75.w_ref), kind=kOutput, calls=%fused_computation.123 | convolution fusion | flops 6710886400 | bytes 20971520 | tf_op jit(solution)/shard_map/dot_general | solution.py:23
  244.7 2.2 multiply_reduce_fusion
  246.9 2.3 copy-done.8
  251.4 50.5 %shard_map.442 = (bf16[2,1024,1920]{2,1,0:T(8,128)(2,1)}, bf16[2,1024,16]{2,1,0:T(8,128)(2,1)}, bf16[1024,2560]{1,0:T(8,128)(2,1)}) custom-call(bf16[2,1024,2560]{2,1,0:T(8,128)(2,1)} %all-gather.5.cloned.1.call-done.refs_0_.refs_6_, bf16[1920,2560]{1,0:T(8,128)(2,1)} %refs_7_.3, bf16[32,2560]{1,0:T(8,128)(2,1)} %get-tuple-element.130.refs_2_.refs_9_, ...), custom_call_target="tpu_custom_call" | custom-call | flops 20132659200 | bytes 28180480 | tf_op jit(solution)/shard_map/pallas_call | solution.py:556
  304.8 63.4 %shard_map.443 = (bf16[1024,1920]{1,0:T(8,128)(2,1)}, bf16[1024,2560]{1,0:T(8,128)(2,1)}, bf16[48,1920]{1,0:T(8,128)(2,1)}, bf16[1024,32]{1,0:T(8,128)(2,1)}) custom-call(bf16[1024,2560]{1,0:T(8,128)(2,1)} %get-tuple-element.78.tok_ref.refs_1_.refs_2_, bf16[2,1024,1920]{2,1,0:T(8,128)(2,1)} %get-tuple-element.79.gh_ref, bf16[2560,1920]{1,0:T(8,128)(2,1)} %wg_rows_ref.3, ...), custom_call_target="tpu_custom_call" | custom-call | flops 40265318400 | bytes 51118080 | tf_op jit(solution)/shard_map/pallas_call | solution.py:627
  369.0 62.5 %shard_map.445 = (bf16[1024,1920]{1,0:T(8,128)(2,1)}, bf16[1024,2560]{1,0:T(8,128)(2,1)}, bf16[48,1920]{1,0:T(8,128)(2,1)}, bf16[1024,32]{1,0:T(8,128)(2,1)}) custom-call(bf16[1024,2560]{1,0:T(8,128)(2,1)} %all-gather.7.cloned.1.call-done.tok_ref.refs_3_, bf16[2,1024,1920]{2,1,0:T(8,128)(2,1)} %get-tuple-element.79.gh_ref, bf16[2560,1920]{1,0:T(8,128)(2,1)} %wg_rows_ref.3, ...), custom_call_target="tpu_custom_call" | custom-call | flops 40265318400 | bytes 51118080 | tf_op jit(solution)/shard_map/pallas_call | solution.py:627
  431.6 52.0 %shard_map.446 = (bf16[2,1024,2560]{2,1,0:T(8,128)(2,1)}, bf16[2,1024,16]{2,1,0:T(8,128)(2,1)}, bf16[96,2560]{1,0:T(8,128)(2,1)}, bf16[256,2560]{1,0:T(8,128)(2,1)}) custom-call(bf16[1024,1920]{1,0:T(8,128)(2,1)} %get-tuple-element.82.refs_0_, bf16[1024,1920]{1,0:T(8,128)(2,1)} %get-tuple-element.83.refs_1_, ...), custom_call_target="tpu_custom_call" | custom-call | flops 20132659200 | bytes 28180480 | tf_op jit(solution)/shard_map/pallas_call | solution.py:741
  487.7 2.4 collective-permute-start.2
  491.4 8.7 %shard_map.447 = (f32[512,2560]{1,0:T(8,128)}, bf16[512,2560]{1,0:T(8,128)(2,1)}) custom-call(f32[512,2560]{1,0:T(8,128)} %copy-done.8, bf16[512,2560]{1,0:T(8,128)(2,1)} %bitcast.135, f32[1,2560]{1,0:T(1,128)} %reshape.186.gain_ref, bf16[256,2560]{1,0:T(8,128)(2,1)} %reduce-scatter.3.cloned.1.call-done.refs_0_, bf16[256,2560]{1,0:T(8,128)(2,1)} %get-tuple-element.87.refs_1_), custom_call_target="tpu_custom_call" | custom-call | flops 26214400 | bytes 18350080 | tf_op jit(solution)/shard_map/pallas_call | solution.py:1000
  500.1 78.3 %shard_map.448 = (bf16[512,2560]{1,0:T(8,128)(2,1)}, bf16[512,64]{1,0:T(8,128)(2,1)}, bf16[512,64]{1,0:T(8,128)(2,1)}, f32[64,2560]{1,0:T(8,128)}, bf16[512,2560]{1,0:T(8,128)(2,1)}, /*index=5*/bf16[512,32]{1,0:T(8,128)(2,1)}) custom-call(bf16[512,2560]{1,0:T(8,128)(2,1)} %get-tuple-element.89.mixed_ref.refs_12_, ...), custom_call_target="tpu_custom_call" | custom-call | flops 13683916800 | bytes 65536000 | tf_op jit(solution)/shard_map/pallas_call | solution.py:432
  579.5 2.7 shard_map.452.refs_0_
  583.9 9.4 %shard_map.449.partial_ref = bf16[4,416,640]{2,1,0:T(8,128)(2,1)} custom-call(bf16[512,64]{1,0:T(8,128)(2,1)} %get-tuple-element.92.refs_0_.through_ref, bf16[512,2560]{1,0:T(8,128)(2,1)} %copy-done.12, bf16[512,64]{1,0:T(8,128)(2,1)} %get-tuple-element.93.refs_2_.refs_4_, bf16[512,2560]{1,0:T(8,128)(2,1)} %copy-done.13, ...), custom_call_target="tpu_custom_call" | custom-call | flops 537919488 | bytes 16809984 | tf_op jit(solution)/shard_map/pallas_call | solution.py:1260
  593.3 66.9 %shard_map.450 = (f32[512,2560]{1,0:T(8,128)}, bf16[8,416,640]{2,1,0:T(8,128)(2,1)}) custom-call(bf16[512,2560]{1,0:T(8,128)(2,1)} %get-tuple-element.90.refs_7_.branch_grad_ref, bf16[512,2560]{1,0:T(8,128)(2,1)} %get-tuple-element.91.refs_9_.fed_grad_ref, bf16[2560,2560]{1,0:T(8,128)(2,1)} %get-tuple-element.74.w_branch_ref, ...), custom_call_target="tpu_custom_call" | custom-call | flops 13421772800 | bytes 36700160 | tf_op jit(solution)/shard_map/pallas_call | solution.py:1174
  661.4 4.0 shard_map.454
  665.9 4.7 shard_map.453
  670.6 11.3 %shard_map.451 = (f32[512,2560]{1,0:T(8,128)}, bf16[512,2560]{1,0:T(8,128)(2,1)}) custom-call(f32[512,2560]{1,0:T(8,128)} %get-tuple-element.88.grad_resid_ref, bf16[512,2560]{1,0:T(8,128)(2,1)} %bitcast.129, f32[1,2560]{1,0:T(1,128)} %broadcast_in_dim.23.gain_ref, f32[512,2560]{1,0:T(8,128)} %get-tuple-element.97.grads_ref, f32[512,2560]{1,0:T(8,128)} %copy-done.8, ...), custom_call_target="tpu_custom_call" | custom-call | flops 27525120 | bytes 28835840 | tf_op jit(solution)/shard_map/pallas_call | solution.py:1024
  (186 shorter events, 24.8 us)
Async XLA Ops:
  7.2 244.2 %all-gather.5.cloned.1.call-start = ((), (), s32[]{:S(2)}) async-start(), calls=%async_computation.2 | async-start | bytes 13107200 | tf_op jit(solution)/shard_map/all_gather | solution.py:1325
  143.4 225.6 %all-gather.7.cloned.1.call-start = ((), (), s32[]{:S(2)}) async-start(), calls=%async_computation.4 | async-start | bytes 6553600 | tf_op jit(solution)/shard_map/all_gather | solution.py:1381
  147.1 13.4 %copy-start.12 = (bf16[512,2560]{1,0:T(8,128)(2,1)}, bf16[512,2560]{1,0:T(8,128)(2,1)S(1)}, u32[]{:S(2)}) copy-start(bf16[512,2560]{1,0:T(8,128)(2,1)S(1)} %fusion.1.refs_1_) | copy-start | bytes 7864324
  149.2 77.5 %copy-start.15 = (bf16[512,64]{1,0:T(8,128)(2,1)}, bf16[512,64]{1,0:T(8,128)(2,1)S(1)}, u32[]{:S(2)}) copy-start(bf16[512,64]{1,0:T(8,128)(2,1)S(1)} %fusion.13) | copy-start | bytes 196612
  160.5 6.8 copy-start.38
  160.5 8.8 %copy-start.31 = (f32[2560]{0:T(1024)S(1)}, f32[2560]{0:T(1024)}, u32[]{:S(2)}) copy-start(f32[2560]{0:T(1024)} %param.42) | copy-start | bytes 30724
  163.8 24.0 %collective-permute-start = (bf16[2,3,2560]{2,1,0:T(4,128)(2,1)S(1)}, bf16[2,3,2560]{2,1,0:T(4,128)(2,1)S(1)}, u32[]{:S(2)}, u32[]{:S(2)}) collective-permute-start(bf16[2,3,2560]{2,1,0:T(4,128)(2,1)S(1)} %slice.275), channel_id=1, source_target_pairs={{0,8},{8,16},{16,24},{1,9},{9,17},{17,25},{2,10},{10,18},{18,26},{... | collective-permute-start | bytes 92168 | tf_op jit(solution)/shard_map/ppermute | solution.py:1278
  173.5 25.8 %copy-start.2 = (bf16[64,2560]{1,0:T(8,128)(2,1)}, bf16[64,2560]{1,0:T(8,128)(2,1)S(1)}, u32[]{:S(2)}) copy-start(bf16[64,2560]{1,0:T(8,128)(2,1)S(1)} %get-tuple-element.127.lift_ref) | copy-start | bytes 983044
  173.5 12.4 %copy-start.30 = (f32[4,2560]{1,0:T(4,128)S(1)}, f32[4,2560]{1,0:T(4,128)}, u32[]{:S(2)}) copy-start(f32[4,2560]{1,0:T(4,128)} %taps_ref.1) | copy-start | bytes 122884
  186.0 13.3 %copy-start.4 = (f32[1,2560]{1,0:T(1,128)}, f32[1,2560]{1,0:T(1,128)S(1)}, u32[]{:S(2)}) copy-start(f32[1,2560]{1,0:T(1,128)S(1)} %reshape.180.soft_ref) | copy-start | bytes 30724
  186.1 13.2 %copy-start.3 = (f32[1,512]{0,1:T(8,128)}, f32[1,512]{0,1:T(8,128)S(1)}, u32[]{:S(2)}) copy-start(f32[1,512]{0,1:T(8,128)S(1)} %copy.98) | copy-start | bytes 6148
  196.0 20.4 %copy-start.13 = (bf16[512,2560]{1,0:T(8,128)(2,1)}, bf16[512,2560]{1,0:T(8,128)(2,1)S(1)}, u32[]{:S(2)}) copy-start(bf16[512,2560]{1,0:T(8,128)(2,1)S(1)} %bitcast_convert_fusion.refs_3_) | copy-start | bytes 7864324
  199.3 17.1 %copy-start.7 = (bf16[512,64]{1,0:T(8,128)(2,1)}, bf16[512,64]{1,0:T(8,128)(2,1)S(1)}, u32[]{:S(2)}) copy-start(bf16[512,64]{1,0:T(8,128)(2,1)S(1)} %fusion.14.inner_ref) | copy-start | bytes 196612
  216.3 16.3 %copy-start = (f32[512,2560]{1,0:T(8,128)}, f32[512,2560]{1,0:T(8,128)S(1)}, u32[]{:S(2)}) copy-start(f32[512,2560]{1,0:T(8,128)S(1)} %get-tuple-element.73.cum_ref) | copy-start | bytes 15728644
  216.4 16.2 %copy-start.1 = (f32[512,2560]{1,0:T(8,128)}, f32[512,2560]{1,0:T(8,128)S(1)}, u32[]{:S(2)}) copy-start(f32[512,2560]{1,0:T(8,128)S(1)} %get-tuple-element.72.local_ref) | copy-start | bytes 15728644
  226.7 5.9 copy-start.34
  226.7 5.9 copy-start.36
  226.7 5.9 copy-start.42
  226.7 5.9 copy-start.44
  226.7 5.9 copy-start.46
  226.7 5.9 copy-start.48
  232.6 12.1 %copy-start.14 = (bf16[512,2560]{1,0:T(8,128)(2,1)}, bf16[512,2560]{1,0:T(8,128)(2,1)S(1)}, u32[]{:S(2)}) copy-start(bf16[512,2560]{1,0:T(8,128)(2,1)S(1)} %get-tuple-element.157.refs_5_) | copy-start | bytes 7864324
  234.6 10.1 %copy-start.19 = (bf16[512,32]{1,0:T(8,128)(2,1)}, bf16[512,32]{1,0:T(8,128)(2,1)S(1)}, u32[]{:S(2)}) copy-start(bf16[512,32]{1,0:T(8,128)(2,1)S(1)} %fusion.12.refs_11_) | copy-start | bytes 98308
  301.9 189.5 %reduce-scatter.3.cloned.1.call-start = ((), (), s32[]{:S(2)}) async-start(), calls=%async_computation.3 | async-start | bytes 6553600 | tf_op jit(solution)/shard_map/reduce_scatter | solution.py:1389
  368.1 302.4 %reduce-scatter.5.cloned.1.call-start = ((), (), s32[]{:S(2)}) async-start(), calls=%async_computation.5 | async-start | bytes 13107200 | tf_op jit(solution)/shard_map/reduce_scatter | solution.py:1402
  486.0 96.2 %copy-start.49 = (s32[8]{0:T(128)}, s32[8]{0:T(128)S(1)}, u32[]{:S(2)}) copy-start(s32[8]{0:T(128)S(1)} %pad_add_fusion.1.from_ref) | copy-start | bytes 100
  486.2 13.9 %copy-start.18 = (bf16[112,1920]{1,0:T(8,128)(2,1)}, bf16[112,1920]{1,0:T(8,128)(2,1)S(1)}, u32[]{:S(2)}) copy-start(bf16[112,1920]{1,0:T(8,128)(2,1)S(1)} %broadcast_dynamic-update-slice_fusion.refs_0_) | copy-start | bytes 1290244
  486.2 92.3 %collective-permute-start.1 = (bf16[112,1920]{1,0:T(8,128)(2,1)S(1)}, bf16[112,1920]{1,0:T(8,128)(2,1)S(1)}, u32[]{:S(2)}, u32[]{:S(2)}) collective-permute-start(bf16[112,1920]{1,0:T(8,128)(2,1)S(1)} %broadcast_dynamic-update-slice_fusion.refs_0_), channel_id=1, source_target_pairs={{0,2},{1,3},{2,4},{3,5},{4,6},{5,7},{6,0},{7,1},{8,10},{9,11},{10,... | collective-permute-start | bytes 1290248 | tf_op jit(solution)/shard_map/ppermute | solution.py:1288
  487.7 90.8 %collective-permute-start.2 = (bf16[112,1920]{1,0:T(8,128)(2,1)S(1)}, bf16[112,1920]{1,0:T(8,128)(2,1)S(1)}, u32[]{:S(2)}, u32[]{:S(2)}) collective-permute-start(bf16[112,1920]{1,0:T(8,128)(2,1)S(1)} %broadcast_dynamic-update-slice_fusion.refs_0_), channel_id=1, source_target_pairs={{0,4},{1,5},{2,6},{3,7},{4,0},{5,1},{6,2},{7,3},{8,12},{9,13},{10,... | collective-permute-start | bytes 1290248 | tf_op jit(solution)/shard_map/ppermute | solution.py:1288
  490.1 88.4 %collective-permute-start.3 = (bf16[112,1920]{1,0:T(8,128)(2,1)S(1)}, bf16[112,1920]{1,0:T(8,128)(2,1)S(1)}, u32[]{:S(2)}, u32[]{:S(2)}) collective-permute-start(bf16[112,1920]{1,0:T(8,128)(2,1)S(1)} %broadcast_dynamic-update-slice_fusion.refs_0_), channel_id=1, source_target_pairs={{0,6},{1,7},{2,0},{3,1},{4,2},{5,3},{6,4},{7,5},{8,14},{9,15},{10,... | collective-permute-start | bytes 1290248 | tf_op jit(solution)/shard_map/ppermute | solution.py:1288
  500.1 82.2 %copy-start.16 = (bf16[512,64]{1,0:T(8,128)(2,1)S(1)}, bf16[512,64]{1,0:T(8,128)(2,1)}, u32[]{:S(2)}) copy-start(bf16[512,64]{1,0:T(8,128)(2,1)} %copy-done.15) | copy-start | bytes 196612
  582.2 78.0 %collective-permute-start.4 = (bf16[4,112,1920]{2,1,0:T(8,128)(2,1)}, bf16[4,112,1920]{2,1,0:T(8,128)(2,1)S(1)}, u32[]{:S(2)}, u32[]{:S(2)}) collective-permute-start(bf16[4,112,1920]{2,1,0:T(8,128)(2,1)} %shard_map.452.refs_0_), channel_id=1, source_target_pairs={{0,1},{1,0},{2,3},{3,2},{4,5},{5,4},{6,7},{7,6},{8,9},{9,8},{10,11... | collective-permute-start | bytes 5160968 | tf_op jit(solution)/shard_map/ppermute | solution.py:1294
  (28 other events, 83.1 us)
Sparse Core Ops, SparseCore 0:
  143.6 106.9 all-gather.4
  302.0 61.4 all-gather.6
  368.3 61.3 reduce-scatter.2
  483.9 107.8 reduce-scatter.4

commit v6 on v5

--- a/solution.py
+++ b/solution.py
@@ -70,11 +70,7 @@
     return a, b
 
 
-def gate_values(conv, inner, lift, table_d, table_a, softrate, restart):
-    rounded = conv.astype(BF16)
-    half = lift.shape[0] // 2
-    pre_d = dot(rounded, table_d) + dot(inner[:, :half], lift[:half])
-    pre_a = dot(rounded, table_a) + dot(inner[:, half:], lift[half:])
+def gate_steps(pre_d, pre_a, softrate, restart):
     decay_gate = 1.0 / (1.0 + jnp.exp(-pre_d))
     admit_gate = 1.0 / (1.0 + jnp.exp(-pre_a))
     safe = jnp.where(restart, -1.0, -8.0 * decay_gate * softrate)
@@ -83,20 +79,53 @@
     return decay_gate, admit_gate, grown, scale
 
 
+def gate_values(conv, inner, lift, table_d, table_a, softrate, restart):
+    rounded = conv.astype(BF16)
+    half = lift.shape[0] // 2
+    pre_d = dot(rounded, table_d) + dot(inner[:, :half], lift[:half])
+    pre_a = dot(rounded, table_a) + dot(inner[:, half:], lift[half:])
+    return gate_steps(pre_d, pre_a, softrate, restart)
+
+
+GROUP = 16
+UNROLL = 16
+
+
+def scan_group(a, b, carry_a, carry_b, moved):
+    by = 1
+    while by < a.shape[0]:
+        b = a * moved(b, by, 0.0) + b
+        a = a * moved(a, by, 1.0)
+        by *= 2
+    return a * carry_a, a * carry_b + b
+
+
 def forward_gates_kernel(seqs, conv_ref, inner_ref, lift_ref, table_d_ref, table_a_ref, soft_ref, restart_ref,
-                         cum_ref, local_ref):
-    stretch = conv_ref.shape[0] // seqs
-    for s in range(seqs):
-        rows = pl.ds(s * stretch, stretch)
-        conv = conv_ref[rows, :]
-        restart = restart_ref[rows, :] > 0.5
-        _, admit, grown, scale = gate_values(
-            conv, inner_ref[rows, :], lift_ref[...], table_d_ref[0], table_a_ref[0], soft_ref[...], restart)
-        decays = jnp.where(restart, 0.0, grown)
-        drive = conv * admit * jnp.where(restart, 1.0, scale)
-        cum, local = scan_rows(decays, drive, rows_shifted)
-        cum_ref[rows, :] = cum
-        local_ref[rows, :] = local
+                         cum_ref, local_ref, pre_d_ref, pre_a_ref):
+    rows, size = conv_ref.shape
+    stretch = rows // seqs
+    half = lift_ref.shape[0] // 2
+    rounded = conv_ref[...].astype(BF16)
+    pre_d_ref[...] = dot(rounded, table_d_ref[0]) + dot(inner_ref[:, :half], lift_ref[:half, :])
+    pre_a_ref[...] = dot(rounded, table_a_ref[0]) + dot(inner_ref[:, half:], lift_ref[half:, :])
+    softrate = soft_ref[...]
+
+    def group(k, carries):
+        after = []
+        for s in range(seqs):
+            at = pl.ds(pl.multiple_of(s * stretch + k * GROUP, GROUP), GROUP)
+            restart = restart_ref[at, :] > 0.5
+            _, admit, grown, scale = gate_steps(pre_d_ref[at, :], pre_a_ref[at, :], softrate, restart)
+            decays = jnp.where(restart, 0.0, grown)
+            drive = conv_ref[at, :] * admit * jnp.where(restart, 1.0, scale)
+            cum, local = scan_group(decays, drive, *carries[s], rows_shifted)
+            cum_ref[at, :] = cum
+            local_ref[at, :] = local
+            after.append((cum[GROUP - 1 :], local[GROUP - 1 :]))
+        return tuple(after)
+
+    start = (jnp.ones((1, size), F32), jnp.zeros((1, size), F32))
+    lax.fori_loop(0, stretch // GROUP, group, (start,) * seqs, unroll=UNROLL)
 
 
 def forward_gates(seqs, conv, inner, lift, table_d, table_a, softrate, restart):
@@ -119,6 +148,7 @@
             pl.BlockSpec(restart.shape, lambda h: (0, 0)),
         ],
         out_specs=(tile, tile),
+        scratch_shapes=[pltpu.VMEM((rows, size), F32)] * 2,
         compiler_params=pltpu.CompilerParams(vmem_limit_bytes=40 * 2**20),
         cost_estimate=pl.CostEstimate(
             flops=4 * rows * width * size + 60 * rows * width,
@@ -263,6 +293,145 @@
     )(conv, inner, lift, table_d, table_a, softrate, restart, cum, local, carried, span, total, incoming)
 
 
+def remote(src, dst, send_sem, recv_sem, partner):
+    return pltpu.make_async_remote_copy(
+        src_ref=src, dst_ref=dst, send_sem=send_sem, recv_sem=recv_sem, device_id=partner,
+        device_id_type=pl.DeviceIdType.MESH)
+
+
+class GroupSum:
+    def __init__(self, block, scratch):
+        first_a, first_b, second_a, second_b, pass_a, pass_b, own, send, recv, local = scratch
+        group, replica = lax.axis_index("group"), lax.axis_index("replica")
+        beside, above, across = group + 1 - 2 * (group % 2), (group + 2) % 4, 3 - group
+        at_beside, at_above = (beside, replica), (above, replica)
+        self.scratch, self.half = scratch, own.shape[0] // 2
+        pairs = [(block(across, 0), first_a.at[1], at_beside), (block(across, 1), first_b.at[1], at_above),
+                 (block(beside, 0), first_a.at[0], at_beside), (block(above, 1), first_b.at[0], at_above),
+                 (pass_a, second_a, at_above), (pass_b, second_b, at_beside)]
+        moves = [remote(src, dst, send.at[slot], recv.at[slot], partner)
+                 for slot, (src, dst, partner) in enumerate(pairs)]
+        self.firsts, self.seconds = moves[:4], moves[4:]
+        pieces = [(block(above, 0), pass_a), (block(beside, 1), pass_b), (block(group, 0), own.at[pl.ds(0, self.half)]),
+                  (block(group, 1), own.at[pl.ds(self.half, self.half)])]
+        self.loads = [pltpu.make_async_copy(src, dst, local.at[i]) for i, (src, dst) in enumerate(pieces)]
+
+    def begin(self):
+        for one in self.firsts + self.loads:
+            one.start()
+
+    def middle(self):
+        first_a, first_b, _, _, pass_a, pass_b = self.scratch[:6]
+        for one in self.loads:
+            one.wait()
+        for one in self.firsts:
+            one.wait_recv()
+        pass_a[...] = (pass_a[...].astype(F32) + first_a[1].astype(F32)).astype(BF16)
+        pass_b[...] = (pass_b[...].astype(F32) + first_b[1].astype(F32)).astype(BF16)
+        for one in self.seconds:
+            one.start()
+
+    def end(self):
+        first_a, first_b, second_a, second_b, _, _, own = self.scratch[:7]
+        half = self.half
+        for one in self.seconds:
+            one.wait_recv()
+        own[:half] = (own[:half].astype(F32) + first_a[0].astype(F32) + second_a[...].astype(F32)).astype(BF16)
+        own[half:] = (own[half:].astype(F32) + first_b[0].astype(F32) + second_b[...].astype(F32)).astype(BF16)
+
+    def clear(self):
+        for one in self.firsts + self.seconds:
+            one.wait_send()
+
+    @staticmethod
+    def shapes(ranks, cols):
+        half = ranks // 2
+        return [pltpu.VMEM((2, half, cols), BF16)] * 2 + [pltpu.VMEM((half, cols), BF16)] * 4 + [
+            pltpu.VMEM((ranks, cols), BF16), pltpu.SemaphoreType.DMA((6,)), pltpu.SemaphoreType.DMA((6,)),
+            pltpu.SemaphoreType.DMA((4,))]
+
+
+class ReplicaChain:
+    def __init__(self, own, got, sems):
+        up_send, low_recv, down_send, high_recv, core_send, core_recv, local = sems
+        group, replica = lax.axis_index("group"), lax.axis_index("replica")
+        count = got.shape[0]
+        self.levels, self.level = count // 2, replica // 2
+        at_core = (group, replica + 1 - 2 * (replica % 2))
+        at_up, at_down = (group, (replica + 2) % count), (group, (replica + count - 2) % count)
+        self.has_up, self.has_down = self.level < self.levels - 1, self.level > 0
+        piece = lambda source: got.at[(source + count) % count]
+        self.to_up = [remote(own, piece(replica), up_send.at[0], low_recv.at[0], at_up)]
+        self.to_down = [remote(own, piece(replica), down_send.at[0], high_recv.at[0], at_down)]
+        self.to_core = [remote(own, piece(replica), core_send.at[0], core_recv.at[0], at_core)]
+        self.keep = pltpu.make_async_copy(own, piece(replica), local.at[0])
+        for d in range(1, self.levels):
+            low, high = piece(replica - 2 * d), piece(replica + 2 * d)
+            self.to_up.append(remote(low, low, up_send.at[d], low_recv.at[d], at_up))
+            self.to_down.append(remote(high, high, down_send.at[d], high_recv.at[d], at_down))
+            self.to_core += [remote(low, low, core_send.at[2 * d - 1], core_recv.at[2 * d - 1], at_core),
+                             remote(high, high, core_send.at[2 * d], core_recv.at[2 * d], at_core)]
+
+    def begin(self):
+        self.keep.start()
+        pl.when(self.has_up)(self.to_up[0].start)
+        pl.when(self.has_down)(self.to_down[0].start)
+        self.to_core[0].start()
+
+    def hop(self, d):
+        @pl.when(self.level >= d)
+        def _():
+            self.to_up[d - 1].wait_recv()
+            pl.when(self.has_up)(self.to_up[d].start)
+            self.to_core[2 * d - 1].start()
+
+        @pl.when(self.level + d < self.levels)
+        def _():
+            self.to_down[d - 1].wait_recv()
+            pl.when(self.has_down)(self.to_down[d].start)
+            self.to_core[2 * d].start()
+
+    def end(self):
+        self.to_core[0].wait()
+        pl.when(self.has_up)(self.to_up[0].wait_send)
+        pl.when(self.has_down)(self.to_down[0].wait_send)
+        for d in range(1, self.levels):
+            from_low, from_high = self.level >= d, self.level + d < self.levels
+            pl.when(from_low)(self.to_core[2 * d - 1].wait)
+            pl.when(from_high)(self.to_core[2 * d].wait)
+            pl.when(from_low & self.has_up)(self.to_up[d].wait_send)
+            pl.when(from_high & self.has_down)(self.to_down[d].wait_send)
+        self.keep.wait()
+
+    @staticmethod
+    def shapes(count):
+        return [pltpu.SemaphoreType.DMA((count // 2,))] * 4 + [pltpu.SemaphoreType.DMA((count,))] * 2 + [
+            pltpu.SemaphoreType.DMA((1,))]
+
+
+def greet_all(levels, group_partners):
+    group, replica = lax.axis_index("group"), lax.axis_index("replica")
+    level = replica // 2
+    barrier = pltpu.get_barrier_semaphore()
+
+    def greet(partner):
+        pl.semaphore_signal(barrier, inc=1, device_id=partner, device_id_type=pl.DeviceIdType.MESH)
+
+    for partner in group_partners + [(group, replica + 1 - 2 * (replica % 2))]:
+        greet(partner)
+
+    @pl.when(level > 0)
+    def _():
+        greet((group, (replica + 2 * levels - 2) % (2 * levels)))
+
+    @pl.when(level < levels - 1)
+    def _():
+        greet((group, (replica + 2) % (2 * levels)))
+
+    ends = (level + levels - 1) // levels + (2 * levels - 2 - level) // levels
+    pl.semaphore_wait(barrier, len(group_partners) + 1 + ends)
+
+
 def sequence_mask(rows, cols, seqs):
     row = lax.broadcasted_iota(jnp.int32, (rows, cols), 0) // (rows // seqs)
     col = lax.broadcasted_iota(jnp.int32, (rows, cols), 1) % (cols // 2) // (cols // 2 // seqs)
@@ -272,9 +441,10 @@
 def mixer_back_kernel(
     seqs, heads, mixed_ref, w_ref, lift_mixer_ref, down_mixer_ref, conv_ref, inner_ref, lift_ref, table_d_ref,
     table_a_ref, soft_ref, restart_ref, cum_ref, local_ref, carried_ref, pre_ref, lift_branch_ref, lift_input_ref,
-    down_gates_ref, taps_ref, agree_ref,
+    down_gates_ref, taps_ref, agree_ref, early_ref, wide_ref,
     branch_grad_ref, through_one_ref, through_gates_ref, lift_grad_ref, fed_grad_ref, thr_mixer_ref,
-    span_ref, total_ref, ends_ref, all_ends_ref, incoming_ref, halo_ref, below_ref, one_ref, gates_ref, send, recv,
+    got_early_ref, got_wide_ref, span_ref, total_ref, ends_ref, all_ends_ref, incoming_ref, halo_ref, below_ref, one_ref, gates_ref, first_ref,
+    second_ref, low_d_ref, low_a_ref, longer_ref, send, recv, *scratch,
 ):
     rows, size = conv_ref.shape
     stretch = rows // seqs
@@ -289,15 +459,24 @@
             src_ref=src, dst_ref=dst, send_sem=send.at[slot], recv_sem=recv.at[slot], device_id=partner,
             device_id_type=pl.DeviceIdType.MESH)
 
+    early_rows, early_cols = got_early_ref.shape[1:]
+    early_half = early_rows // 2
+    total_early = GroupSum(
+        lambda owner, side: early_ref.at[
+            pl.ds(side * early_half, early_half), pl.ds(pl.multiple_of(owner * early_cols, early_cols), early_cols)],
+        scratch[:10])
+    levels = got_early_ref.shape[0] // 2
+    chains = [ReplicaChain(scratch[6], got_early_ref, scratch[10:17]),
+              ReplicaChain(wide_ref, got_wide_ref, scratch[17:])]
+
     exchange = [copy(ends_ref, all_ends_ref.at[group], slot, partner) for slot, partner in enumerate(partners)]
     downward = copy(halo_ref, below_ref, 3, ((group + 3) % 4, replica))
 
     @pl.when(step == 0)
     def _():
-        barrier = pltpu.get_barrier_semaphore()
-        for partner in partners:
-            pl.semaphore_signal(barrier, inc=1, device_id=partner, device_id_type=pl.DeviceIdType.MESH)
-        pl.semaphore_wait(barrier, 3)
+        greet_all(levels, partners)
+        total_early.begin()
+        chains[1].begin()
         one_ref[...] = jnp.zeros_like(one_ref)
         gates_ref[...] = jnp.zeros_like(gates_ref)
         ends_ref[...] = jnp.zeros_like(ends_ref)
@@ -306,28 +485,63 @@
         through = dot(mixed_ref[...], lift_mixer_ref[...], NT)
         thr_mixer_ref[...] = jnp.where(row == col, through, 0.0).astype(BF16)
 
+    stops = 3 * heads // (levels + 2)
+
+    @pl.when(step == stops // 2)
+    def _():
+        total_early.middle()
+
+    @pl.when(step == stops)
+    def _():
+        total_early.end()
+        chains[0].begin()
+
+    for d in range(1, levels):
+        @pl.when(step == (d + 1) * stops)
+        def _(d=d):
+            for chain in chains:
+                chain.hop(d)
+
+    groups = stretch // GROUP
+
+    def rows_of(s, k):
+        return pl.ds(pl.multiple_of(s * stretch + k * GROUP, GROUP), GROUP)
+
     @pl.when(step < heads)
     def _():
         cols = pl.ds(pl.multiple_of(step * size, size), size)
-        merged = dot(mixed_ref[...], w_ref[...], NT) + dot(thr_mixer_ref[...], down_mixer_ref[...])
+        first_ref[...] = dot(mixed_ref[...], w_ref[...], NT) + dot(thr_mixer_ref[...], down_mixer_ref[...])
+        second_ref[...] = (dot(conv_ref[...].astype(BF16), table_d_ref[0])
+                           + dot(inner_ref[:, :half], lift_ref[:half, :]))
+        softrate = soft_ref[...]
+
+        def group(lap, carries):
+            k = groups - 1 - lap
+            after = []
+            for s in range(seqs):
+                at = rows_of(s, k)
+                restart = restart_ref[at, :] > 0.5
+                grown = jnp.exp(-8.0 * softrate / (1.0 + jnp.exp(-second_ref[at, :])))
+                decays = jnp.where(restart, 0.0, grown)
+                state = local_ref[at, :] + cum_ref[at, :] * carried_ref[s : s + 1, :]
+                value, slope = gelu_both(pre_ref[at, :])
+                merged = first_ref[at, :]
+                branch_grad_ref[at, :] = (merged * state * slope).astype(BF16)
+                grads = merged * value
+                carry_a, carry_b = carries[s]
+                a, b = scan_group(decays, decays * grads, carry_a, carry_b, rows_advanced)
+                last = lax.broadcasted_iota(jnp.int32, a.shape, 0) == GROUP - 1
+                span_ref[step, at, :] = jnp.where(last, carry_a, pltpu.roll(a, GROUP - 1, 0))
+                total_ref[step, at, :] = grads + jnp.where(last, carry_b, pltpu.roll(b, GROUP - 1, 0))
+                after.append((a[:1], b[:1]))
+            return tuple(after)
+
+        start = (jnp.ones((1, size), F32), jnp.zeros((1, size), F32))
+        ends = lax.fori_loop(0, groups, group, (start,) * seqs, unroll=UNROLL)
         for s in range(seqs):
-            at = slice(s * stretch, (s + 1) * stretch)
-            restart = restart_ref[at, :] > 0.5
-            rounded = conv_ref[at, :].astype(BF16)
-            pre_d = dot(rounded, table_d_ref[0]) + dot(inner_ref[at, :half], lift_ref[:half, :])
-            grown = jnp.exp(-8.0 * soft_ref[...] / (1.0 + jnp.exp(-pre_d)))
-            decays = jnp.where(restart, 0.0, grown)
-            state = local_ref[at, :] + cum_ref[at, :] * carried_ref[s : s + 1, :]
-            value, slope = gelu_both(pre_ref[at, :])
-            grads = merged[at, :]
-            low = (grads * state * slope).astype(BF16)
-            branch_grad_ref[at, :] = low
-            one_ref[at, :ranks] += dot(low, lift_branch_ref[...], NT)
-            span, total = scan_rows(rows_advanced(decays, 1, 1.0), grads * value, rows_advanced)
-            span_ref[step, at, :] = span
-            total_ref[step, at, :] = total
-            ends_ref[s : s + 1, cols] = decays[:1] * span[:1]
-            ends_ref[seqs + s : seqs + s + 1, cols] = decays[:1] * total[:1]
+            ends_ref[s : s + 1, cols] = ends[s][0]
+            ends_ref[seqs + s : seqs + s + 1, cols] = ends[s][1]
+        one_ref[:, :ranks] += dot(branch_grad_ref[...], lift_branch_ref[...], NT)
 
     @pl.when(step == heads - 1)
     def _():
@@ -348,36 +562,40 @@
     def _():
         head = step - heads
         cols = pl.ds(pl.multiple_of(head * size, size), size)
+        rounded = conv_ref[...].astype(BF16)
+        first_ref[...] = dot(rounded, table_d_ref[0]) + dot(inner_ref[:, :half], lift_ref[:half, :])
+        second_ref[...] = dot(rounded, table_a_ref[0]) + dot(inner_ref[:, half:], lift_ref[half:, :])
         softrate = soft_ref[...]
-        for s in range(seqs):
-            at = slice(s * stretch, (s + 1) * stretch)
-            conv, inner = conv_ref[at, :], inner_ref[at, :]
-            restart = restart_ref[at, :] > 0.5
-            decay_gate, admit, grown, scale = gate_values(
-                conv, inner, lift_ref[...], table_d_ref[0], table_a_ref[0], softrate, restart)
-            carried = carried_ref[s : s + 1, :]
-            state = local_ref[at, :] + cum_ref[at, :] * carried
-            place = lax.broadcasted_iota(jnp.int32, state.shape, 0)
-            before = jnp.where(place >= 1, pltpu.roll(state, 1, 0), carried)
-            grads = total_ref[head, at, :] + span_ref[head, at, :] * incoming_ref[s : s + 1, cols]
-            driven = grads * jnp.where(restart, 1.0, scale)
-            grad_log = jnp.where(
-                restart, 0.0, grads * (before * grown - conv * admit * grown * grown / scale))
-            grad_d = (-8.0 * softrate) * grad_log * decay_gate * (1.0 - decay_gate)
-            grad_a = driven * conv * admit * (1.0 - admit)
-            low_d, low_a = grad_d.astype(BF16), grad_a.astype(BF16)
-            total_ref[head, at, :] = (
-                driven * admit + dot(low_d, table_d_ref[0], NT) + dot(low_a, table_a_ref[0], NT))
-            gates_ref[at, :half] += dot(low_d, lift_ref[:half, :], NT)
-            gates_ref[at, half:] += dot(low_a, lift_ref[half:, :], NT)
-            first = dot(inner[:, :half], low_d, TN)
-            second = dot(inner[:, half:], low_a, TN)
-            if s == 0:
-                lift_grad_ref[:half, :] = first
-                lift_grad_ref[half:, :] = second
-            else:
-                lift_grad_ref[:half, :] += first
-                lift_grad_ref[half:, :] += second
+        rate = -8.0 * softrate
+
+        def group(k, carries):
+            after = []
+            for s in range(seqs):
+                at = rows_of(s, k)
+                conv = conv_ref[at, :]
+                restart = restart_ref[at, :] > 0.5
+                decay_gate, admit, grown, scale = gate_steps(
+                    first_ref[at, :], second_ref[at, :], softrate, restart)
+                state = local_ref[at, :] + cum_ref[at, :] * carried_ref[s : s + 1, :]
+                place = lax.broadcasted_iota(jnp.int32, state.shape, 0)
+                before = jnp.where(place >= 1, pltpu.roll(state, 1, 0), carries[s])
+                grads = total_ref[head, at, :] + span_ref[head, at, :] * incoming_ref[s : s + 1, cols]
+                driven = grads * jnp.where(restart, 1.0, scale)
+                admitted = conv * admit
+                grad_log = jnp.where(restart, 0.0, grads * (before * grown - admitted * grown * grown / scale))
+                low_d_ref[at, :] = (rate * grad_log * decay_gate * (1.0 - decay_gate)).astype(BF16)
+                low_a_ref[at, :] = (driven * admitted * (1.0 - admit)).astype(BF16)
+                total_ref[head, at, :] = driven * admit
+                after.append(state[GROUP - 1 :])
+            return tuple(after)
+
+        lax.fori_loop(0, groups, group, tuple(carried_ref[s : s + 1, :] for s in range(seqs)), unroll=UNROLL)
+        low_d, low_a = low_d_ref[...], low_a_ref[...]
+        total_ref[head] += dot(low_d, table_d_ref[0], NT) + dot(low_a, table_a_ref[0], NT)
+        gates_ref[:, :half] += dot(low_d, lift_ref[:half, :], NT)
+        gates_ref[:, half:] += dot(low_a, lift_ref[half:, :], NT)
+        lift_grad_ref[:half, :] = dot(inner_ref[:, :half], low_d, TN)
+        lift_grad_ref[half:, :] = dot(inner_ref[:, half:], low_a, TN)
 
     @pl.when(step == 2 * heads)
     def _():
@@ -397,15 +615,22 @@
         cols = pl.ds(pl.multiple_of(head * size, size), size)
         grads = total_ref[head] + dot(through_gates_ref[...], down_gates_ref[:, cols])
         for s in range(seqs):
-            at = slice(s * stretch, (s + 1) * stretch)
-            longer = jnp.concatenate([grads[at, :], below_ref[s * 8 : (s + 1) * 8, cols].astype(F32)], 0)
-            total = taps_ref[0:1, :] * agree_ref[at, 0:1] * grads[at, :]
-            for j in range(1, taps_ref.shape[0]):
-                moved = pltpu.roll(longer, stretch + 8 - j, 0)[:stretch]
-                total += taps_ref[j : j + 1, :] * agree_ref[at, j : j + 1] * moved
-            low = total.astype(BF16)
-            fed_grad_ref[at, :] = low
-            one_ref[at, ranks:] += dot(low, lift_input_ref[...], NT)
+            longer_ref[s, :stretch, :] = grads[s * stretch : (s + 1) * stretch, :]
+            longer_ref[s, stretch:, :] = below_ref[s * 8 : (s + 1) * 8, cols].astype(F32)
+
+        def group(k, _):
+            for s in range(seqs):
+                at = rows_of(s, k)
+                ahead = longer_ref[s, pl.ds(pl.multiple_of(k * GROUP, GROUP), GROUP + 8), :]
+                total = taps_ref[0:1, :] * agree_ref[at, 0:1] * ahead[:GROUP]
+                for j in range(1, taps_ref.shape[0]):
+                    moved = pltpu.roll(ahead, GROUP + 8 - j, 0)[:GROUP]
+                    total += taps_ref[j : j + 1, :] * agree_ref[at, j : j + 1] * moved
+                fed_grad_ref[at, :] = total.astype(BF16)
+            return 0
+
+        lax.fori_loop(0, groups, group, 0, unroll=UNROLL)
+        one_ref[:, ranks:] += dot(fed_grad_ref[...], lift_input_ref[...], NT)
 
     @pl.when(step == 3 * heads - 1)
     def _():
@@ -413,11 +638,15 @@
         for one in exchange:
             one.wait_send()
         downward.wait_send()
+        total_early.clear()
+        for chain in chains:
+            chain.end()
 
 
 def mixer_back(seqs, mixed, w_mixer, lift_mixer, down_mixer, conv, inner, lift, table_d, table_a, softrate, restart,
-               cum, local, carried, pre, lift_branch, lift_input, down_gates, taps, agree):
+               cum, local, carried, pre, lift_branch, lift_input, down_gates, taps, agree, early, wide):
     rows, width = conv.shape
+    count, early_cols = lax.axis_size("replica"), width // 4
     heads, size = table_d.shape[:2]
     first = lambda i: jnp.minimum(i, heads - 1)
     second = lambda i: jnp.clip(i - heads, 0, heads - 1)
@@ -439,28 +668,34 @@
             jax.ShapeDtypeStruct(lift.shape, F32),
             jax.ShapeDtypeStruct((rows, width), BF16),
             jax.ShapeDtypeStruct((rows, lift_mixer.shape[0]), BF16),
+            jax.ShapeDtypeStruct((count, early.shape[0], early_cols), BF16),
+            jax.ShapeDtypeStruct((count,) + wide.shape, BF16),
         ],
         in_specs=[
             full(mixed), pl.BlockSpec((size, width), lambda i: (first(i), 0)), full(lift_mixer), cols(down_mixer, first),
             cols(conv, either), full(inner), cols(lift, either), table, table, cols(softrate, either), full(restart),
             cols(cum, either), cols(local, either), cols(carried, either), cols(pre, first), cols(lift_branch, first),
-            cols(lift_input, third), full(down_gates), cols(taps, third), full(agree),
+            cols(lift_input, third), full(down_gates), cols(taps, third), full(agree), ANYWHERE, ANYWHERE,
         ],
         out_specs=[tile(first), whole(2 * lift_branch.shape[0]), whole(middle),
                    pl.BlockSpec((lift.shape[0], size), lambda i: (0, second(i))), tile(third),
-                   whole(lift_mixer.shape[0])],
+                   whole(lift_mixer.shape[0]), ANYWHERE, ANYWHERE],
         scratch_shapes=[
             pltpu.VMEM((heads, rows, size), F32), pltpu.VMEM((heads, rows, size), F32), pltpu.VMEM((8, width), F32),
             pltpu.VMEM((4, 8, width), F32), pltpu.VMEM((seqs, width), F32), pltpu.VMEM((8 * seqs, width), BF16),
             pltpu.VMEM((8 * seqs, width), BF16), pltpu.VMEM((rows, 2 * lift_branch.shape[0]), F32),
-            pltpu.VMEM((rows, middle), F32), pltpu.SemaphoreType.DMA((4,)), pltpu.SemaphoreType.DMA((4,))],
+            pltpu.VMEM((rows, middle), F32), pltpu.VMEM((rows, size), F32), pltpu.VMEM((rows, size), F32),
+            pltpu.VMEM((rows, size), BF16), pltpu.VMEM((rows, size), BF16),
+            pltpu.VMEM((seqs, rows // seqs + 8, size), F32), pltpu.SemaphoreType.DMA((4,)),
+            pltpu.SemaphoreType.DMA((4,))]
+        + GroupSum.shapes(early.shape[0], early_cols) + ReplicaChain.shapes(count) + ReplicaChain.shapes(count),
         compiler_params=pltpu.CompilerParams(
             vmem_limit_bytes=VMEM, collective_id=3, has_side_effects=True),
         cost_estimate=pl.CostEstimate(
             flops=2 * rows * width * width + 20 * rows * width * size + 200 * rows * width,
             bytes_accessed=40 * rows * width + 2 * width * width, transcendentals=12 * rows * width),
     )(mixed, w_mixer, lift_mixer, down_mixer, conv, inner, lift, table_d, table_a, softrate, restart, cum, local,
-      carried, pre, lift_branch, lift_input, down_gates, taps, agree)
+      carried, pre, lift_branch, lift_input, down_gates, taps, agree, early, wide)
 
 
 def resident(array):
@@ -960,21 +1195,6 @@
     )(value, *earlier)
 
 
-def ordered_stack_kernel(count, *refs):
-    for i in range(count):
-        refs[-1][i] = refs[i][...]
-
-
-def ordered_stack(values, *earlier):
-    vmem = pl.BlockSpec(memory_space=pltpu.VMEM)
-    return pl.pallas_call(
-        functools.partial(ordered_stack_kernel, len(values)),
-        out_shape=jax.ShapeDtypeStruct((len(values),) + values[0].shape, values[0].dtype),
-        in_specs=[vmem] * len(values) + [ANYWHERE] * len(earlier),
-        out_specs=vmem,
-    )(*values, *earlier)
-
-
 def row_tiles(rows, width, count):
     step = min(rows, 128)
     return (rows // step,), [pl.BlockSpec((step, width), lambda i: (i, 0))] * count
@@ -1035,142 +1255,45 @@
 
 def tail_kernel(
     steps, branch_grad_ref, fed_grad_ref, w_branch_ref, w_input_ref, through_ref, down_ref, partial_ref,
-    out_ref, got_ref, first_a, first_b, second_a, second_b, pass_a, pass_b, own_ref, send, recv, up_send, low_recv,
-    down_send, high_recv, core_send, core_recv, local,
+    out_ref, got_ref, *scratch,
 ):
     step = pl.program_id(0)
+    levels = got_ref.shape[0] // 2
     group, replica = lax.axis_index("group"), lax.axis_index("replica")
-    beside, above, across = group + 1 - 2 * (group % 2), (group + 2) % 4, 3 - group
-    at_beside, at_above = (beside, replica), (above, replica)
-    count = got_ref.shape[0]
-    levels = count // 2
-    core, level = replica % 2, replica // 2
-    at_core = (group, replica + 1 - 2 * core)
-    at_up, at_down = (group, (replica + 2) % count), (group, (replica + count - 2) % count)
-    rows = own_ref.shape[0]
-    half = rows // 2
-
-    def part(owner, side):
-        return partial_ref.at[owner, pl.ds(side * half, half), :]
-
-    def copy(src, dst, send_sem, recv_sem, partner):
-        return pltpu.make_async_remote_copy(
-            src_ref=src, dst_ref=dst, send_sem=send_sem, recv_sem=recv_sem, device_id=partner,
-            device_id_type=pl.DeviceIdType.MESH)
-
-    pairs = [(part(across, 0), first_a.at[1], at_beside), (part(across, 1), first_b.at[1], at_above),
-             (part(beside, 0), first_a.at[0], at_beside), (part(above, 1), first_b.at[0], at_above),
-             (pass_a, second_a, at_above), (pass_b, second_b, at_beside)]
-    moves = [copy(src, dst, send.at[slot], recv.at[slot], partner) for slot, (src, dst, partner) in enumerate(pairs)]
-    firsts, seconds = moves[:4], moves[4:]
-    loads = [pltpu.make_async_copy(part(above, 0), pass_a, local.at[0]),
-             pltpu.make_async_copy(part(beside, 1), pass_b, local.at[1]),
-             pltpu.make_async_copy(partial_ref.at[group], own_ref, local.at[2])]
+    ranks = got_ref.shape[1]
+    half = ranks // 2
+    total = GroupSum(lambda owner, side: partial_ref.at[owner, pl.ds(side * half, half), :], scratch[:10])
+    chain = ReplicaChain(scratch[6], got_ref, scratch[10:])
 
     @pl.when(step == 0)
     def _():
-        barrier = pltpu.get_barrier_semaphore()
-
-        def greet(partner):
-            pl.semaphore_signal(barrier, inc=1, device_id=partner, device_id_type=pl.DeviceIdType.MESH)
-
-        for partner in (at_beside, at_above, at_core):
-            greet(partner)
-
-        @pl.when(level > 0)
-        def _():
-            greet(at_down)
-
-        @pl.when(level < levels - 1)
-        def _():
-            greet(at_up)
-
-        ends = (level + levels - 1) // levels + (2 * levels - 2 - level) // levels
-        pl.semaphore_wait(barrier, 3 + ends)
-        for one in firsts + loads:
-            one.start()
+        greet_all(levels, [(group + 1 - 2 * (group % 2), replica), ((group + 2) % 4, replica)])
+        total.begin()
 
     out_ref[...] = (dot(branch_grad_ref[...], w_branch_ref[...], NT) + dot(fed_grad_ref[...], w_input_ref[...], NT)
                     + dot(through_ref[...], down_ref[...]))
 
     @pl.when(step == max(steps - 2, 0))
     def _():
-        for one in loads:
-            one.wait()
-        for one in firsts:
-            one.wait_recv()
-        pass_a[...] = (pass_a[...].astype(F32) + first_a[1].astype(F32)).astype(BF16)
-        pass_b[...] = (pass_b[...].astype(F32) + first_b[1].astype(F32)).astype(BF16)
-        for one in seconds:
-            one.start()
+        total.middle()
 
     @pl.when(step == steps - 1)
     def _():
-        for one in seconds:
-            one.wait_recv()
-        own_ref[:half] = (own_ref[:half].astype(F32) + first_a[0].astype(F32) + second_a[...].astype(F32)).astype(BF16)
-        own_ref[half:] = (own_ref[half:].astype(F32) + first_b[0].astype(F32) + second_b[...].astype(F32)).astype(BF16)
-        keep = pltpu.make_async_copy(own_ref, got_ref.at[replica], local.at[3])
-        keep.start()
-
-        def piece(source):
-            return got_ref.at[(source + count) % count]
-
-        to_up = [copy(own_ref, piece(replica), up_send.at[0], low_recv.at[0], at_up)]
-        to_down = [copy(own_ref, piece(replica), down_send.at[0], high_recv.at[0], at_down)]
-        to_core = [copy(own_ref, piece(replica), core_send.at[0], core_recv.at[0], at_core)]
-        has_up, has_down = level < levels - 1, level > 0
-
-        def when(condition, action):
-            pl.when(condition)(action)
-
-        when(has_up, to_up[0].start)
-        when(has_down, to_down[0].start)
-        to_core[0].start()
+        total.end()
+        chain.begin()
         for d in range(1, levels):
-            low, high = piece(replica - 2 * d), piece(replica + 2 * d)
-            to_up.append(copy(low, low, up_send.at[d], low_recv.at[d], at_up))
-            to_down.append(copy(high, high, down_send.at[d], high_recv.at[d], at_down))
-            core_low = copy(low, low, core_send.at[2 * d - 1], core_recv.at[2 * d - 1], at_core)
-            core_high = copy(high, high, core_send.at[2 * d], core_recv.at[2 * d], at_core)
-            to_core += [core_low, core_high]
-            from_low, from_high = level >= d, level + d < levels
-
-            @pl.when(from_low)
-            def _(d=d, core_low=core_low):
-                to_up[d - 1].wait_recv()
-                when(has_up, to_up[d].start)
-                core_low.start()
-
-            @pl.when(from_high)
-            def _(d=d, core_high=core_high):
-                to_down[d - 1].wait_recv()
-                when(has_down, to_down[d].start)
-                core_high.start()
-
-        to_core[0].wait()
-        when(has_up, to_up[0].wait_send)
-        when(has_down, to_down[0].wait_send)
-        for d in range(1, levels):
-            when(level >= d, to_core[2 * d - 1].wait)
-            when(level + d < levels, to_core[2 * d].wait)
-            when((level >= d) & has_up, to_up[d].wait_send)
-            when((level + d < levels) & has_down, to_down[d].wait_send)
-        for one in firsts + seconds:
-            one.wait_send()
-        keep.wait()
+            chain.hop(d)
+        chain.end()
+        total.clear()
 
 
 def tail_call(branch_grad, fed_grad, w_branch, w_input, through, down, partial):
     rows, width = branch_grad.shape
     ranks, cols = partial.shape[1:]
     count = lax.axis_size("replica")
-    levels = count // 2
     tile = tile_of(width, 512)
     steps = pl.cdiv(width, tile)
     weight = pl.BlockSpec((tile, width), lambda i: (i, 0))
-    half = ranks // 2
-    dma = pltpu.SemaphoreType.DMA
     return pl.pallas_call(
         functools.partial(tail_kernel, steps),
         grid=(steps,),
@@ -1178,9 +1301,7 @@
         in_specs=[resident(branch_grad), resident(fed_grad), weight, weight, resident(through),
                   pl.BlockSpec((down.shape[0], tile), lambda i: (0, i)), ANYWHERE],
         out_specs=[pl.BlockSpec((rows, tile), lambda i: (0, i)), ANYWHERE],
-        scratch_shapes=[pltpu.VMEM((2, half, cols), BF16)] * 2 + [pltpu.VMEM((half, cols), BF16)] * 4
-        + [pltpu.VMEM((ranks, cols), BF16), dma((6,)), dma((6,)), dma((levels,)), dma((levels,)), dma((levels,)),
-           dma((levels,)), dma((count,)), dma((count,)), dma((4,))],
+        scratch_shapes=GroupSum.shapes(ranks, cols) + ReplicaChain.shapes(count),
         compiler_params=pltpu.CompilerParams(
             vmem_limit_bytes=VMEM, collective_id=4, has_side_effects=True),
         cost_estimate=pl.CostEstimate(
@@ -1188,39 +1309,36 @@
     )(branch_grad, fed_grad, w_branch, w_input, through, down, partial)
 
 
-def spread_kernel(tables, pieces, ids_ref, from_ref, *refs):
-    gots, out_refs = refs[:pieces], refs[-tables:]
-    ranks = out_refs[0].shape[1]
-    replicas = from_ref.shape[0]
+def spread_kernel(counts, ids_ref, *refs):
+    gots, outs = refs[: len(counts)], refs[len(counts) :]
+    ranks = outs[0].shape[1]
+    replicas = gots[0].shape[0]
     seqs = ids_ref.shape[0] // replicas
-    for table in range(tables):
-        out_refs[table][...] = jnp.zeros_like(out_refs[table])
-    replica = 0
-    for got_ref in gots:
-        for at in range(got_ref.shape[0]):
-            for s in range(seqs):
-                place = ids_ref[from_ref[replica] * seqs + s]
-                for table in range(tables):
-                    rows = pl.ds((table * seqs + s) * ranks, ranks)
-                    out_refs[table][place] += got_ref[at, rows, :].astype(F32)
-            replica += 1
-
-
-def spread(ids, source, gots, tables, sets, seqs, ranks, earlier=()):
-    rows, width = gots[0].shape[1:]
-    replicas = source.shape[0]
-    scalars = pl.BlockSpec(memory_space=pltpu.SMEM)
+    for out_ref in outs:
+        out_ref[...] = jnp.zeros_like(out_ref)
+    for replica in range(replicas):
+        for s in range(seqs):
+            place = ids_ref[replica * seqs + s]
+            table = 0
+            for count, got_ref in zip(counts, gots):
+                for at in range(count):
+                    rows = pl.ds((at * seqs + s) * ranks, ranks)
+                    outs[table][place] += got_ref[replica, rows, :].astype(F32)
+                    table += 1
+
+
+def spread(ids, gots, counts, sets, ranks):
+    vmem = pl.BlockSpec(memory_space=pltpu.VMEM)
     return pl.pallas_call(
-        functools.partial(spread_kernel, tables, len(gots)),
-        out_shape=[jax.ShapeDtypeStruct((sets, ranks, width), F32)] * tables,
-        in_specs=[scalars, scalars] + [pl.BlockSpec(memory_space=pltpu.VMEM)] * len(gots)
-        + [ANYWHERE] * len(earlier),
-        out_specs=[pl.BlockSpec(memory_space=pltpu.VMEM)] * tables,
-        compiler_params=pltpu.CompilerParams(vmem_limit_bytes=56 * 2**20),
+        functools.partial(spread_kernel, counts),
+        out_shape=[jax.ShapeDtypeStruct((sets, ranks, got.shape[2]), F32)
+                   for got, count in zip(gots, counts) for _ in range(count)],
+        in_specs=[pl.BlockSpec(memory_space=pltpu.SMEM)] + [vmem] * len(gots),
+        out_specs=[vmem] * sum(counts),
+        compiler_params=pltpu.CompilerParams(vmem_limit_bytes=VMEM),
         cost_estimate=pl.CostEstimate(
-            flops=replicas * rows * width,
-            bytes_accessed=2 * replicas * rows * width + 4 * tables * sets * ranks * width, transcendentals=0),
-    )(ids, source, *gots, *earlier)
+            flops=sum(got.size for got in gots), bytes_accessed=4 * sum(got.size for got in gots), transcendentals=0),
+    )(ids, *gots)
 
 
 def products_kernel(plan, *refs):
@@ -1278,23 +1396,6 @@
     return lax.ppermute(block, axis, route)
 
 
-def over_replicas(value, direct, *earlier):
-    count, here = lax.axis_size("replica"), lax.axis_index("replica")
-    if count % 2:
-        return [lax.all_gather(value, "replica")], jnp.arange(count, dtype=jnp.int32)
-    steps = jnp.arange(count // 2, dtype=jnp.int32)
-    if direct:
-        got = ordered_stack([value] + [
-            lax.ppermute(value, "replica", [(i, (i + 2 * step) % count) for i in range(count)])
-            for step in range(1, count // 2)], *earlier)
-        source = (here + count - 2 * steps) % count
-    else:
-        got = lax.all_gather(value, "replica", axis_index_groups=[list(range(p, count, 2)) for p in range(2)])
-        source = here % 2 + 2 * steps
-    swapped = lax.ppermute(got, "replica", [(i, i ^ 1) for i in range(count)])
-    return [got, swapped], jnp.concatenate([source, source + 1 - 2 * (here % 2)], 0)
-
-
 def body(
     inputs, segment_ids, adapter_ids, gain_mix, gain_mlp, w_branch, w_input, conv_taps, decay_heads, admit_heads,
     decay_param, w_mixer, w_gate, w_upper, w_down, down_branch, lift_branch, down_input, lift_input, down_decay,
@@ -1401,12 +1502,14 @@
         resid, out_grad.reshape(rows, width), gain_mlp.reshape(1, width), backs)
     outward = lax.psum_scatter(outward, "group", scatter_dimension=1, tiled=True).reshape(rows, width)
 
-    if group == 4 and 2 * seqs <= 8 and stretch % 8 == 0:
+    kernels = (group == 4 and lax.axis_size("replica") % 2 == 0 and 2 * seqs <= 8 and stretch % GROUP == 0
+               and width % 512 == 0 and seqs % 2 == 0)
+    if kernels:
         agree_cols = jnp.stack([agree[j][:, j : j + stretch].reshape(rows) for j in range(taps)], 1)
-        grad_branch_pre, through_one, through_gates, grad_lift_gates, grad_fed, through_mixer = mixer_back(
+        grad_branch_pre, through_one, through_gates, grad_lift_gates, grad_fed, through_mixer, got_early, got_wide = mixer_back(
             seqs, grad_mixed, full_mixer, p_lift_mixer, p_down_mixer, convolved, inner_gates, lift_gates, decay_heads,
             admit_heads, softrate, restart, cum, local, carried, branch_pre, p_lift_branch, p_lift_input,
-            stack[2 * mask_cols : 4 * mask_cols], conv_taps, agree_cols)
+            stack[2 * mask_cols : 4 * mask_cols], conv_taps, agree_cols, early, wide)
     else:
         through_mixer = (dot(grad_mixed, p_lift_mixer, NT) * own).astype(BF16)
         grad_merged = dot(grad_mixed, full_mixer, NT) + dot(through_mixer, p_down_mixer)
@@ -1433,30 +1536,26 @@
         through_branch = (dot(grad_branch_pre, p_lift_branch, NT) * own).astype(BF16)
         through_input = (dot(grad_fed, p_lift_input, NT) * own).astype(BF16)
         through_one = jnp.concatenate([through_branch, through_input], 1)
-    all_wide, wide_source = over_replicas(wide, True, through_gates)
     both = 2 * mask_cols
-    got_ids = jnp.concatenate([part[:, 3 * mask_cols : 3 * mask_cols + seqs, 0] for part in all_wide], 0)
-    in_order = wide_source[:, None] == jnp.arange(wide_source.shape[0], dtype=jnp.int32)[None, :]
-    all_ids = jnp.sum(jnp.where(in_order[:, :, None], got_ids.astype(jnp.int32)[:, None, :], 0), 0).reshape(-1)
-    partial = products(
+    late = products(
         [(through_one, 0, both, normed), (through_gates, 0, both, rounded), (through_mixer, 0, mask_cols, merged),
          (inner_branch, 0, mask_cols, grad_branch_pre), (inner_input, 0, mask_cols, grad_fed), (grad_lift_gates,),
-         (inner_mixer, 0, mask_cols, grad_mixed), (early,)], (), group)
-    if group == 4 and lax.axis_size("replica") % 2 == 0 and partial.shape[1] % 32 == 0:
-        grad_normed, got = tail_call(
-            grad_branch_pre, grad_fed, full_branch, full_input, through_one, stack[:both], partial)
-        all_owned, owned_source = [got], jnp.arange(lax.axis_size("replica"), dtype=jnp.int32)
+         (inner_mixer, 0, mask_cols, grad_mixed)], (), group)
+    if kernels:
+        grad_normed, got_late = tail_call(
+            grad_branch_pre, grad_fed, full_branch, full_input, through_one, stack[:both], late)
     else:
         grad_normed = (dot(grad_branch_pre, full_branch, NT) + dot(grad_fed, full_input, NT)
                        + dot(through_one, stack[:both]))
-        owned = lax.psum_scatter(partial, "group", scatter_dimension=0, tiled=False)
-        all_owned, owned_source = over_replicas(owned, False)
+        got_late = lax.all_gather(lax.psum_scatter(late, "group", scatter_dimension=0, tiled=False), "replica")
+        got_early = lax.all_gather(lax.psum_scatter(early, "group", scatter_dimension=1, tiled=True), "replica")
+        got_wide = lax.all_gather(wide, "replica")
     grad_inputs, block_out = finish(
         grad_resid, inputs.reshape(rows, width), gain_mix.reshape(1, width), grad_normed, resid, outward)
-    wides = spread(all_ids, wide_source, all_wide, 3, sets, seqs, ranks)
-    totals = spread(all_ids, owned_source, all_owned, 13, sets, seqs, ranks)
+    all_ids = got_wide[:, 3 * mask_cols : 3 * mask_cols + seqs, 0].astype(jnp.int32).reshape(-1)
+    totals = spread(all_ids, [got_late, got_early, got_wide], (10, 3, 3), sets, ranks)
     (t_down_branch, t_down_input, t_down_decay, t_down_admit, t_down_mixer, t_lift_branch, t_lift_input, t_lift_decay,
-     t_lift_admit, t_lift_mixer, t_down_gate, t_down_upper, t_lift_outward) = totals
+     t_lift_admit, t_lift_mixer, t_down_gate, t_down_upper, t_lift_outward, *wides) = totals
     return (
         block_out.reshape(seqs, stretch, width), grad_inputs.reshape(seqs, stretch, width),
         turned(t_down_branch), t_lift_branch, turned(t_down_input), t_lift_input, turned(t_down_decay), t_lift_decay,

time: 696 us -> 677 us (0.973)
  Pallas kernels: 567 us -> 554 us
    pallas_call x1, Pallas kernels: 66.9 us -> 55 us  [tail_call(): pl.pallas_call(functools.partial(tail_kernel, steps), grid=(steps,), out_...]
  transfers between devices with their start and end apart: 9 -> 5, of which waited for: 0 -> 1; matrix products, arithmetic and copies ran while one was open for 12% -> 12% of each run, Pallas kernels for 54% -> 53%
where the time goes in v6:
time: 677 us; the launch traced here: 668 us
  Pallas kernels  554 us (82%)
  matrix products  50.7 us (7%)
  local copies, waits for them, and re-layouts  18.2 us (3%)
  other arithmetic  15.8 us (2%)
  between operations  15 us (2%)
  blocking collectives  10.1 us (1%)
    pallas_call x1, Pallas kernels, gather_weights(): pl.pallas_call(functools.partial(gather_kernel, units), out_shape=[jax.Sh...  133 us
    pallas_call x2, Pallas kernels, feed_call(): pl.pallas_call(functools.partial(feed_kernel, steps, tile, units), grid=(...  126 us
    pallas_call x1, Pallas kernels, mixer_back(): pl.pallas_call(functools.partial(mixer_back_kernel, seqs, heads), grid=(3...  81 us
    pallas_call x1, Pallas kernels, tail_call(): pl.pallas_call(functools.partial(tail_kernel, steps), grid=(steps,), out_...  55 us
    pallas_call x1, Pallas kernels, outward_call(): pl.pallas_call(functools.partial(outward_kernel, seqs, reduce, steps), gr...  52 us
    pallas_call x1, Pallas kernels, grad_hidden_call(): pl.pallas_call(functools.partial(grad_hidden_kernel, seqs, gather, pl.cdi...  51.2 us
    dot_general x9, matrix products, dot(): return lax.dot_general(a, b, dims, preferred_element_type=F32)  50.7 us
    pallas_call x1, Pallas kernels, forward_gates(): pl.pallas_call(functools.partial(forward_gates_kernel, seqs), out_shape=(...  15.5 us
  transfers between devices with their start and end apart: 5, of which 1 were waited for; matrix products, arithmetic and copies ran while one was open for 12% of the time, Pallas kernels for 53%

profile of v6, /device:TPU:0, one launch (start us, length us, event | category | flops | bytes accessed | tf_op | source)
XLA Modules:
  0.0 668.1 jit_solution(7532174281581792102)
XLA Ops:
  7.2 3.0 shard_map.439
  10.2 133.2 %shard_map.440 = (bf16[2560,2560]{1,0:T(8,128)(2,1)}, bf16[2560,2560]{1,0:T(8,128)(2,1)}, bf16[2560,2560]{1,0:T(8,128)(2,1)}, bf16[416,2560]{1,0:T(8,128)(2,1)}, bf16[2,256,2560]{2,1,0:T(8,128)(2,1)}) custom-call(bf16[2560,640]{1,0:T(8,128)(2,1)} %refs_0_.1, bf16[2560,640]{1,0:T(8,128)(2,1)} %refs_1_.2, bf16[640,2560]{1,0:T(8,128)(2,1)} %refs_2_.1, ...), custom_call_target="tpu_custom_call" | custom-call | bytes 419430400 | tf_op jit(solution)/shard_map/pallas_call | solution.py:1169
  143.6 2.5 multiply_reduce_fusion.1
  147.1 2.0 fusion.13
  149.2 11.3 %fusion.40 = f32[512,2560]{1,0:T(8,128)S(1)} fusion(bf16[512,2560]{1,0:T(8,128)(2,1)S(1)} %fusion.1.refs_1_, bf16[2560,2560]{1,0:T(8,128)(2,1)} %get-tuple-element.72.w_input_ref), kind=kOutput, calls=%fused_computation.113 | convolution fusion | flops 6710886400 | bytes 20971520 | tf_op jit(solution)/shard_map/dot_general | solution.py:23
  160.5 1.8 add_convert_fusion
  163.8 3.7 collective-permute-start
  169.5 2.1 fusion.37
  171.7 2.1 fusion.36
  173.7 12.3 %fusion.41 = f32[512,2560]{1,0:T(8,128)} fusion(bf16[512,2560]{1,0:T(8,128)(2,1)} %copy-done.12, bf16[2560,2560]{1,0:T(8,128)(2,1)} %get-tuple-element.76.w_branch_ref), kind=kOutput, calls=%fused_computation.114 | convolution fusion | flops 6710886400 | bytes 20971520 | tf_op jit(solution)/shard_map/dot_general | solution.py:23
  186.4 1.6 slice.243
  188.0 2.5 maximum_convert_fusion
  190.6 5.3 fusion.8
  196.2 3.3 fusion.14.inner_ref
  199.9 15.5 %shard_map.441 = (f32[512,2560]{1,0:T(8,128)S(1)}, f32[512,2560]{1,0:T(8,128)S(1)}) custom-call(f32[512,2560]{1,0:T(8,128)} %bitcast.129, bf16[512,64]{1,0:T(8,128)(2,1)S(1)} %fusion.14.inner_ref, bf16[64,2560]{1,0:T(8,128)(2,1)S(1)} %get-tuple-element.131.lift_ref, bf16[10,256,256]{2,1,0:T(8,128)(2,1)S(1)} %copy-done.5, ...), custom_call_target="tpu_custom_call" | custom-call | flops 1420820480 | bytes 15728640 | tf_op jit(solution)/shard_map/pallas_call | solution.py:137
  215.6 10.1 %all-gather.1 = f32[4,4,2560]{2,1,0:T(4,128)S(1)} all-gather(f32[1,4,2560]{2,1,0:T(4,128)S(1)} %maximum_bitcast_fusion), channel_id=2, replica_groups=mesh['group'=4,'replica'=8] {'group'}, dimensions={0}, use_global_device_ids=true | all-gather | bytes 204800 | tf_op jit(solution)/shard_map/all_gather | solution.py:1464
  225.8 5.9 fusion.7
  231.8 1.9 fusion.12.refs_11_
  233.7 10.0 %fusion.42 = f32[512,2560]{1,0:T(8,128)S(1)} fusion(bf16[512,2560]{1,0:T(8,128)(2,1)S(1)} %get-tuple-element.161.refs_5_, bf16[2560,2560]{1,0:T(8,128)(2,1)} %get-tuple-element.77.w_ref), kind=kOutput, calls=%fused_computation.115 | convolution fusion | flops 6710886400 | bytes 20971520 | tf_op jit(solution)/shard_map/dot_general | solution.py:23
  243.8 2.2 multiply_reduce_fusion
  246.0 2.3 copy-done.8
  248.8 1.7 fusion.35
  250.6 51.2 %shard_map.442 = (bf16[2,1024,1920]{2,1,0:T(8,128)(2,1)}, bf16[2,1024,16]{2,1,0:T(8,128)(2,1)}, bf16[1024,2560]{1,0:T(8,128)(2,1)}) custom-call(bf16[2,1024,2560]{2,1,0:T(8,128)(2,1)} %all-gather.5.cloned.1.call-done.refs_0_.refs_6_, bf16[1920,2560]{1,0:T(8,128)(2,1)} %refs_7_.3, bf16[32,2560]{1,0:T(8,128)(2,1)} %get-tuple-element.134.refs_2_.refs_9_, ...), custom_call_target="tpu_custom_call" | custom-call | flops 20132659200 | bytes 28180480 | tf_op jit(solution)/shard_map/pallas_call | solution.py:791
  304.5 63.3 %shard_map.443 = (bf16[1024,1920]{1,0:T(8,128)(2,1)}, bf16[1024,2560]{1,0:T(8,128)(2,1)}, bf16[48,1920]{1,0:T(8,128)(2,1)}, bf16[1024,32]{1,0:T(8,128)(2,1)}) custom-call(bf16[1024,2560]{1,0:T(8,128)(2,1)} %get-tuple-element.80.tok_ref.refs_1_.refs_2_, bf16[2,1024,1920]{2,1,0:T(8,128)(2,1)} %get-tuple-element.81.gh_ref, bf16[2560,1920]{1,0:T(8,128)(2,1)} %wg_rows_ref.3, ...), custom_call_target="tpu_custom_call" | custom-call | flops 40265318400 | bytes 51118080 | tf_op jit(solution)/shard_map/pallas_call | solution.py:862
  369.0 62.8 %shard_map.445 = (bf16[1024,1920]{1,0:T(8,128)(2,1)}, bf16[1024,2560]{1,0:T(8,128)(2,1)}, bf16[48,1920]{1,0:T(8,128)(2,1)}, bf16[1024,32]{1,0:T(8,128)(2,1)}) custom-call(bf16[1024,2560]{1,0:T(8,128)(2,1)} %all-gather.7.cloned.1.call-done.tok_ref.refs_3_, bf16[2,1024,1920]{2,1,0:T(8,128)(2,1)} %get-tuple-element.81.gh_ref, bf16[2560,1920]{1,0:T(8,128)(2,1)} %wg_rows_ref.3, ...), custom_call_target="tpu_custom_call" | custom-call | flops 40265318400 | bytes 51118080 | tf_op jit(solution)/shard_map/pallas_call | solution.py:862
  431.8 52.0 %shard_map.446 = (bf16[2,1024,2560]{2,1,0:T(8,128)(2,1)}, bf16[2,1024,16]{2,1,0:T(8,128)(2,1)}, bf16[96,2560]{1,0:T(8,128)(2,1)}, bf16[256,2560]{1,0:T(8,128)(2,1)}) custom-call(bf16[1024,1920]{1,0:T(8,128)(2,1)} %get-tuple-element.84.refs_0_, bf16[1024,1920]{1,0:T(8,128)(2,1)} %get-tuple-element.85.refs_1_, ...), custom_call_target="tpu_custom_call" | custom-call | flops 20132659200 | bytes 28180480 | tf_op jit(solution)/shard_map/pallas_call | solution.py:976
  487.1 8.7 %shard_map.447 = (f32[512,2560]{1,0:T(8,128)}, bf16[512,2560]{1,0:T(8,128)(2,1)}) custom-call(f32[512,2560]{1,0:T(8,128)} %copy-done.8, bf16[512,2560]{1,0:T(8,128)(2,1)} %bitcast.133, f32[1,2560]{1,0:T(1,128)} %reshape.149.gain_ref, bf16[256,2560]{1,0:T(8,128)(2,1)} %reduce-scatter.3.cloned.1.call-done.refs_0_, bf16[256,2560]{1,0:T(8,128)(2,1)} %get-tuple-element.89.refs_1_), custom_call_target="tpu_custom_call" | custom-call | flops 26214400 | bytes 18350080 | tf_op jit(solution)/shard_map/pallas_call | solution.py:1220
  495.7 81.0 %shard_map.448 = (bf16[512,2560]{1,0:T(8,128)(2,1)}, bf16[512,64]{1,0:T(8,128)(2,1)}, bf16[512,64]{1,0:T(8,128)(2,1)}, f32[64,2560]{1,0:T(8,128)}, bf16[512,2560...) custom-call(bf16[512,2560]{1,0:T(8,128)(2,1)} %get-tuple-element.91.mixed_r, ...), custom_call_target="tpu_custom_call" | custom-call | flops 13683916800 | bytes 65536000 | tf_op jit(solution)/shard_map/pallas_call | solution.py:661
  578.3 9.5 %shard_map.449.partial_ref = bf16[4,320,640]{2,1,0:T(8,128)(2,1)} custom-call(bf16[512,64]{1,0:T(8,128)(2,1)} %get-tuple-element.97.refs_0_.through_ref, bf16[512,2560]{1,0:T(8,128)(2,1)} %copy-done.12, bf16[512,64]{1,0:T(8,128)(2,1)} %get-tuple-element.98.refs_2_, bf16[512,2560]{1,0:T(8,128)(2,1)} %copy-done.13, bf16[512,32]{1,0:T(8,128)(2,1)} %get-tuple-element.99.refs_4_, ...), custom_call_target="tpu_custom_call" | custom-call | flops 522190848 | bytes 16318464 | tf_op jit(solution)/shard_map/pallas_call | solution.py:1378
  587.8 55.0 %shard_map.450 = (f32[512,2560]{1,0:T(8,128)}, bf16[8,320,640]{2,1,0:T(8,128)(2,1)}) custom-call(bf16[512,2560]{1,0:T(8,128)(2,1)} %get-tuple-element.95.refs_7_.branch_grad_ref, bf16[512,2560]{1,0:T(8,128)(2,1)} %get-tuple-element.96.refs_9_.fed_grad_ref, bf16[2560,2560]{1,0:T(8,128)(2,1)} %get-tuple-element.76.w_branch_ref, ...), custom_call_target="tpu_custom_call" | custom-call | flops 13421772800 | bytes 36700160 | tf_op jit(solution)/shard_map/pallas_call | solution.py:1297
  642.8 7.0 %shard_map.452 = (f32[8,16,640]{2,1,0:T(8,128)}, f32[8,16,640]{2,1,0:T(8,128)}, f32[8,16,640]{2,1,0:T(8,128)}, f32[8,16,640]{2,1,0:T(8,128)}, f32[8,16,640]{2,1,...) custom-call(s32[16]{0:T(128)} %reshape.153.ids_ref, ...), custom_call_target="tpu_custom_call" | custom-call | flops 3850240 | bytes 15400960 | tf_op jit(solution)/shard_map/pallas_call | solution.py:1332
  649.8 11.5 %shard_map.451 = (f32[512,2560]{1,0:T(8,128)}, bf16[512,2560]{1,0:T(8,128)(2,1)}) custom-call(f32[512,2560]{1,0:T(8,128)} %get-tuple-element.90.grad_resid_ref, bf16[512,2560]{1,0:T(8,128)(2,1)} %bitcast.127, f32[1,2560]{1,0:T(1,128)} %broadcast_in_dim.10.gain_ref, f32[512,2560]{1,0:T(8,128)} %get-tuple-element.101.grads_ref, f32[512,2560]{1,0:T(8,128)} %copy-done.8, ...), custom_call_target="tpu_custom_call" | custom-call | flops 27525120 | bytes 28835840 | tf_op jit(solution)/shard_map/pallas_call | solution.py:1244
  (156 shorter events, 14.9 us)
Async XLA Ops:
  7.2 243.4 %all-gather.5.cloned.1.call-start = ((), (), s32[]{:S(2)}) async-start(), calls=%async_computation.2 | async-start | bytes 13107200 | tf_op jit(solution)/shard_map/all_gather | solution.py:1426
  143.5 225.6 %all-gather.7.cloned.1.call-start = ((), (), s32[]{:S(2)}) async-start(), calls=%async_computation.4 | async-start | bytes 6553600 | tf_op jit(solution)/shard_map/all_gather | solution.py:1482
  143.5 5.6 copy-start.37
  143.5 5.6 copy-start.39
  143.6 5.6 copy-start.29
  143.6 5.6 copy-start.31
  143.6 5.6 copy-start.41
  147.1 13.4 %copy-start.12 = (bf16[512,2560]{1,0:T(8,128)(2,1)}, bf16[512,2560]{1,0:T(8,128)(2,1)S(1)}, u32[]{:S(2)}) copy-start(bf16[512,2560]{1,0:T(8,128)(2,1)S(1)} %fusion.1.refs_1_) | copy-start | bytes 7864324
  149.2 76.6 %copy-start.15 = (bf16[512,64]{1,0:T(8,128)(2,1)}, bf16[512,64]{1,0:T(8,128)(2,1)S(1)}, u32[]{:S(2)}) copy-start(bf16[512,64]{1,0:T(8,128)(2,1)S(1)} %fusion.13) | copy-start | bytes 196612
  160.5 7.1 %copy-start.34 = (s32[2,1024]{1,0:T(2,128)S(1)}, s32[2,1024]{1,0:T(2,128)}, u32[]{:S(2)}) copy-start(s32[2,1024]{1,0:T(2,128)} %param.33) | copy-start | bytes 24580
  160.5 9.0 %copy-start.26 = (f32[2560]{0:T(1024)S(1)}, f32[2560]{0:T(1024)}, u32[]{:S(2)}) copy-start(f32[2560]{0:T(1024)} %param.42) | copy-start | bytes 30724
  163.8 24.2 %collective-permute-start = (bf16[2,3,2560]{2,1,0:T(4,128)(2,1)S(1)}, bf16[2,3,2560]{2,1,0:T(4,128)(2,1)S(1)}, u32[]{:S(2)}, u32[]{:S(2)}) collective-permute-start(bf16[2,3,2560]{2,1,0:T(4,128)(2,1)S(1)} %slice.271), channel_id=1, source_target_pairs={{0,8},{8,16},{16,24},{1,9},{9,17},{17,25},{2,10},{10,18},{18,26},{... | collective-permute-start | bytes 92168 | tf_op jit(solution)/shard_map/ppermute | solution.py:1396
  173.7 25.8 %copy-start.2 = (bf16[64,2560]{1,0:T(8,128)(2,1)}, bf16[64,2560]{1,0:T(8,128)(2,1)S(1)}, u32[]{:S(2)}) copy-start(bf16[64,2560]{1,0:T(8,128)(2,1)S(1)} %get-tuple-element.131.lift_ref) | copy-start | bytes 983044
  173.7 12.3 %copy-start.25 = (f32[4,2560]{1,0:T(4,128)S(1)}, f32[4,2560]{1,0:T(4,128)}, u32[]{:S(2)}) copy-start(f32[4,2560]{1,0:T(4,128)} %taps_ref.1) | copy-start | bytes 122884
  186.2 13.3 %copy-start.4 = (f32[1,2560]{1,0:T(1,128)}, f32[1,2560]{1,0:T(1,128)S(1)}, u32[]{:S(2)}) copy-start(f32[1,2560]{1,0:T(1,128)S(1)} %reshape.143.soft_ref) | copy-start | bytes 30724
  186.4 13.2 %copy-start.3 = (f32[1,512]{0,1:T(8,128)}, f32[1,512]{0,1:T(8,128)S(1)}, u32[]{:S(2)}) copy-start(f32[1,512]{0,1:T(8,128)S(1)} %copy.79) | copy-start | bytes 6148
  196.2 19.2 %copy-start.13 = (bf16[512,2560]{1,0:T(8,128)(2,1)}, bf16[512,2560]{1,0:T(8,128)(2,1)S(1)}, u32[]{:S(2)}) copy-start(bf16[512,2560]{1,0:T(8,128)(2,1)S(1)} %bitcast_convert_fusion.refs_3_) | copy-start | bytes 7864324
  199.5 15.9 %copy-start.7 = (bf16[512,64]{1,0:T(8,128)(2,1)}, bf16[512,64]{1,0:T(8,128)(2,1)S(1)}, u32[]{:S(2)}) copy-start(bf16[512,64]{1,0:T(8,128)(2,1)S(1)} %fusion.14.inner_ref) | copy-start | bytes 196612
  215.4 16.3 %copy-start = (f32[512,2560]{1,0:T(8,128)}, f32[512,2560]{1,0:T(8,128)S(1)}, u32[]{:S(2)}) copy-start(f32[512,2560]{1,0:T(8,128)S(1)} %get-tuple-element.75.cum_ref) | copy-start | bytes 15728644
  215.4 16.3 %copy-start.1 = (f32[512,2560]{1,0:T(8,128)}, f32[512,2560]{1,0:T(8,128)S(1)}, u32[]{:S(2)}) copy-start(f32[512,2560]{1,0:T(8,128)S(1)} %get-tuple-element.74.local_ref) | copy-start | bytes 15728644
  225.8 6.0 copy-start.21
  225.8 6.0 copy-start.30
  225.8 6.0 copy-start.32
  225.8 6.0 copy-start.38
  225.8 6.0 copy-start.40
  225.8 6.0 copy-start.42
  225.8 6.0 copy-start.44
  231.7 12.1 %copy-start.14 = (bf16[512,2560]{1,0:T(8,128)(2,1)}, bf16[512,2560]{1,0:T(8,128)(2,1)S(1)}, u32[]{:S(2)}) copy-start(bf16[512,2560]{1,0:T(8,128)(2,1)S(1)} %get-tuple-element.161.refs_5_) | copy-start | bytes 7864324
  233.7 10.1 %copy-start.17 = (bf16[512,32]{1,0:T(8,128)(2,1)}, bf16[512,32]{1,0:T(8,128)(2,1)S(1)}, u32[]{:S(2)}) copy-start(bf16[512,32]{1,0:T(8,128)(2,1)S(1)} %fusion.12.refs_11_) | copy-start | bytes 98308
  301.9 185.2 %reduce-scatter.3.cloned.1.call-start = ((), (), s32[]{:S(2)}) async-start(), calls=%async_computation.3 | async-start | bytes 6553600 | tf_op jit(solution)/shard_map/reduce_scatter | solution.py:1490
  367.9 281.9 %reduce-scatter.5.cloned.1.call-start = ((), (), s32[]{:S(2)}) async-start(), calls=%async_computation.5 | async-start | bytes 13107200 | tf_op jit(solution)/shard_map/reduce_scatter | solution.py:1503
  487.1 8.7 %copy-start.27 = (bf16[112,1920]{1,0:T(8,128)(2,1)}, bf16[112,1920]{1,0:T(8,128)(2,1)S(1)}, u32[]{:S(2)}) copy-start(bf16[112,1920]{1,0:T(8,128)(2,1)S(1)} %broadcast_dynamic-update-slice_fusion.wide_ref) | copy-start | bytes 1290244
  (19 other events, 48.8 us)
Sparse Core Ops, SparseCore 0:
  143.6 106.9 all-gather.4
  302.0 61.4 all-gather.6
  368.0 61.2 reduce-scatter.2
  484.0 110.9 reduce-scatter.4

commit v7 on v6

--- a/solution.py
+++ b/solution.py
@@ -450,6 +450,8 @@
     stretch = rows // seqs
     half = lift_ref.shape[0] // 2
     ranks = lift_branch_ref.shape[0]
+    each = table_d_ref.shape[1]
+    lanes = [slice(q * each, (q + 1) * each) for q in range(size // each)]
     step = pl.program_id(0)
     group, replica = lax.axis_index("group"), lax.axis_index("replica")
     partners = [(group + 1 - 2 * (group % 2), replica), ((group + 2) % 4, replica), (3 - group, replica)]
@@ -485,19 +487,19 @@
         through = dot(mixed_ref[...], lift_mixer_ref[...], NT)
         thr_mixer_ref[...] = jnp.where(row == col, through, 0.0).astype(BF16)
 
-    stops = 3 * heads // (levels + 2)
-
-    @pl.when(step == stops // 2)
+    stops = 3 * heads / (levels + 2)
+
+    @pl.when(step == int(stops / 2))
     def _():
         total_early.middle()
 
-    @pl.when(step == stops)
+    @pl.when(step == int(stops))
     def _():
         total_early.end()
         chains[0].begin()
 
     for d in range(1, levels):
-        @pl.when(step == (d + 1) * stops)
+        @pl.when(step == int((d + 1) * stops))
         def _(d=d):
             for chain in chains:
                 chain.hop(d)
@@ -511,8 +513,9 @@
     def _():
         cols = pl.ds(pl.multiple_of(step * size, size), size)
         first_ref[...] = dot(mixed_ref[...], w_ref[...], NT) + dot(thr_mixer_ref[...], down_mixer_ref[...])
-        second_ref[...] = (dot(conv_ref[...].astype(BF16), table_d_ref[0])
-                           + dot(inner_ref[:, :half], lift_ref[:half, :]))
+        for q, at in enumerate(lanes):
+            second_ref[:, at] = (dot(conv_ref[:, at].astype(BF16), table_d_ref[q])
+                                 + dot(inner_ref[:, :half], lift_ref[:half, at]))
         softrate = soft_ref[...]
 
         def group(lap, carries):
@@ -562,9 +565,10 @@
     def _():
         head = step - heads
         cols = pl.ds(pl.multiple_of(head * size, size), size)
-        rounded = conv_ref[...].astype(BF16)
-        first_ref[...] = dot(rounded, table_d_ref[0]) + dot(inner_ref[:, :half], lift_ref[:half, :])
-        second_ref[...] = dot(rounded, table_a_ref[0]) + dot(inner_ref[:, half:], lift_ref[half:, :])
+        for q, at in enumerate(lanes):
+            rounded = conv_ref[:, at].astype(BF16)
+            first_ref[:, at] = dot(rounded, table_d_ref[q]) + dot(inner_ref[:, :half], lift_ref[:half, at])
+            second_ref[:, at] = dot(rounded, table_a_ref[q]) + dot(inner_ref[:, half:], lift_ref[half:, at])
         softrate = soft_ref[...]
         rate = -8.0 * softrate
 
@@ -591,7 +595,8 @@
 
         lax.fori_loop(0, groups, group, tuple(carried_ref[s : s + 1, :] for s in range(seqs)), unroll=UNROLL)
         low_d, low_a = low_d_ref[...], low_a_ref[...]
-        total_ref[head] += dot(low_d, table_d_ref[0], NT) + dot(low_a, table_a_ref[0], NT)
+        for q, at in enumerate(lanes):
+            total_ref[head, :, at] += dot(low_d[:, at], table_d_ref[q], NT) + dot(low_a[:, at], table_a_ref[q], NT)
         gates_ref[:, :half] += dot(low_d, lift_ref[:half, :], NT)
         gates_ref[:, half:] += dot(low_a, lift_ref[half:, :], NT)
         lift_grad_ref[:half, :] = dot(inner_ref[:, :half], low_d, TN)
@@ -647,14 +652,16 @@
                cum, local, carried, pre, lift_branch, lift_input, down_gates, taps, agree, early, wide):
     rows, width = conv.shape
     count, early_cols = lax.axis_size("replica"), width // 4
-    heads, size = table_d.shape[:2]
+    heads, each = table_d.shape[:2]
+    per = 2 if heads % 2 == 0 else 1
+    heads, size = heads // per, per * each
     first = lambda i: jnp.minimum(i, heads - 1)
     second = lambda i: jnp.clip(i - heads, 0, heads - 1)
     third = lambda i: jnp.maximum(i - 2 * heads, 0)
     either = lambda i: jnp.minimum(i, 2 * heads - 1) % heads
     full = lambda array: pl.BlockSpec(array.shape, lambda i: (0, 0), pipeline_mode=pl.Buffered(1))
     cols = lambda array, at: pl.BlockSpec((array.shape[0], size), lambda i: (0, at(i)))
-    table = pl.BlockSpec((1, size, size), lambda i: (either(i), 0, 0))
+    table = pl.BlockSpec((per, each, each), lambda i: (either(i), 0, 0))
     middle = inner.shape[1]
     tile = lambda at: pl.BlockSpec((rows, size), lambda i: (0, at(i)))
     whole = lambda count: pl.BlockSpec((rows, count), lambda i: (0, 0))
@@ -708,8 +715,8 @@
 
 def grad_hidden_kernel(seqs, gather, steps, *refs):
     if gather:
-        cot_ref, wd_ref, lift_out_ref, do_ref, block_ref, out_ref, through_ref, all_ref = refs[:8]
-        staged_ref, send, recv, local = refs[8:]
+        cot_ref, wd_ref, lift_out_ref, do_ref, block_ref = refs[:5]
+        out_ref, through_ref, all_ref, staged_ref, send, recv, local = refs[-7:]
     else:
         cot_ref, wd_ref, lift_out_ref, do_ref, out_ref, through_ref = refs
     ranks = do_ref.shape[0] // seqs
@@ -783,7 +790,7 @@
             keep.wait()
 
 
-def grad_hidden_call(cot, wd, lift_out, do, block):
+def grad_hidden_call(cot, wd, lift_out, do, block, earlier):
     seqs, rows, width = cot.shape
     units, ranks = wd.shape[0], do.shape[0] // seqs
     tile = tile_of(units, 512)
@@ -795,7 +802,7 @@
         + [jax.ShapeDtypeStruct((rows, width), BF16)] * gather,
         in_specs=[pl.BlockSpec(cot.shape, lambda i: (0, 0, 0), pipeline_mode=pl.Buffered(1)),
                   pl.BlockSpec((tile, width), lambda i: (i, 0)), resident(lift_out),
-                  pl.BlockSpec((seqs * ranks, tile), lambda i: (0, i))] + [ANYWHERE] * gather,
+                  pl.BlockSpec((seqs * ranks, tile), lambda i: (0, i))] + [ANYWHERE] * (gather + gather * len(earlier)),
         out_specs=[pl.BlockSpec((seqs, rows, tile), lambda i: (0, 0, i)),
                    pl.BlockSpec((seqs, rows, ranks), lambda i: (0, 0, 0))] + [ANYWHERE] * gather,
         scratch_shapes=[pltpu.VMEM(block.shape, BF16), pltpu.SemaphoreType.DMA((6,)), pltpu.SemaphoreType.DMA((6,)),
@@ -805,7 +812,7 @@
         cost_estimate=pl.CostEstimate(
             flops=2 * seqs * rows * width * units,
             bytes_accessed=2 * width * units + 2 * seqs * rows * (units + width), transcendentals=0),
-    )(cot, wd, lift_out, do, *([block] if gather else []))
+    )(cot, wd, lift_out, do, *([block, *earlier] if gather else []))
     return got if gather else list(got) + [lax.all_gather(block, "group", axis=0, tiled=True)]
 
 
@@ -880,8 +887,9 @@
 
 
 def outward_kernel(seqs, reduce, steps, *refs):
-    hiddens, tokens, throughs, cot_ref, refs = (
-        refs[:seqs], refs[seqs : 2 * seqs], refs[2 * seqs : 3 * seqs], refs[3 * seqs], refs[3 * seqs + 1 :])
+    hiddens, tokens, throughs, (cot_ref, resid_ref), refs = (
+        refs[:seqs], refs[seqs : 2 * seqs], refs[2 * seqs : 3 * seqs], refs[3 * seqs : 3 * seqs + 2],
+        refs[3 * seqs + 2 :])
     if reduce:
         wd_ref, do_ref, lift_out_ref, back_ref, out_ref, inner_ref, early_ref, sum_ref = refs[:8]
         first_a, first_b, second_a, second_b, pass_a, pass_b, own_ref, send, recv, local = refs[8:]
@@ -932,6 +940,9 @@
     for s, hidden_ref in enumerate(hiddens):
         out_ref[s] = (dot(hidden_ref[...], wd_ref[...])
                       + dot(inner_ref[s], lift_out_ref[s * ranks : (s + 1) * ranks, :])).astype(BF16)
+        own = resid_ref.shape[0] // seqs
+        mine = pl.ds(pl.multiple_of(lax.axis_index("group") * own, own), own)
+        out_ref[s, mine, :] = (out_ref[s, mine, :].astype(F32) + resid_ref[s * own : (s + 1) * own, :]).astype(BF16)
         both = dot(throughs[s][...], tokens[s][...], TN).astype(BF16)
         for kind, rows_of in enumerate((both[:ranks], both[ranks:], dot(inner_ref[s], cot_ref[s], TN).astype(BF16))):
             row = (kind * seqs + s) * ranks
@@ -961,7 +972,7 @@
                 one.wait_send()
 
 
-def outward_call(hiddens, tokens, throughs, cot, wd, do, lift_out, back):
+def outward_call(hiddens, tokens, throughs, cot, resid, wd, do, lift_out, back):
     rows, units = hiddens[0].shape
     seqs = len(hiddens)
     width, ranks = wd.shape[1], do.shape[0] // seqs
@@ -981,6 +992,7 @@
         + [jax.ShapeDtypeStruct((own, width), BF16)] * reduce,
         in_specs=[resident(hidden) for hidden in hiddens] + [pl.BlockSpec((rows, tile), lambda i: (0, i))] * seqs
         + [resident(through) for through in throughs] + [pl.BlockSpec((seqs, rows, tile), lambda i: (0, 0, i))]
+        + [pl.BlockSpec((resid.shape[0], tile), lambda i: (0, i))]
         + [pl.BlockSpec((units, tile), lambda i: (0, i)), resident(do),
            pl.BlockSpec((seqs * ranks, tile), lambda i: (0, i))] + [ANYWHERE] * reduce,
         out_specs=[pl.BlockSpec((seqs, rows, tile), lambda i: (0, 0, i)),
@@ -993,7 +1005,7 @@
         cost_estimate=pl.CostEstimate(
             flops=2 * seqs * rows * width * units,
             bytes_accessed=2 * width * units + 2 * seqs * rows * (units + width), transcendentals=0),
-    )(*hiddens, *tokens, *throughs, cot, wd, do, lift_out, *([back] if reduce else []))
+    )(*hiddens, *tokens, *throughs, cot, resid, wd, do, lift_out, *([back] if reduce else []))
     return got if reduce else list(got) + [lax.psum_scatter(back, "group", scatter_dimension=0, tiled=True)]
 
 
@@ -1025,9 +1037,13 @@
     return [part.reshape(-1, part.shape[-1]) for part in picked]
 
 
-def gather_kernel(units, *refs):
-    weights, passed, wholes, handed_out = refs[:4], refs[4], refs[5:9], refs[9]
-    staged, handed, (send, recv, local) = refs[10:14], refs[14], refs[15:]
+def gather_kernel(units, counts, seqs, *refs):
+    refs = list(refs)
+    take = lambda count: [refs.pop(0) for _ in range(count)]
+    weights, (passed, values, gain_ref, ids_ref), tables = take(3), take(4), take(sum(counts))
+    wholes, (handed_out, normed_ref, own_ref) = take(4), take(3)
+    staged, (handed, values_ref), loaded, (send, recv, local, table_sems) = take(4), take(2), take(sum(counts)), refs
+    weights = weights + [staged[3]]
     group, replica = lax.axis_index("group"), lax.axis_index("replica")
     beside, above, across = group + 1 - 2 * (group % 2), (group + 2) % 4, 3 - group
     core, level = replica % 2, (replica // 2) % 2
@@ -1042,9 +1058,7 @@
     pl.semaphore_wait(barrier, 4)
 
     kept = [pltpu.make_async_copy(weight, stage, local.at[m])
-            for m, (weight, stage) in enumerate(zip(weights, staged))]
-    for one in kept:
-        one.start()
+            for m, (weight, stage) in enumerate(zip(weights[:3], staged))] + [None]
 
     def keep(m):
         whole = wholes[m]
@@ -1053,7 +1067,8 @@
             into = whole.at[pl.ds(pl.multiple_of(group * rows, rows), rows), :]
         else:
             into = whole.at[:, pl.ds(pl.multiple_of(group * cols, cols), cols)]
-        kept[m].wait()
+        if kept[m] is not None:
+            kept[m].wait()
         kept[m] = pltpu.make_async_copy(staged[m], into, local.at[m])
         kept[m].start()
 
@@ -1101,10 +1116,37 @@
 
     begin(0)
     begin(1)
-    for m in range(4):
+    onward = pltpu.make_async_copy(passed, handed, local.at[4])
+    fetch = [pltpu.make_async_copy(values, values_ref, local.at[5])] + [
+        pltpu.make_async_copy(table, place, table_sems.at[i]) for i, (table, place) in enumerate(zip(tables, loaded))]
+    for one in kept[:3] + [onward] + fetch:
+        one.start()
+    for m in range(3):
         keep(m)
-    onward = pltpu.make_async_copy(passed, handed, local.at[4])
-    onward.start()
+
+    def pick_sets():
+        for one in fetch[1:]:
+            one.wait()
+        depth = loaded[0].shape[1]
+        for i, table in enumerate(loaded):
+            out, first = (staged[3], i) if i < counts[0] else (own_ref, i - counts[0])
+            for s in range(seqs):
+                row = (first * seqs + s) * depth
+                out[row : row + depth, :] = table[ids_ref[s]]
+        keep(3)
+
+    def norm_values():
+        fetch[0].wait()
+        count = values_ref.shape[0]
+        step = 64 if count % 64 == 0 else count
+
+        def some_rows(i, _):
+            at = pl.ds(pl.multiple_of(i * step, step), step)
+            normed_ref[at, :] = norm_rows(values_ref[at, :].astype(F32), gain_ref[...])[0].astype(BF16)
+            return 0
+
+        lax.fori_loop(0, count // step, some_rows, 0)
+
     for t in range(len(steps) + 2):
         if t < len(steps):
             m, part = steps[t]
@@ -1116,6 +1158,10 @@
             made[t, 8] = forward(m, part, beside, mine, t, 8, at_core)
             if t + 2 < len(steps):
                 begin(t + 2)
+            if t == len(steps) // 3:
+                pick_sets()
+            if t == len(steps) // 2:
+                norm_values()
             if t + 3 == len(steps):
                 stack_beside = copy(weights[3], stack_piece(0, ranks, group), last, 0, at_beside)
                 stack_above = copy(weights[3], stack_piece(0, ranks, group), last, 1, at_above)
@@ -1157,28 +1203,35 @@
         one.wait()
 
 
-def gather_weights(w_branch, w_input, w_mixer, stack, passed):
-    width = w_branch.shape[0]
+def gather_weights(w_branch, w_input, w_mixer, passed, values, gain, ids, narrow, wide):
+    width, (rows, _), seqs = w_branch.shape[0], values.shape, ids.shape[0]
     if lax.axis_size("group") != 4 or lax.axis_size("replica") % 4 != 0:
+        stack, own = pick(ids, narrow, wide)
         return (lax.all_gather(w_branch, "group", axis=1, tiled=True),
                 lax.all_gather(w_input, "group", axis=1, tiled=True),
                 lax.all_gather(w_mixer, "group", axis=0, tiled=True),
-                lax.all_gather(stack, "group", axis=1, tiled=True), passed)
+                lax.all_gather(stack, "group", axis=1, tiled=True), passed,
+                norm_rows(values.astype(F32), gain)[0].astype(BF16), own)
     units = 4
-    operands = (w_branch, w_input, w_mixer, stack, passed)
+    counts = (len(narrow), len(wide))
+    ranks = narrow[0].shape[1]
+    vmem = pl.BlockSpec(memory_space=pltpu.VMEM)
+    stack = jax.ShapeDtypeStruct((counts[0] * seqs * ranks, narrow[0].shape[2]), BF16)
+    dma = pltpu.SemaphoreType.DMA
     return pl.pallas_call(
-        functools.partial(gather_kernel, units),
+        functools.partial(gather_kernel, units, counts, seqs),
         out_shape=[jax.ShapeDtypeStruct((width, width), BF16)] * 3
-        + [jax.ShapeDtypeStruct((stack.shape[0], width), BF16), jax.ShapeDtypeStruct(passed.shape, passed.dtype)],
-        in_specs=[ANYWHERE] * 5,
-        out_specs=[ANYWHERE] * 5,
-        scratch_shapes=[pltpu.VMEM(operand.shape, BF16) for operand in operands]
-        + [pltpu.SemaphoreType.DMA((3 * units + 1, 12)), pltpu.SemaphoreType.DMA((3 * units + 1, 12)),
-           pltpu.SemaphoreType.DMA((5,))],
-        compiler_params=pltpu.CompilerParams(
-            collective_id=0, has_side_effects=True, vmem_limit_bytes=VMEM),
+        + [jax.ShapeDtypeStruct((stack.shape[0], width), BF16), jax.ShapeDtypeStruct(passed.shape, passed.dtype),
+           jax.ShapeDtypeStruct(values.shape, BF16),
+           jax.ShapeDtypeStruct((counts[1] * seqs * ranks, wide[0].shape[2]), BF16)],
+        in_specs=[ANYWHERE] * 5 + [vmem, pl.BlockSpec(memory_space=pltpu.SMEM)] + [ANYWHERE] * sum(counts),
+        out_specs=[ANYWHERE] * 5 + [vmem] * 2,
+        scratch_shapes=[pltpu.VMEM(part.shape, BF16)
+                        for part in (w_branch, w_input, w_mixer, stack, passed, values, *narrow, *wide)]
+        + [dma((3 * units + 1, 12)), dma((3 * units + 1, 12)), dma((6,)), dma((sum(counts),))],
+        compiler_params=pltpu.CompilerParams(collective_id=0, has_side_effects=True, vmem_limit_bytes=VMEM),
         cost_estimate=pl.CostEstimate(flops=0, bytes_accessed=400 * 2**20, transcendentals=0),
-    )(*operands)
+    )(w_branch, w_input, w_mixer, passed, values, gain, ids, *narrow, *wide)
 
 
 def ordered_kernel(*refs):
@@ -1200,16 +1253,30 @@
     return (rows // step,), [pl.BlockSpec((step, width), lambda i: (i, 0))] * count
 
 
+def by_groups(count, action):
+    size = GROUP if count % GROUP == 0 else count
+
+    def one(k, _):
+        action(pl.ds(pl.multiple_of(k * size, size), size))
+        return 0
+
+    lax.fori_loop(0, count // size, one, 0, unroll=2 if count % (2 * size) == 0 else 1)
+
+
 def resid_grad_kernel(per, resid_ref, cot_ref, gain_ref, *refs):
     pieces, (full_ref, low_ref) = refs[:-2], refs[-2:]
-    grads = pieces[0][...]
-    for s, piece in enumerate(pieces[1:], 1):
-        grads = jnp.where(pl.program_id(0) >= s * per, piece[...], grads)
-    values = resid_ref[...]
-    rate = lax.rsqrt(jnp.mean(values * values, axis=-1, keepdims=True) + EPS)
-    grads = cot_ref[...].astype(F32) + norm_back(values, gain_ref[...], rate, grads.astype(F32))
-    full_ref[...] = grads
-    low_ref[...] = grads.astype(BF16)
+
+    def some_rows(at):
+        values = resid_ref[at, :]
+        rate = lax.rsqrt(jnp.mean(values * values, axis=-1, keepdims=True) + EPS)
+        grads = pieces[0][at, :]
+        for s, piece in enumerate(pieces[1:], 1):
+            grads = jnp.where(pl.program_id(0) >= s * per, piece[at, :], grads)
+        grads = cot_ref[at, :].astype(F32) + norm_back(values, gain_ref[...], rate, grads.astype(F32))
+        full_ref[at, :] = grads
+        low_ref[at, :] = grads.astype(BF16)
+
+    by_groups(resid_ref.shape[0], some_rows)
 
 
 def resid_grad(resid, cot, gain, pieces):
@@ -1231,26 +1298,29 @@
     )(resid, cot, gain, *pieces)
 
 
-def finish_kernel(grad_resid_ref, inputs_ref, gain_ref, grads_ref, resid_ref, outward_ref, out_ref, block_ref):
-    values = inputs_ref[...].astype(F32)
-    rate = lax.rsqrt(jnp.mean(values * values, axis=-1, keepdims=True) + EPS)
-    out_ref[...] = grad_resid_ref[...] + norm_back(values, gain_ref[...], rate, grads_ref[...])
-    block_ref[...] = (resid_ref[...] + outward_ref[...].astype(F32)).astype(BF16)
-
-
-def finish(grad_resid, inputs, gain, grads, resid, outward):
+def finish_kernel(grad_resid_ref, inputs_ref, gain_ref, grads_ref, out_ref):
+    def some_rows(at):
+        values = inputs_ref[at, :].astype(F32)
+        rate = lax.rsqrt(jnp.mean(values * values, axis=-1, keepdims=True) + EPS)
+        out_ref[at, :] = grad_resid_ref[at, :] + norm_back(values, gain_ref[...], rate, grads_ref[at, :])
+
+    by_groups(inputs_ref.shape[0], some_rows)
+
+
+def finish(grad_resid, inputs, gain, grads):
     rows, width = inputs.shape
-    grid, tiles = row_tiles(rows, width, 5)
+    step = min(rows, 128)
+    tile = pl.BlockSpec((step, width), lambda i: (i, 0))
     return pl.pallas_call(
         finish_kernel,
-        grid=grid,
-        out_shape=[jax.ShapeDtypeStruct((rows, width), F32), jax.ShapeDtypeStruct((rows, width), BF16)],
-        in_specs=tiles[:2] + [pl.BlockSpec((1, width), lambda i: (0, 0))] + tiles[:3],
-        out_specs=tiles[:2],
+        grid=(rows // step,),
+        out_shape=jax.ShapeDtypeStruct((rows, width), F32),
+        in_specs=[tile, tile, pl.BlockSpec((1, width), lambda i: (0, 0)), tile],
+        out_specs=tile,
         compiler_params=pltpu.CompilerParams(vmem_limit_bytes=VMEM),
         cost_estimate=pl.CostEstimate(
-            flops=21 * rows * width, bytes_accessed=22 * rows * width, transcendentals=rows),
-    )(grad_resid, inputs, gain, grads, resid, outward)
+            flops=21 * rows * width, bytes_accessed=14 * rows * width, transcendentals=rows),
+    )(grad_resid, inputs, gain, grads)
 
 
 def tail_kernel(
@@ -1410,14 +1480,12 @@
     mask_cols = seqs * ranks
 
     turned = lambda table: jnp.swapaxes(table, 1, 2)
-    stack, own_tables = pick(
-        adapter_ids,
+    full_branch, full_input, full_mixer, stack, late_grad, normed, own_tables = gather_weights(
+        w_branch, w_input, w_mixer, out_grad, inputs.reshape(rows, width), gain_mix.reshape(1, width), adapter_ids,
         [turned(down_branch), turned(down_input), turned(down_decay), turned(down_admit), turned(down_mixer),
          turned(down_gate), turned(down_upper), lift_branch, lift_input, lift_decay, lift_admit, lift_mixer,
          lift_outward],
         [lift_gate, lift_upper, turned(down_outward)])
-    full_branch, full_input, full_mixer, stack, late_grad = gather_weights(
-        w_branch, w_input, w_mixer, stack, out_grad)
     (p_down_branch, p_down_input, p_down_decay, p_down_admit, p_down_mixer, p_down_gate, p_down_upper,
      p_lift_branch, p_lift_input, p_lift_decay, p_lift_admit, p_lift_mixer, p_lift_outward) = [
         stack[i * mask_cols : (i + 1) * mask_cols] for i in range(13)]
@@ -1441,8 +1509,6 @@
     restart = (1.0 - agree[1][:, :stretch]).reshape(rows, 1)
 
     x_float = inputs.reshape(rows, width).astype(F32)
-    normed_f, _ = norm_rows(x_float, gain_mix)
-    normed = normed_f.astype(BF16)
     inner_one = (dot(normed, stack[: 2 * mask_cols], NT) * own_two).astype(BF16)
     inner_branch, inner_input = inner_one[:, :mask_cols], inner_one[:, mask_cols:]
     branch_pre = dot(normed, full_branch) + dot(inner_branch, p_lift_branch)
@@ -1476,8 +1542,12 @@
     normed_two = normed_two_f.astype(BF16).reshape(seqs, stretch, width)
 
     spans = [slice(s * ranks, (s + 1) * ranks) for s in range(seqs)]
+    named = jnp.broadcast_to(jnp.pad(adapter_ids, (0, -seqs % 16)).astype(BF16)[:, None], (-(-seqs // 16) * 16,
+                                                                                   w_gate.shape[1]))
+    gain_one, gain_two = gain_mix.reshape(1, width), gain_mlp.reshape(1, width)
+    agree_cols = jnp.stack([agree[j][:, j : j + stretch].reshape(rows) for j in range(taps)], 1)
     grad_hiddens, through_out, first_tokens = grad_hidden_call(
-        cotangents, w_down, p_lift_outward, own_down_outward, normed_two[0])
+        cotangents, w_down, p_lift_outward, own_down_outward, normed_two[0], (gain_two, gain_one, agree_cols, named))
     all_tokens = [first_tokens] + [
         lax.all_gather(ordered(normed_two[s], first_tokens), "group", axis=0, tiled=True) for s in range(1, seqs)]
     backs, hiddens, throughs, wides = [], [], [], []
@@ -1492,20 +1562,17 @@
         throughs.append(through)
         wides.append(wide)
     outward, _, early, reduced = outward_call(
-        hiddens, all_tokens, throughs, cotangents, w_down, own_down_outward, p_lift_outward, back)
+        hiddens, all_tokens, throughs, cotangents, resid, w_down, own_down_outward, p_lift_outward, back)
     backs.append(reduced)
-    named = jnp.broadcast_to(jnp.pad(adapter_ids, (0, -seqs % 16)).astype(BF16)[:, None], (-(-seqs // 16) * 16,
-                                                                                   wides[0].shape[1]))
     wide = jnp.concatenate(
         [wides[s][i * ranks : (i + 1) * ranks] for i in range(3) for s in range(seqs)] + [named], 0)
     grad_resid, grad_mixed = resid_grad(
-        resid, out_grad.reshape(rows, width), gain_mlp.reshape(1, width), backs)
-    outward = lax.psum_scatter(outward, "group", scatter_dimension=1, tiled=True).reshape(rows, width)
+        resid, out_grad.reshape(rows, width), gain_two, backs)
+    block_out = lax.psum_scatter(outward, "group", scatter_dimension=1, tiled=True)
 
     kernels = (group == 4 and lax.axis_size("replica") % 2 == 0 and 2 * seqs <= 8 and stretch % GROUP == 0
                and width % 512 == 0 and seqs % 2 == 0)
     if kernels:
-        agree_cols = jnp.stack([agree[j][:, j : j + stretch].reshape(rows) for j in range(taps)], 1)
         grad_branch_pre, through_one, through_gates, grad_lift_gates, grad_fed, through_mixer, got_early, got_wide = mixer_back(
             seqs, grad_mixed, full_mixer, p_lift_mixer, p_down_mixer, convolved, inner_gates, lift_gates, decay_heads,
             admit_heads, softrate, restart, cum, local, carried, branch_pre, p_lift_branch, p_lift_input,
@@ -1550,14 +1617,13 @@
         got_late = lax.all_gather(lax.psum_scatter(late, "group", scatter_dimension=0, tiled=False), "replica")
         got_early = lax.all_gather(lax.psum_scatter(early, "group", scatter_dimension=1, tiled=True), "replica")
         got_wide = lax.all_gather(wide, "replica")
-    grad_inputs, block_out = finish(
-        grad_resid, inputs.reshape(rows, width), gain_mix.reshape(1, width), grad_normed, resid, outward)
+    grad_inputs = finish(grad_resid, inputs.reshape(rows, width), gain_one, grad_normed)
     all_ids = got_wide[:, 3 * mask_cols : 3 * mask_cols + seqs, 0].astype(jnp.int32).reshape(-1)
     totals = spread(all_ids, [got_late, got_early, got_wide], (10, 3, 3), sets, ranks)
     (t_down_branch, t_down_input, t_down_decay, t_down_admit, t_down_mixer, t_lift_branch, t_lift_input, t_lift_decay,
      t_lift_admit, t_lift_mixer, t_down_gate, t_down_upper, t_lift_outward, *wides) = totals
     return (
-        block_out.reshape(seqs, stretch, width), grad_inputs.reshape(seqs, stretch, width),
+        block_out, grad_inputs.reshape(seqs, stretch, width),
         turned(t_down_branch), t_lift_branch, turned(t_down_input), t_lift_input, turned(t_down_decay), t_lift_decay,
         turned(t_down_admit), t_lift_admit, turned(t_down_mixer), t_lift_mixer, turned(t_down_gate), wides[0],
         turned(t_down_upper), wides[1], turned(wides[2]), t_lift_outward,

time: 677 us -> 672 us (level)
    pallas_call x1, Pallas kernels: 55 us -> 63.3 us  [tail_call(): pl.pallas_call(functools.partial(tail_kernel, steps), grid=(steps,), out_...]
    pallas_call x1, Pallas kernels: 81 us -> 73.2 us  [mixer_back(): pl.pallas_call(functools.partial(mixer_back_kernel, seqs, heads), grid=(3...]
    pallas_call x3 -> x2, Pallas kernels: 148 us -> 144 us  [the longest x1 136 us: gather_weights(): pl.pallas_call(functools.partial(gather_kernel, units, counts, seqs), out...]
  transfers between devices with their start and end apart: 5 -> 5, of which waited for: 1 -> 1; matrix products, arithmetic and copies ran while one was open for 12% -> 11% of each run, Pallas kernels for 53% -> 55%
where the time goes in v7:
time: 672 us; the launch traced here: 666 us
  Pallas kernels  552 us (82%)
  matrix products  49.9 us (7%)
  local copies, waits for them, and re-layouts  20.3 us (3%)
  between operations  14.8 us (2%)
  blocking collectives  10.1 us (2%)
  other arithmetic  9.96 us (1%)
    pallas_call x1, Pallas kernels, gather_weights(): pl.pallas_call(functools.partial(gather_kernel, units, counts, seqs), out...  136 us
    pallas_call x2, Pallas kernels, feed_call(): pl.pallas_call(functools.partial(feed_kernel, steps, tile, units), grid=(...  126 us
    pallas_call x1, Pallas kernels, mixer_back(): pl.pallas_call(functools.partial(mixer_back_kernel, seqs, heads), grid=(3...  73.2 us
    pallas_call x1, Pallas kernels, tail_call(): pl.pallas_call(functools.partial(tail_kernel, steps), grid=(steps,), out_...  63.3 us
    pallas_call x1, Pallas kernels, outward_call(): pl.pallas_call(functools.partial(outward_kernel, seqs, reduce, steps), gr...  52.1 us
    pallas_call x1, Pallas kernels, grad_hidden_call(): pl.pallas_call(functools.partial(grad_hidden_kernel, seqs, gather, pl.cdi...  51.2 us
    dot_general x9, matrix products, dot(): return lax.dot_general(a, b, dims, preferred_element_type=F32)  49.9 us
    pallas_call x1, Pallas kernels, forward_gates(): pl.pallas_call(functools.partial(forward_gates_kernel, seqs), out_shape=(...  15.6 us
  transfers between devices with their start and end apart: 5, of which 1 were waited for; matrix products, arithmetic and copies ran while one was open for 11% of the time, Pallas kernels for 55%

profile of v7, /device:TPU:0, one launch (start us, length us, event | category | flops | bytes accessed | tf_op | source)
XLA Modules:
  0.0 666.5 jit_solution(1582786335815211770)
XLA Ops:
  7.2 1.3 reshape.107.refs_5_.refs_6_.gain_ref
  8.5 135.7 %shard_map.439 = (bf16[2560,2560]{1,0:T(8,128)(2,1)}, bf16[2560,2560]{1,0:T(8,128)(2,1)}, bf16[2560,2560]{1,0:T(8,128)(2,1)}, bf16[416,2560]{1,0:T(8,128)(2,1)},...) custom-call(bf16[2560,640]{1,0:T(8,128)(2,1)} %refs_0_.1, ...), custom_call_target="tpu_custom_call" | custom-call | bytes 419430400 | tf_op jit(solution)/shard_map/pallas_call | solution.py:1221
  144.7 2.8 fusion.11
  147.5 10.1 %fusion.39 = f32[512,2560]{1,0:T(8,128)S(1)} fusion(bf16[512,2560]{1,0:T(8,128)(2,1)S(1)} %copy-done.13, bf16[2560,2560]{1,0:T(8,128)(2,1)} %get-tuple-element.73.w_input_ref), kind=kOutput, calls=%fused_computation.105 | convolution fusion | flops 6710886400 | bytes 20971520 | tf_op jit(solution)/shard_map/dot_general | solution.py:23
  157.7 1.8 add_convert_fusion
  160.1 3.5 collective-permute-start
  164.6 2.1 fusion.35
  166.7 2.1 fusion.34
  168.8 12.4 %fusion.40 = f32[512,2560]{1,0:T(8,128)} fusion(bf16[512,2560]{1,0:T(8,128)(2,1)} %get-tuple-element.72.refs_1_, bf16[2560,2560]{1,0:T(8,128)(2,1)} %get-tuple-element.76.w_branch_ref), kind=kOutput, calls=%fused_computation.106 | convolution fusion | flops 6710886400 | bytes 20971520 | tf_op jit(solution)/shard_map/dot_general | solution.py:23
  181.7 1.6 slice.191.refs_3_.refs_9_
  186.5 5.1 fusion.6
  191.8 3.5 fusion.12.inner_ref
  195.7 15.6 %shard_map.440 = (f32[512,2560]{1,0:T(8,128)S(1)}, f32[512,2560]{1,0:T(8,128)S(1)}) custom-call(f32[512,2560]{1,0:T(8,128)} %bitcast.114, bf16[512,64]{1,0:T(8,128)(2,1)S(1)} %fusion.12.inner_ref, bf16[64,2560]{1,0:T(8,128)(2,1)S(1)} %get-tuple-element.127.lift_ref, bf16[10,256,256]{2,1,0:T(8,128)(2,1)S(1)} %copy-done.5, ...), custom_call_target="tpu_custom_call" | custom-call | flops 1420820480 | bytes 15728640 | tf_op jit(solution)/shard_map/pallas_call | solution.py:137
  211.5 10.1 %all-gather.1 = f32[4,4,2560]{2,1,0:T(4,128)S(1)} all-gather(f32[1,4,2560]{2,1,0:T(4,128)S(1)} %maximum_bitcast_fusion), channel_id=2, replica_groups=mesh['group'=4,'replica'=8] {'group'}, dimensions={0}, use_global_device_ids=true | all-gather | bytes 204800 | tf_op jit(solution)/shard_map/all_gather | solution.py:1530
  221.7 5.1 fusion.5
  226.9 1.9 fusion.10.refs_11_
  228.9 10.1 %fusion.41 = f32[512,2560]{1,0:T(8,128)S(1)} fusion(bf16[512,2560]{1,0:T(8,128)(2,1)S(1)} %get-tuple-element.157.refs_5_, bf16[2560,2560]{1,0:T(8,128)(2,1)} %get-tuple-element.77.w_ref), kind=kOutput, calls=%fused_computation.107 | convolution fusion | flops 6710886400 | bytes 20971520 | tf_op jit(solution)/shard_map/dot_general | solution.py:23
  239.1 2.1 multiply_reduce_fusion
  241.2 2.5 copy-done.8
  244.2 1.7 fusion.33
  245.8 5.5 all-gather.5.cloned.1.call-done.refs_0_.refs_6_
  252.0 51.2 %shard_map.441 = (bf16[2,1024,1920]{2,1,0:T(8,128)(2,1)}, bf16[2,1024,16]{2,1,0:T(8,128)(2,1)}, bf16[1024,2560]{1,0:T(8,128)(2,1)}) custom-call(bf16[2,1024,2560]{2,1,0:T(8,128)(2,1)} %all-gather.5.cloned.1.call-done.refs_0_.refs_6_, bf16[1920,2560]{1,0:T(8,128)(2,1)} %refs_8_.1, bf16[32,2560]{1,0:T(8,128)(2,1)} %get-tuple-element.133.refs_2_.refs_10_, ...), custom_call_target="tpu_custom_call" | custom-call | flops 20132659200 | bytes 28180480 | tf_op jit(solution)/shard_map/pallas_call | solution.py:798
  303.8 1.0 fusion.36
  306.2 63.4 %shard_map.442 = (bf16[1024,1920]{1,0:T(8,128)(2,1)}, bf16[1024,2560]{1,0:T(8,128)(2,1)}, bf16[48,1920]{1,0:T(8,128)(2,1)}, bf16[1024,32]{1,0:T(8,128)(2,1)}) custom-call(bf16[1024,2560]{1,0:T(8,128)(2,1)} %get-tuple-element.78.tok_ref.refs_1_.refs_2_, bf16[2,1024,1920]{2,1,0:T(8,128)(2,1)} %get-tuple-element.79.gh_ref, bf16[2560,1920]{1,0:T(8,128)(2,1)} %wg_rows_ref.3, ...), custom_call_target="tpu_custom_call" | custom-call | flops 40265318400 | bytes 51118080 | tf_op jit(solution)/shard_map/pallas_call | solution.py:869
  370.5 62.6 %shard_map.444 = (bf16[1024,1920]{1,0:T(8,128)(2,1)}, bf16[1024,2560]{1,0:T(8,128)(2,1)}, bf16[48,1920]{1,0:T(8,128)(2,1)}, bf16[1024,32]{1,0:T(8,128)(2,1)}) custom-call(bf16[1024,2560]{1,0:T(8,128)(2,1)} %all-gather.7.cloned.1.call-done.tok_ref.refs_3_, bf16[2,1024,1920]{2,1,0:T(8,128)(2,1)} %get-tuple-element.79.gh_ref, bf16[2560,1920]{1,0:T(8,128)(2,1)} %wg_rows_ref.3, ...), custom_call_target="tpu_custom_call" | custom-call | flops 40265318400 | bytes 51118080 | tf_op jit(solution)/shard_map/pallas_call | solution.py:869
  433.1 52.1 %shard_map.445 = (bf16[2,1024,2560]{2,1,0:T(8,128)(2,1)}, bf16[2,1024,16]{2,1,0:T(8,128)(2,1)}, bf16[96,2560]{1,0:T(8,128)(2,1)}, bf16[256,2560]{1,0:T(8,128)(2,1)}) custom-call(bf16[1024,1920]{1,0:T(8,128)(2,1)} %get-tuple-element.81.refs_0_, bf16[1024,1920]{1,0:T(8,128)(2,1)} %get-tuple-element.82.refs_1_, ...), custom_call_target="tpu_custom_call" | custom-call | flops 20132659200 | bytes 28180480 | tf_op jit(solution)/shard_map/pallas_call | solution.py:987
  487.1 9.3 %shard_map.446 = (f32[512,2560]{1,0:T(8,128)}, bf16[512,2560]{1,0:T(8,128)(2,1)}) custom-call(f32[512,2560]{1,0:T(8,128)} %copy-done.8, bf16[512,2560]{1,0:T(8,128)(2,1)} %bitcast.118, f32[1,2560]{1,0:T(1,128)} %broadcast_in_dim.10.refs_5_.gain_ref, bf16[256,2560]{1,0:T(8,128)(2,1)} %reduce-scatter.5.cloned.1.call-done.refs_0_, ...), custom_call_target="tpu_custom_call" | custom-call | flops 26214400 | bytes 18350080 | tf_op jit(solution)/shard_map/pallas_call | solution.py:1287
  496.4 73.2 %shard_map.447 = (bf16[512,2560]{1,0:T(8,128)(2,1)}, bf16[512,64]{1,0:T(8,128)(2,1)}, bf16[512,64]{1,0:T(8,128)(2,1)}, f32[64,2560]{1,0:T(8,128)}, bf16[512,2560...) custom-call(bf16[512,2560]{1,0:T(8,128)(2,1)} %get-tuple-element.90.mixed_r, ...), custom_call_target="tpu_custom_call" | custom-call | flops 20394803200 | bytes 65536000 | tf_op jit(solution)/shard_map/pallas_call | solution.py:668
  571.2 9.6 %shard_map.448.partial_ref = bf16[4,320,640]{2,1,0:T(8,128)(2,1)} custom-call(bf16[512,64]{1,0:T(8,128)(2,1)} %get-tuple-element.96.refs_0_.through_ref, bf16[512,2560]{1,0:T(8,128)(2,1)} %get-tuple-element.72.refs_1_, bf16[512,64]{1,0:T(8,128)(2,1)} %get-tuple-element.97.refs_2_, bf16[512,2560]{1,0:T(8,128)(2,1)} %copy-done.11, ...), custom_call_target="tpu_custom_call" | custom-call | flops 522190848 | bytes 16318464 | tf_op jit(solution)/shard_map/pallas_call | solution.py:1448
  580.8 63.3 %shard_map.449 = (f32[512,2560]{1,0:T(8,128)}, bf16[8,320,640]{2,1,0:T(8,128)(2,1)}) custom-call(bf16[512,2560]{1,0:T(8,128)(2,1)} %get-tuple-element.94.refs_7_.branch_grad_ref, bf16[512,2560]{1,0:T(8,128)(2,1)} %get-tuple-element.95.refs_9_.fed_grad_ref, bf16[2560,2560]{1,0:T(8,128)(2,1)} %get-tuple-element.76.w_branch_ref, ...), custom_call_target="tpu_custom_call" | custom-call | flops 13421772800 | bytes 36700160 | tf_op jit(solution)/shard_map/pallas_call | solution.py:1367
  644.2 7.0 %shard_map.451 = (f32[8,16,640]{2,1,0:T(8,128)}, f32[8,16,640]{2,1,0:T(8,128)}, f32[8,16,640]{2,1,0:T(8,128)}, f32[8,16,640]{2,1,0:T(8,128)}, f32[8,16,640]{2,1,...) custom-call(s32[16]{0:T(128)} %reshape.117.ids_ref, ...), custom_call_target="tpu_custom_call" | custom-call | flops 3850240 | bytes 15400960 | tf_op jit(solution)/shard_map/pallas_call | solution.py:1402
  651.2 8.5 %shard_map.450 = f32[512,2560]{1,0:T(8,128)} custom-call(f32[512,2560]{1,0:T(8,128)} %get-tuple-element.89.grad_resid_ref, bf16[512,2560]{1,0:T(8,128)(2,1)} %bitcast.112, f32[1,2560]{1,0:T(1,128)} %reshape.107.refs_5_.refs_6_.gain_ref, f32[512,2560]{1,0:T(8,128)} %get-tuple-element.100.grads_ref), custom_call_target="tpu_custom_call" | custom-call | flops 27525120 | bytes 18350080 | tf_op jit(solution)/shard_map/pallas_call | solution.py:1314
  (135 shorter events, 13.8 us)
Async XLA Ops:
  7.2 244.2 %all-gather.5.cloned.1.call-start = ((), (), s32[]{:S(2)}) async-start(), calls=%async_computation.2 | async-start | bytes 13107200 | tf_op jit(solution)/shard_map/all_gather | solution.py:1494
  144.3 226.3 %all-gather.7.cloned.1.call-start = ((), (), s32[]{:S(2)}) async-start(), calls=%async_computation.3 | async-start | bytes 6553600 | tf_op jit(solution)/shard_map/all_gather | solution.py:1552
  144.3 13.3 %copy-start.27 = (s32[32]{0:T(128)}, s32[32]{0:T(128)S(1)}, u32[]{:S(2)}) copy-start(s32[32]{0:T(128)S(1)} %get-tuple-element.163) | copy-start | bytes 388
  144.3 13.3 %copy-start.29 = (s32[32]{0:T(128)}, s32[32]{0:T(128)S(1)}, u32[]{:S(2)}) copy-start(s32[32]{0:T(128)S(1)} %get-tuple-element.164) | copy-start | bytes 388
  144.4 13.3 %copy-start.31 = (pred[512]{0:T(512)(128)(4,1)}, pred[512]{0:T(512)(128)(4,1)S(1)}, u32[]{:S(2)}) copy-start(pred[512]{0:T(512)(128)(4,1)S(1)} %fusion.23) | copy-start | bytes 1540
  144.4 13.2 %copy-start.33 = (pred[32]{0:T(512)(128)(4,1)}, pred[32]{0:T(512)(128)(4,1)S(1)}, u32[]{:S(2)}) copy-start(pred[32]{0:T(512)(128)(4,1)S(1)} %compare_and_fusion) | copy-start | bytes 100
  147.5 74.1 %copy-start.14 = (bf16[512,64]{1,0:T(8,128)(2,1)}, bf16[512,64]{1,0:T(8,128)(2,1)S(1)}, u32[]{:S(2)}) copy-start(bf16[512,64]{1,0:T(8,128)(2,1)S(1)} %fusion.11) | copy-start | bytes 196612
  157.6 6.0 copy-start.25
  157.6 6.8 %copy-start.22 = (f32[4,2560]{1,0:T(4,128)S(1)}, f32[4,2560]{1,0:T(4,128)}, u32[]{:S(2)}) copy-start(f32[4,2560]{1,0:T(4,128)} %taps_ref.1) | copy-start | bytes 122884
  157.7 6.9 %copy-start.23 = (f32[2560]{0:T(1024)S(1)}, f32[2560]{0:T(1024)}, u32[]{:S(2)}) copy-start(f32[2560]{0:T(1024)} %param.42) | copy-start | bytes 30724
  160.1 25.6 %collective-permute-start = (bf16[2,3,2560]{2,1,0:T(4,128)(2,1)}, bf16[2,3,2560]{2,1,0:T(4,128)(2,1)S(1)}, u32[]{:S(2)}, u32[]{:S(2)}) collective-permute-start(bf16[2,3,2560]{2,1,0:T(4,128)(2,1)} %slice.249), channel_id=1, source_target_pairs={{0,8},{8,16},{16,24},{1,9},{9,17},{17,25},{2,10},{10,18},{18,26},{... | collective-permute-start | bytes 92168 | tf_op jit(solution)/shard_map/ppermute | solution.py:1466
  168.8 26.8 %copy-start.2 = (bf16[64,2560]{1,0:T(8,128)(2,1)}, bf16[64,2560]{1,0:T(8,128)(2,1)S(1)}, u32[]{:S(2)}) copy-start(bf16[64,2560]{1,0:T(8,128)(2,1)S(1)} %get-tuple-element.127.lift_ref) | copy-start | bytes 983044
  168.8 12.4 %copy-start.26 = (s32[2]{0:T(128)S(1)}, s32[2]{0:T(128)}, u32[]{:S(2)}) copy-start(s32[2]{0:T(128)} %refs_6_.1) | copy-start | bytes 28
  168.8 14.7 %copy-start.21 = (f32[2560]{0:T(1024)S(1)}, f32[2560]{0:T(1024)}, u32[]{:S(2)}) copy-start(f32[2560]{0:T(1024)} %param.36) | copy-start | bytes 30724
  183.3 12.3 %copy-start.4 = (f32[1,2560]{1,0:T(1,128)}, f32[1,2560]{1,0:T(1,128)S(1)}, u32[]{:S(2)}) copy-start(f32[1,2560]{1,0:T(1,128)S(1)} %reshape.110.soft_ref) | copy-start | bytes 30724
  183.5 12.1 %copy-start.3 = (f32[1,512]{0,1:T(8,128)}, f32[1,512]{0,1:T(8,128)S(1)}, u32[]{:S(2)}) copy-start(f32[1,512]{0,1:T(8,128)S(1)} %copy.79) | copy-start | bytes 6148
  191.8 29.8 %slice-start = ((s8[5242880]{0:T(1024)(128)(4,1)}), s8[1048576]{0:T(1024)(128)(4,1)S(1)}, s32[]{:S(2)}) async-start(s8[5242880]{0:T(1024)(128)(4,1)} %bitcast.119), calls=%async_computation.6 | async-start | bytes 2097152
  195.4 16.0 %copy-start.7 = (bf16[512,64]{1,0:T(8,128)(2,1)}, bf16[512,64]{1,0:T(8,128)(2,1)S(1)}, u32[]{:S(2)}) copy-start(bf16[512,64]{1,0:T(8,128)(2,1)S(1)} %fusion.12.inner_ref) | copy-start | bytes 196612
  195.7 25.9 %slice-start.1 = ((s8[5242880]{0:T(1024)(128)(4,1)}), s8[4194304]{0:T(1024)(128)(4,1)S(1)}, s32[]{:S(2)}) async-start(s8[5242880]{0:T(1024)(128)(4,1)} %bitcast.119), calls=%async_computation.7 | async-start | bytes 8388608
  211.4 15.5 %copy-start = (f32[512,2560]{1,0:T(8,128)}, f32[512,2560]{1,0:T(8,128)S(1)}, u32[]{:S(2)}) copy-start(f32[512,2560]{1,0:T(8,128)S(1)} %get-tuple-element.75.cum_ref) | copy-start | bytes 15728644
  211.4 15.5 %copy-start.1 = (f32[512,2560]{1,0:T(8,128)}, f32[512,2560]{1,0:T(8,128)S(1)}, u32[]{:S(2)}) copy-start(f32[512,2560]{1,0:T(8,128)S(1)} %get-tuple-element.74.local_ref) | copy-start | bytes 15728644
  221.7 5.2 copy-start.20
  221.7 5.2 copy-start.28
  221.7 5.2 copy-start.30
  221.7 5.2 copy-start.32
  221.7 5.2 copy-start.34
  226.9 12.2 %copy-start.12 = (bf16[512,2560]{1,0:T(8,128)(2,1)}, bf16[512,2560]{1,0:T(8,128)(2,1)S(1)}, u32[]{:S(2)}) copy-start(bf16[512,2560]{1,0:T(8,128)(2,1)S(1)} %get-tuple-element.157.refs_5_) | copy-start | bytes 7864324
  228.9 10.2 %copy-start.16 = (bf16[512,32]{1,0:T(8,128)(2,1)}, bf16[512,32]{1,0:T(8,128)(2,1)S(1)}, u32[]{:S(2)}) copy-start(bf16[512,32]{1,0:T(8,128)(2,1)S(1)} %fusion.10.refs_11_) | copy-start | bytes 98308
  228.9 10.2 %copy-start.9 = (bf16[2,256,2560]{2,1,0:T(8,128)(2,1)S(1)}, bf16[2,256,2560]{2,1,0:T(8,128)(2,1)}, u32[]{:S(2)}) copy-start(bf16[2,256,2560]{2,1,0:T(8,128)(2,1)} %param.32) | copy-start | bytes 7864324
  303.3 183.7 %reduce-scatter.5.cloned.1.call-start = ((), (), s32[]{:S(2)}) async-start(), calls=%async_computation.5 | async-start | bytes 6553600 | tf_op jit(solution)/shard_map/reduce_scatter | solution.py:1560
  369.6 290.1 %reduce-scatter.3.cloned.1.call-start = ((), (), s32[]{:S(2)}) async-start(), calls=%async_computation.4 | async-start | bytes 13107200 | tf_op jit(solution)/shard_map/reduce_scatter | solution.py:1571
  487.0 9.3 %copy-start.24 = (bf16[112,1920]{1,0:T(8,128)(2,1)}, bf16[112,1920]{1,0:T(8,128)(2,1)S(1)}, u32[]{:S(2)}) copy-start(bf16[112,1920]{1,0:T(8,128)(2,1)S(1)} %broadcast_dynamic-update-slice_fusion.wide_ref) | copy-start | bytes 1290244
  (10 other events, 28.0 us)
Sparse Core Ops, SparseCore 0:
  144.4 106.9 all-gather.4
  303.4 61.4 all-gather.6
  369.7 61.3 reduce-scatter.4
  485.4 118.7 reduce-scatter.2

commit v8 on v7

--- a/solution.py
+++ b/solution.py
@@ -607,10 +607,10 @@
         through_gates_ref[...] = (gates_ref[...] * sequence_mask(rows, 2 * half, seqs)).astype(BF16)
         tops = []
         for s in range(seqs):
-            top = slice(s * stretch, s * stretch + 8)
+            top = slice(s * stretch, s * stretch + GROUP)
             direct = jnp.concatenate([total_ref[h, top, :] for h in range(heads)], 1)
-            tops.append(direct + dot(through_gates_ref[top, :], down_gates_ref[...]))
-        halo_ref[...] = jnp.concatenate(tops, 0).astype(BF16)
+            tops.append((direct + dot(through_gates_ref[top, :], down_gates_ref[...]))[:8])
+        halo_ref[...] = jnp.concatenate(tops, 0).astype(BF16).astype(F32)
         downward.start()
         downward.wait_recv()
 
@@ -621,7 +621,7 @@
         grads = total_ref[head] + dot(through_gates_ref[...], down_gates_ref[:, cols])
         for s in range(seqs):
             longer_ref[s, :stretch, :] = grads[s * stretch : (s + 1) * stretch, :]
-            longer_ref[s, stretch:, :] = below_ref[s * 8 : (s + 1) * 8, cols].astype(F32)
+            longer_ref[s, stretch:, :] = below_ref[s * 8 : (s + 1) * 8, cols]
 
         def group(k, _):
             for s in range(seqs):
@@ -689,8 +689,8 @@
                    whole(lift_mixer.shape[0]), ANYWHERE, ANYWHERE],
         scratch_shapes=[
             pltpu.VMEM((heads, rows, size), F32), pltpu.VMEM((heads, rows, size), F32), pltpu.VMEM((8, width), F32),
-            pltpu.VMEM((4, 8, width), F32), pltpu.VMEM((seqs, width), F32), pltpu.VMEM((8 * seqs, width), BF16),
-            pltpu.VMEM((8 * seqs, width), BF16), pltpu.VMEM((rows, 2 * lift_branch.shape[0]), F32),
+            pltpu.VMEM((4, 8, width), F32), pltpu.VMEM((seqs, width), F32), pltpu.VMEM((8 * seqs, width), F32),
+            pltpu.VMEM((8 * seqs, width), F32), pltpu.VMEM((rows, 2 * lift_branch.shape[0]), F32),
             pltpu.VMEM((rows, middle), F32), pltpu.VMEM((rows, size), F32), pltpu.VMEM((rows, size), F32),
             pltpu.VMEM((rows, size), BF16), pltpu.VMEM((rows, size), BF16),
             pltpu.VMEM((seqs, rows // seqs + 8, size), F32), pltpu.SemaphoreType.DMA((4,)),

time: 672 us -> 672 us (level)
  no operation moved by 1% of the time
where the time goes in v8:
time: 672 us; the launch traced here: 667 us
  Pallas kernels  552 us (82%)
  matrix products  49.9 us (7%)
  local copies, waits for them, and re-layouts  20.3 us (3%)
  between operations  14.8 us (2%)
  blocking collectives  10.1 us (2%)
  other arithmetic  9.96 us (1%)
    pallas_call x1, Pallas kernels, gather_weights(): pl.pallas_call(functools.partial(gather_kernel, units, counts, seqs), out...  136 us
    pallas_call x2, Pallas kernels, feed_call(): pl.pallas_call(functools.partial(feed_kernel, steps, tile, units), grid=(...  126 us
    pallas_call x1, Pallas kernels, mixer_back(): pl.pallas_call(functools.partial(mixer_back_kernel, seqs, heads), grid=(3...  74.1 us
    pallas_call x1, Pallas kernels, tail_call(): pl.pallas_call(functools.partial(tail_kernel, steps), grid=(steps,), out_...  62.6 us
    pallas_call x1, Pallas kernels, outward_call(): pl.pallas_call(functools.partial(outward_kernel, seqs, reduce, steps), gr...  52.1 us
    pallas_call x1, Pallas kernels, grad_hidden_call(): pl.pallas_call(functools.partial(grad_hidden_kernel, seqs, gather, pl.cdi...  51.2 us
    dot_general x9, matrix products, dot(): return lax.dot_general(a, b, dims, preferred_element_type=F32)  49.9 us
    pallas_call x1, Pallas kernels, forward_gates(): pl.pallas_call(functools.partial(forward_gates_kernel, seqs), out_shape=(...  15.6 us
  transfers between devices with their start and end apart: 5, of which 1 were waited for; matrix products, arithmetic and copies ran while one was open for 11% of the time, Pallas kernels for 55%

profile of v8, /device:TPU:0, one launch (start us, length us, event | category | flops | bytes accessed | tf_op | source)
XLA Modules:
  0.0 666.6 jit_solution(10408369145405175190)
XLA Ops:
  7.2 1.3 reshape.107.refs_5_.refs_6_.gain_ref
  8.5 135.7 %shard_map.439 = (bf16[2560,2560]{1,0:T(8,128)(2,1)}, bf16[2560,2560]{1,0:T(8,128)(2,1)}, bf16[2560,2560]{1,0:T(8,128)(2,1)}, bf16[416,2560]{1,0:T(8,128)(2,1)},...) custom-call(bf16[2560,640]{1,0:T(8,128)(2,1)} %refs_0_.1, ...), custom_call_target="tpu_custom_call" | custom-call | bytes 419430400 | tf_op jit(solution)/shard_map/pallas_call | solution.py:1221
  144.7 2.8 fusion.11
  147.5 10.1 %fusion.39 = f32[512,2560]{1,0:T(8,128)S(1)} fusion(bf16[512,2560]{1,0:T(8,128)(2,1)S(1)} %copy-done.13, bf16[2560,2560]{1,0:T(8,128)(2,1)} %get-tuple-element.73.w_input_ref), kind=kOutput, calls=%fused_computation.105 | convolution fusion | flops 6710886400 | bytes 20971520 | tf_op jit(solution)/shard_map/dot_general | solution.py:23
  157.7 1.8 add_convert_fusion
  160.1 3.5 collective-permute-start
  164.6 2.1 fusion.35
  166.7 2.1 fusion.34
  168.8 12.4 %fusion.40 = f32[512,2560]{1,0:T(8,128)} fusion(bf16[512,2560]{1,0:T(8,128)(2,1)} %get-tuple-element.72.refs_1_, bf16[2560,2560]{1,0:T(8,128)(2,1)} %get-tuple-element.76.w_branch_ref), kind=kOutput, calls=%fused_computation.106 | convolution fusion | flops 6710886400 | bytes 20971520 | tf_op jit(solution)/shard_map/dot_general | solution.py:23
  181.7 1.6 slice.191.refs_3_.refs_9_
  186.5 5.1 fusion.6
  191.8 3.5 fusion.12.inner_ref
  195.7 15.6 %shard_map.440 = (f32[512,2560]{1,0:T(8,128)S(1)}, f32[512,2560]{1,0:T(8,128)S(1)}) custom-call(f32[512,2560]{1,0:T(8,128)} %bitcast.114, bf16[512,64]{1,0:T(8,128)(2,1)S(1)} %fusion.12.inner_ref, bf16[64,2560]{1,0:T(8,128)(2,1)S(1)} %get-tuple-element.127.lift_ref, bf16[10,256,256]{2,1,0:T(8,128)(2,1)S(1)} %copy-done.5, ...), custom_call_target="tpu_custom_call" | custom-call | flops 1420820480 | bytes 15728640 | tf_op jit(solution)/shard_map/pallas_call | solution.py:137
  211.5 10.1 %all-gather.1 = f32[4,4,2560]{2,1,0:T(4,128)S(1)} all-gather(f32[1,4,2560]{2,1,0:T(4,128)S(1)} %maximum_bitcast_fusion), channel_id=2, replica_groups=mesh['group'=4,'replica'=8] {'group'}, dimensions={0}, use_global_device_ids=true | all-gather | bytes 204800 | tf_op jit(solution)/shard_map/all_gather | solution.py:1530
  221.7 5.1 fusion.5
  226.9 1.9 fusion.10.refs_11_
  228.9 10.1 %fusion.41 = f32[512,2560]{1,0:T(8,128)S(1)} fusion(bf16[512,2560]{1,0:T(8,128)(2,1)S(1)} %get-tuple-element.157.refs_5_, bf16[2560,2560]{1,0:T(8,128)(2,1)} %get-tuple-element.77.w_ref), kind=kOutput, calls=%fused_computation.107 | convolution fusion | flops 6710886400 | bytes 20971520 | tf_op jit(solution)/shard_map/dot_general | solution.py:23
  239.1 2.1 multiply_reduce_fusion
  241.2 2.5 copy-done.8
  244.2 1.7 fusion.33
  245.8 5.5 all-gather.5.cloned.1.call-done.refs_0_.refs_6_
  252.0 51.2 %shard_map.441 = (bf16[2,1024,1920]{2,1,0:T(8,128)(2,1)}, bf16[2,1024,16]{2,1,0:T(8,128)(2,1)}, bf16[1024,2560]{1,0:T(8,128)(2,1)}) custom-call(bf16[2,1024,2560]{2,1,0:T(8,128)(2,1)} %all-gather.5.cloned.1.call-done.refs_0_.refs_6_, bf16[1920,2560]{1,0:T(8,128)(2,1)} %refs_8_.1, bf16[32,2560]{1,0:T(8,128)(2,1)} %get-tuple-element.133.refs_2_.refs_10_, ...), custom_call_target="tpu_custom_call" | custom-call | flops 20132659200 | bytes 28180480 | tf_op jit(solution)/shard_map/pallas_call | solution.py:798
  303.8 1.0 fusion.36
  306.2 63.4 %shard_map.442 = (bf16[1024,1920]{1,0:T(8,128)(2,1)}, bf16[1024,2560]{1,0:T(8,128)(2,1)}, bf16[48,1920]{1,0:T(8,128)(2,1)}, bf16[1024,32]{1,0:T(8,128)(2,1)}) custom-call(bf16[1024,2560]{1,0:T(8,128)(2,1)} %get-tuple-element.78.tok_ref.refs_1_.refs_2_, bf16[2,1024,1920]{2,1,0:T(8,128)(2,1)} %get-tuple-element.79.gh_ref, bf16[2560,1920]{1,0:T(8,128)(2,1)} %wg_rows_ref.3, ...), custom_call_target="tpu_custom_call" | custom-call | flops 40265318400 | bytes 51118080 | tf_op jit(solution)/shard_map/pallas_call | solution.py:869
  370.5 62.6 %shard_map.444 = (bf16[1024,1920]{1,0:T(8,128)(2,1)}, bf16[1024,2560]{1,0:T(8,128)(2,1)}, bf16[48,1920]{1,0:T(8,128)(2,1)}, bf16[1024,32]{1,0:T(8,128)(2,1)}) custom-call(bf16[1024,2560]{1,0:T(8,128)(2,1)} %all-gather.7.cloned.1.call-done.tok_ref.refs_3_, bf16[2,1024,1920]{2,1,0:T(8,128)(2,1)} %get-tuple-element.79.gh_ref, bf16[2560,1920]{1,0:T(8,128)(2,1)} %wg_rows_ref.3, ...), custom_call_target="tpu_custom_call" | custom-call | flops 40265318400 | bytes 51118080 | tf_op jit(solution)/shard_map/pallas_call | solution.py:869
  433.1 52.1 %shard_map.445 = (bf16[2,1024,2560]{2,1,0:T(8,128)(2,1)}, bf16[2,1024,16]{2,1,0:T(8,128)(2,1)}, bf16[96,2560]{1,0:T(8,128)(2,1)}, bf16[256,2560]{1,0:T(8,128)(2,1)}) custom-call(bf16[1024,1920]{1,0:T(8,128)(2,1)} %get-tuple-element.81.refs_0_, bf16[1024,1920]{1,0:T(8,128)(2,1)} %get-tuple-element.82.refs_1_, ...), custom_call_target="tpu_custom_call" | custom-call | flops 20132659200 | bytes 28180480 | tf_op jit(solution)/shard_map/pallas_call | solution.py:987
  487.1 9.3 %shard_map.446 = (f32[512,2560]{1,0:T(8,128)}, bf16[512,2560]{1,0:T(8,128)(2,1)}) custom-call(f32[512,2560]{1,0:T(8,128)} %copy-done.8, bf16[512,2560]{1,0:T(8,128)(2,1)} %bitcast.118, f32[1,2560]{1,0:T(1,128)} %broadcast_in_dim.10.refs_5_.gain_ref, bf16[256,2560]{1,0:T(8,128)(2,1)} %reduce-scatter.5.cloned.1.call-done.refs_0_, ...), custom_call_target="tpu_custom_call" | custom-call | flops 26214400 | bytes 18350080 | tf_op jit(solution)/shard_map/pallas_call | solution.py:1287
  496.4 74.1 %shard_map.447 = (bf16[512,2560]{1,0:T(8,128)(2,1)}, bf16[512,64]{1,0:T(8,128)(2,1)}, bf16[512,64]{1,0:T(8,128)(2,1)}, f32[64,2560]{1,0:T(8,128)}, bf16[512,2560...) custom-call(bf16[512,2560]{1,0:T(8,128)(2,1)} %get-tuple-element.90.mixed_r, ...), custom_call_target="tpu_custom_call" | custom-call | flops 20394803200 | bytes 65536000 | tf_op jit(solution)/shard_map/pallas_call | solution.py:668
  572.1 9.6 %shard_map.448.partial_ref = bf16[4,320,640]{2,1,0:T(8,128)(2,1)} custom-call(bf16[512,64]{1,0:T(8,128)(2,1)} %get-tuple-element.96.refs_0_.through_ref, bf16[512,2560]{1,0:T(8,128)(2,1)} %get-tuple-element.72.refs_1_, bf16[512,64]{1,0:T(8,128)(2,1)} %get-tuple-element.97.refs_2_, bf16[512,2560]{1,0:T(8,128)(2,1)} %copy-done.11, ...), custom_call_target="tpu_custom_call" | custom-call | flops 522190848 | bytes 16318464 | tf_op jit(solution)/shard_map/pallas_call | solution.py:1448
  581.7 62.6 %shard_map.449 = (f32[512,2560]{1,0:T(8,128)}, bf16[8,320,640]{2,1,0:T(8,128)(2,1)}) custom-call(bf16[512,2560]{1,0:T(8,128)(2,1)} %get-tuple-element.94.refs_7_.branch_grad_ref, bf16[512,2560]{1,0:T(8,128)(2,1)} %get-tuple-element.95.refs_9_.fed_grad_ref, bf16[2560,2560]{1,0:T(8,128)(2,1)} %get-tuple-element.76.w_branch_ref, ...), custom_call_target="tpu_custom_call" | custom-call | flops 13421772800 | bytes 36700160 | tf_op jit(solution)/shard_map/pallas_call | solution.py:1367
  644.3 7.0 %shard_map.451 = (f32[8,16,640]{2,1,0:T(8,128)}, f32[8,16,640]{2,1,0:T(8,128)}, f32[8,16,640]{2,1,0:T(8,128)}, f32[8,16,640]{2,1,0:T(8,128)}, f32[8,16,640]{2,1,...) custom-call(s32[16]{0:T(128)} %reshape.117.ids_ref, ...), custom_call_target="tpu_custom_call" | custom-call | flops 3850240 | bytes 15400960 | tf_op jit(solution)/shard_map/pallas_call | solution.py:1402
  651.3 8.5 %shard_map.450 = f32[512,2560]{1,0:T(8,128)} custom-call(f32[512,2560]{1,0:T(8,128)} %get-tuple-element.89.grad_resid_ref, bf16[512,2560]{1,0:T(8,128)(2,1)} %bitcast.112, f32[1,2560]{1,0:T(1,128)} %reshape.107.refs_5_.refs_6_.gain_ref, f32[512,2560]{1,0:T(8,128)} %get-tuple-element.100.grads_ref), custom_call_target="tpu_custom_call" | custom-call | flops 27525120 | bytes 18350080 | tf_op jit(solution)/shard_map/pallas_call | solution.py:1314
  (135 shorter events, 13.8 us)
Async XLA Ops:
  7.2 244.2 %all-gather.5.cloned.1.call-start = ((), (), s32[]{:S(2)}) async-start(), calls=%async_computation.2 | async-start | bytes 13107200 | tf_op jit(solution)/shard_map/all_gather | solution.py:1494
  144.3 226.3 %all-gather.7.cloned.1.call-start = ((), (), s32[]{:S(2)}) async-start(), calls=%async_computation.3 | async-start | bytes 6553600 | tf_op jit(solution)/shard_map/all_gather | solution.py:1552
  144.3 13.3 %copy-start.27 = (s32[32]{0:T(128)}, s32[32]{0:T(128)S(1)}, u32[]{:S(2)}) copy-start(s32[32]{0:T(128)S(1)} %get-tuple-element.163) | copy-start | bytes 388
  144.3 13.3 %copy-start.29 = (s32[32]{0:T(128)}, s32[32]{0:T(128)S(1)}, u32[]{:S(2)}) copy-start(s32[32]{0:T(128)S(1)} %get-tuple-element.164) | copy-start | bytes 388
  144.4 13.3 %copy-start.31 = (pred[512]{0:T(512)(128)(4,1)}, pred[512]{0:T(512)(128)(4,1)S(1)}, u32[]{:S(2)}) copy-start(pred[512]{0:T(512)(128)(4,1)S(1)} %fusion.23) | copy-start | bytes 1540
  144.4 13.2 %copy-start.33 = (pred[32]{0:T(512)(128)(4,1)}, pred[32]{0:T(512)(128)(4,1)S(1)}, u32[]{:S(2)}) copy-start(pred[32]{0:T(512)(128)(4,1)S(1)} %compare_and_fusion) | copy-start | bytes 100
  147.5 74.1 %copy-start.14 = (bf16[512,64]{1,0:T(8,128)(2,1)}, bf16[512,64]{1,0:T(8,128)(2,1)S(1)}, u32[]{:S(2)}) copy-start(bf16[512,64]{1,0:T(8,128)(2,1)S(1)} %fusion.11) | copy-start | bytes 196612
  157.6 6.0 copy-start.25
  157.6 6.8 %copy-start.22 = (f32[4,2560]{1,0:T(4,128)S(1)}, f32[4,2560]{1,0:T(4,128)}, u32[]{:S(2)}) copy-start(f32[4,2560]{1,0:T(4,128)} %taps_ref.1) | copy-start | bytes 122884
  157.7 6.9 %copy-start.23 = (f32[2560]{0:T(1024)S(1)}, f32[2560]{0:T(1024)}, u32[]{:S(2)}) copy-start(f32[2560]{0:T(1024)} %param.42) | copy-start | bytes 30724
  160.1 25.6 %collective-permute-start = (bf16[2,3,2560]{2,1,0:T(4,128)(2,1)}, bf16[2,3,2560]{2,1,0:T(4,128)(2,1)S(1)}, u32[]{:S(2)}, u32[]{:S(2)}) collective-permute-start(bf16[2,3,2560]{2,1,0:T(4,128)(2,1)} %slice.249), channel_id=1, source_target_pairs={{0,8},{8,16},{16,24},{1,9},{9,17},{17,25},{2,10},{10,18},{18,26},{... | collective-permute-start | bytes 92168 | tf_op jit(solution)/shard_map/ppermute | solution.py:1466
  168.8 26.8 %copy-start.2 = (bf16[64,2560]{1,0:T(8,128)(2,1)}, bf16[64,2560]{1,0:T(8,128)(2,1)S(1)}, u32[]{:S(2)}) copy-start(bf16[64,2560]{1,0:T(8,128)(2,1)S(1)} %get-tuple-element.127.lift_ref) | copy-start | bytes 983044
  168.8 12.4 %copy-start.26 = (s32[2]{0:T(128)S(1)}, s32[2]{0:T(128)}, u32[]{:S(2)}) copy-start(s32[2]{0:T(128)} %refs_6_.1) | copy-start | bytes 28
  168.8 14.7 %copy-start.21 = (f32[2560]{0:T(1024)S(1)}, f32[2560]{0:T(1024)}, u32[]{:S(2)}) copy-start(f32[2560]{0:T(1024)} %param.36) | copy-start | bytes 30724
  183.3 12.3 %copy-start.4 = (f32[1,2560]{1,0:T(1,128)}, f32[1,2560]{1,0:T(1,128)S(1)}, u32[]{:S(2)}) copy-start(f32[1,2560]{1,0:T(1,128)S(1)} %reshape.110.soft_ref) | copy-start | bytes 30724
  183.5 12.1 %copy-start.3 = (f32[1,512]{0,1:T(8,128)}, f32[1,512]{0,1:T(8,128)S(1)}, u32[]{:S(2)}) copy-start(f32[1,512]{0,1:T(8,128)S(1)} %copy.79) | copy-start | bytes 6148
  191.8 29.8 %slice-start = ((s8[5242880]{0:T(1024)(128)(4,1)}), s8[1048576]{0:T(1024)(128)(4,1)S(1)}, s32[]{:S(2)}) async-start(s8[5242880]{0:T(1024)(128)(4,1)} %bitcast.119), calls=%async_computation.6 | async-start | bytes 2097152
  195.4 16.0 %copy-start.7 = (bf16[512,64]{1,0:T(8,128)(2,1)}, bf16[512,64]{1,0:T(8,128)(2,1)S(1)}, u32[]{:S(2)}) copy-start(bf16[512,64]{1,0:T(8,128)(2,1)S(1)} %fusion.12.inner_ref) | copy-start | bytes 196612
  195.7 25.9 %slice-start.1 = ((s8[5242880]{0:T(1024)(128)(4,1)}), s8[4194304]{0:T(1024)(128)(4,1)S(1)}, s32[]{:S(2)}) async-start(s8[5242880]{0:T(1024)(128)(4,1)} %bitcast.119), calls=%async_computation.7 | async-start | bytes 8388608
  211.4 15.5 %copy-start = (f32[512,2560]{1,0:T(8,128)}, f32[512,2560]{1,0:T(8,128)S(1)}, u32[]{:S(2)}) copy-start(f32[512,2560]{1,0:T(8,128)S(1)} %get-tuple-element.75.cum_ref) | copy-start | bytes 15728644
  211.4 15.5 %copy-start.1 = (f32[512,2560]{1,0:T(8,128)}, f32[512,2560]{1,0:T(8,128)S(1)}, u32[]{:S(2)}) copy-start(f32[512,2560]{1,0:T(8,128)S(1)} %get-tuple-element.74.local_ref) | copy-start | bytes 15728644
  221.7 5.2 copy-start.20
  221.7 5.2 copy-start.28
  221.7 5.2 copy-start.30
  221.7 5.2 copy-start.32
  221.7 5.2 copy-start.34
  226.9 12.2 %copy-start.12 = (bf16[512,2560]{1,0:T(8,128)(2,1)}, bf16[512,2560]{1,0:T(8,128)(2,1)S(1)}, u32[]{:S(2)}) copy-start(bf16[512,2560]{1,0:T(8,128)(2,1)S(1)} %get-tuple-element.157.refs_5_) | copy-start | bytes 7864324
  228.9 10.2 %copy-start.16 = (bf16[512,32]{1,0:T(8,128)(2,1)}, bf16[512,32]{1,0:T(8,128)(2,1)S(1)}, u32[]{:S(2)}) copy-start(bf16[512,32]{1,0:T(8,128)(2,1)S(1)} %fusion.10.refs_11_) | copy-start | bytes 98308
  228.9 10.2 %copy-start.9 = (bf16[2,256,2560]{2,1,0:T(8,128)(2,1)S(1)}, bf16[2,256,2560]{2,1,0:T(8,128)(2,1)}, u32[]{:S(2)}) copy-start(bf16[2,256,2560]{2,1,0:T(8,128)(2,1)} %param.32) | copy-start | bytes 7864324
  303.3 183.7 %reduce-scatter.5.cloned.1.call-start = ((), (), s32[]{:S(2)}) async-start(), calls=%async_computation.5 | async-start | bytes 6553600 | tf_op jit(solution)/shard_map/reduce_scatter | solution.py:1560
  369.6 290.2 %reduce-scatter.3.cloned.1.call-start = ((), (), s32[]{:S(2)}) async-start(), calls=%async_computation.4 | async-start | bytes 13107200 | tf_op jit(solution)/shard_map/reduce_scatter | solution.py:1571
  487.0 9.3 %copy-start.24 = (bf16[112,1920]{1,0:T(8,128)(2,1)}, bf16[112,1920]{1,0:T(8,128)(2,1)S(1)}, u32[]{:S(2)}) copy-start(bf16[112,1920]{1,0:T(8,128)(2,1)S(1)} %broadcast_dynamic-update-slice_fusion.wide_ref) | copy-start | bytes 1290244
  (10 other events, 28.0 us)
Sparse Core Ops, SparseCore 0:
  144.4 106.9 all-gather.4
  303.4 61.4 all-gather.6
  369.7 61.3 reduce-scatter.4
  485.4 119.4 reduce-scatter.2
